TPU v7x, 32 devices: a whole 2x2x4 slice. The times are simulated.
32 devices in a mesh: group: 2 (over x), head: 16 (over z, y, core).
Axes of the slice: x: 2, y: 2, z: 4, core: 2. Of those that a mesh axis runs over, the one named last changes fastest.
Arguments:
- q_heads: bfloat16 [64, 24576], P('group', 'head'), parts along dimension 0, may hold values from -16 to 16
- w_absorb: bfloat16 [128, 128, 512], P('head'), may hold values from -0.5 to 0.5
- w_value: bfloat16 [128, 512, 128], P('head'), may hold values from -0.25 to 0.25
- w_out: bfloat16 [16384, 7168], P('head'), may hold values from -0.1875 to 0.1875
- latent_cache: bfloat16 [64, 128, 576], P(('group', 'head')), parts along dimension 0, may hold values from -6 to 6
- ctx_blocks: int32 [16], P('group'), parts along dimension 0, may hold values from 1 to 8, 32 in all
- block_table: int32 [16, 8], P('group'), parts along dimension 0, may hold values from 0 to 31, as said below
- owner: int32 [16], P('group'), parts along dimension 0, may hold values from 0 to 15, as said below
Outputs:
- attended: bfloat16 [128, 7168], P(('group', 'head')), parts along dimension 0
There are 2 independent parts, one for each index of `group`. A program takes and returns all parts, laid end to end along the dimension named above; an argument that names none is the same for every part. Nothing has to cross between parts.
Inputs may be any that keep to these rules, and one draw needn't show every extreme that they name: `block_table`: the entries of a row are distinct, every cache block appears exactly twice in the table; entries at or beyond a request's length are not used. `owner`: requests of a group have distinct decode devices.
All inputs are finite; a program needn't handle non-finite values.
Results may differ from a plain program's by a relative error of at most 0.0085.
Values may be sent and summed in bfloat16 or wider, within the bound.
No kernel may reach another device: no remote copies, remote signals or barrier semaphores. Data moves between devices by JAX's collectives and lax.ppermute only.
A program may use at most 128 MiB of HBM per device.

v0:
```python
import math

import jax
import jax.numpy as jnp
from jax import lax
from jax.sharding import PartitionSpec as P


def attend_group(gathered, queries, tables, lengths, kv_rank, score_scale):
    group_size, step_count, heads_here, row_width = queries.shape
    max_blocks = tables.shape[1]
    block_rows = gathered.shape[1]
    key_rows = gathered[tables].reshape(group_size, max_blocks * block_rows, row_width)
    scores = (
        jnp.einsum("gshc,gtc->gsht", queries, key_rows, preferred_element_type=jnp.float32)
        * score_scale
    )
    offsets = jnp.arange(max_blocks * block_rows, dtype=jnp.int32)
    step_ids = jnp.arange(step_count, dtype=jnp.int32)
    limits = lengths[:, None] * block_rows - (step_count - 1 - step_ids)[None, :]
    visible = offsets[None, None, :] < limits[:, :, None]
    scores = jnp.where(visible[:, :, None, :], scores, -jnp.inf)
    weights = jax.nn.softmax(scores, axis=-1).astype(jnp.bfloat16)
    latent_out = jnp.einsum(
        "gsht,gtc->gshc", weights, key_rows[:, :, :kv_rank], preferred_element_type=jnp.float32
    )
    return latent_out.astype(jnp.bfloat16)


def local(q_heads, w_absorb, w_value, w_out, latent_cache, ctx_blocks, block_table, owner):
    heads_here = w_absorb.shape[0]
    nope_width = w_absorb.shape[1]
    kv_rank = w_absorb.shape[2]
    row_count = q_heads.shape[0]
    head_width = q_heads.shape[1] // heads_here
    requests = block_table.shape[0]
    max_blocks = block_table.shape[1]
    step_count = row_count // requests
    row_width = latent_cache.shape[2]
    score_scale = head_width ** (-0.5)
    queries = q_heads.reshape(row_count, heads_here, head_width)
    q_latent = jnp.einsum(
        "rhn,hnc->rhc", queries[:, :, :nope_width], w_absorb, preferred_element_type=jnp.float32
    ).astype(jnp.bfloat16)
    q_full = jnp.concatenate([q_latent, queries[:, :, nope_width:]], axis=2)
    gathered = lax.all_gather(latent_cache, "head", axis=0, tiled=True)
    per_group = math.gcd(requests, 8)
    grouped = (
        q_full.reshape(requests // per_group, per_group, step_count, heads_here, row_width),
        block_table.reshape(requests // per_group, per_group, max_blocks),
        ctx_blocks.reshape(requests // per_group, per_group),
    )

    def attend_members(members):
        return attend_group(gathered, members[0], members[1], members[2], kv_rank, score_scale)

    latent_out = lax.map(attend_members, grouped).reshape(row_count, heads_here, kv_rank)
    value_out = jnp.einsum(
        "rhc,hcv->rhv", latent_out, w_value, preferred_element_type=jnp.float32
    ).astype(jnp.bfloat16)
    head_out = value_out.reshape(row_count, heads_here * w_value.shape[2])
    step_ids = jnp.arange(step_count, dtype=jnp.int32)
    slot_index = (owner[:, None] * step_count + step_ids[None, :]).reshape(row_count)
    targets = jnp.arange(lax.axis_size("head") * step_count, dtype=jnp.int32)
    picker = (targets[:, None] == slot_index[None, :]).astype(jnp.bfloat16)
    chosen = jnp.dot(picker, head_out, preferred_element_type=jnp.float32).astype(jnp.bfloat16)
    summed = lax.psum_scatter(
        jnp.dot(chosen, w_out, preferred_element_type=jnp.float32),
        "head",
        scatter_dimension=0,
        tiled=True,
    )
    return summed.astype(jnp.bfloat16)


def solution(mesh):
    return jax.shard_map(
        local,
        mesh=mesh,
        in_specs=(
            P("group", "head"),
            P("head", None, None),
            P("head", None, None),
            P("head", None),
            P(("group", "head"), None, None),
            P("group"),
            P("group", None),
            P("group"),
        ),
        out_specs=P(("group", "head"), None),
        check_vma=False,
    )
```

profile of v0, /device:TPU:0, one launch (start us, length us, event | category | flops | bytes accessed | tf_op | source)
XLA Modules:
  0.0 188.9 jit_solution(13481450215261871668)
XLA Ops:
  6.5 0.0 copy-start
  6.5 0.0 all-gather.2.cloned.1.call-start
  6.5 0.7 all-gather.2.cloned.1.call-update
  7.3 1.1 reshape.77
  8.4 0.7 compare_select_fusion
  9.0 0.1 reshape.83
  9.1 0.0 copy-done
  9.2 0.3 fusion.6
  9.5 0.1 copy.29
  9.6 0.7 broadcast_multiply_fusion.1
  10.2 0.1 iota_add_fusion
  10.3 0.1 add.31
  10.4 1.2 dynamic-slice.2
  12.3 0.7 broadcast_multiply_fusion
  13.0 0.1 broadcast_subtract_fusion
  13.0 0.1 iota_compare_fusion
  13.2 52.6 %all-gather.2.cloned.1.call-done = bf16[32,128,576]{1,2,0:T(8,128)(2,1)} async-done(((bf16[2,128,576]{1,2,0:T(8,128)(2,1)}), bf16[32,128,576]{1,2,0:T(8,128)(2,1)}) %all-gather.2.cloned.1.call-update) | async-done | bytes 4718608 | tf_op jit(solution)/shard_map/all_gather | solution.py:46
  65.8 8.4 %gather_fusion = bf16[64,128,576]{1,2,0:T(8,128)(2,1)} fusion(bf16[32,128,576]{1,2,0:T(8,128)(2,1)} %all-gather.2.cloned.1.call-done, s32[1024]{0:T(1024)S(1)} %pad_clamp_fusion), kind=kCustom, calls=%fused_computation | custom fusion | bytes 18874624 | tf_op jit(solution)/shard_map/while/body/eval_jaxpr/gather | solution.py:13
  74.2 14.1 %copy.22 = bf16[64,128,576]{2,1,0:T(8,128)(2,1)} copy(bf16[64,128,576]{1,2,0:T(8,128)(2,1)} %gather_fusion) | data formatting | bytes 18874368 | tf_op jit(solution)/shard_map/while/body/eval_jaxpr/gather | solution.py:13
  88.2 7.3 %fusion.18 = (f32[8,4,8]{2,1,0:T(4,128)S(1)}, f32[8,4,8,1024]{3,2,1,0:T(8,128)S(1)}) fusion(bf16[8,4,8,576]{3,2,1,0:T(8,128)(2,1)S(1)} %bitcast.31, bf16[8,1024,576,1]{2,1,3,0:T(8,128)(2,1)} %bitcast.29, pred[8,4,1024]{2,1,0:T(4,128)(4,1)S(1)} %iota_compare_fusion), kind=kOutput, calls=%fused_computation.33 | convolution fusion | flops 303039488 | bytes 10814464 | tf_op jit(solution)/shard_map/while/body/eval_jaxpr/sub | solution.py:23
  95.6 0.0 copy-start.1
  95.6 5.0 %fusion.5 = bf16[8,4,8,512]{3,2,1,0:T(8,128)(2,1)S(1)} fusion(bf16[8,1024,576]{2,1,0:T(8,128)(2,1)} %bitcast.30, f32[8,4,8,1024]{3,2,1,0:T(8,128)S(1)} %get-tuple-element.16, f32[8,4,8]{2,1,0:T(4,128)S(1)} %get-tuple-element.15), kind=kOutput, calls=%fused_computation.8 | convolution fusion | flops 269090816 | bytes 9700352 | tf_op jit(solution)/shard_map/while/body/eval_jaxpr/gsht,gtc->gshc/dot_general | solution.py:24
  100.6 0.0 copy-done.1
  100.6 0.3 fusion.8
  100.9 6.7 %fusion.7 = f32[64,7168]{1,0:T(8,128)S(1)} fusion(bf16[1024,7168]{1,0:T(8,128)(2,1)} %param.11, bf16[8,4,8,128]{3,2,1,0:T(8,128)(2,1)S(1)} %fusion.8, s32[32]{0:T(128)S(1)} %add.31), kind=kOutput, calls=%fused_computation.12 | convolution fusion | flops 943785984 | bytes 16580736 | tf_op jit(solution)/shard_map/dot_general | solution.py:68
  107.6 72.9 %all-reduce.2 = bf16[64,7168]{1,0:T(8,128)(2,1)} all-reduce(f32[64,7168]{1,0:T(8,128)S(1)} %fusion.7), channel_id=2, replica_groups=mesh['group'=2,'head'=16] {'head'}, use_global_device_ids=true, to_apply=%region_2.3.clone | all-reduce | flops 458752 | bytes 2752512
  180.5 1.6 dynamic-slice_convert_fusion
  (6 shorter events, 0.1 us)
Async XLA Ops:
  6.5 2.6 %copy-start = (bf16[8,128,512]{2,1,0:T(8,128)(2,1)S(1)}, bf16[8,128,512]{2,1,0:T(8,128)(2,1)}, u32[]{:S(2)}) copy-start(bf16[8,128,512]{2,1,0:T(8,128)(2,1)} %param.9) | copy-start | bytes 3145732
  6.5 59.2 %all-gather.2.cloned.1.call-start = ((), (), s32[]{:S(2)}) async-start(), calls=%async_computation | async-start | bytes 5013504 | tf_op jit(solution)/shard_map/all_gather | solution.py:46
  95.6 5.0 %copy-start.1 = (bf16[8,512,128]{2,1,0:T(8,128)(2,1)S(1)}, bf16[8,512,128]{2,1,0:T(8,128)(2,1)}, u32[]{:S(2)}) copy-start(bf16[8,512,128]{2,1,0:T(8,128)(2,1)} %param.10) | copy-start | bytes 3145732
Sparse Core Ops, SparseCore 0:
  9.6 56.0 all-gather.1
where the time goes:
time: 189 us
  blocking collectives  72.9 us (39%)
  waiting for transfers between devices  53.3 us (28%)
  local copies, waits for them, and re-layouts  26.6 us (14%)
  matrix products  19.6 us (10%)
  between operations  14.2 us (8%)
  other arithmetic  2.31 us (1%)
    unnamed x1, blocking collectives  72.9 us
    all_gather x1, waiting for transfers between devices, local(): gathered = lax.all_gather(latent_cache, 'head', axis=0, tiled=True)  52.6 us
    gather x2, local copies, waits for them, and re-layouts, attend_group(): gathered[tables].reshape(group_size, max_blocks * block_rows, row_width)  22.5 us
    sub x1, matrix products, attend_group(): weights = jax.nn.softmax(scores, axis=-1).astype(jnp.bfloat16)  7.32 us
    dot_general x1, matrix products, local(): jnp.dot(chosen, w_out, preferred_element_type=jnp.float32)  6.69 us
    dot_general x1, matrix products, attend_group(): jnp.einsum('gsht,gtc->gshc', weights, key_rows[:, :, :kv_rank], preferred...  5 us
  transfers between devices with their start and end apart: 1, of which 1 were waited for; matrix products, arithmetic and copies ran while one was open for 3% of the time, Pallas kernels for 0%

commit v1 on v0

v1 whole, which is shorter than its diff:
```python
import functools

import jax
import jax.numpy as jnp
import numpy as np
from jax import lax
from jax.experimental import pallas as pl
from jax.experimental.pallas import tpu as pltpu
from jax.sharding import PartitionSpec as P

OUT_TILE = 1024
LANES = 128


def ring_of(chips):
    if chips == 8:
        return [0, 2, 4, 6, 7, 5, 3, 1]
    return list(range(chips))


def gather_pieces(keys, chips):
    ring = ring_of(chips)
    up = [
        (ring[i] * 2 + core, ring[(i + 1) % chips] * 2 + core)
        for i in range(chips)
        for core in range(2)
    ]
    down = [(b, a) for a, b in up]
    swap = [(i, i ^ 1) for i in range(2 * chips)]
    half = keys.shape[0] // 2
    lower, upper = keys[:half], keys[half:]
    ups, downs = [lower, upper], [lower, upper]
    pieces, places = [lower, upper], [(0, 0), (0, 1)]
    for hop in range(1, chips // 2 + 1):
        last = hop == chips // 2
        for part in range(2):
            if not last or part == 0:
                ups[part] = lax.ppermute(ups[part], "head", up)
                pieces.append(ups[part])
                places.append((-hop, part))
            if not last or part == 1:
                downs[part] = lax.ppermute(downs[part], "head", down)
                pieces.append(downs[part])
                places.append((hop, part))
    own = len(pieces)
    pieces = pieces + [lax.ppermute(p, "head", swap) for p in pieces]
    places = [(hop, part, 0) for hop, part in places] + [(hop, part, 1) for hop, part in places]
    return pieces, places


def slots_by_device(places, chips, half):
    ring = ring_of(chips)
    position = {chip: i for i, chip in enumerate(ring)}
    table = np.zeros((2 * chips, 4 * chips * half), np.int32)
    for device in range(2 * chips):
        for index, (hop, part, flip) in enumerate(places):
            chip = ring[(position[device // 2] + hop) % chips]
            source = chip * 2 + (device % 2 ^ flip)
            for i in range(half):
                table[device, (source * 2 + part) * half + i] = index * half + i
    return table


def attend_kernel(
    piece_count, half, heads, steps, scale,
    me_ref, length_ref, table_ref, owner_ref, slot_ref, query_ref, value_ref, out_w_ref, *rest,
):
    pieces = rest[:piece_count]
    (away_ref, keep_ref, cache, weight, scores, top, total, latent, head_rows,
     use_request, use_block, use_last, cache_sems, weight_sems) = rest[piece_count:]
    requests, row_block, _ = query_ref.shape
    kv_rank = value_ref.shape[1]
    v_width = value_ref.shape[2]
    block_rows = cache.shape[2]
    rows = requests * steps
    tiles, _, tile = weight.shape
    uses = scores.shape[0]

    piece_copies = [
        pltpu.make_async_copy(p, cache.at[pl.ds(i * half, half)], cache_sems.at[i])
        for i, p in enumerate(pieces)
    ]
    for copy in piece_copies:
        copy.start()
    weight_copies = [
        pltpu.make_async_copy(out_w_ref.at[:, pl.ds(i * tile, tile)], weight.at[i], weight_sems.at[i])
        for i in range(tiles)
    ]
    for copy in weight_copies:
        copy.start()

    def list_request(r, at):
        count = length_ref[r]

        def list_block(j, _):
            use_request[at + j] = r
            use_block[at + j] = slot_ref[table_ref[r, j]]
            use_last[at + j] = (j == count - 1).astype(jnp.int32)
            return 0

        lax.fori_loop(0, count, list_block, 0)
        return at + count

    lax.fori_loop(0, requests, list_request, 0)

    top[...] = jnp.full_like(top, -jnp.inf)
    total[...] = jnp.zeros_like(total)
    latent[...] = jnp.zeros_like(latent)
    column = lax.broadcasted_iota(jnp.int32, (row_block, block_rows), 1)
    step = lax.broadcasted_iota(jnp.int32, (row_block, block_rows), 0) // heads
    hidden = steps - 1 - step
    for copy in piece_copies:
        copy.wait()

    def score(u, _):
        r = use_request[u]
        s = jnp.dot(query_ref[r], cache[use_block[u]], preferred_element_type=jnp.float32) * scale
        s = jnp.where(column + hidden * use_last[u] < block_rows, s, -jnp.inf)
        scores[u] = s
        top[r] = jnp.maximum(top[r], s)
        return 0

    lax.fori_loop(0, uses, score, 0, unroll=4)

    def peak(r, _):
        top[r] = jnp.broadcast_to(jnp.max(top[r], axis=1, keepdims=True), (row_block, block_rows))
        return 0

    lax.fori_loop(0, requests, peak, 0, unroll=4)

    def gather(u, _):
        r = use_request[u]
        p = jnp.exp(scores[u] - top[r])
        total[r] += p
        mixed = lax.dot_general(
            p.astype(jnp.bfloat16),
            cache[use_block[u], :kv_rank],
            (((1,), (1,)), ((), ())),
            preferred_element_type=jnp.float32,
        )
        at = pl.ds(pl.multiple_of(r * row_block, row_block), row_block)
        for c in range(kv_rank // LANES):
            latent[c, at] += mixed[:, c * LANES : (c + 1) * LANES]
        return 0

    lax.fori_loop(0, uses, gather, 0, unroll=4)

    def normalise(r, _):
        at = pl.ds(pl.multiple_of(r * row_block, row_block), row_block)
        norm = jnp.sum(total[r], axis=1, keepdims=True)
        for c in range(kv_rank // LANES):
            latent[c, at] = latent[c, at] / norm
        return 0

    lax.fori_loop(0, requests, normalise, 0, unroll=4)

    for h in range(heads):
        mine = jnp.concatenate(
            [latent[c, pl.ds(h, rows, stride=heads)] for c in range(kv_rank // LANES)], axis=1
        ).astype(jnp.bfloat16)
        head_rows[:, h * v_width : (h + 1) * v_width] = jnp.dot(
            mine, value_ref[h], preferred_element_type=jnp.float32
        ).astype(jnp.bfloat16)

    half_rows = away_ref.shape[0]
    chips = half_rows // steps
    me = me_ref[0]
    target = lax.broadcasted_iota(jnp.int32, (2 * half_rows, rows), 0)
    origin = lax.broadcasted_iota(jnp.int32, (2 * half_rows, rows), 1)

    def place(r, picked):
        apart = owner_ref[r] ^ me
        order = (apart & 1) * chips + ((apart >> 1) & 1) * (chips // 2) + (apart >> 2)
        shifted = origin - r * steps
        hit = (target - order * steps == shifted) & (shifted >= 0) & (shifted < steps)
        return jnp.where(hit, 1.0, picked)

    picker = lax.fori_loop(0, requests, place, jnp.zeros((2 * half_rows, rows), jnp.float32))
    placed = jnp.dot(
        picker.astype(jnp.bfloat16), head_rows[...], preferred_element_type=jnp.float32
    ).astype(jnp.bfloat16)
    for i in range(tiles):
        weight_copies[i].wait()
        result = jnp.dot(placed, weight[i], preferred_element_type=jnp.float32).astype(jnp.bfloat16)
        keep_ref[:, i * tile : (i + 1) * tile] = result[:half_rows]
        away_ref[:, i * tile : (i + 1) * tile] = result[half_rows:]


def local(q_heads, w_absorb, w_value, w_out, latent_cache, ctx_blocks, block_table, owner):
    heads, nope_width, kv_rank = w_absorb.shape
    row_count = q_heads.shape[0]
    head_width = q_heads.shape[1] // heads
    requests, max_blocks = block_table.shape
    steps = row_count // requests
    devices = lax.axis_size("head")
    chips = devices // 2
    blocks_here, block_rows, row_width = latent_cache.shape
    half = blocks_here // 2
    width = w_out.shape[1]
    v_width = w_value.shape[2]
    me = lax.axis_index("head").astype(jnp.int32)

    pieces, places = gather_pieces(jnp.swapaxes(latent_cache, 1, 2), chips)
    slots = jnp.asarray(slots_by_device(places, chips, half))[me]

    queries = q_heads.reshape(row_count, heads, head_width)
    q_latent = jnp.einsum(
        "rhn,hnc->rhc", queries[:, :, :nope_width], w_absorb, preferred_element_type=jnp.float32
    ).astype(jnp.bfloat16)
    q_full = jnp.concatenate([q_latent, queries[:, :, nope_width:]], axis=2)
    q_full = q_full.reshape(requests, steps * heads, row_width)

    uses = blocks_here * devices
    row_block = steps * heads
    tiles = width // OUT_TILE
    smem = pl.BlockSpec(memory_space=pltpu.SMEM)
    vmem = pl.BlockSpec(memory_space=pltpu.VMEM)
    anywhere = pl.BlockSpec(memory_space=pl.ANY)
    part = jax.ShapeDtypeStruct((chips * steps, width), jnp.bfloat16)
    away, keep = pl.pallas_call(
        functools.partial(
            attend_kernel, len(pieces), half, heads, steps, float(head_width) ** -0.5
        ),
        out_shape=(part, part),
        in_specs=[smem] * 5 + [vmem] * 2 + [anywhere] * (1 + len(pieces)),
        out_specs=(vmem, vmem),
        scratch_shapes=[
            pltpu.VMEM((uses, row_width, block_rows), jnp.bfloat16),
            pltpu.VMEM((tiles, w_out.shape[0], OUT_TILE), jnp.bfloat16),
            pltpu.VMEM((uses, row_block, block_rows), jnp.float32),
            pltpu.VMEM((requests, row_block, block_rows), jnp.float32),
            pltpu.VMEM((requests, row_block, block_rows), jnp.float32),
            pltpu.VMEM((kv_rank // LANES, requests * row_block, LANES), jnp.float32),
            pltpu.VMEM((row_count, heads * v_width), jnp.bfloat16),
            pltpu.SMEM((uses,), jnp.int32),
            pltpu.SMEM((uses,), jnp.int32),
            pltpu.SMEM((uses,), jnp.int32),
            pltpu.SemaphoreType.DMA((len(pieces),)),
            pltpu.SemaphoreType.DMA((tiles,)),
        ],
        compiler_params=pltpu.CompilerParams(vmem_limit_bytes=48 * 1024 * 1024),
        name="attend_and_project",
    )(me.reshape(1), ctx_blocks, block_table, owner, slots, q_full, w_value, w_out, *pieces)

    def exchange(x, distance):
        return lax.ppermute(x, "head", [(i, i ^ distance) for i in range(devices)])

    def add(x, *others):
        total = x.astype(jnp.float32)
        for other in others:
            total = total + other.astype(jnp.float32)
        return total.astype(jnp.bfloat16)

    both = add(keep, exchange(away, 1))
    middle = both.shape[0] // 2
    line = add(both[:middle], exchange(both[middle:], 2))
    received = [
        exchange(line[k * steps : (k + 1) * steps], 4 * k) for k in range(1, chips // 2)
    ]
    return add(line[:steps], *received)


def solution(mesh):
    return jax.shard_map(
        local,
        mesh=mesh,
        in_specs=(
            P("group", "head"),
            P("head", None, None),
            P("head", None, None),
            P("head", None),
            P(("group", "head"), None, None),
            P("group"),
            P("group", None),
            P("group"),
        ),
        out_specs=P(("group", "head"), None),
        check_vma=False,
    )
```

time: 189 us -> 84.2 us (0.45)
  blocking collectives: 72.9 us -> 0 us
  waiting for transfers between devices: 53.3 us -> 25.4 us
  starting transfers between devices: 0.01 us -> 25 us
  matrix products: 19.6 us -> 0.26 us
  Pallas kernels: 0 us -> 18.8 us
  between operations: 14.2 us -> 0.18 us
  local copies, waits for them, and re-layouts: 26.6 us -> 12.6 us
    unnamed x1 -> x0, blocking collectives: 72.9 us -> none
    all_gather x1 -> x0, waiting for transfers between devices: 52.6 us -> none  [local(): gathered = lax.all_gather(latent_cache, 'head', axis=0, tiled=True)]
    ppermute x0 -> x35, waiting for transfers between devices: none -> 25.4 us  [the longest x5 13.4 us: exchange(): return lax.ppermute(x, 'head', [(i, i ^ distance) for i in range(devices)])]
    ppermute x0 -> x35, starting transfers between devices: none -> 25 us  [the longest x7 11.8 us: gather_pieces(): downs[part] = lax.ppermute(downs[part], 'head', down)]
    gather x2 -> x0, local copies, waits for them, and re-layouts: 22.5 us -> none  [attend_group(): gathered[tables].reshape(group_size, max_blocks * block_rows, row_width)]
    pallas_call x0 -> x1, Pallas kernels: none -> 18.8 us  [local(): pl.pallas_call(functools.partial(attend_kernel, len(pieces), half, heads,...]
    dot_general x3 -> x0, matrix products: 12 us -> none  [the longest x1 6.69 us: local(): jnp.dot(chosen, w_out, preferred_element_type=jnp.float32)]
    sub x1 -> x0, matrix products: 7.32 us -> none  [attend_group(): weights = jax.nn.softmax(scores, axis=-1).astype(jnp.bfloat16)]
  transfers between devices with their start and end apart: 1 -> 35, of which waited for: 1 -> 15; matrix products, arithmetic and copies ran while one was open for 3% -> 5% of each run, Pallas kernels for 0% -> 0%
where the time goes in v1:
time: 84.2 us; the launch traced here: 83.8 us
  waiting for transfers between devices  25.4 us (30%)
  starting transfers between devices  25 us (30%)
  Pallas kernels  18.8 us (22%)
  local copies, waits for them, and re-layouts  12.6 us (15%)
  other arithmetic  1.6 us (2%)
    pallas_call x1, Pallas kernels, local(): pl.pallas_call(functools.partial(attend_kernel, len(pieces), half, heads,...  18.8 us
    ppermute x5, waiting for transfers between devices, exchange(): return lax.ppermute(x, 'head', [(i, i ^ distance) for i in range(devices)])  13.4 us
    ppermute x7, starting transfers between devices, gather_pieces(): downs[part] = lax.ppermute(downs[part], 'head', down)  11.8 us
    unnamed x29, local copies, waits for them, and re-layouts  8.56 us
    ppermute x7, waiting for transfers between devices, gather_pieces(): ups[part] = lax.ppermute(ups[part], 'head', up)  6.83 us
    ppermute x5, starting transfers between devices, exchange(): return lax.ppermute(x, 'head', [(i, i ^ distance) for i in range(devices)])  5.97 us
    ppermute x7, starting transfers between devices, gather_pieces(): ups[part] = lax.ppermute(ups[part], 'head', up)  5.91 us
    ppermute x7, waiting for transfers between devices, gather_pieces(): downs[part] = lax.ppermute(downs[part], 'head', down)  5.12 us
  transfers between devices with their start and end apart: 35, of which 15 were waited for; matrix products, arithmetic and copies ran while one was open for 5% of the time, Pallas kernels for 0%

profile of v1, /device:TPU:0, one launch (start us, length us, event | category | flops | bytes accessed | tf_op | source)
XLA Modules:
  0.0 83.8 jit_solution(14828427042718709537)
XLA Ops:
  0.0 1.1 %fusion.2 = (bf16[1,576,128]{2,1,0:T(8,128)(2,1)S(1)}, bf16[1,576,128]{2,1,0:T(8,128)(2,1)S(1)}) fusion(bf16[2,576,128]{2,1,0:T(8,128)(2,1)} %bitcast.9), kind=kLoop, calls=%fused_computation.8 | loop fusion | bytes 589824 | tf_op jit(solution)/shard_map/slice | solution.py:31
  1.1 0.5 collective-permute-start.15
  1.6 2.6 %collective-permute-start.3 = (bf16[1,576,128]{2,1,0:T(8,128)(2,1)S(1)}, bf16[1,576,128]{2,1,0:T(8,128)(2,1)S(1)}, u32[]{:S(2)}, u32[]{:S(2)}) collective-permute-start(bf16[1,576,128]{2,1,0:T(8,128)(2,1)S(1)} %get-tuple-element.9.rest_1_), channel_id=1, source_target_pairs={{4,0},{5,1},{8,4},{9,5},{12,8},{13,9},{14,12},{15,13},{10,14},{11,... | collective-permute-start | bytes 442376 | tf_op jit(solution)/shard_map/ppermute | solution.py:42
  4.4 1.8 %collective-permute-start.1 = (bf16[1,576,128]{2,1,0:T(8,128)(2,1)S(1)}, bf16[1,576,128]{2,1,0:T(8,128)(2,1)S(1)}, u32[]{:S(2)}, u32[]{:S(2)}) collective-permute-start(bf16[1,576,128]{2,1,0:T(8,128)(2,1)S(1)} %get-tuple-element.10.rest_0_), channel_id=1, source_target_pairs={{4,0},{5,1},{8,4},{9,5},{12,8},{13,9},{14,12},{15,13},{10,14},{11,... | collective-permute-start | bytes 442376 | tf_op jit(solution)/shard_map/ppermute | solution.py:42
  6.5 2.5 %collective-permute-done.3.rest_5_ = bf16[1,576,128]{2,1,0:T(8,128)(2,1)S(1)} collective-permute-done((bf16[1,576,128]{2,1,0:T(8,128)(2,1)S(1)}, bf16[1,576,128]{2,1,0:T(8,128)(2,1)S(1)}, u32[]{:S(2)}, u32[]{:S(2)}) %collective-permute-start.3) | collective-permute-done | bytes 147488 | tf_op jit(solution)/shard_map/ppermute | solution.py:42
  9.0 1.9 %collective-permute-done.2.rest_4_ = bf16[1,576,128]{2,1,0:T(8,128)(2,1)S(1)} collective-permute-done((bf16[1,576,128]{2,1,0:T(8,128)(2,1)S(1)}, bf16[1,576,128]{2,1,0:T(8,128)(2,1)S(1)}, u32[]{:S(2)}, u32[]{:S(2)}) %collective-permute-start.2) | collective-permute-done | bytes 147488 | tf_op jit(solution)/shard_map/ppermute | solution.py:38
  10.9 1.6 %collective-permute-start.7 = (bf16[1,576,128]{2,1,0:T(8,128)(2,1)S(1)}, bf16[1,576,128]{2,1,0:T(8,128)(2,1)S(1)}, u32[]{:S(2)}, u32[]{:S(2)}) collective-permute-start(bf16[1,576,128]{2,1,0:T(8,128)(2,1)S(1)} %collective-permute-done.3.rest_5_), channel_id=1, source_target_pairs={{4,0},{5,1},{8,4},{9,5},{12,8},{13,9},{14,12},{15,13},{10,14},{11,... | collective-permute-start | bytes 442376 | tf_op jit(solution)/shard_map/ppermute | solution.py:42
  12.5 1.1 %collective-permute-start.6 = (bf16[1,576,128]{2,1,0:T(8,128)(2,1)S(1)}, bf16[1,576,128]{2,1,0:T(8,128)(2,1)S(1)}, u32[]{:S(2)}, u32[]{:S(2)}) collective-permute-start(bf16[1,576,128]{2,1,0:T(8,128)(2,1)S(1)} %collective-permute-done.2.rest_4_), channel_id=1, source_target_pairs={{0,4},{1,5},{4,8},{5,9},{8,12},{9,13},{12,14},{13,15},{14,10},{15,... | collective-permute-start | bytes 442376 | tf_op jit(solution)/shard_map/ppermute | solution.py:38
  13.6 1.2 %collective-permute-start.5 = (bf16[1,576,128]{2,1,0:T(8,128)(2,1)S(1)}, bf16[1,576,128]{2,1,0:T(8,128)(2,1)S(1)}, u32[]{:S(2)}, u32[]{:S(2)}) collective-permute-start(bf16[1,576,128]{2,1,0:T(8,128)(2,1)S(1)} %collective-permute-done.1.rest_3_), channel_id=1, source_target_pairs={{4,0},{5,1},{8,4},{9,5},{12,8},{13,9},{14,12},{15,13},{10,14},{11,... | collective-permute-start | bytes 442376 | tf_op jit(solution)/shard_map/ppermute | solution.py:42
  14.9 1.2 %collective-permute-done.7.rest_9_ = bf16[1,576,128]{2,1,0:T(8,128)(2,1)S(1)} collective-permute-done((bf16[1,576,128]{2,1,0:T(8,128)(2,1)S(1)}, bf16[1,576,128]{2,1,0:T(8,128)(2,1)S(1)}, u32[]{:S(2)}, u32[]{:S(2)}) %collective-permute-start.7) | collective-permute-done | bytes 147488 | tf_op jit(solution)/shard_map/ppermute | solution.py:42
  16.0 1.2 %collective-permute-start.4 = (bf16[1,576,128]{2,1,0:T(8,128)(2,1)S(1)}, bf16[1,576,128]{2,1,0:T(8,128)(2,1)S(1)}, u32[]{:S(2)}, u32[]{:S(2)}) collective-permute-start(bf16[1,576,128]{2,1,0:T(8,128)(2,1)S(1)} %collective-permute-done.rest_2_), channel_id=1, source_target_pairs={{0,4},{1,5},{4,8},{5,9},{8,12},{9,13},{12,14},{13,15},{14,10},{15,... | collective-permute-start | bytes 442376 | tf_op jit(solution)/shard_map/ppermute | solution.py:38
  17.2 1.5 %collective-permute-done.6.rest_8_ = bf16[1,576,128]{2,1,0:T(8,128)(2,1)S(1)} collective-permute-done((bf16[1,576,128]{2,1,0:T(8,128)(2,1)S(1)}, bf16[1,576,128]{2,1,0:T(8,128)(2,1)S(1)}, u32[]{:S(2)}, u32[]{:S(2)}) %collective-permute-start.6) | collective-permute-done | bytes 147488 | tf_op jit(solution)/shard_map/ppermute | solution.py:38
  18.7 1.6 %collective-permute-start.11 = (bf16[1,576,128]{2,1,0:T(8,128)(2,1)S(1)}, bf16[1,576,128]{2,1,0:T(8,128)(2,1)}, u32[]{:S(2)}, u32[]{:S(2)}) collective-permute-start(bf16[1,576,128]{2,1,0:T(8,128)(2,1)S(1)} %collective-permute-done.7.rest_9_), channel_id=1, source_target_pairs={{4,0},{5,1},{8,4},{9,5},{12,8},{13,9},{14,12},{15,13},{10,14},{11,... | collective-permute-start | bytes 442376 | tf_op jit(solution)/shard_map/ppermute | solution.py:42
  20.6 1.0 %collective-permute-start.10 = (bf16[1,576,128]{2,1,0:T(8,128)(2,1)S(1)}, bf16[1,576,128]{2,1,0:T(8,128)(2,1)}, u32[]{:S(2)}, u32[]{:S(2)}) collective-permute-start(bf16[1,576,128]{2,1,0:T(8,128)(2,1)S(1)} %collective-permute-done.6.rest_8_), channel_id=1, source_target_pairs={{0,4},{1,5},{4,8},{5,9},{8,12},{9,13},{12,14},{13,15},{14,10},{15,... | collective-permute-start | bytes 442376 | tf_op jit(solution)/shard_map/ppermute | solution.py:38
  21.5 0.8 collective-permute-done.4.rest_6_
  22.3 0.7 copy-done.5
  23.0 1.2 %collective-permute-start.8 = (bf16[1,576,128]{2,1,0:T(8,128)(2,1)S(1)}, bf16[1,576,128]{2,1,0:T(8,128)(2,1)}, u32[]{:S(2)}, u32[]{:S(2)}) collective-permute-start(bf16[1,576,128]{2,1,0:T(8,128)(2,1)S(1)} %collective-permute-done.4.rest_6_), channel_id=1, source_target_pairs={{0,4},{1,5},{4,8},{5,9},{8,12},{9,13},{12,14},{13,15},{14,10},{15,... | collective-permute-start | bytes 442376 | tf_op jit(solution)/shard_map/ppermute | solution.py:38
  24.2 1.0 %reshape.10 = bf16[32,8,192]{2,1,0:T(8,128)(2,1)S(1)} reshape(bf16[32,1536]{1,0:T(8,128)(2,1)} %param.9) | data formatting | bytes 196608 | tf_op jit(solution)/shard_map/reshape | solution.py:206
  25.3 1.4 %collective-permute-start.9 = (bf16[1,576,128]{2,1,0:T(8,128)(2,1)S(1)}, bf16[1,576,128]{2,1,0:T(8,128)(2,1)}, u32[]{:S(2)}, u32[]{:S(2)}) collective-permute-start(bf16[1,576,128]{2,1,0:T(8,128)(2,1)S(1)} %collective-permute-done.5.rest_7_), channel_id=1, source_target_pairs={{4,0},{5,1},{8,4},{9,5},{12,8},{13,9},{14,12},{15,13},{10,14},{11,... | collective-permute-start | bytes 442376 | tf_op jit(solution)/shard_map/ppermute | solution.py:42
  27.2 1.6 %collective-permute-start.13 = (bf16[1,576,128]{2,1,0:T(8,128)(2,1)}, bf16[1,576,128]{2,1,0:T(8,128)(2,1)}, u32[]{:S(2)}, u32[]{:S(2)}) collective-permute-start(bf16[1,576,128]{2,1,0:T(8,128)(2,1)} %collective-permute-done.11.rest_13_), channel_id=1, source_target_pairs={{4,0},{5,1},{8,4},{9,5},{12,8},{13,9},{14,12},{15,13},{10,14},{11,... | collective-permute-start | bytes 442376 | tf_op jit(solution)/shard_map/ppermute | solution.py:42
  28.8 1.1 %collective-permute-done.8.rest_10_ = bf16[1,576,128]{2,1,0:T(8,128)(2,1)} collective-permute-done((bf16[1,576,128]{2,1,0:T(8,128)(2,1)S(1)}, bf16[1,576,128]{2,1,0:T(8,128)(2,1)}, u32[]{:S(2)}, u32[]{:S(2)}) %collective-permute-start.8) | collective-permute-done | bytes 147488 | tf_op jit(solution)/shard_map/ppermute | solution.py:38
  29.9 1.1 %collective-permute-start.12 = (bf16[1,576,128]{2,1,0:T(8,128)(2,1)}, bf16[1,576,128]{2,1,0:T(8,128)(2,1)}, u32[]{:S(2)}, u32[]{:S(2)}) collective-permute-start(bf16[1,576,128]{2,1,0:T(8,128)(2,1)} %collective-permute-done.8.rest_10_), channel_id=1, source_target_pairs={{0,4},{1,5},{4,8},{5,9},{8,12},{9,13},{12,14},{13,15},{14,10},{15,... | collective-permute-start | bytes 442376 | tf_op jit(solution)/shard_map/ppermute | solution.py:38
  31.3 0.9 %collective-permute-done.9.rest_11_ = bf16[1,576,128]{2,1,0:T(8,128)(2,1)} collective-permute-done((bf16[1,576,128]{2,1,0:T(8,128)(2,1)S(1)}, bf16[1,576,128]{2,1,0:T(8,128)(2,1)}, u32[]{:S(2)}, u32[]{:S(2)}) %collective-permute-start.9) | collective-permute-done | bytes 147488 | tf_op jit(solution)/shard_map/ppermute | solution.py:42
  32.1 0.6 copy-done.7
  33.3 0.7 copy-done.9
  34.0 0.6 collective-permute-done.13.rest_15_
  34.5 1.0 %collective-permute-done.12.rest_14_ = bf16[1,576,128]{2,1,0:T(8,128)(2,1)} collective-permute-done((bf16[1,576,128]{2,1,0:T(8,128)(2,1)}, bf16[1,576,128]{2,1,0:T(8,128)(2,1)}, u32[]{:S(2)}, u32[]{:S(2)}) %collective-permute-start.12) | collective-permute-done | bytes 147488 | tf_op jit(solution)/shard_map/ppermute | solution.py:38
  35.6 0.7 pad_maximum_fusion
  36.3 1.1 %copy.13 = bf16[32,8,576]{2,1,0:T(8,128)(2,1)S(1)} copy(bf16[32,8,576]{2,0,1:T(8,128)(2,1)} %pad_maximum_fusion) | data formatting | bytes 589824 | tf_op jit(solution)/shard_map/concatenate | solution.py:210
  37.4 0.7 dynamic-slice_bitcast_fusion.slot_ref
  38.2 0.9 %copy-done.2 = bf16[1,576,128]{2,1,0:T(8,128)(2,1)S(1)} copy-done((bf16[1,576,128]{2,1,0:T(8,128)(2,1)S(1)}, bf16[1,576,128]{2,1,0:T(8,128)(2,1)}, u32[]{:S(2)}) %copy-start.2) | copy-done | bytes 147480
  39.1 0.9 %copy-done.4 = bf16[1,576,128]{2,1,0:T(8,128)(2,1)S(1)} copy-done((bf16[1,576,128]{2,1,0:T(8,128)(2,1)S(1)}, bf16[1,576,128]{2,1,0:T(8,128)(2,1)}, u32[]{:S(2)}) %copy-start.4) | copy-done | bytes 147480
  40.0 0.9 %copy-done.6 = bf16[1,576,128]{2,1,0:T(8,128)(2,1)S(1)} copy-done((bf16[1,576,128]{2,1,0:T(8,128)(2,1)S(1)}, bf16[1,576,128]{2,1,0:T(8,128)(2,1)}, u32[]{:S(2)}) %copy-start.6) | copy-done | bytes 147480
  40.9 0.9 %copy-done.8 = bf16[1,576,128]{2,1,0:T(8,128)(2,1)S(1)} copy-done((bf16[1,576,128]{2,1,0:T(8,128)(2,1)S(1)}, bf16[1,576,128]{2,1,0:T(8,128)(2,1)}, u32[]{:S(2)}) %copy-start.8) | copy-done | bytes 147480
  41.8 0.9 %copy-done.10 = bf16[1,576,128]{2,1,0:T(8,128)(2,1)S(1)} copy-done((bf16[1,576,128]{2,1,0:T(8,128)(2,1)S(1)}, bf16[1,576,128]{2,1,0:T(8,128)(2,1)}, u32[]{:S(2)}) %copy-start.10) | copy-done | bytes 147480
  42.7 0.7 copy-done.11
  43.4 0.7 copy-done.12
  44.1 0.7 copy-done.13
  44.7 18.8 %attend_and_project.1 = (bf16[32,7168]{1,0:T(8,128)(2,1)S(1)}, bf16[32,7168]{1,0:T(8,128)(2,1)S(1)}) custom-call(s32[1]{0:T(128)} %bitcast.me_ref, s32[8]{0:T(128)S(1)} %copy-done.12, s32[8,8]{1,0:T(8,128)S(1)} %copy-done.11, s32[8]{0:T(128)S(1)} %copy-done.13, s32[32]{0:T(128)S(1)} %dynamic-slice_bitcast_fusion.slot_ref, bf16[8,32,576]{2,1,0:T(8,128)(2,1)S(1)} %bitcast.8, ...), custom_call_target="tpu_custom_call" | custom-call | tf_op jit(solution)/shard_map/attend_and_project/pallas_call | solution.py:220
  63.5 0.6 collective-permute-start.30
  64.1 1.4 %collective-permute-done.30 = bf16[32,7168]{1,0:T(8,128)(2,1)S(1)} collective-permute-done((bf16[32,7168]{1,0:T(8,128)(2,1)S(1)}, bf16[32,7168]{1,0:T(8,128)(2,1)S(1)}, u32[]{:S(2)}, u32[]{:S(2)}) %collective-permute-start.30) | collective-permute-done | bytes 458784 | tf_op jit(solution)/shard_map/ppermute | solution.py:246
  65.7 1.7 %collective-permute-start.31 = (bf16[16,7168]{1,0:T(8,128)(2,1)S(1)}, bf16[16,7168]{1,0:T(8,128)(2,1)S(1)}, u32[]{:S(2)}, u32[]{:S(2)}) collective-permute-start(bf16[16,7168]{1,0:T(8,128)(2,1)S(1)} %slice.45), channel_id=1, source_target_pairs={{0,2},{1,3},{2,0},{3,1},{4,6},{5,7},{6,4},{7,5},{8,10},{9,11},{10,... | collective-permute-start | bytes 688136 | tf_op jit(solution)/shard_map/ppermute | solution.py:246
  67.3 6.3 %collective-permute-done.31 = bf16[16,7168]{1,0:T(8,128)(2,1)S(1)} collective-permute-done((bf16[16,7168]{1,0:T(8,128)(2,1)S(1)}, bf16[16,7168]{1,0:T(8,128)(2,1)S(1)}, u32[]{:S(2)}, u32[]{:S(2)}) %collective-permute-start.31) | collective-permute-done | bytes 229408 | tf_op jit(solution)/shard_map/ppermute | solution.py:246
  73.8 1.2 %collective-permute-start.32 = (bf16[4,7168]{1,0:T(4,128)(2,1)S(1)}, bf16[4,7168]{1,0:T(4,128)(2,1)S(1)}, u32[]{:S(2)}, u32[]{:S(2)}) collective-permute-start(bf16[4,7168]{1,0:T(4,128)(2,1)S(1)} %get-tuple-element.11), channel_id=1, source_target_pairs={{0,4},{1,5},{2,6},{3,7},{4,0},{5,1},{6,2},{7,3},{8,12},{9,13},{10,... | collective-permute-start | bytes 172040 | tf_op jit(solution)/shard_map/ppermute | solution.py:246
  75.0 2.5 %collective-permute-start.34 = (bf16[4,7168]{1,0:T(4,128)(2,1)S(1)}, bf16[4,7168]{1,0:T(4,128)(2,1)S(1)}, u32[]{:S(2)}, u32[]{:S(2)}) collective-permute-start(bf16[4,7168]{1,0:T(4,128)(2,1)S(1)} %get-tuple-element.12), channel_id=1, source_target_pairs={{0,12},{1,13},{2,14},{3,15},{4,8},{5,9},{6,10},{7,11},{8,4},{9,5},... | collective-permute-start | bytes 172040 | tf_op jit(solution)/shard_map/ppermute | solution.py:246
  78.0 3.3 %collective-permute-done.34 = bf16[4,7168]{1,0:T(4,128)(2,1)S(1)} collective-permute-done((bf16[4,7168]{1,0:T(4,128)(2,1)S(1)}, bf16[4,7168]{1,0:T(4,128)(2,1)S(1)}, u32[]{:S(2)}, u32[]{:S(2)}) %collective-permute-start.34) | collective-permute-done | bytes 57376 | tf_op jit(solution)/shard_map/ppermute | solution.py:246
  81.3 1.8 %collective-permute-done.33 = bf16[4,7168]{1,0:T(4,128)(2,1)S(1)} collective-permute-done((bf16[4,7168]{1,0:T(4,128)(2,1)S(1)}, bf16[4,7168]{1,0:T(4,128)(2,1)S(1)}, u32[]{:S(2)}, u32[]{:S(2)}) %collective-permute-start.33) | collective-permute-done | bytes 57376 | tf_op jit(solution)/shard_map/ppermute | solution.py:246
  83.1 0.7 add_convert_fusion.2
  (65 shorter events, 2.9 us)
Async XLA Ops:
  0.0 31.0 %copy-start = (bf16[8,128,512]{2,1,0:T(8,128)(2,1)S(1)}, bf16[8,128,512]{2,1,0:T(8,128)(2,1)}, u32[]{:S(2)}) copy-start(bf16[8,128,512]{2,1,0:T(8,128)(2,1)} %param.10) | copy-start | bytes 3145732
  1.1 5.1 %collective-permute-start.15 = (bf16[1,576,128]{2,1,0:T(8,128)(2,1)S(1)}, bf16[1,576,128]{2,1,0:T(8,128)(2,1)S(1)}, u32[]{:S(2)}, u32[]{:S(2)}) collective-permute-start(bf16[1,576,128]{2,1,0:T(8,128)(2,1)S(1)} %get-tuple-element.9.rest_1_), channel_id=1, source_target_pairs={{0,1},{1,0},{2,3},{3,2},{4,5},{5,4},{6,7},{7,6},{8,9},{9,8},{10,11... | collective-permute-start | bytes 442376 | tf_op jit(solution)/shard_map/ppermute | solution.py:46
  1.6 7.3 %collective-permute-start.3 = (bf16[1,576,128]{2,1,0:T(8,128)(2,1)S(1)}, bf16[1,576,128]{2,1,0:T(8,128)(2,1)S(1)}, u32[]{:S(2)}, u32[]{:S(2)}) collective-permute-start(bf16[1,576,128]{2,1,0:T(8,128)(2,1)S(1)} %get-tuple-element.9.rest_1_), channel_id=1, source_target_pairs={{4,0},{5,1},{8,4},{9,5},{12,8},{13,9},{14,12},{15,13},{10,14},{11,... | collective-permute-start | bytes 442376 | tf_op jit(solution)/shard_map/ppermute | solution.py:42
  4.2 6.7 %collective-permute-start.2 = (bf16[1,576,128]{2,1,0:T(8,128)(2,1)S(1)}, bf16[1,576,128]{2,1,0:T(8,128)(2,1)S(1)}, u32[]{:S(2)}, u32[]{:S(2)}) collective-permute-start(bf16[1,576,128]{2,1,0:T(8,128)(2,1)S(1)} %get-tuple-element.9.rest_1_), channel_id=1, source_target_pairs={{0,4},{1,5},{4,8},{5,9},{8,12},{9,13},{12,14},{13,15},{14,10},{15,... | collective-permute-start | bytes 442376 | tf_op jit(solution)/shard_map/ppermute | solution.py:38
  4.3 8.1 %collective-permute-start.14 = (bf16[1,576,128]{2,1,0:T(8,128)(2,1)S(1)}, bf16[1,576,128]{2,1,0:T(8,128)(2,1)S(1)}, u32[]{:S(2)}, u32[]{:S(2)}) collective-permute-start(bf16[1,576,128]{2,1,0:T(8,128)(2,1)S(1)} %get-tuple-element.10.rest_0_), channel_id=1, source_target_pairs={{0,1},{1,0},{2,3},{3,2},{4,5},{5,4},{6,7},{7,6},{8,9},{9,8},{10,11... | collective-permute-start | bytes 442376 | tf_op jit(solution)/shard_map/ppermute | solution.py:46
  4.4 8.1 %collective-permute-start.1 = (bf16[1,576,128]{2,1,0:T(8,128)(2,1)S(1)}, bf16[1,576,128]{2,1,0:T(8,128)(2,1)S(1)}, u32[]{:S(2)}, u32[]{:S(2)}) collective-permute-start(bf16[1,576,128]{2,1,0:T(8,128)(2,1)S(1)} %get-tuple-element.10.rest_0_), channel_id=1, source_target_pairs={{4,0},{5,1},{8,4},{9,5},{12,8},{13,9},{14,12},{15,13},{10,14},{11,... | collective-permute-start | bytes 442376 | tf_op jit(solution)/shard_map/ppermute | solution.py:42
  6.2 7.4 %collective-permute-start = (bf16[1,576,128]{2,1,0:T(8,128)(2,1)S(1)}, bf16[1,576,128]{2,1,0:T(8,128)(2,1)S(1)}, u32[]{:S(2)}, u32[]{:S(2)}) collective-permute-start(bf16[1,576,128]{2,1,0:T(8,128)(2,1)S(1)} %get-tuple-element.10.rest_0_), channel_id=1, source_target_pairs={{0,4},{1,5},{4,8},{5,9},{8,12},{9,13},{12,14},{13,15},{14,10},{15,... | collective-permute-start | bytes 442376 | tf_op jit(solution)/shard_map/ppermute | solution.py:38
  9.0 4.7 %collective-permute-start.19 = (bf16[1,576,128]{2,1,0:T(8,128)(2,1)S(1)}, bf16[1,576,128]{2,1,0:T(8,128)(2,1)S(1)}, u32[]{:S(2)}, u32[]{:S(2)}) collective-permute-start(bf16[1,576,128]{2,1,0:T(8,128)(2,1)S(1)} %collective-permute-done.3.rest_5_), channel_id=1, source_target_pairs={{0,1},{1,0},{2,3},{3,2},{4,5},{5,4},{6,7},{7,6},{8,9},{9,8},{10,11... | collective-permute-start | bytes 442376 | tf_op jit(solution)/shard_map/ppermute | solution.py:46
  10.9 5.1 %collective-permute-start.7 = (bf16[1,576,128]{2,1,0:T(8,128)(2,1)S(1)}, bf16[1,576,128]{2,1,0:T(8,128)(2,1)S(1)}, u32[]{:S(2)}, u32[]{:S(2)}) collective-permute-start(bf16[1,576,128]{2,1,0:T(8,128)(2,1)S(1)} %collective-permute-done.3.rest_5_), channel_id=1, source_target_pairs={{4,0},{5,1},{8,4},{9,5},{12,8},{13,9},{14,12},{15,13},{10,14},{11,... | collective-permute-start | bytes 442376 | tf_op jit(solution)/shard_map/ppermute | solution.py:42
  12.5 3.6 %collective-permute-start.18 = (bf16[1,576,128]{2,1,0:T(8,128)(2,1)S(1)}, bf16[1,576,128]{2,1,0:T(8,128)(2,1)S(1)}, u32[]{:S(2)}, u32[]{:S(2)}) collective-permute-start(bf16[1,576,128]{2,1,0:T(8,128)(2,1)S(1)} %collective-permute-done.2.rest_4_), channel_id=1, source_target_pairs={{0,1},{1,0},{2,3},{3,2},{4,5},{5,4},{6,7},{7,6},{8,9},{9,8},{10,11... | collective-permute-start | bytes 442376 | tf_op jit(solution)/shard_map/ppermute | solution.py:46
  12.5 6.3 %collective-permute-start.6 = (bf16[1,576,128]{2,1,0:T(8,128)(2,1)S(1)}, bf16[1,576,128]{2,1,0:T(8,128)(2,1)S(1)}, u32[]{:S(2)}, u32[]{:S(2)}) collective-permute-start(bf16[1,576,128]{2,1,0:T(8,128)(2,1)S(1)} %collective-permute-done.2.rest_4_), channel_id=1, source_target_pairs={{0,4},{1,5},{4,8},{5,9},{8,12},{9,13},{12,14},{13,15},{14,10},{15,... | collective-permute-start | bytes 442376 | tf_op jit(solution)/shard_map/ppermute | solution.py:38
  13.6 5.1 %collective-permute-start.17 = (bf16[1,576,128]{2,1,0:T(8,128)(2,1)S(1)}, bf16[1,576,128]{2,1,0:T(8,128)(2,1)S(1)}, u32[]{:S(2)}, u32[]{:S(2)}) collective-permute-start(bf16[1,576,128]{2,1,0:T(8,128)(2,1)S(1)} %collective-permute-done.1.rest_3_), channel_id=1, source_target_pairs={{0,1},{1,0},{2,3},{3,2},{4,5},{5,4},{6,7},{7,6},{8,9},{9,8},{10,11... | collective-permute-start | bytes 442376 | tf_op jit(solution)/shard_map/ppermute | solution.py:46
  13.6 6.7 %collective-permute-start.5 = (bf16[1,576,128]{2,1,0:T(8,128)(2,1)S(1)}, bf16[1,576,128]{2,1,0:T(8,128)(2,1)S(1)}, u32[]{:S(2)}, u32[]{:S(2)}) collective-permute-start(bf16[1,576,128]{2,1,0:T(8,128)(2,1)S(1)} %collective-permute-done.1.rest_3_), channel_id=1, source_target_pairs={{4,0},{5,1},{8,4},{9,5},{12,8},{13,9},{14,12},{15,13},{10,14},{11,... | collective-permute-start | bytes 442376 | tf_op jit(solution)/shard_map/ppermute | solution.py:42
  16.0 4.5 %collective-permute-start.16 = (bf16[1,576,128]{2,1,0:T(8,128)(2,1)S(1)}, bf16[1,576,128]{2,1,0:T(8,128)(2,1)S(1)}, u32[]{:S(2)}, u32[]{:S(2)}) collective-permute-start(bf16[1,576,128]{2,1,0:T(8,128)(2,1)S(1)} %collective-permute-done.rest_2_), channel_id=1, source_target_pairs={{0,1},{1,0},{2,3},{3,2},{4,5},{5,4},{6,7},{7,6},{8,9},{9,8},{10,11... | collective-permute-start | bytes 442376 | tf_op jit(solution)/shard_map/ppermute | solution.py:46
  16.0 6.3 %collective-permute-start.4 = (bf16[1,576,128]{2,1,0:T(8,128)(2,1)S(1)}, bf16[1,576,128]{2,1,0:T(8,128)(2,1)S(1)}, u32[]{:S(2)}, u32[]{:S(2)}) collective-permute-start(bf16[1,576,128]{2,1,0:T(8,128)(2,1)S(1)} %collective-permute-done.rest_2_), channel_id=1, source_target_pairs={{0,4},{1,5},{4,8},{5,9},{8,12},{9,13},{12,14},{13,15},{14,10},{15,... | collective-permute-start | bytes 442376 | tf_op jit(solution)/shard_map/ppermute | solution.py:38
  18.7 3.6 %collective-permute-start.23 = (bf16[1,576,128]{2,1,0:T(8,128)(2,1)S(1)}, bf16[1,576,128]{2,1,0:T(8,128)(2,1)S(1)}, u32[]{:S(2)}, u32[]{:S(2)}) collective-permute-start(bf16[1,576,128]{2,1,0:T(8,128)(2,1)S(1)} %collective-permute-done.7.rest_9_), channel_id=1, source_target_pairs={{0,1},{1,0},{2,3},{3,2},{4,5},{5,4},{6,7},{7,6},{8,9},{9,8},{10,11... | collective-permute-start | bytes 442376 | tf_op jit(solution)/shard_map/ppermute | solution.py:46
  18.7 6.5 %collective-permute-start.11 = (bf16[1,576,128]{2,1,0:T(8,128)(2,1)S(1)}, bf16[1,576,128]{2,1,0:T(8,128)(2,1)}, u32[]{:S(2)}, u32[]{:S(2)}) collective-permute-start(bf16[1,576,128]{2,1,0:T(8,128)(2,1)S(1)} %collective-permute-done.7.rest_9_), channel_id=1, source_target_pairs={{4,0},{5,1},{8,4},{9,5},{12,8},{13,9},{14,12},{15,13},{10,14},{11,... | collective-permute-start | bytes 442376 | tf_op jit(solution)/shard_map/ppermute | solution.py:42
  20.3 6.4 %collective-permute-start.22 = (bf16[1,576,128]{2,1,0:T(8,128)(2,1)S(1)}, bf16[1,576,128]{2,1,0:T(8,128)(2,1)}, u32[]{:S(2)}, u32[]{:S(2)}) collective-permute-start(bf16[1,576,128]{2,1,0:T(8,128)(2,1)S(1)} %collective-permute-done.6.rest_8_), channel_id=1, source_target_pairs={{0,1},{1,0},{2,3},{3,2},{4,5},{5,4},{6,7},{7,6},{8,9},{9,8},{10,11... | collective-permute-start | bytes 442376 | tf_op jit(solution)/shard_map/ppermute | solution.py:46
  20.6 15.8 %copy-start.1 = (bf16[1,576,128]{2,1,0:T(8,128)(2,1)}, bf16[1,576,128]{2,1,0:T(8,128)(2,1)S(1)}, u32[]{:S(2)}) copy-start(bf16[1,576,128]{2,1,0:T(8,128)(2,1)S(1)} %collective-permute-done.16.rest_18_) | copy-start | bytes 442372
  20.6 6.6 %collective-permute-start.10 = (bf16[1,576,128]{2,1,0:T(8,128)(2,1)S(1)}, bf16[1,576,128]{2,1,0:T(8,128)(2,1)}, u32[]{:S(2)}, u32[]{:S(2)}) collective-permute-start(bf16[1,576,128]{2,1,0:T(8,128)(2,1)S(1)} %collective-permute-done.6.rest_8_), channel_id=1, source_target_pairs={{0,4},{1,5},{4,8},{5,9},{8,12},{9,13},{12,14},{13,15},{14,10},{15,... | collective-permute-start | bytes 442376 | tf_op jit(solution)/shard_map/ppermute | solution.py:38
  22.3 14.0 %copy-start.3 = (bf16[1,576,128]{2,1,0:T(8,128)(2,1)}, bf16[1,576,128]{2,1,0:T(8,128)(2,1)S(1)}, u32[]{:S(2)}) copy-start(bf16[1,576,128]{2,1,0:T(8,128)(2,1)S(1)} %collective-permute-done.4.rest_6_) | copy-start | bytes 442372
  22.3 4.9 %collective-permute-start.21 = (bf16[1,576,128]{2,1,0:T(8,128)(2,1)S(1)}, bf16[1,576,128]{2,1,0:T(8,128)(2,1)}, u32[]{:S(2)}, u32[]{:S(2)}) collective-permute-start(bf16[1,576,128]{2,1,0:T(8,128)(2,1)S(1)} %collective-permute-done.5.rest_7_), channel_id=1, source_target_pairs={{0,1},{1,0},{2,3},{3,2},{4,5},{5,4},{6,7},{7,6},{8,9},{9,8},{10,11... | collective-permute-start | bytes 442376 | tf_op jit(solution)/shard_map/ppermute | solution.py:46
  22.3 0.7 copy-start.5
  23.0 6.8 %collective-permute-start.8 = (bf16[1,576,128]{2,1,0:T(8,128)(2,1)S(1)}, bf16[1,576,128]{2,1,0:T(8,128)(2,1)}, u32[]{:S(2)}, u32[]{:S(2)}) collective-permute-start(bf16[1,576,128]{2,1,0:T(8,128)(2,1)S(1)} %collective-permute-done.4.rest_6_), channel_id=1, source_target_pairs={{0,4},{1,5},{4,8},{5,9},{8,12},{9,13},{12,14},{13,15},{14,10},{15,... | collective-permute-start | bytes 442376 | tf_op jit(solution)/shard_map/ppermute | solution.py:38
  25.3 6.8 %collective-permute-start.9 = (bf16[1,576,128]{2,1,0:T(8,128)(2,1)S(1)}, bf16[1,576,128]{2,1,0:T(8,128)(2,1)}, u32[]{:S(2)}, u32[]{:S(2)}) collective-permute-start(bf16[1,576,128]{2,1,0:T(8,128)(2,1)S(1)} %collective-permute-done.5.rest_7_), channel_id=1, source_target_pairs={{4,0},{5,1},{8,4},{9,5},{12,8},{13,9},{14,12},{15,13},{10,14},{11,... | collective-permute-start | bytes 442376 | tf_op jit(solution)/shard_map/ppermute | solution.py:42
  26.7 5.4 %collective-permute-start.20 = (bf16[1,576,128]{2,1,0:T(8,128)(2,1)S(1)}, bf16[1,576,128]{2,1,0:T(8,128)(2,1)S(1)}, u32[]{:S(2)}, u32[]{:S(2)}) collective-permute-start(bf16[1,576,128]{2,1,0:T(8,128)(2,1)S(1)} %collective-permute-done.4.rest_6_), channel_id=1, source_target_pairs={{0,1},{1,0},{2,3},{3,2},{4,5},{5,4},{6,7},{7,6},{8,9},{9,8},{10,11... | collective-permute-start | bytes 442376 | tf_op jit(solution)/shard_map/ppermute | solution.py:46
  27.2 6.1 %collective-permute-start.27 = (bf16[1,576,128]{2,1,0:T(8,128)(2,1)}, bf16[1,576,128]{2,1,0:T(8,128)(2,1)S(1)}, u32[]{:S(2)}, u32[]{:S(2)}) collective-permute-start(bf16[1,576,128]{2,1,0:T(8,128)(2,1)} %collective-permute-done.11.rest_13_), channel_id=1, source_target_pairs={{0,1},{1,0},{2,3},{3,2},{4,5},{5,4},{6,7},{7,6},{8,9},{9,8},{10,11... | collective-permute-start | bytes 442376 | tf_op jit(solution)/shard_map/ppermute | solution.py:46
  27.2 7.3 %collective-permute-start.13 = (bf16[1,576,128]{2,1,0:T(8,128)(2,1)}, bf16[1,576,128]{2,1,0:T(8,128)(2,1)}, u32[]{:S(2)}, u32[]{:S(2)}) collective-permute-start(bf16[1,576,128]{2,1,0:T(8,128)(2,1)} %collective-permute-done.11.rest_13_), channel_id=1, source_target_pairs={{4,0},{5,1},{8,4},{9,5},{12,8},{13,9},{14,12},{15,13},{10,14},{11,... | collective-permute-start | bytes 442376 | tf_op jit(solution)/shard_map/ppermute | solution.py:42
  29.9 5.7 %collective-permute-start.12 = (bf16[1,576,128]{2,1,0:T(8,128)(2,1)}, bf16[1,576,128]{2,1,0:T(8,128)(2,1)}, u32[]{:S(2)}, u32[]{:S(2)}) collective-permute-start(bf16[1,576,128]{2,1,0:T(8,128)(2,1)} %collective-permute-done.8.rest_10_), channel_id=1, source_target_pairs={{0,4},{1,5},{4,8},{5,9},{8,12},{9,13},{12,14},{13,15},{14,10},{15,... | collective-permute-start | bytes 442376 | tf_op jit(solution)/shard_map/ppermute | solution.py:38
  32.1 6.0 %collective-permute-start.24 = (bf16[1,576,128]{2,1,0:T(8,128)(2,1)}, bf16[1,576,128]{2,1,0:T(8,128)(2,1)}, u32[]{:S(2)}, u32[]{:S(2)}) collective-permute-start(bf16[1,576,128]{2,1,0:T(8,128)(2,1)} %collective-permute-done.8.rest_10_), channel_id=1, source_target_pairs={{0,1},{1,0},{2,3},{3,2},{4,5},{5,4},{6,7},{7,6},{8,9},{9,8},{10,11... | collective-permute-start | bytes 442376 | tf_op jit(solution)/shard_map/ppermute | solution.py:46
  32.8 5.3 %collective-permute-start.26 = (bf16[1,576,128]{2,1,0:T(8,128)(2,1)}, bf16[1,576,128]{2,1,0:T(8,128)(2,1)}, u32[]{:S(2)}, u32[]{:S(2)}) collective-permute-start(bf16[1,576,128]{2,1,0:T(8,128)(2,1)} %collective-permute-done.10.rest_12_), channel_id=1, source_target_pairs={{0,1},{1,0},{2,3},{3,2},{4,5},{5,4},{6,7},{7,6},{8,9},{9,8},{10,11... | collective-permute-start | bytes 442376 | tf_op jit(solution)/shard_map/ppermute | solution.py:46
  33.3 0.7 copy-start.9
  34.0 4.2 %collective-permute-start.25 = (bf16[1,576,128]{2,1,0:T(8,128)(2,1)}, bf16[1,576,128]{2,1,0:T(8,128)(2,1)}, u32[]{:S(2)}, u32[]{:S(2)}) collective-permute-start(bf16[1,576,128]{2,1,0:T(8,128)(2,1)} %collective-permute-done.9.rest_11_), channel_id=1, source_target_pairs={{0,1},{1,0},{2,3},{3,2},{4,5},{5,4},{6,7},{7,6},{8,9},{9,8},{10,11... | collective-permute-start | bytes 442376 | tf_op jit(solution)/shard_map/ppermute | solution.py:46
  34.5 3.6 %collective-permute-start.29 = (bf16[1,576,128]{2,1,0:T(8,128)(2,1)}, bf16[1,576,128]{2,1,0:T(8,128)(2,1)}, u32[]{:S(2)}, u32[]{:S(2)}) collective-permute-start(bf16[1,576,128]{2,1,0:T(8,128)(2,1)} %collective-permute-done.13.rest_15_), channel_id=1, source_target_pairs={{0,1},{1,0},{2,3},{3,2},{4,5},{5,4},{6,7},{7,6},{8,9},{9,8},{10,11... | collective-permute-start | bytes 442376 | tf_op jit(solution)/shard_map/ppermute | solution.py:46
  35.6 2.6 %collective-permute-start.28 = (bf16[1,576,128]{2,1,0:T(8,128)(2,1)}, bf16[1,576,128]{2,1,0:T(8,128)(2,1)}, u32[]{:S(2)}, u32[]{:S(2)}) collective-permute-start(bf16[1,576,128]{2,1,0:T(8,128)(2,1)} %collective-permute-done.12.rest_14_), channel_id=1, source_target_pairs={{0,1},{1,0},{2,3},{3,2},{4,5},{5,4},{6,7},{7,6},{8,9},{9,8},{10,11... | collective-permute-start | bytes 442376 | tf_op jit(solution)/shard_map/ppermute | solution.py:46
  38.2 0.9 %copy-start.2 = (bf16[1,576,128]{2,1,0:T(8,128)(2,1)S(1)}, bf16[1,576,128]{2,1,0:T(8,128)(2,1)}, u32[]{:S(2)}) copy-start(bf16[1,576,128]{2,1,0:T(8,128)(2,1)} %copy-done.1) | copy-start | bytes 442372
  39.1 0.9 %copy-start.4 = (bf16[1,576,128]{2,1,0:T(8,128)(2,1)S(1)}, bf16[1,576,128]{2,1,0:T(8,128)(2,1)}, u32[]{:S(2)}) copy-start(bf16[1,576,128]{2,1,0:T(8,128)(2,1)} %copy-done.3) | copy-start | bytes 442372
  40.0 0.9 %copy-start.6 = (bf16[1,576,128]{2,1,0:T(8,128)(2,1)S(1)}, bf16[1,576,128]{2,1,0:T(8,128)(2,1)}, u32[]{:S(2)}) copy-start(bf16[1,576,128]{2,1,0:T(8,128)(2,1)} %copy-done.5) | copy-start | bytes 442372
  40.9 0.9 %copy-start.8 = (bf16[1,576,128]{2,1,0:T(8,128)(2,1)S(1)}, bf16[1,576,128]{2,1,0:T(8,128)(2,1)}, u32[]{:S(2)}) copy-start(bf16[1,576,128]{2,1,0:T(8,128)(2,1)} %copy-done.7) | copy-start | bytes 442372
  41.8 0.9 %copy-start.10 = (bf16[1,576,128]{2,1,0:T(8,128)(2,1)S(1)}, bf16[1,576,128]{2,1,0:T(8,128)(2,1)}, u32[]{:S(2)}) copy-start(bf16[1,576,128]{2,1,0:T(8,128)(2,1)} %copy-done.9) | copy-start | bytes 442372
  42.7 0.7 copy-start.11
  43.4 0.7 copy-start.12
  44.0 0.7 copy-start.13
  63.5 2.0 %collective-permute-start.30 = (bf16[32,7168]{1,0:T(8,128)(2,1)S(1)}, bf16[32,7168]{1,0:T(8,128)(2,1)S(1)}, u32[]{:S(2)}, u32[]{:S(2)}) collective-permute-start(bf16[32,7168]{1,0:T(8,128)(2,1)S(1)} %get-tuple-element.8), channel_id=1, source_target_pairs={{0,1},{1,0},{2,3},{3,2},{4,5},{5,4},{6,7},{7,6},{8,9},{9,8},{10,11... | collective-permute-start | bytes 1376264 | tf_op jit(solution)/shard_map/ppermute | solution.py:246
  65.7 7.9 %collective-permute-start.31 = (bf16[16,7168]{1,0:T(8,128)(2,1)S(1)}, bf16[16,7168]{1,0:T(8,128)(2,1)S(1)}, u32[]{:S(2)}, u32[]{:S(2)}) collective-permute-start(bf16[16,7168]{1,0:T(8,128)(2,1)S(1)} %slice.45), channel_id=1, source_target_pairs={{0,2},{1,3},{2,0},{3,1},{4,6},{5,7},{6,4},{7,5},{8,10},{9,11},{10,... | collective-permute-start | bytes 688136 | tf_op jit(solution)/shard_map/ppermute | solution.py:246
  73.8 4.2 %collective-permute-start.32 = (bf16[4,7168]{1,0:T(4,128)(2,1)S(1)}, bf16[4,7168]{1,0:T(4,128)(2,1)S(1)}, u32[]{:S(2)}, u32[]{:S(2)}) collective-permute-start(bf16[4,7168]{1,0:T(4,128)(2,1)S(1)} %get-tuple-element.11), channel_id=1, source_target_pairs={{0,4},{1,5},{2,6},{3,7},{4,0},{5,1},{6,2},{7,3},{8,12},{9,13},{10,... | collective-permute-start | bytes 172040 | tf_op jit(solution)/shard_map/ppermute | solution.py:246
  75.0 6.4 %collective-permute-start.34 = (bf16[4,7168]{1,0:T(4,128)(2,1)S(1)}, bf16[4,7168]{1,0:T(4,128)(2,1)S(1)}, u32[]{:S(2)}, u32[]{:S(2)}) collective-permute-start(bf16[4,7168]{1,0:T(4,128)(2,1)S(1)} %get-tuple-element.12), channel_id=1, source_target_pairs={{0,12},{1,13},{2,14},{3,15},{4,8},{5,9},{6,10},{7,11},{8,4},{9,5},... | collective-permute-start | bytes 172040 | tf_op jit(solution)/shard_map/ppermute | solution.py:246
  77.4 5.7 %collective-permute-start.33 = (bf16[4,7168]{1,0:T(4,128)(2,1)S(1)}, bf16[4,7168]{1,0:T(4,128)(2,1)S(1)}, u32[]{:S(2)}, u32[]{:S(2)}) collective-permute-start(bf16[4,7168]{1,0:T(4,128)(2,1)S(1)} %get-tuple-element.13), channel_id=1, source_target_pairs={{0,8},{1,9},{2,10},{3,11},{4,12},{5,13},{6,14},{7,15},{8,0},{9,1},... | collective-permute-start | bytes 172040 | tf_op jit(solution)/shard_map/ppermute | solution.py:246
  (1 other events, 0.7 us)

commit v2 on v1

v2 whole, which is shorter than its diff:
```python
import functools

import jax
import jax.numpy as jnp
import numpy as np
from jax import lax
from jax.experimental import pallas as pl
from jax.experimental.pallas import tpu as pltpu
from jax.sharding import PartitionSpec as P

OUT_TILE = 1024
LANES = 128
UNROLL = 4
EMPTY = -1e30


def ring_of(chips):
    if chips == 8:
        return [0, 2, 4, 6, 7, 5, 3, 1]
    return list(range(chips))


def ring_places(chips):
    places = [(0, 0), (0, 1)]
    for hop in range(1, chips // 2 + 1):
        last = hop == chips // 2
        places += [(-hop, 0)] if last else [(-hop, 0), (hop, 0), (-hop, 1)]
        places += [(hop, 1)]
    return places


def slots_by_device(chips, half):
    ring = ring_of(chips)
    position = {chip: i for i, chip in enumerate(ring)}
    table = np.full((2 * chips, 4 * chips * half), -1, np.int32)
    for device in range(2 * chips):
        for index, (hop, part) in enumerate(ring_places(chips)):
            source = ring[(position[device // 2] + hop) % chips] * 2 + device % 2
            for i in range(half):
                table[device, (source * 2 + part) * half + i] = index * half + i
    return table


def query_kernel(heads, query_ref, absorb_ref, out_ref, ordered):
    rows = query_ref.shape[0]
    nope = absorb_ref.shape[1]
    head_width = query_ref.shape[1] // heads
    rope = head_width - nope
    kv_rank = absorb_ref.shape[2]
    for h in range(heads):
        own = query_ref[:, h * head_width : (h + 1) * head_width]
        latent = jnp.dot(own[:, :nope], absorb_ref[h], preferred_element_type=jnp.float32)
        turned = jnp.concatenate(
            [own[:, nope:].astype(jnp.float32), jnp.zeros((rows, LANES - rope), jnp.float32)], axis=1
        )
        at = pl.ds(h, rows, stride=heads)
        for c in range(kv_rank // LANES):
            ordered[c, at] = latent[:, c * LANES : (c + 1) * LANES]
        ordered[kv_rank // LANES, at] = turned
    for c in range(kv_rank // LANES):
        out_ref[:, c * LANES : (c + 1) * LANES] = ordered[c].astype(jnp.bfloat16)
    out_ref[:, kv_rank:] = ordered[kv_rank // LANES, :, :rope].astype(jnp.bfloat16)


def attend_kernel(
    piece_count, first_slot, heads, steps, max_blocks, kv_rank, scale,
    info_ref, mine_ref, theirs_ref, *rest,
):
    pieces = rest[:piece_count]
    (out_ref, lse_ref, away_ref, queries, cache, scores, top, total, latent,
     use_request, use_block, use_last, cache_sems) = rest[piece_count:]
    requests = top.shape[0] - 1
    row_block = queries.shape[1] // 2
    both = 2 * row_block
    block_rows = cache.shape[2]
    half = cache.shape[0] // piece_count
    slot_at = requests * (max_blocks + 2)

    copies = [
        pltpu.make_async_copy(p, cache.at[pl.ds(i * half, half)], cache_sems.at[i])
        for i, p in enumerate(pieces)
    ]
    for copy in copies:
        copy.start()

    def list_request(r, at):
        count = info_ref[r]

        def list_block(j, at):
            slot = info_ref[slot_at + info_ref[requests * 2 + r * max_blocks + j]] - first_slot
            here = (slot >= 0) & (slot < cache.shape[0])

            @pl.when(here)
            def _():
                use_request[at] = r
                use_block[at] = slot
                use_last[at] = (j == count - 1).astype(jnp.int32)

            return at + here.astype(jnp.int32)

        return lax.fori_loop(0, count, list_block, at)

    uses = lax.fori_loop(0, requests, list_request, 0)
    for i in range(UNROLL):
        use_request[uses + i] = requests
        use_block[uses + i] = 0
        use_last[uses + i] = 0
    turns = (uses + UNROLL - 1) // UNROLL

    queries[:, :row_block] = mine_ref[...]
    queries[:, row_block:] = theirs_ref[...]
    top[...] = jnp.full_like(top, -jnp.inf)
    total[...] = jnp.zeros_like(total)
    latent[...] = jnp.zeros_like(latent)
    column = lax.broadcasted_iota(jnp.int32, (both, block_rows), 1)
    row = lax.broadcasted_iota(jnp.int32, (both, block_rows), 0)
    hidden = steps - 1 - (row % row_block) // heads
    for copy in copies:
        copy.wait()

    def score(turn, _):
        for i in range(UNROLL):
            u = turn * UNROLL + i
            r = use_request[u]
            s = jnp.dot(
                queries[jnp.minimum(r, requests - 1)], cache[use_block[u]],
                preferred_element_type=jnp.float32,
            ) * scale
            s = jnp.where(column + hidden * use_last[u] < block_rows, s, -jnp.inf)
            scores[u] = s
            top[r] = jnp.maximum(top[r], s)
        return 0

    lax.fori_loop(0, turns, score, 0)

    def peak(r, _):
        top[r] = jnp.broadcast_to(jnp.max(top[r], axis=1, keepdims=True), (both, block_rows))
        return 0

    lax.fori_loop(0, requests + 1, peak, 0)

    def mix(turn, _):
        for i in range(UNROLL):
            u = turn * UNROLL + i
            r = use_request[u]
            p = jnp.exp(scores[u] - top[r])
            total[r] += p
            latent[r] += lax.dot_general(
                p.astype(jnp.bfloat16),
                cache[use_block[u], :kv_rank],
                (((1,), (1,)), ((), ())),
                preferred_element_type=jnp.float32,
            )
        return 0

    lax.fori_loop(0, turns, mix, 0)

    lane = lax.broadcasted_iota(jnp.int32, (row_block, LANES), 1)

    def finish(r, _):
        at = pl.ds(pl.multiple_of(r * row_block, row_block), row_block)
        norm = jnp.sum(total[r], axis=1, keepdims=True)
        some = norm > 0
        safe = jnp.where(some, norm, 1.0)
        lse = jnp.where(some, top[r][:, :1] + jnp.log(safe), EMPTY)
        result = latent[r] / safe
        out_ref[at] = result[:row_block]
        lse_ref[at] = jnp.broadcast_to(lse[:row_block], (row_block, LANES))
        rest = lse[row_block:]
        high = rest.astype(jnp.bfloat16).astype(jnp.float32)
        middle = (rest - high).astype(jnp.bfloat16).astype(jnp.float32)
        low = rest - high - middle
        terms = jnp.where(lane == 0, high, jnp.where(lane == 1, middle, jnp.where(lane == 2, low, 0.0)))
        away_ref[at, :kv_rank] = result[row_block:].astype(jnp.bfloat16)
        away_ref[at, kv_rank:] = terms.astype(jnp.bfloat16)
        return 0

    lax.fori_loop(0, requests, finish, 0)


def project_kernel(
    stages, heads, steps, max_blocks, chips,
    info_ref, value_ref, out_w_ref, *rest,
):
    outs, lses, others = rest[:stages], rest[stages : 2 * stages], rest[2 * stages : 3 * stages]
    away_ref, keep_ref, latent, weight, head_rows, weight_sems = rest[3 * stages :]
    kv_rank, v_width = value_ref.shape[1:]
    rows = head_rows.shape[0]
    requests = rows // steps
    tiles, _, tile = weight.shape
    weight_copies = [
        pltpu.make_async_copy(out_w_ref.at[:, pl.ds(i * tile, tile)], weight.at[i], weight_sems.at[i])
        for i in range(tiles)
    ]
    for copy in weight_copies:
        copy.start()

    chunk = 64

    def merge(i, _):
        at = pl.ds(pl.multiple_of(i * chunk, chunk), chunk)
        parts = [(o[at], e[at][:, :1]) for o, e in zip(outs, lses)]
        for other in others:
            terms = jnp.sum(other[at, kv_rank:].astype(jnp.float32), axis=1, keepdims=True)
            parts.append((other[at, :kv_rank].astype(jnp.float32), terms))
        peak = functools.reduce(jnp.maximum, [e for _, e in parts])
        shares = [jnp.exp(e - peak) for _, e in parts]
        norm = functools.reduce(jnp.add, shares)
        whole = functools.reduce(jnp.add, [o * (w / norm) for (o, _), w in zip(parts, shares)])
        for c in range(kv_rank // LANES):
            latent[c, at] = whole[:, c * LANES : (c + 1) * LANES]
        return 0

    lax.fori_loop(0, rows * heads // chunk, merge, 0)

    for h in range(heads):
        mine = jnp.concatenate(
            [latent[c, pl.ds(h, rows, stride=heads)] for c in range(kv_rank // LANES)], axis=1
        ).astype(jnp.bfloat16)
        head_rows[:, h * v_width : (h + 1) * v_width] = jnp.dot(
            mine, value_ref[h], preferred_element_type=jnp.float32
        ).astype(jnp.bfloat16)

    half_rows = away_ref.shape[0]
    me = info_ref[info_ref.shape[0] - 1]
    target = lax.broadcasted_iota(jnp.int32, (2 * half_rows, rows), 0)
    origin = lax.broadcasted_iota(jnp.int32, (2 * half_rows, rows), 1)

    def place(r, picked):
        apart = info_ref[requests + r] ^ me
        order = (apart & 1) * chips + ((apart >> 1) & 1) * (chips // 2) + (apart >> 2)
        shifted = origin - r * steps
        hit = (target - order * steps == shifted) & (shifted >= 0) & (shifted < steps)
        return jnp.where(hit, 1.0, picked)

    picker = lax.fori_loop(0, requests, place, jnp.zeros((2 * half_rows, rows), jnp.float32))
    placed = jnp.dot(
        picker.astype(jnp.bfloat16), head_rows[...], preferred_element_type=jnp.float32
    ).astype(jnp.bfloat16)
    for i in range(tiles):
        weight_copies[i].wait()
        result = jnp.dot(placed, weight[i], preferred_element_type=jnp.float32).astype(jnp.bfloat16)
        keep_ref[:, i * tile : (i + 1) * tile] = result[:half_rows]
        away_ref[:, i * tile : (i + 1) * tile] = result[half_rows:]


def local(q_heads, w_absorb, w_value, w_out, latent_cache, ctx_blocks, block_table, owner):
    heads, _, kv_rank = w_absorb.shape
    row_count = q_heads.shape[0]
    head_width = q_heads.shape[1] // heads
    requests, max_blocks = block_table.shape
    steps = row_count // requests
    devices = lax.axis_size("head")
    chips = devices // 2
    blocks_here, block_rows, row_width = latent_cache.shape
    half = blocks_here // 2
    width = w_out.shape[1]
    v_width = w_value.shape[2]
    row_block = steps * heads
    flat_rows = requests * row_block
    me = lax.axis_index("head").astype(jnp.int32)
    smem = pl.BlockSpec(memory_space=pltpu.SMEM)
    vmem = pl.BlockSpec(memory_space=pltpu.VMEM)
    hbm = pl.BlockSpec(memory_space=pltpu.HBM)

    def exchange(x, distance):
        return lax.ppermute(x, "head", [(i, i ^ distance) for i in range(devices)])

    def attend(info, mine, theirs, pieces, first):
        slots = len(pieces) * half
        uses = requests * max_blocks + UNROLL
        return pl.pallas_call(
            functools.partial(
                attend_kernel, len(pieces), first * half, heads, steps, max_blocks, kv_rank,
                float(head_width) ** -0.5,
            ),
            out_shape=(
                jax.ShapeDtypeStruct((flat_rows, kv_rank), jnp.float32),
                jax.ShapeDtypeStruct((flat_rows, LANES), jnp.float32),
                jax.ShapeDtypeStruct((flat_rows, kv_rank + LANES), jnp.bfloat16),
            ),
            in_specs=[smem, vmem, vmem] + [hbm] * len(pieces),
            out_specs=(vmem, vmem, vmem),
            scratch_shapes=[
                pltpu.VMEM((requests, 2 * row_block, row_width), jnp.bfloat16),
                pltpu.VMEM((slots, row_width, block_rows), jnp.bfloat16),
                pltpu.VMEM((min(uses, 2 * slots + UNROLL), 2 * row_block, block_rows), jnp.float32),
                pltpu.VMEM((requests + 1, 2 * row_block, block_rows), jnp.float32),
                pltpu.VMEM((requests + 1, 2 * row_block, block_rows), jnp.float32),
                pltpu.VMEM((requests + 1, 2 * row_block, kv_rank), jnp.float32),
                pltpu.SMEM((uses,), jnp.int32),
                pltpu.SMEM((uses,), jnp.int32),
                pltpu.SMEM((uses,), jnp.int32),
                pltpu.SemaphoreType.DMA((len(pieces),)),
            ],
            compiler_params=pltpu.CompilerParams(vmem_limit_bytes=32 * 1024 * 1024),
            cost_estimate=pl.CostEstimate(
                flops=2 * slots * 2 * row_block * block_rows * 2 * row_width,
                bytes_accessed=slots * block_rows * row_width * 2,
                transcendentals=0,
            ),
            name="attend",
        )(info, mine, theirs, *pieces)

    ring = ring_of(chips)
    up = [
        (ring[i] * 2 + core, ring[(i + 1) % chips] * 2 + core)
        for i in range(chips)
        for core in range(2)
    ]
    down = [(b, a) for a, b in up]
    keys = jnp.swapaxes(latent_cache, 1, 2)
    ups = [keys[:half], keys[half:]]
    downs = list(ups)
    pieces = list(ups)
    partial = []
    done = 0
    for hop in range(1, chips // 2 + 1):
        last = hop == chips // 2
        if hop == 2:
            table = jnp.asarray(slots_by_device(chips, half))
            info = jnp.concatenate(
                [ctx_blocks, owner, block_table.reshape(-1), table[me], me.reshape(1)]
            )
            mine = pl.pallas_call(
                functools.partial(query_kernel, heads),
                out_shape=jax.ShapeDtypeStruct((flat_rows, row_width), jnp.bfloat16),
                in_specs=[vmem, vmem],
                out_specs=vmem,
                scratch_shapes=[
                    pltpu.VMEM((kv_rank // LANES + 1, flat_rows, LANES), jnp.float32)
                ],
                compiler_params=pltpu.CompilerParams(vmem_limit_bytes=16 * 1024 * 1024),
                cost_estimate=pl.CostEstimate(
                    flops=2 * w_absorb.size * row_count, bytes_accessed=2 * w_absorb.size, transcendentals=0
                ),
                name="absorb_queries",
            )(q_heads, w_absorb)
            mine = mine.reshape(requests, row_block, row_width)
            theirs = exchange(mine, 1)
            ups, downs, info, mine = lax.optimization_barrier((ups, downs, info, mine))
        before = list(pieces)
        for part in range(2):
            if not last or part == 0:
                ups[part] = lax.ppermute(ups[part], "head", up)
                pieces.append(ups[part])
            if not last or part == 1:
                downs[part] = lax.ppermute(downs[part], "head", down)
                pieces.append(downs[part])
        if last:
            for stage in (before, pieces[len(before) :]):
                out, lse, away = attend(info, mine, theirs, stage, done)
                partial.append((out, lse, exchange(away, 1)))
                done += len(stage)

    tiles = width // OUT_TILE
    part = jax.ShapeDtypeStruct((chips * steps, width), jnp.bfloat16)
    outs, lses, others = zip(*partial)
    away, keep = pl.pallas_call(
        functools.partial(project_kernel, len(partial), heads, steps, max_blocks, chips),
        out_shape=(part, part),
        in_specs=[smem, vmem, hbm] + [vmem] * (3 * len(partial)),
        out_specs=(vmem, vmem),
        scratch_shapes=[
            pltpu.VMEM((kv_rank // LANES, flat_rows, LANES), jnp.float32),
            pltpu.VMEM((tiles, w_out.shape[0], OUT_TILE), jnp.bfloat16),
            pltpu.VMEM((row_count, heads * v_width), jnp.bfloat16),
            pltpu.SemaphoreType.DMA((tiles,)),
        ],
        compiler_params=pltpu.CompilerParams(vmem_limit_bytes=40 * 1024 * 1024),
        name="merge_and_project",
    )(info, w_value, w_out, *outs, *lses, *others)

    def add(x, *others):
        total = x.astype(jnp.float32)
        for other in others:
            total = total + other.astype(jnp.float32)
        return total.astype(jnp.bfloat16)

    both = add(keep, exchange(away, 1))
    middle = both.shape[0] // 2
    line = add(both[:middle], exchange(both[middle:], 2))
    received = [
        exchange(line[k * steps : (k + 1) * steps], 4 * k) for k in range(1, chips // 2)
    ]
    return add(line[:steps], *received)


def solution(mesh):
    return jax.shard_map(
        local,
        mesh=mesh,
        in_specs=(
            P("group", "head"),
            P("head", None, None),
            P("head", None, None),
            P("head", None),
            P(("group", "head"), None, None),
            P("group"),
            P("group", None),
            P("group"),
        ),
        out_specs=P(("group", "head"), None),
        check_vma=False,
    )
```

time: 84.2 us -> 74 us (0.88)
  local copies, waits for them, and re-layouts: 12.6 us -> 6.64 us
  starting transfers between devices: 25 us -> 21.4 us
    unnamed x29 -> x6, local copies, waits for them, and re-layouts: 8.56 us -> 3.34 us
    ppermute x30 -> x14, starting transfers between devices: 19.1 us -> 15.3 us  [the longest x7 12.4 us: local(): ups[part] = lax.ppermute(ups[part], 'head', up)]
    ppermute x5 -> x8, waiting for transfers between devices: 13.4 us -> 14.4 us  [exchange(): return lax.ppermute(x, 'head', [(i, i ^ distance) for i in range(devices)])]
    ppermute x30 -> x14, waiting for transfers between devices: 12 us -> 10.9 us  [the longest x7 9.66 us: local(): downs[part] = lax.ppermute(downs[part], 'head', down)]
    pallas_call x1 -> x4, Pallas kernels: 18.8 us -> 19.3 us  [the longest x2 12.5 us: attend(): pl.pallas_call(functools.partial(attend_kernel, len(pieces), first * half...]
    ppermute x5 -> x8, starting transfers between devices: 5.97 us -> 6.14 us  [exchange(): return lax.ppermute(x, 'head', [(i, i ^ distance) for i in range(devices)])]
  transfers between devices with their start and end apart: 35 -> 22, of which waited for: 15 -> 12; matrix products, arithmetic and copies ran while one was open for 5% -> 3% of each run, Pallas kernels for 0% -> 17%
where the time goes in v2:
time: 74 us; the launch traced here: 73.7 us
  waiting for transfers between devices  25.4 us (34%)
  starting transfers between devices  21.4 us (29%)
  Pallas kernels  19.3 us (26%)
  local copies, waits for them, and re-layouts  6.64 us (9%)
  other arithmetic  0.87 us (1%)
    ppermute x8, waiting for transfers between devices, exchange(): return lax.ppermute(x, 'head', [(i, i ^ distance) for i in range(devices)])  14.4 us
    pallas_call x2, Pallas kernels, attend(): pl.pallas_call(functools.partial(attend_kernel, len(pieces), first * half...  12.5 us
    ppermute x7, starting transfers between devices, local(): ups[part] = lax.ppermute(ups[part], 'head', up)  12.4 us
    ppermute x7, waiting for transfers between devices, local(): downs[part] = lax.ppermute(downs[part], 'head', down)  9.66 us
    pallas_call x1, Pallas kernels, local(): pl.pallas_call(functools.partial(project_kernel, len(partial), heads, ste...  6.39 us
    ppermute x8, starting transfers between devices, exchange(): return lax.ppermute(x, 'head', [(i, i ^ distance) for i in range(devices)])  6.14 us
    unnamed x6, local copies, waits for them, and re-layouts  3.34 us
    ppermute x7, starting transfers between devices, local(): downs[part] = lax.ppermute(downs[part], 'head', down)  2.83 us
  transfers between devices with their start and end apart: 22, of which 12 were waited for; matrix products, arithmetic and copies ran while one was open for 3% of the time, Pallas kernels for 17%

profile of v2, /device:TPU:0, one launch (start us, length us, event | category | flops | bytes accessed | tf_op | source)
XLA Modules:
  0.0 73.7 jit_solution(5327310372493129796)
XLA Ops:
  0.0 1.0 %fusion = (bf16[1,576,128]{2,1,0:T(8,128)(2,1)S(1)}, bf16[1,576,128]{2,1,0:T(8,128)(2,1)S(1)}) fusion(bf16[2,576,128]{2,1,0:T(8,128)(2,1)} %bitcast.8), kind=kLoop, calls=%fused_computation.4 | loop fusion | bytes 589824 | tf_op jit(solution)/shard_map/slice | solution.py:313
  1.0 3.1 %collective-permute-start = (bf16[1,576,128]{2,1,0:T(8,128)(2,1)S(1)}, bf16[1,576,128]{2,1,0:T(8,128)(2,1)S(1)}, u32[]{:S(2)}, u32[]{:S(2)}) collective-permute-start(bf16[1,576,128]{2,1,0:T(8,128)(2,1)S(1)} %get-tuple-element.34.rest_0_), channel_id=1, source_target_pairs={{0,4},{1,5},{4,8},{5,9},{8,12},{9,13},{12,14},{13,15},{14,10},{15,... | collective-permute-start | bytes 442376 | tf_op jit(solution)/shard_map/ppermute | solution.py:345
  4.1 1.6 %collective-permute-start.1 = (bf16[1,576,128]{2,1,0:T(8,128)(2,1)S(1)}, bf16[1,576,128]{2,1,0:T(8,128)(2,1)S(1)}, u32[]{:S(2)}, u32[]{:S(2)}) collective-permute-start(bf16[1,576,128]{2,1,0:T(8,128)(2,1)S(1)} %get-tuple-element.33.rest_1_), channel_id=1, source_target_pairs={{0,4},{1,5},{4,8},{5,9},{8,12},{9,13},{12,14},{13,15},{14,10},{15,... | collective-permute-start | bytes 442376 | tf_op jit(solution)/shard_map/ppermute | solution.py:345
  5.7 0.4 collective-permute-start.2
  6.1 0.0 collective-permute-start.3
  6.1 0.8 %reshape.9 = s32[64]{0:T(128)S(1)} reshape(s32[8,8]{1,0:T(8,128)} %param.15) | data formatting | bytes 512 | tf_op jit(solution)/shard_map/reshape | solution.py:323
  6.9 0.7 dynamic-slice_bitcast_fusion
  7.6 0.7 %concatenate.3.info_ref = s32[113]{0:T(128)S(1)} concatenate(s32[8]{0:T(128)} %param.14, s32[8]{0:T(128)} %param.16, s32[64]{0:T(128)S(1)} %reshape.9, s32[32]{0:T(128)S(1)} %dynamic-slice_bitcast_fusion, s32[1]{0:T(128)} %bitcast.2), dimensions={0} | concatenate | bytes 904 | tf_op jit(solution)/shard_map/concatenate | solution.py:322
  8.4 1.2 %copy-done.1 = bf16[8,128,512]{2,1,0:T(8,128)(2,1)S(1)} copy-done((bf16[8,128,512]{2,1,0:T(8,128)(2,1)S(1)}, bf16[8,128,512]{2,1,0:T(8,128)(2,1)}, u32[]{:S(2)}) %copy-start.1) | copy-done | bytes 1048600
  9.6 0.9 %copy-done.2 = bf16[32,1536]{1,0:T(8,128)(2,1)S(1)} copy-done((bf16[32,1536]{1,0:T(8,128)(2,1)S(1)}, bf16[32,1536]{1,0:T(8,128)(2,1)}, u32[]{:S(2)}) %copy-start.2) | copy-done | bytes 98328
  10.5 0.4 absorb_queries.1
  10.8 0.2 collective-permute-done.1.rest_4_
  11.0 1.2 %collective-permute-done.2.rest_3_ = bf16[1,576,128]{2,1,0:T(8,128)(2,1)S(1)} collective-permute-done((bf16[1,576,128]{2,1,0:T(8,128)(2,1)S(1)}, bf16[1,576,128]{2,1,0:T(8,128)(2,1)S(1)}, u32[]{:S(2)}, u32[]{:S(2)}) %collective-permute-start.2) | collective-permute-done | bytes 147488 | tf_op jit(solution)/shard_map/ppermute | solution.py:348
  12.3 1.6 %collective-permute-done.3.rest_5_ = bf16[1,576,128]{2,1,0:T(8,128)(2,1)S(1)} collective-permute-done((bf16[1,576,128]{2,1,0:T(8,128)(2,1)S(1)}, bf16[1,576,128]{2,1,0:T(8,128)(2,1)S(1)}, u32[]{:S(2)}, u32[]{:S(2)}) %collective-permute-start.3) | collective-permute-done | bytes 147488 | tf_op jit(solution)/shard_map/ppermute | solution.py:348
  13.8 1.6 %collective-permute-start.5 = (bf16[1,576,128]{2,1,0:T(8,128)(2,1)S(1)}, bf16[1,576,128]{2,1,0:T(8,128)(2,1)S(1)}, u32[]{:S(2)}, u32[]{:S(2)}) collective-permute-start(bf16[1,576,128]{2,1,0:T(8,128)(2,1)S(1)} %collective-permute-done.rest_2_), channel_id=1, source_target_pairs={{0,4},{1,5},{4,8},{5,9},{8,12},{9,13},{12,14},{13,15},{14,10},{15,... | collective-permute-start | bytes 442376 | tf_op jit(solution)/shard_map/ppermute | solution.py:345
  15.4 0.4 collective-permute-start.8
  15.9 0.4 collective-permute-start.6
  16.3 1.6 %collective-permute-start.7 = (bf16[1,576,128]{2,1,0:T(8,128)(2,1)S(1)}, bf16[1,576,128]{2,1,0:T(8,128)(2,1)S(1)}, u32[]{:S(2)}, u32[]{:S(2)}) collective-permute-start(bf16[1,576,128]{2,1,0:T(8,128)(2,1)S(1)} %collective-permute-done.1.rest_4_), channel_id=1, source_target_pairs={{0,4},{1,5},{4,8},{5,9},{8,12},{9,13},{12,14},{13,15},{14,10},{15,... | collective-permute-start | bytes 442376 | tf_op jit(solution)/shard_map/ppermute | solution.py:345
  17.9 1.1 %collective-permute-done.5.rest_6_ = bf16[1,576,128]{2,1,0:T(8,128)(2,1)S(1)} collective-permute-done((bf16[1,576,128]{2,1,0:T(8,128)(2,1)S(1)}, bf16[1,576,128]{2,1,0:T(8,128)(2,1)S(1)}, u32[]{:S(2)}, u32[]{:S(2)}) %collective-permute-start.5) | collective-permute-done | bytes 147488 | tf_op jit(solution)/shard_map/ppermute | solution.py:345
  19.0 1.6 %collective-permute-start.9 = (bf16[1,576,128]{2,1,0:T(8,128)(2,1)S(1)}, bf16[1,576,128]{2,1,0:T(8,128)(2,1)S(1)}, u32[]{:S(2)}, u32[]{:S(2)}) collective-permute-start(bf16[1,576,128]{2,1,0:T(8,128)(2,1)S(1)} %collective-permute-done.5.rest_6_), channel_id=1, source_target_pairs={{0,4},{1,5},{4,8},{5,9},{8,12},{9,13},{12,14},{13,15},{14,10},{15,... | collective-permute-start | bytes 442376 | tf_op jit(solution)/shard_map/ppermute | solution.py:345
  20.6 1.6 %collective-permute-done.8.rest_9_ = bf16[1,576,128]{2,1,0:T(8,128)(2,1)S(1)} collective-permute-done((bf16[1,576,128]{2,1,0:T(8,128)(2,1)S(1)}, bf16[1,576,128]{2,1,0:T(8,128)(2,1)S(1)}, u32[]{:S(2)}, u32[]{:S(2)}) %collective-permute-start.8) | collective-permute-done | bytes 147488 | tf_op jit(solution)/shard_map/ppermute | solution.py:348
  22.1 0.4 collective-permute-start.12
  22.6 2.7 %collective-permute-done.6.rest_7_ = bf16[1,576,128]{2,1,0:T(8,128)(2,1)S(1)} collective-permute-done((bf16[1,576,128]{2,1,0:T(8,128)(2,1)S(1)}, bf16[1,576,128]{2,1,0:T(8,128)(2,1)S(1)}, u32[]{:S(2)}, u32[]{:S(2)}) %collective-permute-start.6) | collective-permute-done | bytes 147488 | tf_op jit(solution)/shard_map/ppermute | solution.py:348
  25.3 0.4 collective-permute-start.10
  25.8 1.6 %collective-permute-start.11 = (bf16[1,576,128]{2,1,0:T(8,128)(2,1)S(1)}, bf16[1,576,128]{2,1,0:T(8,128)(2,1)S(1)}, u32[]{:S(2)}, u32[]{:S(2)}) collective-permute-start(bf16[1,576,128]{2,1,0:T(8,128)(2,1)S(1)} %collective-permute-done.7.rest_8_), channel_id=1, source_target_pairs={{0,4},{1,5},{4,8},{5,9},{8,12},{9,13},{12,14},{13,15},{14,10},{15,... | collective-permute-start | bytes 442376 | tf_op jit(solution)/shard_map/ppermute | solution.py:345
  27.3 1.5 %collective-permute-start.13 = (bf16[1,576,128]{2,1,0:T(8,128)(2,1)S(1)}, bf16[1,576,128]{2,1,0:T(8,128)(2,1)S(1)}, u32[]{:S(2)}, u32[]{:S(2)}) collective-permute-start(bf16[1,576,128]{2,1,0:T(8,128)(2,1)S(1)} %collective-permute-done.9.rest_10_), channel_id=1, source_target_pairs={{0,4},{1,5},{4,8},{5,9},{8,12},{9,13},{12,14},{13,15},{14,10},{15,... | collective-permute-start | bytes 442376 | tf_op jit(solution)/shard_map/ppermute | solution.py:345
  28.8 0.6 collective-permute-start.14
  29.4 2.6 %collective-permute-done.10.rest_11_ = bf16[1,576,128]{2,1,0:T(8,128)(2,1)S(1)} collective-permute-done((bf16[1,576,128]{2,1,0:T(8,128)(2,1)S(1)}, bf16[1,576,128]{2,1,0:T(8,128)(2,1)S(1)}, u32[]{:S(2)}, u32[]{:S(2)}) %collective-permute-start.10) | collective-permute-done | bytes 147488 | tf_op jit(solution)/shard_map/ppermute | solution.py:348
  31.9 8.6 %attend.2 = (f32[256,512]{1,0:T(8,128)S(1)}, f32[256,128]{1,0:T(8,128)S(1)}, bf16[256,640]{1,0:T(8,128)(2,1)S(1)}) custom-call(s32[113]{0:T(128)S(1)} %concatenate.3.info_ref, bf16[8,32,576]{2,1,0:T(8,128)(2,1)S(1)} %bitcast.6, bf16[8,32,576]{2,1,0:T(8,128)(2,1)S(1)} %collective-permute-done.4.theirs_ref, ...), custom_call_target="tpu_custom_call" | custom-call | flops 264241152 | bytes 2064384 | tf_op jit(solution)/shard_map/attend/pallas_call | solution.py:272
  40.5 0.1 collective-permute-start.15
  40.6 3.9 %attend.3 = (f32[256,512]{1,0:T(8,128)S(1)}, f32[256,128]{1,0:T(8,128)S(1)}, bf16[256,640]{1,0:T(8,128)(2,1)S(1)}) custom-call(s32[113]{0:T(128)S(1)} %concatenate.3.info_ref, bf16[8,32,576]{2,1,0:T(8,128)(2,1)S(1)} %bitcast.7, bf16[8,32,576]{2,1,0:T(8,128)(2,1)S(1)} %collective-permute-done.4.theirs_ref, ...), custom_call_target="tpu_custom_call" | custom-call | flops 37748736 | bytes 294912 | tf_op jit(solution)/shard_map/attend/pallas_call | solution.py:272
  44.6 1.1 %collective-permute-start.16 = (bf16[256,640]{1,0:T(8,128)(2,1)S(1)}, bf16[256,640]{1,0:T(8,128)(2,1)S(1)}, u32[]{:S(2)}, u32[]{:S(2)}) collective-permute-start(bf16[256,640]{1,0:T(8,128)(2,1)S(1)} %get-tuple-element.30), channel_id=1, source_target_pairs={{0,1},{1,0},{2,3},{3,2},{4,5},{5,4},{6,7},{7,6},{8,9},{9,8},{10,11... | collective-permute-start | bytes 983048 | tf_op jit(solution)/shard_map/ppermute | solution.py:267
  45.7 1.3 %collective-permute-done.16.rest_5_ = bf16[256,640]{1,0:T(8,128)(2,1)S(1)} collective-permute-done((bf16[256,640]{1,0:T(8,128)(2,1)S(1)}, bf16[256,640]{1,0:T(8,128)(2,1)S(1)}, u32[]{:S(2)}, u32[]{:S(2)}) %collective-permute-start.16) | collective-permute-done | bytes 327712 | tf_op jit(solution)/shard_map/ppermute | solution.py:267
  46.9 1.2 %copy-done = bf16[8,512,128]{2,1,0:T(8,128)(2,1)S(1)} copy-done((bf16[8,512,128]{2,1,0:T(8,128)(2,1)S(1)}, bf16[8,512,128]{2,1,0:T(8,128)(2,1)}, u32[]{:S(2)}) %copy-start) | copy-done | bytes 1048600
  48.1 6.4 %merge_and_project.1 = (bf16[32,7168]{1,0:T(8,128)(2,1)S(1)}, bf16[32,7168]{1,0:T(8,128)(2,1)S(1)}) custom-call(s32[113]{0:T(128)S(1)} %concatenate.3.info_ref, bf16[8,512,128]{2,1,0:T(8,128)(2,1)S(1)} %copy-done, bf16[1024,7168]{1,0:T(8,128)(2,1)} %out_w_ref.1, f32[256,512]{1,0:T(8,128)S(1)} %get-tuple-element.25.rest_0_, ...), custom_call_target="tpu_custom_call" | custom-call | tf_op jit(solution)/shard_map/merge_and_project/pallas_call | solution.py:359
  54.5 0.4 collective-permute-start.17
  55.0 1.4 %collective-permute-done.17 = bf16[32,7168]{1,0:T(8,128)(2,1)S(1)} collective-permute-done((bf16[32,7168]{1,0:T(8,128)(2,1)S(1)}, bf16[32,7168]{1,0:T(8,128)(2,1)S(1)}, u32[]{:S(2)}, u32[]{:S(2)}) %collective-permute-start.17) | collective-permute-done | bytes 458784 | tf_op jit(solution)/shard_map/ppermute | solution.py:267
  56.4 0.1 add_convert_fusion
  56.6 0.1 collective-permute-start.18
  56.7 7.9 %collective-permute-done.18 = bf16[16,7168]{1,0:T(8,128)(2,1)S(1)} collective-permute-done((bf16[16,7168]{1,0:T(8,128)(2,1)S(1)}, bf16[16,7168]{1,0:T(8,128)(2,1)S(1)}, u32[]{:S(2)}, u32[]{:S(2)}) %collective-permute-start.18) | collective-permute-done | bytes 229408 | tf_op jit(solution)/shard_map/ppermute | solution.py:267
  64.5 0.1 add_convert_fusion.1
  64.6 0.1 fusion.1
  64.7 1.7 %collective-permute-start.21 = (bf16[4,7168]{1,0:T(4,128)(2,1)S(1)}, bf16[4,7168]{1,0:T(4,128)(2,1)S(1)}, u32[]{:S(2)}, u32[]{:S(2)}) collective-permute-start(bf16[4,7168]{1,0:T(4,128)(2,1)S(1)} %get-tuple-element.36), channel_id=1, source_target_pairs={{0,12},{1,13},{2,14},{3,15},{4,8},{5,9},{6,10},{7,11},{8,4},{9,5},... | collective-permute-start | bytes 172040 | tf_op jit(solution)/shard_map/ppermute | solution.py:267
  66.4 0.8 %collective-permute-start.20 = (bf16[4,7168]{1,0:T(4,128)(2,1)S(1)}, bf16[4,7168]{1,0:T(4,128)(2,1)S(1)}, u32[]{:S(2)}, u32[]{:S(2)}) collective-permute-start(bf16[4,7168]{1,0:T(4,128)(2,1)S(1)} %get-tuple-element.37), channel_id=1, source_target_pairs={{0,8},{1,9},{2,10},{3,11},{4,12},{5,13},{6,14},{7,15},{8,0},{9,1},... | collective-permute-start | bytes 172040 | tf_op jit(solution)/shard_map/ppermute | solution.py:267
  67.2 1.9 %collective-permute-start.19 = (bf16[4,7168]{1,0:T(4,128)(2,1)S(1)}, bf16[4,7168]{1,0:T(4,128)(2,1)S(1)}, u32[]{:S(2)}, u32[]{:S(2)}) collective-permute-start(bf16[4,7168]{1,0:T(4,128)(2,1)S(1)} %get-tuple-element.35), channel_id=1, source_target_pairs={{0,4},{1,5},{2,6},{3,7},{4,0},{5,1},{6,2},{7,3},{8,12},{9,13},{10,... | collective-permute-start | bytes 172040 | tf_op jit(solution)/shard_map/ppermute | solution.py:267
  69.1 1.9 %collective-permute-done.21 = bf16[4,7168]{1,0:T(4,128)(2,1)S(1)} collective-permute-done((bf16[4,7168]{1,0:T(4,128)(2,1)S(1)}, bf16[4,7168]{1,0:T(4,128)(2,1)S(1)}, u32[]{:S(2)}, u32[]{:S(2)}) %collective-permute-start.21) | collective-permute-done | bytes 57376 | tf_op jit(solution)/shard_map/ppermute | solution.py:267
  71.1 1.9 %collective-permute-done.20 = bf16[4,7168]{1,0:T(4,128)(2,1)S(1)} collective-permute-done((bf16[4,7168]{1,0:T(4,128)(2,1)S(1)}, bf16[4,7168]{1,0:T(4,128)(2,1)S(1)}, u32[]{:S(2)}, u32[]{:S(2)}) %collective-permute-start.20) | collective-permute-done | bytes 57376 | tf_op jit(solution)/shard_map/ppermute | solution.py:267
  73.0 0.7 add_convert_fusion.2
  (15 shorter events, 0.1 us)
Async XLA Ops:
  1.0 9.8 %collective-permute-start = (bf16[1,576,128]{2,1,0:T(8,128)(2,1)S(1)}, bf16[1,576,128]{2,1,0:T(8,128)(2,1)S(1)}, u32[]{:S(2)}, u32[]{:S(2)}) collective-permute-start(bf16[1,576,128]{2,1,0:T(8,128)(2,1)S(1)} %get-tuple-element.34.rest_0_), channel_id=1, source_target_pairs={{0,4},{1,5},{4,8},{5,9},{8,12},{9,13},{12,14},{13,15},{14,10},{15,... | collective-permute-start | bytes 442376 | tf_op jit(solution)/shard_map/ppermute | solution.py:345
  4.1 7.0 %collective-permute-start.1 = (bf16[1,576,128]{2,1,0:T(8,128)(2,1)S(1)}, bf16[1,576,128]{2,1,0:T(8,128)(2,1)S(1)}, u32[]{:S(2)}, u32[]{:S(2)}) collective-permute-start(bf16[1,576,128]{2,1,0:T(8,128)(2,1)S(1)} %get-tuple-element.33.rest_1_), channel_id=1, source_target_pairs={{0,4},{1,5},{4,8},{5,9},{8,12},{9,13},{12,14},{13,15},{14,10},{15,... | collective-permute-start | bytes 442376 | tf_op jit(solution)/shard_map/ppermute | solution.py:345
  5.7 6.6 %collective-permute-start.2 = (bf16[1,576,128]{2,1,0:T(8,128)(2,1)S(1)}, bf16[1,576,128]{2,1,0:T(8,128)(2,1)S(1)}, u32[]{:S(2)}, u32[]{:S(2)}) collective-permute-start(bf16[1,576,128]{2,1,0:T(8,128)(2,1)S(1)} %get-tuple-element.34.rest_0_), channel_id=1, source_target_pairs={{4,0},{5,1},{8,4},{9,5},{12,8},{13,9},{14,12},{15,13},{10,14},{11,... | collective-permute-start | bytes 442376 | tf_op jit(solution)/shard_map/ppermute | solution.py:348
  6.1 7.7 %collective-permute-start.3 = (bf16[1,576,128]{2,1,0:T(8,128)(2,1)S(1)}, bf16[1,576,128]{2,1,0:T(8,128)(2,1)S(1)}, u32[]{:S(2)}, u32[]{:S(2)}) collective-permute-start(bf16[1,576,128]{2,1,0:T(8,128)(2,1)S(1)} %get-tuple-element.33.rest_1_), channel_id=1, source_target_pairs={{4,0},{5,1},{8,4},{9,5},{12,8},{13,9},{14,12},{15,13},{10,14},{11,... | collective-permute-start | bytes 442376 | tf_op jit(solution)/shard_map/ppermute | solution.py:348
  8.3 1.2 %copy-start.1 = (bf16[8,128,512]{2,1,0:T(8,128)(2,1)S(1)}, bf16[8,128,512]{2,1,0:T(8,128)(2,1)}, u32[]{:S(2)}) copy-start(bf16[8,128,512]{2,1,0:T(8,128)(2,1)} %absorb_ref.1) | copy-start | bytes 3145732
  9.6 0.9 %copy-start.2 = (bf16[32,1536]{1,0:T(8,128)(2,1)S(1)}, bf16[32,1536]{1,0:T(8,128)(2,1)}, u32[]{:S(2)}) copy-start(bf16[32,1536]{1,0:T(8,128)(2,1)} %query_ref.1) | copy-start | bytes 294916
  13.8 5.1 %collective-permute-start.5 = (bf16[1,576,128]{2,1,0:T(8,128)(2,1)S(1)}, bf16[1,576,128]{2,1,0:T(8,128)(2,1)S(1)}, u32[]{:S(2)}, u32[]{:S(2)}) collective-permute-start(bf16[1,576,128]{2,1,0:T(8,128)(2,1)S(1)} %collective-permute-done.rest_2_), channel_id=1, source_target_pairs={{0,4},{1,5},{4,8},{5,9},{8,12},{9,13},{12,14},{13,15},{14,10},{15,... | collective-permute-start | bytes 442376 | tf_op jit(solution)/shard_map/ppermute | solution.py:345
  15.4 6.7 %collective-permute-start.8 = (bf16[1,576,128]{2,1,0:T(8,128)(2,1)S(1)}, bf16[1,576,128]{2,1,0:T(8,128)(2,1)S(1)}, u32[]{:S(2)}, u32[]{:S(2)}) collective-permute-start(bf16[1,576,128]{2,1,0:T(8,128)(2,1)S(1)} %collective-permute-done.3.rest_5_), channel_id=1, source_target_pairs={{4,0},{5,1},{8,4},{9,5},{12,8},{13,9},{14,12},{15,13},{10,14},{11,... | collective-permute-start | bytes 442376 | tf_op jit(solution)/shard_map/ppermute | solution.py:348
  15.9 13.5 %collective-permute-start.4 = (bf16[8,32,576]{2,1,0:T(8,128)(2,1)S(1)}, bf16[8,32,576]{2,1,0:T(8,128)(2,1)S(1)}, u32[]{:S(2)}, u32[]{:S(2)}) collective-permute-start(bf16[8,32,576]{2,1,0:T(8,128)(2,1)S(1)} %bitcast.5), channel_id=1, source_target_pairs={{0,1},{1,0},{2,3},{3,2},{4,5},{5,4},{6,7},{7,6},{8,9},{9,8},{10,11... | collective-permute-start | bytes 884744 | tf_op jit(solution)/shard_map/ppermute | solution.py:267
  15.9 9.4 %collective-permute-start.6 = (bf16[1,576,128]{2,1,0:T(8,128)(2,1)S(1)}, bf16[1,576,128]{2,1,0:T(8,128)(2,1)S(1)}, u32[]{:S(2)}, u32[]{:S(2)}) collective-permute-start(bf16[1,576,128]{2,1,0:T(8,128)(2,1)S(1)} %collective-permute-done.2.rest_3_), channel_id=1, source_target_pairs={{4,0},{5,1},{8,4},{9,5},{12,8},{13,9},{14,12},{15,13},{10,14},{11,... | collective-permute-start | bytes 442376 | tf_op jit(solution)/shard_map/ppermute | solution.py:348
  16.3 9.4 %collective-permute-start.7 = (bf16[1,576,128]{2,1,0:T(8,128)(2,1)S(1)}, bf16[1,576,128]{2,1,0:T(8,128)(2,1)S(1)}, u32[]{:S(2)}, u32[]{:S(2)}) collective-permute-start(bf16[1,576,128]{2,1,0:T(8,128)(2,1)S(1)} %collective-permute-done.1.rest_4_), channel_id=1, source_target_pairs={{0,4},{1,5},{4,8},{5,9},{8,12},{9,13},{12,14},{13,15},{14,10},{15,... | collective-permute-start | bytes 442376 | tf_op jit(solution)/shard_map/ppermute | solution.py:345
  19.0 8.3 %collective-permute-start.9 = (bf16[1,576,128]{2,1,0:T(8,128)(2,1)S(1)}, bf16[1,576,128]{2,1,0:T(8,128)(2,1)S(1)}, u32[]{:S(2)}, u32[]{:S(2)}) collective-permute-start(bf16[1,576,128]{2,1,0:T(8,128)(2,1)S(1)} %collective-permute-done.5.rest_6_), channel_id=1, source_target_pairs={{0,4},{1,5},{4,8},{5,9},{8,12},{9,13},{12,14},{13,15},{14,10},{15,... | collective-permute-start | bytes 442376 | tf_op jit(solution)/shard_map/ppermute | solution.py:345
  22.1 6.7 %collective-permute-start.12 = (bf16[1,576,128]{2,1,0:T(8,128)(2,1)S(1)}, bf16[1,576,128]{2,1,0:T(8,128)(2,1)S(1)}, u32[]{:S(2)}, u32[]{:S(2)}) collective-permute-start(bf16[1,576,128]{2,1,0:T(8,128)(2,1)S(1)} %collective-permute-done.8.rest_9_), channel_id=1, source_target_pairs={{4,0},{5,1},{8,4},{9,5},{12,8},{13,9},{14,12},{15,13},{10,14},{11,... | collective-permute-start | bytes 442376 | tf_op jit(solution)/shard_map/ppermute | solution.py:348
  25.3 6.6 %collective-permute-start.10 = (bf16[1,576,128]{2,1,0:T(8,128)(2,1)S(1)}, bf16[1,576,128]{2,1,0:T(8,128)(2,1)S(1)}, u32[]{:S(2)}, u32[]{:S(2)}) collective-permute-start(bf16[1,576,128]{2,1,0:T(8,128)(2,1)S(1)} %collective-permute-done.6.rest_7_), channel_id=1, source_target_pairs={{4,0},{5,1},{8,4},{9,5},{12,8},{13,9},{14,12},{15,13},{10,14},{11,... | collective-permute-start | bytes 442376 | tf_op jit(solution)/shard_map/ppermute | solution.py:348
  25.8 6.2 %collective-permute-start.11 = (bf16[1,576,128]{2,1,0:T(8,128)(2,1)S(1)}, bf16[1,576,128]{2,1,0:T(8,128)(2,1)S(1)}, u32[]{:S(2)}, u32[]{:S(2)}) collective-permute-start(bf16[1,576,128]{2,1,0:T(8,128)(2,1)S(1)} %collective-permute-done.7.rest_8_), channel_id=1, source_target_pairs={{0,4},{1,5},{4,8},{5,9},{8,12},{9,13},{12,14},{13,15},{14,10},{15,... | collective-permute-start | bytes 442376 | tf_op jit(solution)/shard_map/ppermute | solution.py:345
  27.3 13.3 %collective-permute-start.13 = (bf16[1,576,128]{2,1,0:T(8,128)(2,1)S(1)}, bf16[1,576,128]{2,1,0:T(8,128)(2,1)S(1)}, u32[]{:S(2)}, u32[]{:S(2)}) collective-permute-start(bf16[1,576,128]{2,1,0:T(8,128)(2,1)S(1)} %collective-permute-done.9.rest_10_), channel_id=1, source_target_pairs={{0,4},{1,5},{4,8},{5,9},{8,12},{9,13},{12,14},{13,15},{14,10},{15,... | collective-permute-start | bytes 442376 | tf_op jit(solution)/shard_map/ppermute | solution.py:345
  28.8 11.8 %collective-permute-start.14 = (bf16[1,576,128]{2,1,0:T(8,128)(2,1)S(1)}, bf16[1,576,128]{2,1,0:T(8,128)(2,1)S(1)}, u32[]{:S(2)}, u32[]{:S(2)}) collective-permute-start(bf16[1,576,128]{2,1,0:T(8,128)(2,1)S(1)} %collective-permute-done.12.rest_13_), channel_id=1, source_target_pairs={{4,0},{5,1},{8,4},{9,5},{12,8},{13,9},{14,12},{15,13},{10,14},{11,... | collective-permute-start | bytes 442376 | tf_op jit(solution)/shard_map/ppermute | solution.py:348
  40.5 5.1 %collective-permute-start.15 = (bf16[256,640]{1,0:T(8,128)(2,1)S(1)}, bf16[256,640]{1,0:T(8,128)(2,1)S(1)}, u32[]{:S(2)}, u32[]{:S(2)}) collective-permute-start(bf16[256,640]{1,0:T(8,128)(2,1)S(1)} %get-tuple-element.29), channel_id=1, source_target_pairs={{0,1},{1,0},{2,3},{3,2},{4,5},{5,4},{6,7},{7,6},{8,9},{9,8},{10,11... | collective-permute-start | bytes 983048 | tf_op jit(solution)/shard_map/ppermute | solution.py:267
  44.6 2.4 %collective-permute-start.16 = (bf16[256,640]{1,0:T(8,128)(2,1)S(1)}, bf16[256,640]{1,0:T(8,128)(2,1)S(1)}, u32[]{:S(2)}, u32[]{:S(2)}) collective-permute-start(bf16[256,640]{1,0:T(8,128)(2,1)S(1)} %get-tuple-element.30), channel_id=1, source_target_pairs={{0,1},{1,0},{2,3},{3,2},{4,5},{5,4},{6,7},{7,6},{8,9},{9,8},{10,11... | collective-permute-start | bytes 983048 | tf_op jit(solution)/shard_map/ppermute | solution.py:267
  46.9 1.2 %copy-start = (bf16[8,512,128]{2,1,0:T(8,128)(2,1)S(1)}, bf16[8,512,128]{2,1,0:T(8,128)(2,1)}, u32[]{:S(2)}) copy-start(bf16[8,512,128]{2,1,0:T(8,128)(2,1)} %value_ref.1) | copy-start | bytes 3145732
  54.5 1.9 %collective-permute-start.17 = (bf16[32,7168]{1,0:T(8,128)(2,1)S(1)}, bf16[32,7168]{1,0:T(8,128)(2,1)S(1)}, u32[]{:S(2)}, u32[]{:S(2)}) collective-permute-start(bf16[32,7168]{1,0:T(8,128)(2,1)S(1)} %get-tuple-element.32), channel_id=1, source_target_pairs={{0,1},{1,0},{2,3},{3,2},{4,5},{5,4},{6,7},{7,6},{8,9},{9,8},{10,11... | collective-permute-start | bytes 1376264 | tf_op jit(solution)/shard_map/ppermute | solution.py:267
  56.6 7.9 %collective-permute-start.18 = (bf16[16,7168]{1,0:T(8,128)(2,1)S(1)}, bf16[16,7168]{1,0:T(8,128)(2,1)S(1)}, u32[]{:S(2)}, u32[]{:S(2)}) collective-permute-start(bf16[16,7168]{1,0:T(8,128)(2,1)S(1)} %slice.35), channel_id=1, source_target_pairs={{0,2},{1,3},{2,0},{3,1},{4,6},{5,7},{6,4},{7,5},{8,10},{9,11},{10,... | collective-permute-start | bytes 688136 | tf_op jit(solution)/shard_map/ppermute | solution.py:267
  64.7 6.4 %collective-permute-start.21 = (bf16[4,7168]{1,0:T(4,128)(2,1)S(1)}, bf16[4,7168]{1,0:T(4,128)(2,1)S(1)}, u32[]{:S(2)}, u32[]{:S(2)}) collective-permute-start(bf16[4,7168]{1,0:T(4,128)(2,1)S(1)} %get-tuple-element.36), channel_id=1, source_target_pairs={{0,12},{1,13},{2,14},{3,15},{4,8},{5,9},{6,10},{7,11},{8,4},{9,5},... | collective-permute-start | bytes 172040 | tf_op jit(solution)/shard_map/ppermute | solution.py:267
  66.4 6.6 %collective-permute-start.20 = (bf16[4,7168]{1,0:T(4,128)(2,1)S(1)}, bf16[4,7168]{1,0:T(4,128)(2,1)S(1)}, u32[]{:S(2)}, u32[]{:S(2)}) collective-permute-start(bf16[4,7168]{1,0:T(4,128)(2,1)S(1)} %get-tuple-element.37), channel_id=1, source_target_pairs={{0,8},{1,9},{2,10},{3,11},{4,12},{5,13},{6,14},{7,15},{8,0},{9,1},... | collective-permute-start | bytes 172040 | tf_op jit(solution)/shard_map/ppermute | solution.py:267
  67.2 5.8 %collective-permute-start.19 = (bf16[4,7168]{1,0:T(4,128)(2,1)S(1)}, bf16[4,7168]{1,0:T(4,128)(2,1)S(1)}, u32[]{:S(2)}, u32[]{:S(2)}) collective-permute-start(bf16[4,7168]{1,0:T(4,128)(2,1)S(1)} %get-tuple-element.35), channel_id=1, source_target_pairs={{0,4},{1,5},{2,6},{3,7},{4,0},{5,1},{6,2},{7,3},{8,12},{9,13},{10,... | collective-permute-start | bytes 172040 | tf_op jit(solution)/shard_map/ppermute | solution.py:267

commit v3 on v2

v3 whole, which is shorter than its diff:
```python
import functools
import math

import jax
import jax.numpy as jnp
import numpy as np
from jax import lax
from jax.experimental import pallas as pl
from jax.experimental.pallas import tpu as pltpu
from jax.sharding import PartitionSpec as P

OUT_TILE = 1024
LANES = 128
UNROLL = 4
LATE = 4
EMPTY = -1e30


def ring_of(chips):
    if chips == 8:
        return [0, 2, 4, 6, 7, 5, 3, 1]
    return list(range(chips))


def ring_places(chips):
    places = [(0, 0), (0, 1)]
    for hop in range(1, chips // 2 + 1):
        last = hop == chips // 2
        places += [(-hop, 0), (hop, 1)] if last else [(-hop, 0), (hop, 1), (hop, 0), (-hop, 1)]
    return places


def slots_by_device(chips, half):
    ring = ring_of(chips)
    position = {chip: i for i, chip in enumerate(ring)}
    table = np.full((2 * chips, 4 * chips * half), -1, np.int32)
    for device in range(2 * chips):
        for index, (hop, part) in enumerate(ring_places(chips)):
            source = ring[(position[device // 2] + hop) % chips] * 2 + device % 2
            for i in range(half):
                table[device, (source * 2 + part) * half + i] = index * half + i
    return table


def prepare_kernel(
    heads, steps, cuts,
    me_ref, query_hbm, absorb_hbm, length_hbm, table_hbm, slot_hbm, out_ref, plan_ref,
    query_ref, absorb_ref, length_ref, table_ref, slot_ref, ordered, sems,
):
    sources = (length_hbm, table_hbm, slot_hbm, query_hbm, absorb_hbm)
    targets = (length_ref, table_ref, slot_ref, query_ref, absorb_ref)
    copies = [
        pltpu.make_async_copy(a, b, sems.at[i]) for i, (a, b) in enumerate(zip(sources, targets))
    ]
    for copy in copies:
        copy.start()
    for copy in copies[:3]:
        copy.wait()
    requests = table_ref.shape[0]
    me = me_ref[0]
    stages = len(cuts) - 1
    capacity = plan_ref.shape[0] // stages

    def list_request(r, counts):
        length = length_ref[r]

        def list_block(j, counts):
            slot = slot_ref[me, table_ref[r, j]]
            use = r + 256 * (j == length - 1).astype(jnp.int32)
            counts = list(counts)
            for k in range(stages):
                here = (slot >= cuts[k]) & (slot < cuts[k + 1])
                at = jnp.where(here, counts[k] + 1, capacity - 1)
                plan_ref[k * capacity + at] = use + 512 * (slot - cuts[k])
                counts[k] = counts[k] + here.astype(jnp.int32)
            return tuple(counts)

        return lax.fori_loop(0, length, list_block, counts)

    counts = lax.fori_loop(0, requests, list_request, (jnp.int32(0),) * stages)
    for k in range(stages):
        plan_ref[k * capacity] = counts[k]
        for i in range(UNROLL):
            plan_ref[k * capacity + 1 + counts[k] + i] = requests

    rows = query_ref.shape[0]
    nope = absorb_ref.shape[1]
    head_width = query_ref.shape[1] // heads
    rope = head_width - nope
    kv_rank = absorb_ref.shape[2]
    for copy in copies[3:]:
        copy.wait()
    for h in range(heads):
        own = query_ref[:, h * head_width : (h + 1) * head_width]
        latent = jnp.dot(own[:, :nope], absorb_ref[h], preferred_element_type=jnp.float32)
        turned = jnp.concatenate(
            [own[:, nope:].astype(jnp.float32), jnp.zeros((rows, LANES - rope), jnp.float32)], axis=1
        )
        at = pl.ds(h, rows, stride=heads)
        for c in range(kv_rank // LANES):
            ordered[c, at] = latent[:, c * LANES : (c + 1) * LANES]
        ordered[kv_rank // LANES, at] = turned
    for c in range(kv_rank // LANES):
        out_ref[:, c * LANES : (c + 1) * LANES] = ordered[c].astype(jnp.bfloat16)
    out_ref[:, kv_rank:] = ordered[kv_rank // LANES, :, :rope].astype(jnp.bfloat16)


def attend_kernel(
    piece_count, stage, stages, heads, steps, kv_rank, scale, with_weight,
    plan_ref, mine_ref, theirs_ref, *rest,
):
    pieces, rest = rest[:piece_count], rest[piece_count:]
    if with_weight:
        weight_hbm, out_ref, lse_ref, away_ref, weight_ref, *rest = rest
    else:
        out_ref, lse_ref, away_ref, *rest = rest
    queries, cache, scores, top, total, latent, cache_sems, weight_sems = rest
    requests = top.shape[0] - 1
    row_block = queries.shape[1] // 2
    both = 2 * row_block
    block_rows = cache.shape[2]
    half = cache.shape[0] // piece_count
    base = plan_ref.shape[0] // stages * stage

    copies = [
        pltpu.make_async_copy(p, cache.at[pl.ds(i * half, half)], cache_sems.at[i])
        for i, p in enumerate(pieces)
    ]
    for copy in copies:
        copy.start()
    weight_copies = []
    if with_weight:
        tiles, _, tile = weight_ref.shape
        weight_copies = [
            pltpu.make_async_copy(
                weight_hbm.at[:, pl.ds(i * tile, tile)], weight_ref.at[i], weight_sems.at[i]
            )
            for i in range(tiles)
        ]
        for copy in weight_copies:
            copy.start()

    turns = (plan_ref[base] + UNROLL - 1) // UNROLL
    queries[:, :row_block] = mine_ref[...]
    queries[:, row_block:] = theirs_ref[...]
    top[...] = jnp.full_like(top, -jnp.inf)
    total[...] = jnp.zeros_like(total)
    latent[...] = jnp.zeros_like(latent)
    column = lax.broadcasted_iota(jnp.int32, (both, block_rows), 1)
    row = lax.broadcasted_iota(jnp.int32, (both, block_rows), 0)
    hidden = column + (steps - 1 - (row % row_block) // heads)
    for copy in copies:
        copy.wait()

    def score(turn, _):
        for i in range(UNROLL):
            u = turn * UNROLL + i
            use = plan_ref[base + 1 + u]
            r = use & 255
            s = jnp.dot(
                queries[jnp.minimum(r, requests - 1)], cache[use >> 9],
                preferred_element_type=jnp.float32,
            ) * scale
            seen = (hidden < block_rows) | ((use & 256) == 0)
            s = jnp.where(seen, s, -jnp.inf)
            scores[u] = s
            top[r] = jnp.maximum(top[r], s)
        return 0

    lax.fori_loop(0, turns, score, 0)
    batch = math.gcd(requests, 8)

    def peak(r, _):
        top[r] = jnp.broadcast_to(jnp.max(top[r], axis=1, keepdims=True), (both, block_rows))
        return 0

    lax.fori_loop(0, requests, peak, 0, unroll=batch)

    def mix(turn, _):
        for i in range(UNROLL):
            u = turn * UNROLL + i
            use = plan_ref[base + 1 + u]
            r = use & 255
            p = jnp.exp(scores[u] - top[r])
            total[r] += p
            latent[r] += lax.dot_general(
                p.astype(jnp.bfloat16),
                cache[use >> 9, :kv_rank],
                (((1,), (1,)), ((), ())),
                preferred_element_type=jnp.float32,
            )
        return 0

    lax.fori_loop(0, turns, mix, 0)

    lane = lax.broadcasted_iota(jnp.int32, (row_block, LANES), 1)

    def finish(r, _):
        at = pl.ds(pl.multiple_of(r * row_block, row_block), row_block)
        norm = jnp.sum(total[r], axis=1, keepdims=True)
        some = norm > 0
        safe = jnp.where(some, norm, 1.0)
        lse = jnp.where(some, top[r][:, :1] + jnp.log(safe), EMPTY)
        result = latent[r] * (1.0 / safe)
        out_ref[at] = result[:row_block]
        lse_ref[at] = jnp.broadcast_to(lse[:row_block], (row_block, LANES))
        rest = lse[row_block:]
        high = rest.astype(jnp.bfloat16).astype(jnp.float32)
        middle = (rest - high).astype(jnp.bfloat16).astype(jnp.float32)
        low = rest - high - middle
        terms = jnp.where(lane == 0, high, jnp.where(lane == 1, middle, jnp.where(lane == 2, low, 0.0)))
        away_ref[at, :kv_rank] = result[row_block:].astype(jnp.bfloat16)
        away_ref[at, kv_rank:] = terms.astype(jnp.bfloat16)
        return 0

    lax.fori_loop(0, requests, finish, 0, unroll=batch)
    for copy in weight_copies:
        copy.wait()


def project(placed, weight_ref, first, keep_ref, away_ref):
    tile = weight_ref.shape[2]
    half_rows = keep_ref.shape[0]
    for i in range(keep_ref.shape[1] // tile):
        result = jnp.dot(
            placed, weight_ref[first + i], preferred_element_type=jnp.float32
        ).astype(jnp.bfloat16)
        keep_ref[:, i * tile : (i + 1) * tile] = result[:half_rows]
        away_ref[:, i * tile : (i + 1) * tile] = result[half_rows:]


def merge_kernel(
    stages, heads, steps, chips,
    me_ref, owner_hbm, value_hbm, weight_ref, *rest,
):
    outs, lses, others = rest[:stages], rest[stages : 2 * stages], rest[2 * stages : 3 * stages]
    (away_ref, keep_ref, placed_ref, latent, head_rows, owner_ref, value_ref, sems) = rest[3 * stages :]
    owner_copy = pltpu.make_async_copy(owner_hbm, owner_ref, sems.at[0])
    value_copy = pltpu.make_async_copy(value_hbm, value_ref, sems.at[1])
    owner_copy.start()
    value_copy.start()
    kv_rank, v_width = value_ref.shape[1:]
    rows = head_rows.shape[0]
    requests = rows // steps
    chunk = 64

    def merge(i, _):
        at = pl.ds(pl.multiple_of(i * chunk, chunk), chunk)
        parts = [(o[at], e[at][:, :1]) for o, e in zip(outs, lses)]
        for other in others:
            terms = jnp.sum(other[at, kv_rank:].astype(jnp.float32), axis=1, keepdims=True)
            parts.append((other[at, :kv_rank].astype(jnp.float32), terms))
        peak = functools.reduce(jnp.maximum, [e for _, e in parts])
        shares = [jnp.exp(e - peak) for _, e in parts]
        inverse = 1.0 / functools.reduce(jnp.add, shares)
        whole = functools.reduce(jnp.add, [o * (w * inverse) for (o, _), w in zip(parts, shares)])
        for c in range(kv_rank // LANES):
            latent[c, at] = whole[:, c * LANES : (c + 1) * LANES]
        return 0

    lax.fori_loop(0, rows * heads // chunk, merge, 0, unroll=True)

    value_copy.wait()
    for h in range(heads):
        mine = jnp.concatenate(
            [latent[c, pl.ds(h, rows, stride=heads)] for c in range(kv_rank // LANES)], axis=1
        ).astype(jnp.bfloat16)
        head_rows[:, h * v_width : (h + 1) * v_width] = jnp.dot(
            mine, value_ref[h], preferred_element_type=jnp.float32
        ).astype(jnp.bfloat16)

    half_rows = away_ref.shape[0]
    me = me_ref[0]
    target = lax.broadcasted_iota(jnp.int32, (2 * half_rows, rows), 0)
    origin = lax.broadcasted_iota(jnp.int32, (2 * half_rows, rows), 1)
    owner_copy.wait()

    def place(r, picked):
        apart = owner_ref[r] ^ me
        order = (apart & 1) * chips + ((apart >> 1) & 1) * (chips // 2) + (apart >> 2)
        shifted = origin - r * steps
        hit = (target - order * steps == shifted) & (shifted >= 0) & (shifted < steps)
        return jnp.where(hit, 1.0, picked)

    picker = lax.fori_loop(
        0, requests, place, jnp.zeros((2 * half_rows, rows), jnp.float32), unroll=math.gcd(requests, 8)
    )
    placed = jnp.dot(
        picker.astype(jnp.bfloat16), head_rows[...], preferred_element_type=jnp.float32
    ).astype(jnp.bfloat16)
    placed_ref[...] = placed
    project(placed, weight_ref, 0, keep_ref, away_ref)


def second_kernel(first, placed_ref, weight_ref, away_ref, keep_ref):
    project(placed_ref[...], weight_ref, first, keep_ref, away_ref)


def local(q_heads, w_absorb, w_value, w_out, latent_cache, ctx_blocks, block_table, owner):
    heads, _, kv_rank = w_absorb.shape
    row_count = q_heads.shape[0]
    head_width = q_heads.shape[1] // heads
    requests, max_blocks = block_table.shape
    steps = row_count // requests
    devices = lax.axis_size("head")
    chips = devices // 2
    blocks_here, block_rows, row_width = latent_cache.shape
    half = blocks_here // 2
    width = w_out.shape[1]
    v_width = w_value.shape[2]
    row_block = steps * heads
    flat_rows = requests * row_block
    tiles = width // OUT_TILE
    mebi = 1024 * 1024
    me = lax.axis_index("head").astype(jnp.int32).reshape(1)
    smem = pl.BlockSpec(memory_space=pltpu.SMEM)
    vmem = pl.BlockSpec(memory_space=pltpu.VMEM)
    hbm = pl.BlockSpec(memory_space=pltpu.HBM)

    def exchange(x, distance):
        return lax.ppermute(x, "head", [(i, i ^ distance) for i in range(devices)])

    piece_total = len(ring_places(chips))
    cuts = (0, (piece_total - LATE) * half, piece_total * half)
    stages = len(cuts) - 1
    capacity = requests * max_blocks + UNROLL + 2

    def prepare():
        slots = jnp.asarray(slots_by_device(chips, half))
        queries, plan = pl.pallas_call(
            functools.partial(prepare_kernel, heads, steps, cuts),
            out_shape=(
                jax.ShapeDtypeStruct((flat_rows, row_width), jnp.bfloat16),
                jax.ShapeDtypeStruct((stages * capacity,), jnp.int32),
            ),
            in_specs=[smem] + [hbm] * 5,
            out_specs=(vmem, smem),
            scratch_shapes=[
                pltpu.VMEM(q_heads.shape, jnp.bfloat16),
                pltpu.VMEM(w_absorb.shape, jnp.bfloat16),
                pltpu.SMEM(ctx_blocks.shape, jnp.int32),
                pltpu.SMEM(block_table.shape, jnp.int32),
                pltpu.SMEM(slots.shape, jnp.int32),
                pltpu.VMEM((kv_rank // LANES + 1, flat_rows, LANES), jnp.float32),
                pltpu.SemaphoreType.DMA((5,)),
            ],
            compiler_params=pltpu.CompilerParams(vmem_limit_bytes=8 * mebi),
            cost_estimate=pl.CostEstimate(
                flops=2 * w_absorb.size * row_count, bytes_accessed=4 * w_absorb.size, transcendentals=0
            ),
            name="prepare",
        )(me, q_heads, w_absorb, ctx_blocks, block_table, slots)
        return queries.reshape(requests, row_block, row_width), plan

    def attend(plan, mine, theirs, pieces, stage):
        slots = len(pieces) * half
        with_weight = stage == 0
        weight_shape = jax.ShapeDtypeStruct((tiles, w_out.shape[0], OUT_TILE), jnp.bfloat16)
        return pl.pallas_call(
            functools.partial(
                attend_kernel, len(pieces), stage, stages, heads, steps, kv_rank,
                float(head_width) ** -0.5, with_weight,
            ),
            out_shape=(
                jax.ShapeDtypeStruct((flat_rows, kv_rank), jnp.float32),
                jax.ShapeDtypeStruct((flat_rows, LANES), jnp.float32),
                jax.ShapeDtypeStruct((flat_rows, kv_rank + LANES), jnp.bfloat16),
            ) + (weight_shape,) * with_weight,
            in_specs=[smem, vmem, vmem] + [hbm] * (len(pieces) + with_weight),
            out_specs=(vmem,) * (3 + with_weight),
            scratch_shapes=[
                pltpu.VMEM((requests, 2 * row_block, row_width), jnp.bfloat16),
                pltpu.VMEM((slots, row_width, block_rows), jnp.bfloat16),
                pltpu.VMEM((2 * slots + UNROLL, 2 * row_block, block_rows), jnp.float32),
                pltpu.VMEM((requests + 1, 2 * row_block, block_rows), jnp.float32),
                pltpu.VMEM((requests + 1, 2 * row_block, block_rows), jnp.float32),
                pltpu.VMEM((requests + 1, 2 * row_block, kv_rank), jnp.float32),
                pltpu.SemaphoreType.DMA((len(pieces),)),
                pltpu.SemaphoreType.DMA((tiles,)),
            ],
            compiler_params=pltpu.CompilerParams(vmem_limit_bytes=28 * mebi),
            cost_estimate=pl.CostEstimate(
                flops=2 * slots * 2 * row_block * block_rows * 2 * row_width,
                bytes_accessed=slots * block_rows * row_width * 2,
                transcendentals=0,
            ),
            name="attend",
        )(plan, mine, theirs, *pieces, *([w_out] * with_weight))

    ring = ring_of(chips)
    up = [
        (ring[i] * 2 + core, ring[(i + 1) % chips] * 2 + core)
        for i in range(chips)
        for core in range(2)
    ]
    down = [(b, a) for a, b in up]
    keys = jnp.swapaxes(latent_cache, 1, 2)
    ups = [keys[:half], keys[half:]]
    downs = list(ups)
    pieces = list(ups)
    for hop in range(1, chips // 2 + 1):
        last = hop == chips // 2
        if hop == 2:
            mine, plan = prepare()
            theirs = exchange(mine, 1)
            ups, downs, mine, plan = lax.optimization_barrier((ups, downs, mine, plan))
        if last:
            ups[0] = lax.ppermute(ups[0], "head", up)
            downs[1] = lax.ppermute(downs[1], "head", down)
            pieces += [ups[0], downs[1]]
        else:
            ups[0] = lax.ppermute(ups[0], "head", up)
            downs[1] = lax.ppermute(downs[1], "head", down)
            downs[0] = lax.ppermute(downs[0], "head", down)
            ups[1] = lax.ppermute(ups[1], "head", up)
            pieces += [ups[0], downs[1], downs[0], ups[1]]
    early, late = pieces[:-LATE], pieces[-LATE:]
    *early_part, weight = attend(plan, mine, theirs, early, 0)
    late_part = attend(plan, mine, theirs, late, 1)
    partial = [(out, lse, exchange(away, 1)) for out, lse, away in (early_part, late_part)]

    first = (tiles + 1) // 2
    part_rows = chips * steps
    parts = [
        jax.ShapeDtypeStruct((part_rows, n * OUT_TILE), jnp.bfloat16) for n in (first, tiles - first)
    ]
    placed_shape = jax.ShapeDtypeStruct((2 * part_rows, heads * v_width), jnp.bfloat16)
    outs, lses, others = zip(*partial)
    away, keep, placed = pl.pallas_call(
        functools.partial(merge_kernel, stages, heads, steps, chips),
        out_shape=(parts[0], parts[0], placed_shape),
        in_specs=[smem, hbm, hbm] + [vmem] * (1 + 3 * stages),
        out_specs=(vmem, vmem, vmem),
        scratch_shapes=[
            pltpu.VMEM((kv_rank // LANES, flat_rows, LANES), jnp.float32),
            pltpu.VMEM((row_count, heads * v_width), jnp.bfloat16),
            pltpu.SMEM(owner.shape, jnp.int32),
            pltpu.VMEM(w_value.shape, jnp.bfloat16),
            pltpu.SemaphoreType.DMA((2,)),
        ],
        compiler_params=pltpu.CompilerParams(vmem_limit_bytes=28 * mebi),
        name="merge_and_project",
    )(me, owner, w_value, weight, *outs, *lses, *others)
    away2, keep2 = pl.pallas_call(
        functools.partial(second_kernel, first),
        out_shape=(parts[1], parts[1]),
        in_specs=[vmem, vmem],
        out_specs=(vmem, vmem),
        compiler_params=pltpu.CompilerParams(vmem_limit_bytes=28 * mebi),
        cost_estimate=pl.CostEstimate(
            flops=2 * w_out.size * part_rows, bytes_accessed=w_out.size, transcendentals=0
        ),
        name="project_second",
    )(placed, weight)

    def add(x, *others):
        total = x.astype(jnp.float32)
        for other in others:
            total = total + other.astype(jnp.float32)
        return total.astype(jnp.bfloat16)

    results = []
    for mine_rows, other_rows in ((keep, away), (keep2, away2)):
        both = add(mine_rows, exchange(other_rows, 1))
        middle = part_rows // 2
        line = add(both[:middle], exchange(both[middle:], 2))
        received = [
            exchange(line[k * steps : (k + 1) * steps], 4 * k) for k in range(1, chips // 2)
        ]
        results.append(add(line[:steps], *received))
    return jnp.concatenate(results, axis=1)


def solution(mesh):
    return jax.shard_map(
        local,
        mesh=mesh,
        in_specs=(
            P("group", "head"),
            P("head", None, None),
            P("head", None, None),
            P("head", None),
            P(("group", "head"), None, None),
            P("group"),
            P("group", None),
            P("group"),
        ),
        out_specs=P(("group", "head"), None),
        check_vma=False,
    )
```

time: 74 us -> 68.1 us (0.920)
  waiting for transfers between devices: 25.4 us -> 16.6 us
  starting transfers between devices: 21.4 us -> 27.8 us
  Pallas kernels: 19.3 us -> 16.8 us
  local copies, waits for them, and re-layouts: 6.64 us -> 5.35 us
    ppermute x8 -> x13, starting transfers between devices: 6.14 us -> 12.7 us  [exchange(): return lax.ppermute(x, 'head', [(i, i ^ distance) for i in range(devices)])]
    ppermute x8 -> x13, waiting for transfers between devices: 14.4 us -> 9.62 us  [exchange(): return lax.ppermute(x, 'head', [(i, i ^ distance) for i in range(devices)])]
    ppermute x14, waiting for transfers between devices: 10.9 us -> 6.94 us  [the longest x4 2.98 us: local(): downs[1] = lax.ppermute(downs[1], 'head', down)]
    pallas_call x4 -> x5, Pallas kernels: 19.3 us -> 16.8 us  [the longest x2 11 us: attend(): pl.pallas_call(functools.partial(attend_kernel, len(pieces), stage, stage...]
    unnamed x6 -> x14, local copies, waits for them, and re-layouts: 3.34 us -> 4.16 us
    reshape x1 -> x0, local copies, waits for them, and re-layouts: 0.76 us -> none  [local(): block_table.reshape(-1)]
    concatenate x1 -> x0, local copies, waits for them, and re-layouts: 0.75 us -> none  [local(): jnp.concatenate([ctx_blocks, owner, block_table.reshape(-1), table[me], m...]
  transfers between devices with their start and end apart: 22 -> 27, of which waited for: 12 -> 10; matrix products, arithmetic and copies ran while one was open for 3% -> 0% of each run, Pallas kernels for 17% -> 19%
where the time goes in v3:
time: 68.1 us; the launch traced here: 67.6 us
  starting transfers between devices  27.8 us (41%)
  Pallas kernels  16.8 us (25%)
  waiting for transfers between devices  16.6 us (24%)
  local copies, waits for them, and re-layouts  5.35 us (8%)
  other arithmetic  0.89 us (1%)
    ppermute x13, starting transfers between devices, exchange(): return lax.ppermute(x, 'head', [(i, i ^ distance) for i in range(devices)])  12.7 us
    pallas_call x2, Pallas kernels, attend(): pl.pallas_call(functools.partial(attend_kernel, len(pieces), stage, stage...  11 us
    ppermute x13, waiting for transfers between devices, exchange(): return lax.ppermute(x, 'head', [(i, i ^ distance) for i in range(devices)])  9.62 us
    ppermute x4, starting transfers between devices, local(): ups[0] = lax.ppermute(ups[0], 'head', up)  7.7 us
    ppermute x3, starting transfers between devices, local(): ups[1] = lax.ppermute(ups[1], 'head', up)  4.72 us
    unnamed x14, local copies, waits for them, and re-layouts  4.16 us
    ppermute x4, waiting for transfers between devices, local(): downs[1] = lax.ppermute(downs[1], 'head', down)  2.98 us
    ppermute x3, waiting for transfers between devices, local(): downs[0] = lax.ppermute(downs[0], 'head', down)  2.85 us
  transfers between devices with their start and end apart: 27, of which 10 were waited for; matrix products, arithmetic and copies ran while one was open for 0% of the time, Pallas kernels for 19%

profile of v3, /device:TPU:0, one launch (start us, length us, event | category | flops | bytes accessed | tf_op | source)
XLA Modules:
  0.0 67.6 jit_solution(15471194543059612721)
XLA Ops:
  0.0 1.1 %fusion = (bf16[1,576,128]{2,1,0:T(8,128)(2,1)S(1)}, bf16[1,576,128]{2,1,0:T(8,128)(2,1)S(1)}) fusion(bf16[2,576,128]{2,1,0:T(8,128)(2,1)} %bitcast.6), kind=kLoop, calls=%fused_computation.7 | loop fusion | bytes 589824 | tf_op jit(solution)/shard_map/slice | solution.py:398
  1.1 3.1 %collective-permute-start = (bf16[1,576,128]{2,1,0:T(8,128)(2,1)S(1)}, bf16[1,576,128]{2,1,0:T(8,128)(2,1)S(1)}, u32[]{:S(2)}, u32[]{:S(2)}) collective-permute-start(bf16[1,576,128]{2,1,0:T(8,128)(2,1)S(1)} %get-tuple-element.46.rest_0_), channel_id=1, source_target_pairs={{0,4},{1,5},{4,8},{5,9},{8,12},{9,13},{12,14},{13,15},{14,10},{15,... | collective-permute-start | bytes 442376 | tf_op jit(solution)/shard_map/ppermute | solution.py:412
  4.2 1.6 %collective-permute-start.1 = (bf16[1,576,128]{2,1,0:T(8,128)(2,1)S(1)}, bf16[1,576,128]{2,1,0:T(8,128)(2,1)S(1)}, u32[]{:S(2)}, u32[]{:S(2)}) collective-permute-start(bf16[1,576,128]{2,1,0:T(8,128)(2,1)S(1)} %get-tuple-element.45.rest_1_), channel_id=1, source_target_pairs={{0,4},{1,5},{4,8},{5,9},{8,12},{9,13},{12,14},{13,15},{14,10},{15,... | collective-permute-start | bytes 442376 | tf_op jit(solution)/shard_map/ppermute | solution.py:415
  5.7 0.4 collective-permute-start.2
  6.2 1.2 %copy-done.1 = bf16[8,128,512]{2,1,0:T(8,128)(2,1)S(1)} copy-done((bf16[8,128,512]{2,1,0:T(8,128)(2,1)S(1)}, bf16[8,128,512]{2,1,0:T(8,128)(2,1)}, u32[]{:S(2)}) %copy-start.1) | copy-done | bytes 1048600
  7.5 0.9 %copy-done.2 = bf16[32,1536]{1,0:T(8,128)(2,1)S(1)} copy-done((bf16[32,1536]{1,0:T(8,128)(2,1)S(1)}, bf16[32,1536]{1,0:T(8,128)(2,1)}, u32[]{:S(2)}) %copy-start.2) | copy-done | bytes 98328
  8.4 0.7 %copy-done.3 = s32[16,32]{1,0:T(8,128)S(1)} copy-done((s32[16,32]{1,0:T(8,128)S(1)}, s32[16,32]{1,0:T(8,128)}, u32[]{:S(2)}) %copy-start.3) | copy-done | bytes 2072
  9.1 0.7 %copy-done.4 = s32[8,8]{1,0:T(8,128)S(1)} copy-done((s32[8,8]{1,0:T(8,128)S(1)}, s32[8,8]{1,0:T(8,128)}, u32[]{:S(2)}) %copy-start.4) | copy-done | bytes 280
  9.7 0.7 copy-done.5
  10.4 2.1 %prepare.1 = (bf16[256,576]{1,0:T(8,128)(2,1)S(1)}, s32[140]{0:T(256)S(1)}) custom-call(s32[1]{0:T(128)} %bitcast.me_ref, bf16[32,1536]{1,0:T(8,128)(2,1)S(1)} %copy-done.2, bf16[8,128,512]{2,1,0:T(8,128)(2,1)S(1)} %copy-done.1, s32[8]{0:T(128)S(1)} %copy-done.5, s32[8,8]{1,0:T(8,128)S(1)} %copy-done.4, s32[16,32]{1,0:T(8,128)S(1)} %copy-done.3), custom_call_target="tpu_custom_call" | custom-call | flops 33554432 | bytes 2097152 | tf_op jit(solution)/shard_map/prepare/pallas_call | solution.py:330
  12.5 1.4 %collective-permute-done.3.rest_3_ = bf16[1,576,128]{2,1,0:T(8,128)(2,1)S(1)} collective-permute-done((bf16[1,576,128]{2,1,0:T(8,128)(2,1)S(1)}, bf16[1,576,128]{2,1,0:T(8,128)(2,1)S(1)}, u32[]{:S(2)}, u32[]{:S(2)}) %collective-permute-start.3) | collective-permute-done | bytes 147488 | tf_op jit(solution)/shard_map/ppermute | solution.py:413
  13.9 1.6 %collective-permute-start.5 = (bf16[1,576,128]{2,1,0:T(8,128)(2,1)S(1)}, bf16[1,576,128]{2,1,0:T(8,128)(2,1)S(1)}, u32[]{:S(2)}, u32[]{:S(2)}) collective-permute-start(bf16[1,576,128]{2,1,0:T(8,128)(2,1)S(1)} %collective-permute-done.rest_2_), channel_id=1, source_target_pairs={{0,4},{1,5},{4,8},{5,9},{8,12},{9,13},{12,14},{13,15},{14,10},{15,... | collective-permute-start | bytes 442376 | tf_op jit(solution)/shard_map/ppermute | solution.py:412
  15.5 0.4 collective-permute-start.6
  16.0 0.6 collective-permute-start.7
  16.6 1.4 %collective-permute-start.8 = (bf16[1,576,128]{2,1,0:T(8,128)(2,1)S(1)}, bf16[1,576,128]{2,1,0:T(8,128)(2,1)S(1)}, u32[]{:S(2)}, u32[]{:S(2)}) collective-permute-start(bf16[1,576,128]{2,1,0:T(8,128)(2,1)S(1)} %collective-permute-done.1.rest_5_), channel_id=1, source_target_pairs={{0,4},{1,5},{4,8},{5,9},{8,12},{9,13},{12,14},{13,15},{14,10},{15,... | collective-permute-start | bytes 442376 | tf_op jit(solution)/shard_map/ppermute | solution.py:415
  18.0 1.1 %collective-permute-done.5.rest_6_ = bf16[1,576,128]{2,1,0:T(8,128)(2,1)S(1)} collective-permute-done((bf16[1,576,128]{2,1,0:T(8,128)(2,1)S(1)}, bf16[1,576,128]{2,1,0:T(8,128)(2,1)S(1)}, u32[]{:S(2)}, u32[]{:S(2)}) %collective-permute-start.5) | collective-permute-done | bytes 147488 | tf_op jit(solution)/shard_map/ppermute | solution.py:412
  19.1 1.6 %collective-permute-start.9 = (bf16[1,576,128]{2,1,0:T(8,128)(2,1)S(1)}, bf16[1,576,128]{2,1,0:T(8,128)(2,1)S(1)}, u32[]{:S(2)}, u32[]{:S(2)}) collective-permute-start(bf16[1,576,128]{2,1,0:T(8,128)(2,1)S(1)} %collective-permute-done.5.rest_6_), channel_id=1, source_target_pairs={{0,4},{1,5},{4,8},{5,9},{8,12},{9,13},{12,14},{13,15},{14,10},{15,... | collective-permute-start | bytes 442376 | tf_op jit(solution)/shard_map/ppermute | solution.py:412
  20.7 1.6 %collective-permute-done.6.rest_7_ = bf16[1,576,128]{2,1,0:T(8,128)(2,1)S(1)} collective-permute-done((bf16[1,576,128]{2,1,0:T(8,128)(2,1)S(1)}, bf16[1,576,128]{2,1,0:T(8,128)(2,1)S(1)}, u32[]{:S(2)}, u32[]{:S(2)}) %collective-permute-start.6) | collective-permute-done | bytes 147488 | tf_op jit(solution)/shard_map/ppermute | solution.py:413
  22.2 0.3 collective-permute-start.10
  22.5 2.8 %collective-permute-done.7.rest_8_ = bf16[1,576,128]{2,1,0:T(8,128)(2,1)S(1)} collective-permute-done((bf16[1,576,128]{2,1,0:T(8,128)(2,1)S(1)}, bf16[1,576,128]{2,1,0:T(8,128)(2,1)S(1)}, u32[]{:S(2)}, u32[]{:S(2)}) %collective-permute-start.7) | collective-permute-done | bytes 147488 | tf_op jit(solution)/shard_map/ppermute | solution.py:414
  25.4 0.3 collective-permute-start.11
  25.7 1.7 %collective-permute-start.12 = (bf16[1,576,128]{2,1,0:T(8,128)(2,1)S(1)}, bf16[1,576,128]{2,1,0:T(8,128)(2,1)S(1)}, u32[]{:S(2)}, u32[]{:S(2)}) collective-permute-start(bf16[1,576,128]{2,1,0:T(8,128)(2,1)S(1)} %collective-permute-done.8.rest_9_), channel_id=1, source_target_pairs={{0,4},{1,5},{4,8},{5,9},{8,12},{9,13},{12,14},{13,15},{14,10},{15,... | collective-permute-start | bytes 442376 | tf_op jit(solution)/shard_map/ppermute | solution.py:415
  27.4 1.5 %collective-permute-start.13 = (bf16[1,576,128]{2,1,0:T(8,128)(2,1)S(1)}, bf16[1,576,128]{2,1,0:T(8,128)(2,1)S(1)}, u32[]{:S(2)}, u32[]{:S(2)}) collective-permute-start(bf16[1,576,128]{2,1,0:T(8,128)(2,1)S(1)} %collective-permute-done.9.rest_10_), channel_id=1, source_target_pairs={{0,4},{1,5},{4,8},{5,9},{8,12},{9,13},{12,14},{13,15},{14,10},{15,... | collective-permute-start | bytes 442376 | tf_op jit(solution)/shard_map/ppermute | solution.py:408
  28.9 0.6 collective-permute-start.14
  29.5 8.3 %attend.2 = (f32[256,512]{1,0:T(8,128)S(1)}, f32[256,128]{1,0:T(8,128)S(1)}, bf16[256,640]{1,0:T(8,128)(2,1)S(1)}, bf16[7,1024,1024]{2,1,0:T(8,128)(2,1)S(1)}) custom-call(s32[140]{0:T(256)S(1)} %get-tuple-element.27.plan_ref, bf16[8,32,576]{2,1,0:T(8,128)(2,1)S(1)} %bitcast.4, bf16[8,32,576]{2,1,0:T(8,128)(2,1)S(1)} %collective-permute-done.4.theirs_ref, ...), custom_call_target="tpu_custom_call" | custom-call | flops 226492416 | bytes 1769472 | tf_op jit(solution)/shard_map/attend/pallas_call | solution.py:359
  37.8 0.1 collective-permute-start.15
  37.9 2.6 %attend.3 = (f32[256,512]{1,0:T(8,128)S(1)}, f32[256,128]{1,0:T(8,128)S(1)}, bf16[256,640]{1,0:T(8,128)(2,1)S(1)}) custom-call(s32[140]{0:T(256)S(1)} %get-tuple-element.27.plan_ref, bf16[8,32,576]{2,1,0:T(8,128)(2,1)S(1)} %bitcast.5, bf16[8,32,576]{2,1,0:T(8,128)(2,1)S(1)} %collective-permute-done.4.theirs_ref, ...), custom_call_target="tpu_custom_call" | custom-call | flops 75497472 | bytes 589824 | tf_op jit(solution)/shard_map/attend/pallas_call | solution.py:359
  40.6 1.1 %collective-permute-start.16 = (bf16[256,640]{1,0:T(8,128)(2,1)S(1)}, bf16[256,640]{1,0:T(8,128)(2,1)S(1)}, u32[]{:S(2)}, u32[]{:S(2)}) collective-permute-start(bf16[256,640]{1,0:T(8,128)(2,1)S(1)} %get-tuple-element.39), channel_id=1, source_target_pairs={{0,1},{1,0},{2,3},{3,2},{4,5},{5,4},{6,7},{7,6},{8,9},{9,8},{10,11... | collective-permute-start | bytes 983048 | tf_op jit(solution)/shard_map/ppermute | solution.py:321
  41.7 1.3 %collective-permute-done.16.rest_5_ = bf16[256,640]{1,0:T(8,128)(2,1)S(1)} collective-permute-done((bf16[256,640]{1,0:T(8,128)(2,1)S(1)}, bf16[256,640]{1,0:T(8,128)(2,1)S(1)}, u32[]{:S(2)}, u32[]{:S(2)}) %collective-permute-start.16) | collective-permute-done | bytes 327712 | tf_op jit(solution)/shard_map/ppermute | solution.py:321
  42.9 2.5 %merge_and_project.1 = (bf16[32,4096]{1,0:T(8,128)(2,1)S(1)}, bf16[32,4096]{1,0:T(8,128)(2,1)S(1)}, bf16[64,1024]{1,0:T(8,128)(2,1)S(1)}) custom-call(s32[1]{0:T(128)} %bitcast.me_ref, s32[8]{0:T(128)S(1)} %copy-done.6, bf16[8,512,128]{2,1,0:T(8,128)(2,1)S(1)} %copy-done, bf16[7,1024,1024]{2,1,0:T(8,128)(2,1)S(1)} %get-tuple-element.33.weight_ref, ...), custom_call_target="tpu_custom_call" | custom-call | tf_op jit(solution)/shard_map/merge_and_project/pallas_call | solution.py:429
  45.4 1.2 %project_second.1 = (bf16[32,3072]{1,0:T(8,128)(2,1)S(1)}, bf16[32,3072]{1,0:T(8,128)(2,1)S(1)}) custom-call(bf16[64,1024]{1,0:T(8,128)(2,1)S(1)} %get-tuple-element.42.placed_ref, bf16[7,1024,1024]{2,1,0:T(8,128)(2,1)S(1)} %get-tuple-element.33.weight_ref), custom_call_target="tpu_custom_call" | custom-call | flops 469762048 | bytes 7340032 | tf_op jit(solution)/shard_map/project_second/pallas_call | solution.py:444
  46.6 0.4 collective-permute-start.22
  47.1 0.1 collective-permute-start.17
  47.2 0.9 %collective-permute-done.22 = bf16[32,3072]{1,0:T(8,128)(2,1)S(1)} collective-permute-done((bf16[32,3072]{1,0:T(8,128)(2,1)S(1)}, bf16[32,3072]{1,0:T(8,128)(2,1)S(1)}, u32[]{:S(2)}, u32[]{:S(2)}) %collective-permute-start.22) | collective-permute-done | bytes 196640 | tf_op jit(solution)/shard_map/ppermute | solution.py:321
  48.2 0.3 collective-permute-start.23
  48.5 0.1 collective-permute-done.17
  48.6 0.1 add_convert_fusion
  48.7 1.8 %collective-permute-start.18 = (bf16[16,4096]{1,0:T(8,128)(2,1)S(1)}, bf16[16,4096]{1,0:T(8,128)(2,1)S(1)}, u32[]{:S(2)}, u32[]{:S(2)}) collective-permute-start(bf16[16,4096]{1,0:T(8,128)(2,1)S(1)} %slice.59), channel_id=1, source_target_pairs={{0,2},{1,3},{2,0},{3,1},{4,6},{5,7},{6,4},{7,5},{8,10},{9,11},{10,... | collective-permute-start | bytes 393224 | tf_op jit(solution)/shard_map/ppermute | solution.py:321
  50.5 3.4 %collective-permute-done.23 = bf16[16,3072]{1,0:T(8,128)(2,1)S(1)} collective-permute-done((bf16[16,3072]{1,0:T(8,128)(2,1)S(1)}, bf16[16,3072]{1,0:T(8,128)(2,1)S(1)}, u32[]{:S(2)}, u32[]{:S(2)}) %collective-permute-start.23) | collective-permute-done | bytes 98336 | tf_op jit(solution)/shard_map/ppermute | solution.py:321
  54.0 1.0 %collective-permute-start.24 = (bf16[4,3072]{1,0:T(4,128)(2,1)S(1)}, bf16[4,3072]{1,0:T(4,128)(2,1)S(1)}, u32[]{:S(2)}, u32[]{:S(2)}) collective-permute-start(bf16[4,3072]{1,0:T(4,128)(2,1)S(1)} %get-tuple-element.50), channel_id=1, source_target_pairs={{0,4},{1,5},{2,6},{3,7},{4,0},{5,1},{6,2},{7,3},{8,12},{9,13},{10,... | collective-permute-start | bytes 73736 | tf_op jit(solution)/shard_map/ppermute | solution.py:321
  54.9 1.7 %collective-permute-start.25 = (bf16[4,3072]{1,0:T(4,128)(2,1)S(1)}, bf16[4,3072]{1,0:T(4,128)(2,1)S(1)}, u32[]{:S(2)}, u32[]{:S(2)}) collective-permute-start(bf16[4,3072]{1,0:T(4,128)(2,1)S(1)} %get-tuple-element.52), channel_id=1, source_target_pairs={{0,8},{1,9},{2,10},{3,11},{4,12},{5,13},{6,14},{7,15},{8,0},{9,1},... | collective-permute-start | bytes 73736 | tf_op jit(solution)/shard_map/ppermute | solution.py:321
  56.6 1.8 %collective-permute-start.26 = (bf16[4,3072]{1,0:T(4,128)(2,1)S(1)}, bf16[4,3072]{1,0:T(4,128)(2,1)S(1)}, u32[]{:S(2)}, u32[]{:S(2)}) collective-permute-start(bf16[4,3072]{1,0:T(4,128)(2,1)S(1)} %get-tuple-element.51), channel_id=1, source_target_pairs={{0,12},{1,13},{2,14},{3,15},{4,8},{5,9},{6,10},{7,11},{8,4},{9,5},... | collective-permute-start | bytes 73736 | tf_op jit(solution)/shard_map/ppermute | solution.py:321
  58.5 0.1 collective-permute-start.19
  58.6 2.6 %collective-permute-start.20 = (bf16[4,4096]{1,0:T(4,128)(2,1)S(1)}, bf16[4,4096]{1,0:T(4,128)(2,1)S(1)}, u32[]{:S(2)}, u32[]{:S(2)}) collective-permute-start(bf16[4,4096]{1,0:T(4,128)(2,1)S(1)} %get-tuple-element.49), channel_id=1, source_target_pairs={{0,8},{1,9},{2,10},{3,11},{4,12},{5,13},{6,14},{7,15},{8,0},{9,1},... | collective-permute-start | bytes 98312 | tf_op jit(solution)/shard_map/ppermute | solution.py:321
  61.2 1.8 %collective-permute-start.21 = (bf16[4,4096]{1,0:T(4,128)(2,1)S(1)}, bf16[4,4096]{1,0:T(4,128)(2,1)S(1)}, u32[]{:S(2)}, u32[]{:S(2)}) collective-permute-start(bf16[4,4096]{1,0:T(4,128)(2,1)S(1)} %get-tuple-element.48), channel_id=1, source_target_pairs={{0,12},{1,13},{2,14},{3,15},{4,8},{5,9},{6,10},{7,11},{8,4},{9,5},... | collective-permute-start | bytes 98312 | tf_op jit(solution)/shard_map/ppermute | solution.py:321
  63.0 0.8 %collective-permute-done.20 = bf16[4,4096]{1,0:T(4,128)(2,1)S(1)} collective-permute-done((bf16[4,4096]{1,0:T(4,128)(2,1)S(1)}, bf16[4,4096]{1,0:T(4,128)(2,1)S(1)}, u32[]{:S(2)}, u32[]{:S(2)}) %collective-permute-start.20) | collective-permute-done | bytes 32800 | tf_op jit(solution)/shard_map/ppermute | solution.py:321
  63.8 3.1 %collective-permute-done.21 = bf16[4,4096]{1,0:T(4,128)(2,1)S(1)} collective-permute-done((bf16[4,4096]{1,0:T(4,128)(2,1)S(1)}, bf16[4,4096]{1,0:T(4,128)(2,1)S(1)}, u32[]{:S(2)}, u32[]{:S(2)}) %collective-permute-start.21) | collective-permute-done | bytes 32800 | tf_op jit(solution)/shard_map/ppermute | solution.py:321
  66.9 0.7 pad_maximum_fusion
  (37 shorter events, 0.4 us)
Async XLA Ops:
  0.0 42.9 %copy-start = (bf16[8,512,128]{2,1,0:T(8,128)(2,1)S(1)}, bf16[8,512,128]{2,1,0:T(8,128)(2,1)}, u32[]{:S(2)}) copy-start(bf16[8,512,128]{2,1,0:T(8,128)(2,1)} %value_hbm.1) | copy-start | bytes 3145732
  1.1 11.4 %collective-permute-start = (bf16[1,576,128]{2,1,0:T(8,128)(2,1)S(1)}, bf16[1,576,128]{2,1,0:T(8,128)(2,1)S(1)}, u32[]{:S(2)}, u32[]{:S(2)}) collective-permute-start(bf16[1,576,128]{2,1,0:T(8,128)(2,1)S(1)} %get-tuple-element.46.rest_0_), channel_id=1, source_target_pairs={{0,4},{1,5},{4,8},{5,9},{8,12},{9,13},{12,14},{13,15},{14,10},{15,... | collective-permute-start | bytes 442376 | tf_op jit(solution)/shard_map/ppermute | solution.py:412
  4.2 8.3 %collective-permute-start.1 = (bf16[1,576,128]{2,1,0:T(8,128)(2,1)S(1)}, bf16[1,576,128]{2,1,0:T(8,128)(2,1)S(1)}, u32[]{:S(2)}, u32[]{:S(2)}) collective-permute-start(bf16[1,576,128]{2,1,0:T(8,128)(2,1)S(1)} %get-tuple-element.45.rest_1_), channel_id=1, source_target_pairs={{0,4},{1,5},{4,8},{5,9},{8,12},{9,13},{12,14},{13,15},{14,10},{15,... | collective-permute-start | bytes 442376 | tf_op jit(solution)/shard_map/ppermute | solution.py:415
  5.7 6.8 %collective-permute-start.2 = (bf16[1,576,128]{2,1,0:T(8,128)(2,1)S(1)}, bf16[1,576,128]{2,1,0:T(8,128)(2,1)S(1)}, u32[]{:S(2)}, u32[]{:S(2)}) collective-permute-start(bf16[1,576,128]{2,1,0:T(8,128)(2,1)S(1)} %get-tuple-element.46.rest_0_), channel_id=1, source_target_pairs={{4,0},{5,1},{8,4},{9,5},{12,8},{13,9},{14,12},{15,13},{10,14},{11,... | collective-permute-start | bytes 442376 | tf_op jit(solution)/shard_map/ppermute | solution.py:414
  6.2 7.7 %collective-permute-start.3 = (bf16[1,576,128]{2,1,0:T(8,128)(2,1)S(1)}, bf16[1,576,128]{2,1,0:T(8,128)(2,1)S(1)}, u32[]{:S(2)}, u32[]{:S(2)}) collective-permute-start(bf16[1,576,128]{2,1,0:T(8,128)(2,1)S(1)} %get-tuple-element.45.rest_1_), channel_id=1, source_target_pairs={{4,0},{5,1},{8,4},{9,5},{12,8},{13,9},{14,12},{15,13},{10,14},{11,... | collective-permute-start | bytes 442376 | tf_op jit(solution)/shard_map/ppermute | solution.py:413
  6.2 1.2 %copy-start.1 = (bf16[8,128,512]{2,1,0:T(8,128)(2,1)S(1)}, bf16[8,128,512]{2,1,0:T(8,128)(2,1)}, u32[]{:S(2)}) copy-start(bf16[8,128,512]{2,1,0:T(8,128)(2,1)} %absorb_hbm.1) | copy-start | bytes 3145732
  7.5 0.9 %copy-start.2 = (bf16[32,1536]{1,0:T(8,128)(2,1)S(1)}, bf16[32,1536]{1,0:T(8,128)(2,1)}, u32[]{:S(2)}) copy-start(bf16[32,1536]{1,0:T(8,128)(2,1)} %query_hbm.1) | copy-start | bytes 294916
  8.4 0.7 %copy-start.3 = (s32[16,32]{1,0:T(8,128)S(1)}, s32[16,32]{1,0:T(8,128)}, u32[]{:S(2)}) copy-start(s32[16,32]{1,0:T(8,128)} %constant.6.clone.slot_hbm) | copy-start | bytes 6148
  9.0 0.7 %copy-start.4 = (s32[8,8]{1,0:T(8,128)S(1)}, s32[8,8]{1,0:T(8,128)}, u32[]{:S(2)}) copy-start(s32[8,8]{1,0:T(8,128)} %table_hbm.1) | copy-start | bytes 772
  9.7 0.7 copy-start.5
  10.4 32.5 %copy-start.6 = (s32[8]{0:T(128)S(1)}, s32[8]{0:T(128)}, u32[]{:S(2)}) copy-start(s32[8]{0:T(128)} %owner_hbm.1) | copy-start | bytes 100
  13.9 5.1 %collective-permute-start.5 = (bf16[1,576,128]{2,1,0:T(8,128)(2,1)S(1)}, bf16[1,576,128]{2,1,0:T(8,128)(2,1)S(1)}, u32[]{:S(2)}, u32[]{:S(2)}) collective-permute-start(bf16[1,576,128]{2,1,0:T(8,128)(2,1)S(1)} %collective-permute-done.rest_2_), channel_id=1, source_target_pairs={{0,4},{1,5},{4,8},{5,9},{8,12},{9,13},{12,14},{13,15},{14,10},{15,... | collective-permute-start | bytes 442376 | tf_op jit(solution)/shard_map/ppermute | solution.py:412
  15.5 6.7 %collective-permute-start.6 = (bf16[1,576,128]{2,1,0:T(8,128)(2,1)S(1)}, bf16[1,576,128]{2,1,0:T(8,128)(2,1)S(1)}, u32[]{:S(2)}, u32[]{:S(2)}) collective-permute-start(bf16[1,576,128]{2,1,0:T(8,128)(2,1)S(1)} %collective-permute-done.3.rest_3_), channel_id=1, source_target_pairs={{4,0},{5,1},{8,4},{9,5},{12,8},{13,9},{14,12},{15,13},{10,14},{11,... | collective-permute-start | bytes 442376 | tf_op jit(solution)/shard_map/ppermute | solution.py:413
  16.0 13.5 %collective-permute-start.4 = (bf16[8,32,576]{2,1,0:T(8,128)(2,1)S(1)}, bf16[8,32,576]{2,1,0:T(8,128)(2,1)S(1)}, u32[]{:S(2)}, u32[]{:S(2)}) collective-permute-start(bf16[8,32,576]{2,1,0:T(8,128)(2,1)S(1)} %bitcast.3), channel_id=1, source_target_pairs={{0,1},{1,0},{2,3},{3,2},{4,5},{5,4},{6,7},{7,6},{8,9},{9,8},{10,11... | collective-permute-start | bytes 884744 | tf_op jit(solution)/shard_map/ppermute | solution.py:321
  16.0 9.4 %collective-permute-start.7 = (bf16[1,576,128]{2,1,0:T(8,128)(2,1)S(1)}, bf16[1,576,128]{2,1,0:T(8,128)(2,1)S(1)}, u32[]{:S(2)}, u32[]{:S(2)}) collective-permute-start(bf16[1,576,128]{2,1,0:T(8,128)(2,1)S(1)} %collective-permute-done.2.rest_4_), channel_id=1, source_target_pairs={{4,0},{5,1},{8,4},{9,5},{12,8},{13,9},{14,12},{15,13},{10,14},{11,... | collective-permute-start | bytes 442376 | tf_op jit(solution)/shard_map/ppermute | solution.py:414
  16.6 9.1 %collective-permute-start.8 = (bf16[1,576,128]{2,1,0:T(8,128)(2,1)S(1)}, bf16[1,576,128]{2,1,0:T(8,128)(2,1)S(1)}, u32[]{:S(2)}, u32[]{:S(2)}) collective-permute-start(bf16[1,576,128]{2,1,0:T(8,128)(2,1)S(1)} %collective-permute-done.1.rest_5_), channel_id=1, source_target_pairs={{0,4},{1,5},{4,8},{5,9},{8,12},{9,13},{12,14},{13,15},{14,10},{15,... | collective-permute-start | bytes 442376 | tf_op jit(solution)/shard_map/ppermute | solution.py:415
  19.1 8.3 %collective-permute-start.9 = (bf16[1,576,128]{2,1,0:T(8,128)(2,1)S(1)}, bf16[1,576,128]{2,1,0:T(8,128)(2,1)S(1)}, u32[]{:S(2)}, u32[]{:S(2)}) collective-permute-start(bf16[1,576,128]{2,1,0:T(8,128)(2,1)S(1)} %collective-permute-done.5.rest_6_), channel_id=1, source_target_pairs={{0,4},{1,5},{4,8},{5,9},{8,12},{9,13},{12,14},{13,15},{14,10},{15,... | collective-permute-start | bytes 442376 | tf_op jit(solution)/shard_map/ppermute | solution.py:412
  22.2 6.7 %collective-permute-start.10 = (bf16[1,576,128]{2,1,0:T(8,128)(2,1)S(1)}, bf16[1,576,128]{2,1,0:T(8,128)(2,1)S(1)}, u32[]{:S(2)}, u32[]{:S(2)}) collective-permute-start(bf16[1,576,128]{2,1,0:T(8,128)(2,1)S(1)} %collective-permute-done.6.rest_7_), channel_id=1, source_target_pairs={{4,0},{5,1},{8,4},{9,5},{12,8},{13,9},{14,12},{15,13},{10,14},{11,... | collective-permute-start | bytes 442376 | tf_op jit(solution)/shard_map/ppermute | solution.py:413
  25.4 12.5 %collective-permute-start.11 = (bf16[1,576,128]{2,1,0:T(8,128)(2,1)S(1)}, bf16[1,576,128]{2,1,0:T(8,128)(2,1)S(1)}, u32[]{:S(2)}, u32[]{:S(2)}) collective-permute-start(bf16[1,576,128]{2,1,0:T(8,128)(2,1)S(1)} %collective-permute-done.7.rest_8_), channel_id=1, source_target_pairs={{4,0},{5,1},{8,4},{9,5},{12,8},{13,9},{14,12},{15,13},{10,14},{11,... | collective-permute-start | bytes 442376 | tf_op jit(solution)/shard_map/ppermute | solution.py:414
  25.7 12.2 %collective-permute-start.12 = (bf16[1,576,128]{2,1,0:T(8,128)(2,1)S(1)}, bf16[1,576,128]{2,1,0:T(8,128)(2,1)S(1)}, u32[]{:S(2)}, u32[]{:S(2)}) collective-permute-start(bf16[1,576,128]{2,1,0:T(8,128)(2,1)S(1)} %collective-permute-done.8.rest_9_), channel_id=1, source_target_pairs={{0,4},{1,5},{4,8},{5,9},{8,12},{9,13},{12,14},{13,15},{14,10},{15,... | collective-permute-start | bytes 442376 | tf_op jit(solution)/shard_map/ppermute | solution.py:415
  27.4 10.5 %collective-permute-start.13 = (bf16[1,576,128]{2,1,0:T(8,128)(2,1)S(1)}, bf16[1,576,128]{2,1,0:T(8,128)(2,1)S(1)}, u32[]{:S(2)}, u32[]{:S(2)}) collective-permute-start(bf16[1,576,128]{2,1,0:T(8,128)(2,1)S(1)} %collective-permute-done.9.rest_10_), channel_id=1, source_target_pairs={{0,4},{1,5},{4,8},{5,9},{8,12},{9,13},{12,14},{13,15},{14,10},{15,... | collective-permute-start | bytes 442376 | tf_op jit(solution)/shard_map/ppermute | solution.py:408
  28.9 9.0 %collective-permute-start.14 = (bf16[1,576,128]{2,1,0:T(8,128)(2,1)S(1)}, bf16[1,576,128]{2,1,0:T(8,128)(2,1)S(1)}, u32[]{:S(2)}, u32[]{:S(2)}) collective-permute-start(bf16[1,576,128]{2,1,0:T(8,128)(2,1)S(1)} %collective-permute-done.10.rest_11_), channel_id=1, source_target_pairs={{4,0},{5,1},{8,4},{9,5},{12,8},{13,9},{14,12},{15,13},{10,14},{11,... | collective-permute-start | bytes 442376 | tf_op jit(solution)/shard_map/ppermute | solution.py:409
  37.8 3.8 %collective-permute-start.15 = (bf16[256,640]{1,0:T(8,128)(2,1)S(1)}, bf16[256,640]{1,0:T(8,128)(2,1)S(1)}, u32[]{:S(2)}, u32[]{:S(2)}) collective-permute-start(bf16[256,640]{1,0:T(8,128)(2,1)S(1)} %get-tuple-element.38), channel_id=1, source_target_pairs={{0,1},{1,0},{2,3},{3,2},{4,5},{5,4},{6,7},{7,6},{8,9},{9,8},{10,11... | collective-permute-start | bytes 983048 | tf_op jit(solution)/shard_map/ppermute | solution.py:321
  40.6 2.4 %collective-permute-start.16 = (bf16[256,640]{1,0:T(8,128)(2,1)S(1)}, bf16[256,640]{1,0:T(8,128)(2,1)S(1)}, u32[]{:S(2)}, u32[]{:S(2)}) collective-permute-start(bf16[256,640]{1,0:T(8,128)(2,1)S(1)} %get-tuple-element.39), channel_id=1, source_target_pairs={{0,1},{1,0},{2,3},{3,2},{4,5},{5,4},{6,7},{7,6},{8,9},{9,8},{10,11... | collective-permute-start | bytes 983048 | tf_op jit(solution)/shard_map/ppermute | solution.py:321
  46.6 1.5 %collective-permute-start.22 = (bf16[32,3072]{1,0:T(8,128)(2,1)S(1)}, bf16[32,3072]{1,0:T(8,128)(2,1)S(1)}, u32[]{:S(2)}, u32[]{:S(2)}) collective-permute-start(bf16[32,3072]{1,0:T(8,128)(2,1)S(1)} %get-tuple-element.44), channel_id=1, source_target_pairs={{0,1},{1,0},{2,3},{3,2},{4,5},{5,4},{6,7},{7,6},{8,9},{9,8},{10,11... | collective-permute-start | bytes 589832 | tf_op jit(solution)/shard_map/ppermute | solution.py:321
  47.1 1.5 %collective-permute-start.17 = (bf16[32,4096]{1,0:T(8,128)(2,1)S(1)}, bf16[32,4096]{1,0:T(8,128)(2,1)S(1)}, u32[]{:S(2)}, u32[]{:S(2)}) collective-permute-start(bf16[32,4096]{1,0:T(8,128)(2,1)S(1)} %get-tuple-element.41), channel_id=1, source_target_pairs={{0,1},{1,0},{2,3},{3,2},{4,5},{5,4},{6,7},{7,6},{8,9},{9,8},{10,11... | collective-permute-start | bytes 786440 | tf_op jit(solution)/shard_map/ppermute | solution.py:321
  48.2 5.7 %collective-permute-start.23 = (bf16[16,3072]{1,0:T(8,128)(2,1)S(1)}, bf16[16,3072]{1,0:T(8,128)(2,1)S(1)}, u32[]{:S(2)}, u32[]{:S(2)}) collective-permute-start(bf16[16,3072]{1,0:T(8,128)(2,1)S(1)} %slice.65), channel_id=1, source_target_pairs={{0,2},{1,3},{2,0},{3,1},{4,6},{5,7},{6,4},{7,5},{8,10},{9,11},{10,... | collective-permute-start | bytes 294920 | tf_op jit(solution)/shard_map/ppermute | solution.py:321
  48.7 9.7 %collective-permute-start.18 = (bf16[16,4096]{1,0:T(8,128)(2,1)S(1)}, bf16[16,4096]{1,0:T(8,128)(2,1)S(1)}, u32[]{:S(2)}, u32[]{:S(2)}) collective-permute-start(bf16[16,4096]{1,0:T(8,128)(2,1)S(1)} %slice.59), channel_id=1, source_target_pairs={{0,2},{1,3},{2,0},{3,1},{4,6},{5,7},{6,4},{7,5},{8,10},{9,11},{10,... | collective-permute-start | bytes 393224 | tf_op jit(solution)/shard_map/ppermute | solution.py:321
  54.0 7.2 %collective-permute-start.24 = (bf16[4,3072]{1,0:T(4,128)(2,1)S(1)}, bf16[4,3072]{1,0:T(4,128)(2,1)S(1)}, u32[]{:S(2)}, u32[]{:S(2)}) collective-permute-start(bf16[4,3072]{1,0:T(4,128)(2,1)S(1)} %get-tuple-element.50), channel_id=1, source_target_pairs={{0,4},{1,5},{2,6},{3,7},{4,0},{5,1},{6,2},{7,3},{8,12},{9,13},{10,... | collective-permute-start | bytes 73736 | tf_op jit(solution)/shard_map/ppermute | solution.py:321
  54.9 8.0 %collective-permute-start.25 = (bf16[4,3072]{1,0:T(4,128)(2,1)S(1)}, bf16[4,3072]{1,0:T(4,128)(2,1)S(1)}, u32[]{:S(2)}, u32[]{:S(2)}) collective-permute-start(bf16[4,3072]{1,0:T(4,128)(2,1)S(1)} %get-tuple-element.52), channel_id=1, source_target_pairs={{0,8},{1,9},{2,10},{3,11},{4,12},{5,13},{6,14},{7,15},{8,0},{9,1},... | collective-permute-start | bytes 73736 | tf_op jit(solution)/shard_map/ppermute | solution.py:321
  56.6 6.4 %collective-permute-start.26 = (bf16[4,3072]{1,0:T(4,128)(2,1)S(1)}, bf16[4,3072]{1,0:T(4,128)(2,1)S(1)}, u32[]{:S(2)}, u32[]{:S(2)}) collective-permute-start(bf16[4,3072]{1,0:T(4,128)(2,1)S(1)} %get-tuple-element.51), channel_id=1, source_target_pairs={{0,12},{1,13},{2,14},{3,15},{4,8},{5,9},{6,10},{7,11},{8,4},{9,5},... | collective-permute-start | bytes 73736 | tf_op jit(solution)/shard_map/ppermute | solution.py:321
  58.5 4.5 %collective-permute-start.19 = (bf16[4,4096]{1,0:T(4,128)(2,1)S(1)}, bf16[4,4096]{1,0:T(4,128)(2,1)S(1)}, u32[]{:S(2)}, u32[]{:S(2)}) collective-permute-start(bf16[4,4096]{1,0:T(4,128)(2,1)S(1)} %get-tuple-element.47), channel_id=1, source_target_pairs={{0,4},{1,5},{2,6},{3,7},{4,0},{5,1},{6,2},{7,3},{8,12},{9,13},{10,... | collective-permute-start | bytes 98312 | tf_op jit(solution)/shard_map/ppermute | solution.py:321
  58.6 5.2 %collective-permute-start.20 = (bf16[4,4096]{1,0:T(4,128)(2,1)S(1)}, bf16[4,4096]{1,0:T(4,128)(2,1)S(1)}, u32[]{:S(2)}, u32[]{:S(2)}) collective-permute-start(bf16[4,4096]{1,0:T(4,128)(2,1)S(1)} %get-tuple-element.49), channel_id=1, source_target_pairs={{0,8},{1,9},{2,10},{3,11},{4,12},{5,13},{6,14},{7,15},{8,0},{9,1},... | collective-permute-start | bytes 98312 | tf_op jit(solution)/shard_map/ppermute | solution.py:321
  61.2 5.7 %collective-permute-start.21 = (bf16[4,4096]{1,0:T(4,128)(2,1)S(1)}, bf16[4,4096]{1,0:T(4,128)(2,1)S(1)}, u32[]{:S(2)}, u32[]{:S(2)}) collective-permute-start(bf16[4,4096]{1,0:T(4,128)(2,1)S(1)} %get-tuple-element.48), channel_id=1, source_target_pairs={{0,12},{1,13},{2,14},{3,15},{4,8},{5,9},{6,10},{7,11},{8,4},{9,5},... | collective-permute-start | bytes 98312 | tf_op jit(solution)/shard_map/ppermute | solution.py:321

commit v4 on v3

v4 whole, which is shorter than its diff:
```python
import functools
import math

import jax
import jax.numpy as jnp
import numpy as np
from jax import lax
from jax.experimental import pallas as pl
from jax.experimental.pallas import tpu as pltpu
from jax.sharding import PartitionSpec as P

OUT_TILE = 1024
LANES = 128
LATE = 4
TILES = (4, 1, 2)
EMPTY = -1e30


def ring_of(chips):
    if chips == 8:
        return [0, 2, 4, 6, 7, 5, 3, 1]
    return list(range(chips))


def ring_places(chips):
    places = [(0, 0), (0, 1)]
    for hop in range(1, chips // 2 + 1):
        last = hop == chips // 2
        places += [(-hop, 0), (hop, 1)] if last else [(-hop, 0), (hop, 1), (hop, 0), (-hop, 1)]
    return places


def slots_by_device(chips, half):
    ring = ring_of(chips)
    position = {chip: i for i, chip in enumerate(ring)}
    table = np.full((2 * chips, 4 * chips * half), -1, np.int32)
    for device in range(2 * chips):
        for index, (hop, part) in enumerate(ring_places(chips)):
            source = ring[(position[device // 2] + hop) % chips] * 2 + device % 2
            for i in range(half):
                table[device, (source * 2 + part) * half + i] = index * half + i
    return table


def prepare_kernel(
    heads, me_ref, query_hbm, absorb_hbm, length_hbm, table_hbm, slot_hbm, out_ref, plan_ref,
    query_ref, absorb_ref, length_ref, table_ref, slot_ref, ordered, sems,
):
    sources = (length_hbm, table_hbm, slot_hbm, query_hbm, absorb_hbm)
    targets = (length_ref, table_ref, slot_ref, query_ref, absorb_ref)
    copies = [
        pltpu.make_async_copy(a, b, sems.at[i]) for i, (a, b) in enumerate(zip(sources, targets))
    ]
    for copy in copies:
        copy.start()
    requests = table_ref.shape[0]
    entries = plan_ref.shape[0]

    def clear(i, _):
        plan_ref[i] = requests
        return 0

    lax.fori_loop(0, entries, clear, 0)
    for copy in copies[:3]:
        copy.wait()
    me = me_ref[0]

    def list_request(r, _):
        length = length_ref[r]

        def list_block(j, _):
            slot = slot_ref[me, table_ref[r, j]]
            pair = 2 * jnp.where(slot >= 0, slot, entries // 2 - 1)
            at = pair + (plan_ref[pair] != requests).astype(jnp.int32)
            plan_ref[at] = r + 256 * (j == length - 1).astype(jnp.int32)
            return 0

        return lax.fori_loop(0, length, list_block, 0)

    lax.fori_loop(0, requests, list_request, 0)

    rows = query_ref.shape[0]
    nope = absorb_ref.shape[1]
    head_width = query_ref.shape[1] // heads
    rope = head_width - nope
    kv_rank = absorb_ref.shape[2]
    for copy in copies[3:]:
        copy.wait()
    for h in range(heads):
        own = query_ref[:, h * head_width : (h + 1) * head_width]
        latent = jnp.dot(own[:, :nope], absorb_ref[h], preferred_element_type=jnp.float32)
        turned = jnp.concatenate(
            [own[:, nope:].astype(jnp.float32), jnp.zeros((rows, LANES - rope), jnp.float32)], axis=1
        )
        at = pl.ds(h, rows, stride=heads)
        for c in range(kv_rank // LANES):
            ordered[c, at] = latent[:, c * LANES : (c + 1) * LANES]
        ordered[kv_rank // LANES, at] = turned
    for c in range(kv_rank // LANES):
        out_ref[:, c * LANES : (c + 1) * LANES] = ordered[c].astype(jnp.bfloat16)
    out_ref[:, kv_rank:] = ordered[kv_rank // LANES, :, :rope].astype(jnp.bfloat16)


def chip_bits(chips, swap):
    bits = list(range(chips.bit_length() - 1))
    return [bits[1], bits[0]] + bits[2:] if swap else bits


def slot_of(apart, chips, swap):
    order = apart & 1
    for bit in chip_bits(chips, swap):
        order = 2 * order + ((apart >> (bit + 1)) & 1)
    return order


def weight_copy(weight_hbm, first, weight_ref, sems):
    tile = weight_ref.shape[2]
    return [
        pltpu.make_async_copy(
            weight_hbm.at[:, pl.ds((first + i) * tile, tile)], weight_ref.at[i], sems.at[i]
        )
        for i in range(weight_ref.shape[0])
    ]


def attend_kernel(
    piece_count, first_slot, first_tile, heads, steps, kv_rank, scale,
    plan_ref, mine_ref, theirs_ref, *rest,
):
    pieces, rest = rest[:piece_count], rest[piece_count:]
    weight_hbm, out_ref, lse_ref, away_ref, weight_ref, scores, top, total, latent, weight_sems = rest
    row_block = mine_ref.shape[1]
    half = pieces[0].shape[0]
    weight_copies = weight_copy(weight_hbm, first_tile, weight_ref, weight_sems)
    for copy in weight_copies:
        copy.start()

    requests = top.shape[0] - 1
    both = 2 * row_block
    block_rows = pieces[0].shape[2]
    top[...] = jnp.full_like(top, -jnp.inf)
    total[...] = jnp.zeros_like(total)
    latent[...] = jnp.zeros_like(latent)
    column = lax.broadcasted_iota(jnp.int32, (both, block_rows), 1)
    row = lax.broadcasted_iota(jnp.int32, (both, block_rows), 0)
    inside = column + (steps - 1 - (row % row_block) // heads) < block_rows

    def block_of(k):
        return pieces[k // half].at[k % half]

    slots = piece_count * half
    uses = [[plan_ref[2 * (first_slot + k) + i] for i in range(2)] for k in range(slots)]
    users = [[use & 255 for use in pair] for pair in uses]
    for k in range(slots):
        asked = jnp.concatenate(
            [ref[jnp.minimum(r, requests - 1)] for r in users[k] for ref in (mine_ref, theirs_ref)], axis=0
        )
        s = jnp.dot(asked, block_of(k)[...], preferred_element_type=jnp.float32) * scale
        for i in range(2):
            seen = inside | (uses[k][i] < 256)
            part = jnp.where(seen, s[i * both : (i + 1) * both], -jnp.inf)
            scores[k, i * both : (i + 1) * both] = part
            top[users[k][i]] = jnp.maximum(top[users[k][i]], part)

    batch = math.gcd(requests, 8)

    def peak(r, _):
        top[r] = jnp.broadcast_to(jnp.max(top[r], axis=1, keepdims=True), (both, block_rows))
        return 0

    lax.fori_loop(0, requests, peak, 0, unroll=batch)

    for k in range(slots):
        p = jnp.exp(scores[k] - jnp.concatenate([top[r] for r in users[k]], axis=0))
        mixed = lax.dot_general(
            p.astype(jnp.bfloat16),
            block_of(k)[:kv_rank],
            (((1,), (1,)), ((), ())),
            preferred_element_type=jnp.float32,
        )
        for i in range(2):
            total[users[k][i]] += p[i * both : (i + 1) * both]
            latent[users[k][i]] += mixed[i * both : (i + 1) * both]

    lane = lax.broadcasted_iota(jnp.int32, (row_block, LANES), 1)

    def finish(r, _):
        at = pl.ds(pl.multiple_of(r * row_block, row_block), row_block)
        norm = jnp.sum(total[r], axis=1, keepdims=True)
        some = norm > 0
        safe = jnp.where(some, norm, 1.0)
        lse = jnp.where(some, top[r][:, :1] + jnp.log(safe), EMPTY)
        result = latent[r] * (1.0 / safe)
        out_ref[at] = result[:row_block]
        lse_ref[at] = jnp.broadcast_to(lse[:row_block], (row_block, LANES))
        rest = lse[row_block:]
        high = rest.astype(jnp.bfloat16).astype(jnp.float32)
        middle = (rest - high).astype(jnp.bfloat16).astype(jnp.float32)
        low = rest - high - middle
        terms = jnp.where(lane == 0, high, jnp.where(lane == 1, middle, jnp.where(lane == 2, low, 0.0)))
        away_ref[at, :kv_rank] = result[row_block:].astype(jnp.bfloat16)
        away_ref[at, kv_rank:] = terms.astype(jnp.bfloat16)
        return 0

    lax.fori_loop(0, requests, finish, 0, unroll=batch)
    for copy in weight_copies:
        copy.wait()


def project(placed, weights, keep_ref, away_ref):
    half_rows = keep_ref.shape[0]
    at = 0
    for weight_ref in weights:
        tile = weight_ref.shape[2]
        for i in range(weight_ref.shape[0]):
            result = jnp.dot(
                placed, weight_ref[i], preferred_element_type=jnp.float32
            ).astype(jnp.bfloat16)
            keep_ref[:, at : at + tile] = result[:half_rows]
            away_ref[:, at : at + tile] = result[half_rows:]
            at += tile


def merge_kernel(
    stages, first_tile, heads, steps, chips,
    me_ref, owner_hbm, value_hbm, weight_hbm, weight_ref, *rest,
):
    outs, lses, others = rest[:stages], rest[stages : 2 * stages], rest[2 * stages : 3 * stages]
    (away_ref, keep_ref, placed_ref, later_ref,
     latent, head_rows, owner_ref, value_ref, sems, weight_sems) = rest[3 * stages :]
    owner_copy = pltpu.make_async_copy(owner_hbm, owner_ref, sems.at[0])
    value_copy = pltpu.make_async_copy(value_hbm, value_ref, sems.at[1])
    weight_copies = weight_copy(weight_hbm, first_tile, later_ref, weight_sems)
    for copy in (owner_copy, value_copy, *weight_copies):
        copy.start()
    kv_rank, v_width = value_ref.shape[1:]
    rows = head_rows.shape[0]
    requests = rows // steps
    chunk = 64

    def merge(i, _):
        at = pl.ds(pl.multiple_of(i * chunk, chunk), chunk)
        parts = [(o[at], e[at][:, :1]) for o, e in zip(outs, lses)]
        for other in others:
            terms = jnp.sum(other[at, kv_rank:].astype(jnp.float32), axis=1, keepdims=True)
            parts.append((other[at, :kv_rank].astype(jnp.float32), terms))
        peak = functools.reduce(jnp.maximum, [e for _, e in parts])
        shares = [jnp.exp(e - peak) for _, e in parts]
        inverse = 1.0 / functools.reduce(jnp.add, shares)
        whole = functools.reduce(jnp.add, [o * (w * inverse) for (o, _), w in zip(parts, shares)])
        for c in range(kv_rank // LANES):
            latent[c, at] = whole[:, c * LANES : (c + 1) * LANES]
        return 0

    lax.fori_loop(0, rows * heads // chunk, merge, 0, unroll=True)

    half_rows = away_ref.shape[0]
    me = me_ref[0]
    target = lax.broadcasted_iota(jnp.int32, (2 * half_rows, rows), 0)
    origin = lax.broadcasted_iota(jnp.int32, (2 * half_rows, rows), 1)
    owner_copy.wait()

    def place(r, picked):
        apart = owner_ref[r] ^ me
        shifted = origin - r * steps
        row_here = (shifted >= 0) & (shifted < steps)
        return tuple(
            jnp.where((target - slot_of(apart, chips, swap) * steps == shifted) & row_here, 1.0, old)
            for swap, old in enumerate(picked)
        )

    empty = jnp.zeros((2 * half_rows, rows), jnp.float32)
    pickers = lax.fori_loop(0, requests, place, (empty, empty), unroll=math.gcd(requests, 8))

    value_copy.wait()
    for h in range(heads):
        mine = jnp.concatenate(
            [latent[c, pl.ds(h, rows, stride=heads)] for c in range(kv_rank // LANES)], axis=1
        ).astype(jnp.bfloat16)
        head_rows[:, h * v_width : (h + 1) * v_width] = jnp.dot(
            mine, value_ref[h], preferred_element_type=jnp.float32
        ).astype(jnp.bfloat16)

    placed = [
        jnp.dot(
            picker.astype(jnp.bfloat16), head_rows[...], preferred_element_type=jnp.float32
        ).astype(jnp.bfloat16)
        for picker in pickers
    ]
    placed_ref[...] = placed[1]
    project(placed[0], [weight_ref], keep_ref, away_ref)
    for copy in weight_copies:
        copy.wait()


def second_kernel(placed_ref, weight_ref, later_ref, away_ref, keep_ref):
    project(placed_ref[...], [weight_ref, later_ref], keep_ref, away_ref)


def local(q_heads, w_absorb, w_value, w_out, latent_cache, ctx_blocks, block_table, owner):
    heads, _, kv_rank = w_absorb.shape
    row_count = q_heads.shape[0]
    head_width = q_heads.shape[1] // heads
    requests, max_blocks = block_table.shape
    steps = row_count // requests
    devices = lax.axis_size("head")
    chips = devices // 2
    blocks_here, block_rows, row_width = latent_cache.shape
    half = blocks_here // 2
    v_width = w_value.shape[2]
    row_block = steps * heads
    flat_rows = requests * row_block
    mebi = 1024 * 1024
    me = lax.axis_index("head").astype(jnp.int32).reshape(1)
    smem = pl.BlockSpec(memory_space=pltpu.SMEM)
    vmem = pl.BlockSpec(memory_space=pltpu.VMEM)
    hbm = pl.BlockSpec(memory_space=pltpu.HBM)

    def pin(x):
        return pltpu.with_memory_space_constraint(x, pltpu.HBM)

    def exchange(x, distance):
        return lax.ppermute(x, "head", [(i, i ^ distance) for i in range(devices)])

    piece_total = len(ring_places(chips))
    tile_shapes = [
        jax.ShapeDtypeStruct((n, w_out.shape[0], OUT_TILE), jnp.bfloat16) for n in TILES
    ]

    def prepare():
        slots = jnp.asarray(slots_by_device(chips, half))
        queries, plan = pl.pallas_call(
            functools.partial(prepare_kernel, heads),
            out_shape=(
                jax.ShapeDtypeStruct((flat_rows, row_width), jnp.bfloat16),
                jax.ShapeDtypeStruct((2 * piece_total * half + 2,), jnp.int32),
            ),
            in_specs=[smem] + [hbm] * 5,
            out_specs=(vmem, smem),
            scratch_shapes=[
                pltpu.VMEM(q_heads.shape, jnp.bfloat16),
                pltpu.VMEM(w_absorb.shape, jnp.bfloat16),
                pltpu.SMEM(ctx_blocks.shape, jnp.int32),
                pltpu.SMEM(block_table.shape, jnp.int32),
                pltpu.SMEM(slots.shape, jnp.int32),
                pltpu.VMEM((kv_rank // LANES + 1, flat_rows, LANES), jnp.float32),
                pltpu.SemaphoreType.DMA((5,)),
            ],
            compiler_params=pltpu.CompilerParams(vmem_limit_bytes=12 * mebi),
            cost_estimate=pl.CostEstimate(
                flops=2 * w_absorb.size * row_count, bytes_accessed=4 * w_absorb.size, transcendentals=0
            ),
            name="prepare",
        )(me, *map(pin, (q_heads, w_absorb, ctx_blocks, block_table, slots)))
        return queries.reshape(requests, row_block, row_width), plan

    def attend(plan, mine, theirs, pieces, stage):
        slots = len(pieces) * half
        first_slot = 0 if stage == 0 else piece_total * half - slots
        tiles = tile_shapes[stage]
        both = 2 * row_block
        return pl.pallas_call(
            functools.partial(
                attend_kernel, len(pieces), first_slot, sum(TILES[:stage]), heads, steps, kv_rank,
                float(head_width) ** -0.5,
            ),
            out_shape=(
                jax.ShapeDtypeStruct((flat_rows, kv_rank), jnp.float32),
                jax.ShapeDtypeStruct((flat_rows, LANES), jnp.float32),
                jax.ShapeDtypeStruct((flat_rows, kv_rank + LANES), jnp.bfloat16),
                tiles,
            ),
            in_specs=[smem] + [vmem] * (2 + len(pieces)) + [hbm],
            out_specs=(vmem,) * 4,
            scratch_shapes=[
                pltpu.VMEM((slots, 2 * both, block_rows), jnp.float32),
                pltpu.VMEM((requests + 1, both, block_rows), jnp.float32),
                pltpu.VMEM((requests + 1, both, block_rows), jnp.float32),
                pltpu.VMEM((requests + 1, both, kv_rank), jnp.float32),
                pltpu.SemaphoreType.DMA((tiles.shape[0],)),
            ],
            compiler_params=pltpu.CompilerParams(vmem_limit_bytes=28 * mebi),
            cost_estimate=pl.CostEstimate(
                flops=2 * slots * 2 * both * block_rows * 2 * row_width,
                bytes_accessed=slots * block_rows * row_width * 2,
                transcendentals=0,
            ),
            name="attend",
        )(plan, mine, theirs, *pieces, pin(w_out))

    ring = ring_of(chips)
    up = [
        (ring[i] * 2 + core, ring[(i + 1) % chips] * 2 + core)
        for i in range(chips)
        for core in range(2)
    ]
    down = [(b, a) for a, b in up]
    keys = jnp.swapaxes(latent_cache, 1, 2)
    ups = [keys[:half], keys[half:]]
    downs = list(ups)
    pieces = list(ups)
    for hop in range(1, chips // 2 + 1):
        last = hop == chips // 2
        if hop == 2:
            mine, plan = prepare()
            theirs = exchange(mine, 1)
            ups[0], mine, plan = lax.optimization_barrier((ups[0], mine, plan))
        if last:
            ups[0] = lax.ppermute(ups[0], "head", up)
            downs[1] = lax.ppermute(downs[1], "head", down)
            pieces += [ups[0], downs[1]]
        else:
            ups[0] = lax.ppermute(ups[0], "head", up)
            downs[1] = lax.ppermute(downs[1], "head", down)
            downs[0] = lax.ppermute(downs[0], "head", down)
            ups[1] = lax.ppermute(ups[1], "head", up)
            pieces += [ups[0], downs[1], downs[0], ups[1]]
    early, late = pieces[:-LATE], pieces[-LATE:]
    *early_part, weight = attend(plan, mine, theirs, early, 0)
    *late_part, next_weight = attend(plan, mine, theirs, late, 1)
    partial = [(out, lse, exchange(away, 1)) for out, lse, away in (early_part, late_part)]

    part_rows = chips * steps
    widths = (TILES[0] * OUT_TILE, (TILES[1] + TILES[2]) * OUT_TILE)
    parts = [jax.ShapeDtypeStruct((part_rows, n), jnp.bfloat16) for n in widths]
    placed_shape = jax.ShapeDtypeStruct((2 * part_rows, heads * v_width), jnp.bfloat16)
    outs, lses, others = zip(*partial)
    away, keep, placed, last_weight = pl.pallas_call(
        functools.partial(
            merge_kernel, len(partial), TILES[0] + TILES[1], heads, steps, chips
        ),
        out_shape=(parts[0], parts[0], placed_shape, tile_shapes[2]),
        in_specs=[smem, hbm, hbm, hbm] + [vmem] * (1 + 3 * len(partial)),
        out_specs=(vmem,) * 4,
        scratch_shapes=[
            pltpu.VMEM((kv_rank // LANES, flat_rows, LANES), jnp.float32),
            pltpu.VMEM((row_count, heads * v_width), jnp.bfloat16),
            pltpu.SMEM(owner.shape, jnp.int32),
            pltpu.VMEM(w_value.shape, jnp.bfloat16),
            pltpu.SemaphoreType.DMA((2,)),
            pltpu.SemaphoreType.DMA((TILES[2],)),
        ],
        compiler_params=pltpu.CompilerParams(vmem_limit_bytes=28 * mebi),
        name="merge_and_project",
    )(me, pin(owner), pin(w_value), pin(w_out), weight, *outs, *lses, *others)
    next_away, next_keep = pl.pallas_call(
        second_kernel,
        out_shape=(parts[1], parts[1]),
        in_specs=[vmem] * 3,
        out_specs=(vmem, vmem),
        compiler_params=pltpu.CompilerParams(vmem_limit_bytes=28 * mebi),
        cost_estimate=pl.CostEstimate(
            flops=2 * w_out.size * part_rows, bytes_accessed=8 * w_out.size, transcendentals=0
        ),
        name="project_second",
    )(placed, next_weight, last_weight)

    def add(x, y):
        return (x.astype(jnp.float32) + y.astype(jnp.float32)).astype(jnp.bfloat16)

    def fold(x, bit):
        middle = x.shape[0] // 2
        return add(x[:middle], exchange(x[middle:], 2 << bit))

    halves = [add(keep, exchange(away, 1)), add(next_keep, exchange(next_away, 1))]
    for step in range(2):
        halves = [fold(x, chip_bits(chips, swap)[step]) for swap, x in enumerate(halves)]
    result = jnp.concatenate(halves, axis=1)
    for bit in chip_bits(chips, False)[2:]:
        result = fold(result, bit)
    return result


def solution(mesh):
    return jax.shard_map(
        local,
        mesh=mesh,
        in_specs=(
            P("group", "head"),
            P("head", None, None),
            P("head", None, None),
            P("head", None),
            P(("group", "head"), None, None),
            P("group"),
            P("group", None),
            P("group"),
        ),
        out_specs=P(("group", "head"), None),
        check_vma=False,
    )
```

time: 68.1 us -> 60.8 us (0.89)
  local copies, waits for them, and re-layouts: 5.35 us -> 1.03 us
  starting transfers between devices: 27.8 us -> 24.5 us
  waiting for transfers between devices: 16.6 us -> 18.9 us
  Pallas kernels: 16.8 us -> 15.2 us
    ppermute x13 -> x10, starting transfers between devices: 12.7 us -> 7.63 us  [exchange(): return lax.ppermute(x, 'head', [(i, i ^ distance) for i in range(devices)])]
    unnamed x14 -> x0, local copies, waits for them, and re-layouts: 4.16 us -> none
    ppermute x13 -> x10, waiting for transfers between devices: 9.62 us -> 12.9 us  [exchange(): return lax.ppermute(x, 'head', [(i, i ^ distance) for i in range(devices)])]
    ppermute x3, waiting for transfers between devices: 2.85 us -> 0.01 us  [local(): downs[0] = lax.ppermute(downs[0], 'head', down)]
    pallas_call x5, Pallas kernels: 16.8 us -> 15.2 us  [the longest x2 8.73 us: attend(): pl.pallas_call(functools.partial(attend_kernel, len(pieces), first_slot,...]
    ppermute x4, waiting for transfers between devices: 2.98 us -> 4.5 us  [local(): downs[1] = lax.ppermute(downs[1], 'head', down)]
    ppermute x4, starting transfers between devices: 7.7 us -> 8.82 us  [local(): ups[0] = lax.ppermute(ups[0], 'head', up)]
    ppermute x3, waiting for transfers between devices: 0.01 us -> 1.08 us  [local(): ups[1] = lax.ppermute(ups[1], 'head', up)]
  transfers between devices with their start and end apart: 27 -> 24, of which waited for: 10 -> 12; matrix products, arithmetic and copies ran while one was open for 0% -> 0% of each run, Pallas kernels for 19% -> 18%
where the time goes in v4:
time: 60.8 us; the launch traced here: 60.7 us
  starting transfers between devices  24.5 us (40%)
  waiting for transfers between devices  18.9 us (31%)
  Pallas kernels  15.2 us (25%)
  local copies, waits for them, and re-layouts  1.03 us (2%)
  other arithmetic  0.9 us (1%)
    ppermute x10, waiting for transfers between devices, exchange(): return lax.ppermute(x, 'head', [(i, i ^ distance) for i in range(devices)])  12.9 us
    ppermute x4, starting transfers between devices, local(): ups[0] = lax.ppermute(ups[0], 'head', up)  8.82 us
    pallas_call x2, Pallas kernels, attend(): pl.pallas_call(functools.partial(attend_kernel, len(pieces), first_slot,...  8.73 us
    ppermute x10, starting transfers between devices, exchange(): return lax.ppermute(x, 'head', [(i, i ^ distance) for i in range(devices)])  7.63 us
    ppermute x3, starting transfers between devices, local(): ups[1] = lax.ppermute(ups[1], 'head', up)  5.68 us
    ppermute x4, waiting for transfers between devices, local(): downs[1] = lax.ppermute(downs[1], 'head', down)  4.5 us
    pallas_call x1, Pallas kernels, local(): pl.pallas_call(functools.partial(merge_kernel, len(partial), TILES[0] + T...  3.06 us
    pallas_call x1, Pallas kernels, prepare(): pl.pallas_call(functools.partial(prepare_kernel, heads), out_shape=(jax.S...  2.22 us
  transfers between devices with their start and end apart: 24, of which 12 were waited for; matrix products, arithmetic and copies ran while one was open for 0% of the time, Pallas kernels for 18%

profile of v4, /device:TPU:0, one launch (start us, length us, event | category | flops | bytes accessed | tf_op | source)
XLA Modules:
  0.0 60.7 jit_solution(751293008991045694)
XLA Ops:
  0.0 1.0 %fusion.1 = (bf16[1,576,128]{2,1,0:T(8,128)(2,1)S(1)}, bf16[1,576,128]{2,1,0:T(8,128)(2,1)S(1)}) fusion(bf16[2,576,128]{2,1,0:T(8,128)(2,1)} %bitcast.6), kind=kLoop, calls=%fused_computation.11 | loop fusion | bytes 589824 | tf_op jit(solution)/shard_map/slice | solution.py:399
  1.0 3.1 %collective-permute-start = (bf16[1,576,128]{2,1,0:T(8,128)(2,1)S(1)}, bf16[1,576,128]{2,1,0:T(8,128)(2,1)S(1)}, u32[]{:S(2)}, u32[]{:S(2)}) collective-permute-start(bf16[1,576,128]{2,1,0:T(8,128)(2,1)S(1)} %get-tuple-element.44.rest_0_), channel_id=1, source_target_pairs={{0,4},{1,5},{4,8},{5,9},{8,12},{9,13},{12,14},{13,15},{14,10},{15,... | collective-permute-start | bytes 442376 | tf_op jit(solution)/shard_map/ppermute | solution.py:413
  4.1 0.0 collective-permute-start.2
  4.1 2.0 %collective-permute-start.4 = (bf16[1,576,128]{2,1,0:T(8,128)(2,1)S(1)}, bf16[1,576,128]{2,1,0:T(8,128)(2,1)S(1)}, u32[]{:S(2)}, u32[]{:S(2)}) collective-permute-start(bf16[1,576,128]{2,1,0:T(8,128)(2,1)S(1)} %get-tuple-element.43.rest_1_), channel_id=1, source_target_pairs={{0,4},{1,5},{4,8},{5,9},{8,12},{9,13},{12,14},{13,15},{14,10},{15,... | collective-permute-start | bytes 442376 | tf_op jit(solution)/shard_map/ppermute | solution.py:416
  6.1 0.0 collective-permute-start.3
  6.1 2.2 %prepare.1 = (bf16[256,576]{1,0:T(8,128)(2,1)S(1)}, s32[34]{0:T(128)S(1)}) custom-call(s32[1]{0:T(128)} %bitcast.me_ref, bf16[32,1536]{1,0:T(8,128)(2,1)} %query_hbm.1, bf16[8,128,512]{2,1,0:T(8,128)(2,1)} %absorb_hbm.1, s32[8]{0:T(128)} %length_hbm.1, s32[8,8]{1,0:T(8,128)} %table_hbm.1, s32[16,32]{1,0:T(8,128)} %constant.6.clone.slot_hbm), custom_call_target="tpu_custom_call" | custom-call | flops 33554432 | bytes 2097152 | tf_op jit(solution)/shard_map/prepare/pallas_call | solution.py:332
  8.3 0.4 collective-permute-done.rest_2_
  8.7 2.2 %collective-permute-done.2.rest_3_ = bf16[1,576,128]{2,1,0:T(8,128)(2,1)S(1)} collective-permute-done((bf16[1,576,128]{2,1,0:T(8,128)(2,1)S(1)}, bf16[1,576,128]{2,1,0:T(8,128)(2,1)S(1)}, u32[]{:S(2)}, u32[]{:S(2)}) %collective-permute-start.2) | collective-permute-done | bytes 147488 | tf_op jit(solution)/shard_map/ppermute | solution.py:414
  10.9 2.0 %collective-permute-start.5 = (bf16[1,576,128]{2,1,0:T(8,128)(2,1)S(1)}, bf16[1,576,128]{2,1,0:T(8,128)(2,1)S(1)}, u32[]{:S(2)}, u32[]{:S(2)}) collective-permute-start(bf16[1,576,128]{2,1,0:T(8,128)(2,1)S(1)} %collective-permute-done.rest_2_), channel_id=1, source_target_pairs={{0,4},{1,5},{4,8},{5,9},{8,12},{9,13},{12,14},{13,15},{14,10},{15,... | collective-permute-start | bytes 442376 | tf_op jit(solution)/shard_map/ppermute | solution.py:413
  12.9 1.6 %collective-permute-start.8 = (bf16[1,576,128]{2,1,0:T(8,128)(2,1)S(1)}, bf16[1,576,128]{2,1,0:T(8,128)(2,1)S(1)}, u32[]{:S(2)}, u32[]{:S(2)}) collective-permute-start(bf16[1,576,128]{2,1,0:T(8,128)(2,1)S(1)} %collective-permute-done.4.rest_5_), channel_id=1, source_target_pairs={{0,4},{1,5},{4,8},{5,9},{8,12},{9,13},{12,14},{13,15},{14,10},{15,... | collective-permute-start | bytes 442376 | tf_op jit(solution)/shard_map/ppermute | solution.py:416
  14.5 0.4 collective-permute-start.7
  14.9 1.1 %collective-permute-done.6.rest_7_ = bf16[1,576,128]{2,1,0:T(8,128)(2,1)S(1)} collective-permute-done((bf16[1,576,128]{2,1,0:T(8,128)(2,1)S(1)}, bf16[1,576,128]{2,1,0:T(8,128)(2,1)S(1)}, u32[]{:S(2)}, u32[]{:S(2)}) %collective-permute-start.6) | collective-permute-done | bytes 147488 | tf_op jit(solution)/shard_map/ppermute | solution.py:414
  16.0 0.0 collective-permute-start.10
  16.0 0.0 collective-permute-done.5.rest_6_
  16.0 2.5 %collective-permute-start.9 = (bf16[1,576,128]{2,1,0:T(8,128)(2,1)S(1)}, bf16[1,576,128]{2,1,0:T(8,128)(2,1)S(1)}, u32[]{:S(2)}, u32[]{:S(2)}) collective-permute-start(bf16[1,576,128]{2,1,0:T(8,128)(2,1)S(1)} %collective-permute-done.5.rest_6_), channel_id=1, source_target_pairs={{0,4},{1,5},{4,8},{5,9},{8,12},{9,13},{12,14},{13,15},{14,10},{15,... | collective-permute-start | bytes 442376 | tf_op jit(solution)/shard_map/ppermute | solution.py:413
  18.5 1.1 %collective-permute-done.8.rest_9_ = bf16[1,576,128]{2,1,0:T(8,128)(2,1)S(1)} collective-permute-done((bf16[1,576,128]{2,1,0:T(8,128)(2,1)S(1)}, bf16[1,576,128]{2,1,0:T(8,128)(2,1)S(1)}, u32[]{:S(2)}, u32[]{:S(2)}) %collective-permute-start.8) | collective-permute-done | bytes 147488 | tf_op jit(solution)/shard_map/ppermute | solution.py:416
  19.5 2.1 %collective-permute-start.12 = (bf16[1,576,128]{2,1,0:T(8,128)(2,1)S(1)}, bf16[1,576,128]{2,1,0:T(8,128)(2,1)S(1)}, u32[]{:S(2)}, u32[]{:S(2)}) collective-permute-start(bf16[1,576,128]{2,1,0:T(8,128)(2,1)S(1)} %collective-permute-done.8.rest_9_), channel_id=1, source_target_pairs={{0,4},{1,5},{4,8},{5,9},{8,12},{9,13},{12,14},{13,15},{14,10},{15,... | collective-permute-start | bytes 442376 | tf_op jit(solution)/shard_map/ppermute | solution.py:416
  21.6 0.0 collective-permute-done.7.rest_8_
  21.6 1.1 %collective-permute-start.11 = (bf16[1,576,128]{2,1,0:T(8,128)(2,1)S(1)}, bf16[1,576,128]{2,1,0:T(8,128)(2,1)S(1)}, u32[]{:S(2)}, u32[]{:S(2)}) collective-permute-start(bf16[1,576,128]{2,1,0:T(8,128)(2,1)S(1)} %collective-permute-done.7.rest_8_), channel_id=1, source_target_pairs={{4,0},{5,1},{8,4},{9,5},{12,8},{13,9},{14,12},{15,13},{10,14},{11,... | collective-permute-start | bytes 442376 | tf_op jit(solution)/shard_map/ppermute | solution.py:415
  22.7 1.3 %collective-permute-done.10.rest_11_ = bf16[1,576,128]{2,1,0:T(8,128)(2,1)S(1)} collective-permute-done((bf16[1,576,128]{2,1,0:T(8,128)(2,1)S(1)}, bf16[1,576,128]{2,1,0:T(8,128)(2,1)S(1)}, u32[]{:S(2)}, u32[]{:S(2)}) %collective-permute-start.10) | collective-permute-done | bytes 147488 | tf_op jit(solution)/shard_map/ppermute | solution.py:414
  24.0 0.8 %collective-permute-start.14 = (bf16[1,576,128]{2,1,0:T(8,128)(2,1)S(1)}, bf16[1,576,128]{2,1,0:T(8,128)(2,1)S(1)}, u32[]{:S(2)}, u32[]{:S(2)}) collective-permute-start(bf16[1,576,128]{2,1,0:T(8,128)(2,1)S(1)} %collective-permute-done.10.rest_11_), channel_id=1, source_target_pairs={{4,0},{5,1},{8,4},{9,5},{12,8},{13,9},{14,12},{15,13},{10,14},{11,... | collective-permute-start | bytes 442376 | tf_op jit(solution)/shard_map/ppermute | solution.py:410
  24.7 0.0 collective-permute-done.9.rest_10_
  24.7 1.3 %collective-permute-start.13 = (bf16[1,576,128]{2,1,0:T(8,128)(2,1)S(1)}, bf16[1,576,128]{2,1,0:T(8,128)(2,1)S(1)}, u32[]{:S(2)}, u32[]{:S(2)}) collective-permute-start(bf16[1,576,128]{2,1,0:T(8,128)(2,1)S(1)} %collective-permute-done.9.rest_10_), channel_id=1, source_target_pairs={{0,4},{1,5},{4,8},{5,9},{8,12},{9,13},{12,14},{13,15},{14,10},{15,... | collective-permute-start | bytes 442376 | tf_op jit(solution)/shard_map/ppermute | solution.py:409
  26.0 0.0 collective-permute-done.1.theirs_ref
  26.0 5.7 %attend.2 = (f32[256,512]{1,0:T(8,128)S(1)}, f32[256,128]{1,0:T(8,128)S(1)}, bf16[256,640]{1,0:T(8,128)(2,1)S(1)}, bf16[4,1024,1024]{2,1,0:T(8,128)(2,1)S(1)}) custom-call(s32[34]{0:T(128)S(1)} %get-tuple-element.26.plan_ref, bf16[8,32,576]{2,1,0:T(8,128)(2,1)S(1)} %bitcast.4, bf16[8,32,576]{2,1,0:T(8,128)(2,1)S(1)} %collective-permute-done.1.theirs_ref, ...), custom_call_target="tpu_custom_call" | custom-call | flops 452984832 | bytes 1769472 | tf_op jit(solution)/shard_map/attend/pallas_call | solution.py:362
  31.7 0.1 collective-permute-start.15
  31.8 0.0 collective-permute-done.12.rest_1_
  31.8 0.0 collective-permute-done.14.rest_3_
  31.8 3.0 %attend.3 = (f32[256,512]{1,0:T(8,128)S(1)}, f32[256,128]{1,0:T(8,128)S(1)}, bf16[256,640]{1,0:T(8,128)(2,1)S(1)}, bf16[1,1024,1024]{2,1,0:T(8,128)(2,1)S(1)}) custom-call(s32[34]{0:T(128)S(1)} %get-tuple-element.26.plan_ref, bf16[8,32,576]{2,1,0:T(8,128)(2,1)S(1)} %bitcast.5, bf16[8,32,576]{2,1,0:T(8,128)(2,1)S(1)} %collective-permute-done.1.theirs_ref, ...), custom_call_target="tpu_custom_call" | custom-call | flops 150994944 | bytes 589824 | tf_op jit(solution)/shard_map/attend/pallas_call | solution.py:362
  34.9 0.6 collective-permute-start.16
  35.4 1.3 %collective-permute-done.16.rest_5_ = bf16[256,640]{1,0:T(8,128)(2,1)S(1)} collective-permute-done((bf16[256,640]{1,0:T(8,128)(2,1)S(1)}, bf16[256,640]{1,0:T(8,128)(2,1)S(1)}, u32[]{:S(2)}, u32[]{:S(2)}) %collective-permute-start.16) | collective-permute-done | bytes 327712 | tf_op jit(solution)/shard_map/ppermute | solution.py:323
  36.7 3.1 %merge_and_project.1 = (bf16[32,4096]{1,0:T(8,128)(2,1)S(1)}, bf16[32,4096]{1,0:T(8,128)(2,1)S(1)}, bf16[64,1024]{1,0:T(8,128)(2,1)S(1)}, bf16[2,1024,1024]{2,1,0:T(8,128)(2,1)S(1)}) custom-call(s32[1]{0:T(128)} %bitcast.me_ref, s32[8]{0:T(128)} %owner_hbm.1, bf16[8,512,128]{2,1,0:T(8,128)(2,1)} %value_hbm.1, bf16[1024,7168]{1,0:T(8,128)(2,1)} %weight_hbm.1, ...), custom_call_target="tpu_custom_call" | custom-call | tf_op jit(solution)/shard_map/merge_and_project/pallas_call | solution.py:428
  39.8 1.2 %project_second.1 = (bf16[32,3072]{1,0:T(8,128)(2,1)S(1)}, bf16[32,3072]{1,0:T(8,128)(2,1)S(1)}) custom-call(bf16[64,1024]{1,0:T(8,128)(2,1)S(1)} %get-tuple-element.38.placed_ref, bf16[1,1024,1024]{2,1,0:T(8,128)(2,1)S(1)} %get-tuple-element.39.weight_ref, bf16[2,1024,1024]{2,1,0:T(8,128)(2,1)S(1)} %get-tuple-element.40.later_ref), custom_call_target="tpu_custom_call" | custom-call | flops 469762048 | bytes 58720256 | tf_op jit(solution)/shard_map/project_second/pallas_call | solution.py:446
  41.0 0.4 collective-permute-start.20
  41.4 0.1 collective-permute-start.17
  41.5 0.9 %collective-permute-done.20 = bf16[32,3072]{1,0:T(8,128)(2,1)S(1)} collective-permute-done((bf16[32,3072]{1,0:T(8,128)(2,1)S(1)}, bf16[32,3072]{1,0:T(8,128)(2,1)S(1)}, u32[]{:S(2)}, u32[]{:S(2)}) %collective-permute-start.20) | collective-permute-done | bytes 196640 | tf_op jit(solution)/shard_map/ppermute | solution.py:323
  42.5 1.7 %collective-permute-start.21 = (bf16[16,3072]{1,0:T(8,128)(2,1)S(1)}, bf16[16,3072]{1,0:T(8,128)(2,1)S(1)}, u32[]{:S(2)}, u32[]{:S(2)}) collective-permute-start(bf16[16,3072]{1,0:T(8,128)(2,1)S(1)} %slice.55), channel_id=1, source_target_pairs={{0,4},{1,5},{2,6},{3,7},{4,0},{5,1},{6,2},{7,3},{8,12},{9,13},{10,... | collective-permute-start | bytes 294920 | tf_op jit(solution)/shard_map/ppermute | solution.py:323
  44.2 0.1 add_convert_fusion
  44.3 0.8 %collective-permute-start.18 = (bf16[16,4096]{1,0:T(8,128)(2,1)S(1)}, bf16[16,4096]{1,0:T(8,128)(2,1)S(1)}, u32[]{:S(2)}, u32[]{:S(2)}) collective-permute-start(bf16[16,4096]{1,0:T(8,128)(2,1)S(1)} %slice.51), channel_id=1, source_target_pairs={{0,2},{1,3},{2,0},{3,1},{4,6},{5,7},{6,4},{7,5},{8,10},{9,11},{10,... | collective-permute-start | bytes 393224 | tf_op jit(solution)/shard_map/ppermute | solution.py:323
  45.1 2.5 %collective-permute-done.21 = bf16[16,3072]{1,0:T(8,128)(2,1)S(1)} collective-permute-done((bf16[16,3072]{1,0:T(8,128)(2,1)S(1)}, bf16[16,3072]{1,0:T(8,128)(2,1)S(1)}, u32[]{:S(2)}, u32[]{:S(2)}) %collective-permute-start.21) | collective-permute-done | bytes 98336 | tf_op jit(solution)/shard_map/ppermute | solution.py:323
  47.7 0.8 %collective-permute-start.22 = (bf16[8,3072]{1,0:T(8,128)(2,1)S(1)}, bf16[8,3072]{1,0:T(8,128)(2,1)S(1)}, u32[]{:S(2)}, u32[]{:S(2)}) collective-permute-start(bf16[8,3072]{1,0:T(8,128)(2,1)S(1)} %slice.57), channel_id=1, source_target_pairs={{0,2},{1,3},{2,0},{3,1},{4,6},{5,7},{6,4},{7,5},{8,10},{9,11},{10,... | collective-permute-start | bytes 147464 | tf_op jit(solution)/shard_map/ppermute | solution.py:323
  48.6 1.3 %collective-permute-done.18 = bf16[16,4096]{1,0:T(8,128)(2,1)S(1)} collective-permute-done((bf16[16,4096]{1,0:T(8,128)(2,1)S(1)}, bf16[16,4096]{1,0:T(8,128)(2,1)S(1)}, u32[]{:S(2)}, u32[]{:S(2)}) %collective-permute-start.18) | collective-permute-done | bytes 131104 | tf_op jit(solution)/shard_map/ppermute | solution.py:323
  49.9 0.6 collective-permute-start.19
  50.5 1.4 %collective-permute-done.22 = bf16[8,3072]{1,0:T(8,128)(2,1)S(1)} collective-permute-done((bf16[8,3072]{1,0:T(8,128)(2,1)S(1)}, bf16[8,3072]{1,0:T(8,128)(2,1)S(1)}, u32[]{:S(2)}, u32[]{:S(2)}) %collective-permute-start.22) | collective-permute-done | bytes 49184 | tf_op jit(solution)/shard_map/ppermute | solution.py:323
  51.9 2.3 %collective-permute-done.19 = bf16[8,4096]{1,0:T(8,128)(2,1)S(1)} collective-permute-done((bf16[8,4096]{1,0:T(8,128)(2,1)S(1)}, bf16[8,4096]{1,0:T(8,128)(2,1)S(1)}, u32[]{:S(2)}, u32[]{:S(2)}) %collective-permute-start.19) | collective-permute-done | bytes 65568 | tf_op jit(solution)/shard_map/ppermute | solution.py:323
  54.3 2.5 %collective-permute-start.23 = (bf16[4,7168]{1,0:T(4,128)(2,1)S(1)}, bf16[4,7168]{1,0:T(4,128)(2,1)S(1)}, u32[]{:S(2)}, u32[]{:S(2)}) collective-permute-start(bf16[4,7168]{1,0:T(4,128)(2,1)S(1)} %pad_maximum_fusion), channel_id=1, source_target_pairs={{0,8},{1,9},{2,10},{3,11},{4,12},{5,13},{6,14},{7,15},{8,0},{9,1},... | collective-permute-start | bytes 172040 | tf_op jit(solution)/shard_map/ppermute | solution.py:323
  56.8 3.2 %collective-permute-done.23 = bf16[4,7168]{1,0:T(4,128)(2,1)S(1)} collective-permute-done((bf16[4,7168]{1,0:T(4,128)(2,1)S(1)}, bf16[4,7168]{1,0:T(4,128)(2,1)S(1)}, u32[]{:S(2)}, u32[]{:S(2)}) %collective-permute-start.23) | collective-permute-done | bytes 57376 | tf_op jit(solution)/shard_map/ppermute | solution.py:323
  60.0 0.7 %add_convert_fusion.5 = bf16[4,7168]{1,0:T(4,128)(2,1)} fusion(bf16[4,7168]{1,0:T(4,128)(2,1)S(1)} %collective-permute-done.23, bf16[8,4096]{1,0:T(8,128)(2,1)S(1)} %add_convert_fusion.4, bf16[8,3072]{1,0:T(8,128)(2,1)S(1)} %add_convert_fusion.6), kind=kLoop, calls=%fused_computation.7 | loop fusion | flops 200704 | bytes 229376 | tf_op jit(solution)/shard_map/convert_element_type | solution.py:459
  (18 shorter events, 0.2 us)
Async XLA Ops:
  1.0 7.7 %collective-permute-start = (bf16[1,576,128]{2,1,0:T(8,128)(2,1)S(1)}, bf16[1,576,128]{2,1,0:T(8,128)(2,1)S(1)}, u32[]{:S(2)}, u32[]{:S(2)}) collective-permute-start(bf16[1,576,128]{2,1,0:T(8,128)(2,1)S(1)} %get-tuple-element.44.rest_0_), channel_id=1, source_target_pairs={{0,4},{1,5},{4,8},{5,9},{8,12},{9,13},{12,14},{13,15},{14,10},{15,... | collective-permute-start | bytes 442376 | tf_op jit(solution)/shard_map/ppermute | solution.py:413
  4.1 6.8 %collective-permute-start.2 = (bf16[1,576,128]{2,1,0:T(8,128)(2,1)S(1)}, bf16[1,576,128]{2,1,0:T(8,128)(2,1)S(1)}, u32[]{:S(2)}, u32[]{:S(2)}) collective-permute-start(bf16[1,576,128]{2,1,0:T(8,128)(2,1)S(1)} %get-tuple-element.43.rest_1_), channel_id=1, source_target_pairs={{4,0},{5,1},{8,4},{9,5},{12,8},{13,9},{14,12},{15,13},{10,14},{11,... | collective-permute-start | bytes 442376 | tf_op jit(solution)/shard_map/ppermute | solution.py:414
  4.1 8.8 %collective-permute-start.4 = (bf16[1,576,128]{2,1,0:T(8,128)(2,1)S(1)}, bf16[1,576,128]{2,1,0:T(8,128)(2,1)S(1)}, u32[]{:S(2)}, u32[]{:S(2)}) collective-permute-start(bf16[1,576,128]{2,1,0:T(8,128)(2,1)S(1)} %get-tuple-element.43.rest_1_), channel_id=1, source_target_pairs={{0,4},{1,5},{4,8},{5,9},{8,12},{9,13},{12,14},{13,15},{14,10},{15,... | collective-permute-start | bytes 442376 | tf_op jit(solution)/shard_map/ppermute | solution.py:416
  6.1 8.4 %collective-permute-start.3 = (bf16[1,576,128]{2,1,0:T(8,128)(2,1)S(1)}, bf16[1,576,128]{2,1,0:T(8,128)(2,1)S(1)}, u32[]{:S(2)}, u32[]{:S(2)}) collective-permute-start(bf16[1,576,128]{2,1,0:T(8,128)(2,1)S(1)} %get-tuple-element.44.rest_0_), channel_id=1, source_target_pairs={{4,0},{5,1},{8,4},{9,5},{12,8},{13,9},{14,12},{15,13},{10,14},{11,... | collective-permute-start | bytes 442376 | tf_op jit(solution)/shard_map/ppermute | solution.py:415
  10.9 5.1 %collective-permute-start.6 = (bf16[1,576,128]{2,1,0:T(8,128)(2,1)S(1)}, bf16[1,576,128]{2,1,0:T(8,128)(2,1)S(1)}, u32[]{:S(2)}, u32[]{:S(2)}) collective-permute-start(bf16[1,576,128]{2,1,0:T(8,128)(2,1)S(1)} %collective-permute-done.2.rest_3_), channel_id=1, source_target_pairs={{4,0},{5,1},{8,4},{9,5},{12,8},{13,9},{14,12},{15,13},{10,14},{11,... | collective-permute-start | bytes 442376 | tf_op jit(solution)/shard_map/ppermute | solution.py:414
  10.9 5.1 %collective-permute-start.5 = (bf16[1,576,128]{2,1,0:T(8,128)(2,1)S(1)}, bf16[1,576,128]{2,1,0:T(8,128)(2,1)S(1)}, u32[]{:S(2)}, u32[]{:S(2)}) collective-permute-start(bf16[1,576,128]{2,1,0:T(8,128)(2,1)S(1)} %collective-permute-done.rest_2_), channel_id=1, source_target_pairs={{0,4},{1,5},{4,8},{5,9},{8,12},{9,13},{12,14},{13,15},{14,10},{15,... | collective-permute-start | bytes 442376 | tf_op jit(solution)/shard_map/ppermute | solution.py:413
  12.9 13.1 %collective-permute-start.1 = (bf16[8,32,576]{2,1,0:T(8,128)(2,1)S(1)}, bf16[8,32,576]{2,1,0:T(8,128)(2,1)S(1)}, u32[]{:S(2)}, u32[]{:S(2)}) collective-permute-start(bf16[8,32,576]{2,1,0:T(8,128)(2,1)S(1)} %bitcast.3), channel_id=1, source_target_pairs={{0,1},{1,0},{2,3},{3,2},{4,5},{5,4},{6,7},{7,6},{8,9},{9,8},{10,11... | collective-permute-start | bytes 884744 | tf_op jit(solution)/shard_map/ppermute | solution.py:323
  12.9 6.6 %collective-permute-start.8 = (bf16[1,576,128]{2,1,0:T(8,128)(2,1)S(1)}, bf16[1,576,128]{2,1,0:T(8,128)(2,1)S(1)}, u32[]{:S(2)}, u32[]{:S(2)}) collective-permute-start(bf16[1,576,128]{2,1,0:T(8,128)(2,1)S(1)} %collective-permute-done.4.rest_5_), channel_id=1, source_target_pairs={{0,4},{1,5},{4,8},{5,9},{8,12},{9,13},{12,14},{13,15},{14,10},{15,... | collective-permute-start | bytes 442376 | tf_op jit(solution)/shard_map/ppermute | solution.py:416
  14.5 7.2 %collective-permute-start.7 = (bf16[1,576,128]{2,1,0:T(8,128)(2,1)S(1)}, bf16[1,576,128]{2,1,0:T(8,128)(2,1)S(1)}, u32[]{:S(2)}, u32[]{:S(2)}) collective-permute-start(bf16[1,576,128]{2,1,0:T(8,128)(2,1)S(1)} %collective-permute-done.3.rest_4_), channel_id=1, source_target_pairs={{4,0},{5,1},{8,4},{9,5},{12,8},{13,9},{14,12},{15,13},{10,14},{11,... | collective-permute-start | bytes 442376 | tf_op jit(solution)/shard_map/ppermute | solution.py:415
  16.0 8.0 %collective-permute-start.10 = (bf16[1,576,128]{2,1,0:T(8,128)(2,1)S(1)}, bf16[1,576,128]{2,1,0:T(8,128)(2,1)S(1)}, u32[]{:S(2)}, u32[]{:S(2)}) collective-permute-start(bf16[1,576,128]{2,1,0:T(8,128)(2,1)S(1)} %collective-permute-done.6.rest_7_), channel_id=1, source_target_pairs={{4,0},{5,1},{8,4},{9,5},{12,8},{13,9},{14,12},{15,13},{10,14},{11,... | collective-permute-start | bytes 442376 | tf_op jit(solution)/shard_map/ppermute | solution.py:414
  16.0 8.7 %collective-permute-start.9 = (bf16[1,576,128]{2,1,0:T(8,128)(2,1)S(1)}, bf16[1,576,128]{2,1,0:T(8,128)(2,1)S(1)}, u32[]{:S(2)}, u32[]{:S(2)}) collective-permute-start(bf16[1,576,128]{2,1,0:T(8,128)(2,1)S(1)} %collective-permute-done.5.rest_6_), channel_id=1, source_target_pairs={{0,4},{1,5},{4,8},{5,9},{8,12},{9,13},{12,14},{13,15},{14,10},{15,... | collective-permute-start | bytes 442376 | tf_op jit(solution)/shard_map/ppermute | solution.py:413
  19.5 12.2 %collective-permute-start.12 = (bf16[1,576,128]{2,1,0:T(8,128)(2,1)S(1)}, bf16[1,576,128]{2,1,0:T(8,128)(2,1)S(1)}, u32[]{:S(2)}, u32[]{:S(2)}) collective-permute-start(bf16[1,576,128]{2,1,0:T(8,128)(2,1)S(1)} %collective-permute-done.8.rest_9_), channel_id=1, source_target_pairs={{0,4},{1,5},{4,8},{5,9},{8,12},{9,13},{12,14},{13,15},{14,10},{15,... | collective-permute-start | bytes 442376 | tf_op jit(solution)/shard_map/ppermute | solution.py:416
  21.6 10.2 %collective-permute-start.11 = (bf16[1,576,128]{2,1,0:T(8,128)(2,1)S(1)}, bf16[1,576,128]{2,1,0:T(8,128)(2,1)S(1)}, u32[]{:S(2)}, u32[]{:S(2)}) collective-permute-start(bf16[1,576,128]{2,1,0:T(8,128)(2,1)S(1)} %collective-permute-done.7.rest_8_), channel_id=1, source_target_pairs={{4,0},{5,1},{8,4},{9,5},{12,8},{13,9},{14,12},{15,13},{10,14},{11,... | collective-permute-start | bytes 442376 | tf_op jit(solution)/shard_map/ppermute | solution.py:415
  24.0 7.8 %collective-permute-start.14 = (bf16[1,576,128]{2,1,0:T(8,128)(2,1)S(1)}, bf16[1,576,128]{2,1,0:T(8,128)(2,1)S(1)}, u32[]{:S(2)}, u32[]{:S(2)}) collective-permute-start(bf16[1,576,128]{2,1,0:T(8,128)(2,1)S(1)} %collective-permute-done.10.rest_11_), channel_id=1, source_target_pairs={{4,0},{5,1},{8,4},{9,5},{12,8},{13,9},{14,12},{15,13},{10,14},{11,... | collective-permute-start | bytes 442376 | tf_op jit(solution)/shard_map/ppermute | solution.py:410
  24.7 7.1 %collective-permute-start.13 = (bf16[1,576,128]{2,1,0:T(8,128)(2,1)S(1)}, bf16[1,576,128]{2,1,0:T(8,128)(2,1)S(1)}, u32[]{:S(2)}, u32[]{:S(2)}) collective-permute-start(bf16[1,576,128]{2,1,0:T(8,128)(2,1)S(1)} %collective-permute-done.9.rest_10_), channel_id=1, source_target_pairs={{0,4},{1,5},{4,8},{5,9},{8,12},{9,13},{12,14},{13,15},{14,10},{15,... | collective-permute-start | bytes 442376 | tf_op jit(solution)/shard_map/ppermute | solution.py:409
  31.7 3.7 %collective-permute-start.15 = (bf16[256,640]{1,0:T(8,128)(2,1)S(1)}, bf16[256,640]{1,0:T(8,128)(2,1)S(1)}, u32[]{:S(2)}, u32[]{:S(2)}) collective-permute-start(bf16[256,640]{1,0:T(8,128)(2,1)S(1)} %get-tuple-element.34), channel_id=1, source_target_pairs={{0,1},{1,0},{2,3},{3,2},{4,5},{5,4},{6,7},{7,6},{8,9},{9,8},{10,11... | collective-permute-start | bytes 983048 | tf_op jit(solution)/shard_map/ppermute | solution.py:323
  34.9 1.8 %collective-permute-start.16 = (bf16[256,640]{1,0:T(8,128)(2,1)S(1)}, bf16[256,640]{1,0:T(8,128)(2,1)S(1)}, u32[]{:S(2)}, u32[]{:S(2)}) collective-permute-start(bf16[256,640]{1,0:T(8,128)(2,1)S(1)} %get-tuple-element.35), channel_id=1, source_target_pairs={{0,1},{1,0},{2,3},{3,2},{4,5},{5,4},{6,7},{7,6},{8,9},{9,8},{10,11... | collective-permute-start | bytes 983048 | tf_op jit(solution)/shard_map/ppermute | solution.py:323
  41.0 1.5 %collective-permute-start.20 = (bf16[32,3072]{1,0:T(8,128)(2,1)S(1)}, bf16[32,3072]{1,0:T(8,128)(2,1)S(1)}, u32[]{:S(2)}, u32[]{:S(2)}) collective-permute-start(bf16[32,3072]{1,0:T(8,128)(2,1)S(1)} %get-tuple-element.42), channel_id=1, source_target_pairs={{0,1},{1,0},{2,3},{3,2},{4,5},{5,4},{6,7},{7,6},{8,9},{9,8},{10,11... | collective-permute-start | bytes 589832 | tf_op jit(solution)/shard_map/ppermute | solution.py:323
  41.4 2.8 %collective-permute-start.17 = (bf16[32,4096]{1,0:T(8,128)(2,1)S(1)}, bf16[32,4096]{1,0:T(8,128)(2,1)S(1)}, u32[]{:S(2)}, u32[]{:S(2)}) collective-permute-start(bf16[32,4096]{1,0:T(8,128)(2,1)S(1)} %get-tuple-element.37), channel_id=1, source_target_pairs={{0,1},{1,0},{2,3},{3,2},{4,5},{5,4},{6,7},{7,6},{8,9},{9,8},{10,11... | collective-permute-start | bytes 786440 | tf_op jit(solution)/shard_map/ppermute | solution.py:323
  42.5 5.1 %collective-permute-start.21 = (bf16[16,3072]{1,0:T(8,128)(2,1)S(1)}, bf16[16,3072]{1,0:T(8,128)(2,1)S(1)}, u32[]{:S(2)}, u32[]{:S(2)}) collective-permute-start(bf16[16,3072]{1,0:T(8,128)(2,1)S(1)} %slice.55), channel_id=1, source_target_pairs={{0,4},{1,5},{2,6},{3,7},{4,0},{5,1},{6,2},{7,3},{8,12},{9,13},{10,... | collective-permute-start | bytes 294920 | tf_op jit(solution)/shard_map/ppermute | solution.py:323
  44.3 5.5 %collective-permute-start.18 = (bf16[16,4096]{1,0:T(8,128)(2,1)S(1)}, bf16[16,4096]{1,0:T(8,128)(2,1)S(1)}, u32[]{:S(2)}, u32[]{:S(2)}) collective-permute-start(bf16[16,4096]{1,0:T(8,128)(2,1)S(1)} %slice.51), channel_id=1, source_target_pairs={{0,2},{1,3},{2,0},{3,1},{4,6},{5,7},{6,4},{7,5},{8,10},{9,11},{10,... | collective-permute-start | bytes 393224 | tf_op jit(solution)/shard_map/ppermute | solution.py:323
  47.7 4.2 %collective-permute-start.22 = (bf16[8,3072]{1,0:T(8,128)(2,1)S(1)}, bf16[8,3072]{1,0:T(8,128)(2,1)S(1)}, u32[]{:S(2)}, u32[]{:S(2)}) collective-permute-start(bf16[8,3072]{1,0:T(8,128)(2,1)S(1)} %slice.57), channel_id=1, source_target_pairs={{0,2},{1,3},{2,0},{3,1},{4,6},{5,7},{6,4},{7,5},{8,10},{9,11},{10,... | collective-permute-start | bytes 147464 | tf_op jit(solution)/shard_map/ppermute | solution.py:323
  49.9 4.3 %collective-permute-start.19 = (bf16[8,4096]{1,0:T(8,128)(2,1)S(1)}, bf16[8,4096]{1,0:T(8,128)(2,1)S(1)}, u32[]{:S(2)}, u32[]{:S(2)}) collective-permute-start(bf16[8,4096]{1,0:T(8,128)(2,1)S(1)} %slice.53), channel_id=1, source_target_pairs={{0,4},{1,5},{2,6},{3,7},{4,0},{5,1},{6,2},{7,3},{8,12},{9,13},{10,... | collective-permute-start | bytes 196616 | tf_op jit(solution)/shard_map/ppermute | solution.py:323
  54.3 5.7 %collective-permute-start.23 = (bf16[4,7168]{1,0:T(4,128)(2,1)S(1)}, bf16[4,7168]{1,0:T(4,128)(2,1)S(1)}, u32[]{:S(2)}, u32[]{:S(2)}) collective-permute-start(bf16[4,7168]{1,0:T(4,128)(2,1)S(1)} %pad_maximum_fusion), channel_id=1, source_target_pairs={{0,8},{1,9},{2,10},{3,11},{4,12},{5,13},{6,14},{7,15},{8,0},{9,1},... | collective-permute-start | bytes 172040 | tf_op jit(solution)/shard_map/ppermute | solution.py:323

commit v5 on v4

--- a/solution.py
+++ b/solution.py
@@ -12,7 +12,8 @@
 OUT_TILE = 1024
 LANES = 128
 LATE = 4
-TILES = (4, 1, 2)
+TILES = (3, 4)
+FIRST = 3
 EMPTY = -1e30
 
 
@@ -43,15 +44,17 @@
 
 
 def prepare_kernel(
-    heads, me_ref, query_hbm, absorb_hbm, length_hbm, table_hbm, slot_hbm, out_ref, plan_ref,
-    query_ref, absorb_ref, length_ref, table_ref, slot_ref, ordered, sems,
+    heads, chips, me_ref, query_hbm, absorb_hbm, length_hbm, table_hbm, slot_hbm, owner_hbm, weight_hbm,
+    out_ref, plan_ref, order_ref, weight_ref,
+    query_ref, absorb_ref, length_ref, table_ref, slot_ref, owner_ref, ordered, sems, weight_sems,
 ):
-    sources = (length_hbm, table_hbm, slot_hbm, query_hbm, absorb_hbm)
-    targets = (length_ref, table_ref, slot_ref, query_ref, absorb_ref)
+    sources = (length_hbm, table_hbm, slot_hbm, owner_hbm, query_hbm, absorb_hbm)
+    targets = (length_ref, table_ref, slot_ref, owner_ref, query_ref, absorb_ref)
     copies = [
         pltpu.make_async_copy(a, b, sems.at[i]) for i, (a, b) in enumerate(zip(sources, targets))
     ]
-    for copy in copies:
+    weight_copies = weight_copy(weight_hbm, 0, weight_ref, weight_sems)
+    for copy in copies + weight_copies:
         copy.start()
     requests = table_ref.shape[0]
     entries = plan_ref.shape[0]
@@ -61,12 +64,13 @@
         return 0
 
     lax.fori_loop(0, entries, clear, 0)
-    for copy in copies[:3]:
+    for copy in copies[:4]:
         copy.wait()
     me = me_ref[0]
 
     def list_request(r, _):
         length = length_ref[r]
+        order_ref[r] = slot_of(owner_ref[r] ^ me, chips)
 
         def list_block(j, _):
             slot = slot_ref[me, table_ref[r, j]]
@@ -84,7 +88,7 @@
     head_width = query_ref.shape[1] // heads
     rope = head_width - nope
     kv_rank = absorb_ref.shape[2]
-    for copy in copies[3:]:
+    for copy in copies[4:]:
         copy.wait()
     for h in range(heads):
         own = query_ref[:, h * head_width : (h + 1) * head_width]
@@ -99,18 +103,12 @@
     for c in range(kv_rank // LANES):
         out_ref[:, c * LANES : (c + 1) * LANES] = ordered[c].astype(jnp.bfloat16)
     out_ref[:, kv_rank:] = ordered[kv_rank // LANES, :, :rope].astype(jnp.bfloat16)
-
-
-def chip_bits(chips, swap):
-    bits = list(range(chips.bit_length() - 1))
-    return [bits[1], bits[0]] + bits[2:] if swap else bits
-
-
-def slot_of(apart, chips, swap):
-    order = apart & 1
-    for bit in chip_bits(chips, swap):
-        order = 2 * order + ((apart >> (bit + 1)) & 1)
-    return order
+    for copy in weight_copies:
+        copy.wait()
+
+
+def slot_of(apart, chips):
+    return (apart & 1) * chips + ((apart >> 1) & 1) * (chips // 2) + (apart >> 2)
 
 
 def weight_copy(weight_hbm, first, weight_ref, sems):
@@ -128,10 +126,15 @@
     plan_ref, mine_ref, theirs_ref, *rest,
 ):
     pieces, rest = rest[:piece_count], rest[piece_count:]
-    weight_hbm, out_ref, lse_ref, away_ref, weight_ref, scores, top, total, latent, weight_sems = rest
+    weight_copies = []
+    if first_tile:
+        weight_hbm, out_ref, lse_ref, away_ref, weight_ref, *rest, weight_sems = rest
+        weight_copies = weight_copy(weight_hbm, first_tile, weight_ref, weight_sems)
+    else:
+        out_ref, lse_ref, away_ref, *rest = rest
+    scores, top, total, latent = rest
     row_block = mine_ref.shape[1]
     half = pieces[0].shape[0]
-    weight_copies = weight_copy(weight_hbm, first_tile, weight_ref, weight_sems)
     for copy in weight_copies:
         copy.start()
 
@@ -207,32 +210,28 @@
         copy.wait()
 
 
-def project(placed, weights, keep_ref, away_ref):
+def tiles_of(*weights):
+    return [(ref, i) for ref in weights for i in range(ref.shape[0])]
+
+
+def project(placed, tiles, keep_ref, away_ref):
     half_rows = keep_ref.shape[0]
     at = 0
-    for weight_ref in weights:
+    for weight_ref, i in tiles:
         tile = weight_ref.shape[2]
-        for i in range(weight_ref.shape[0]):
-            result = jnp.dot(
-                placed, weight_ref[i], preferred_element_type=jnp.float32
-            ).astype(jnp.bfloat16)
-            keep_ref[:, at : at + tile] = result[:half_rows]
-            away_ref[:, at : at + tile] = result[half_rows:]
-            at += tile
+        result = jnp.dot(
+            placed, weight_ref[i], preferred_element_type=jnp.float32
+        ).astype(jnp.bfloat16)
+        keep_ref[:, at : at + tile] = result[:half_rows]
+        away_ref[:, at : at + tile] = result[half_rows:]
+        at += tile
 
 
 def merge_kernel(
-    stages, first_tile, heads, steps, chips,
-    me_ref, owner_hbm, value_hbm, weight_hbm, weight_ref, *rest,
+    stages, heads, steps, order_ref, value_ref, weight_ref, next_ref, *rest,
 ):
     outs, lses, others = rest[:stages], rest[stages : 2 * stages], rest[2 * stages : 3 * stages]
-    (away_ref, keep_ref, placed_ref, later_ref,
-     latent, head_rows, owner_ref, value_ref, sems, weight_sems) = rest[3 * stages :]
-    owner_copy = pltpu.make_async_copy(owner_hbm, owner_ref, sems.at[0])
-    value_copy = pltpu.make_async_copy(value_hbm, value_ref, sems.at[1])
-    weight_copies = weight_copy(weight_hbm, first_tile, later_ref, weight_sems)
-    for copy in (owner_copy, value_copy, *weight_copies):
-        copy.start()
+    away_ref, keep_ref, placed_ref, latent, head_rows = rest[3 * stages :]
     kv_rank, v_width = value_ref.shape[1:]
     rows = head_rows.shape[0]
     requests = rows // steps
@@ -255,24 +254,18 @@
     lax.fori_loop(0, rows * heads // chunk, merge, 0, unroll=True)
 
     half_rows = away_ref.shape[0]
-    me = me_ref[0]
     target = lax.broadcasted_iota(jnp.int32, (2 * half_rows, rows), 0)
     origin = lax.broadcasted_iota(jnp.int32, (2 * half_rows, rows), 1)
-    owner_copy.wait()
 
     def place(r, picked):
-        apart = owner_ref[r] ^ me
         shifted = origin - r * steps
-        row_here = (shifted >= 0) & (shifted < steps)
-        return tuple(
-            jnp.where((target - slot_of(apart, chips, swap) * steps == shifted) & row_here, 1.0, old)
-            for swap, old in enumerate(picked)
-        )
-
-    empty = jnp.zeros((2 * half_rows, rows), jnp.float32)
-    pickers = lax.fori_loop(0, requests, place, (empty, empty), unroll=math.gcd(requests, 8))
-
-    value_copy.wait()
+        hit = (target - order_ref[r] * steps == shifted) & (shifted >= 0) & (shifted < steps)
+        return jnp.where(hit, 1.0, picked)
+
+    picker = lax.fori_loop(
+        0, requests, place, jnp.zeros((2 * half_rows, rows), jnp.float32), unroll=math.gcd(requests, 8)
+    )
+
     for h in range(heads):
         mine = jnp.concatenate(
             [latent[c, pl.ds(h, rows, stride=heads)] for c in range(kv_rank // LANES)], axis=1
@@ -281,20 +274,16 @@
             mine, value_ref[h], preferred_element_type=jnp.float32
         ).astype(jnp.bfloat16)
 
-    placed = [
-        jnp.dot(
-            picker.astype(jnp.bfloat16), head_rows[...], preferred_element_type=jnp.float32
-        ).astype(jnp.bfloat16)
-        for picker in pickers
-    ]
-    placed_ref[...] = placed[1]
-    project(placed[0], [weight_ref], keep_ref, away_ref)
-    for copy in weight_copies:
-        copy.wait()
-
-
-def second_kernel(placed_ref, weight_ref, later_ref, away_ref, keep_ref):
-    project(placed_ref[...], [weight_ref, later_ref], keep_ref, away_ref)
+    placed = jnp.dot(
+        picker.astype(jnp.bfloat16), head_rows[...], preferred_element_type=jnp.float32
+    ).astype(jnp.bfloat16)
+    placed_ref[...] = placed
+    project(placed, tiles_of(weight_ref, next_ref)[:FIRST], keep_ref, away_ref)
+
+
+def second_kernel(placed_ref, weight_ref, next_ref, away_ref, keep_ref):
+    tiles = tiles_of(weight_ref, next_ref)
+    project(placed_ref[...], tiles[FIRST:], keep_ref, away_ref)
 
 
 def local(q_heads, w_absorb, w_value, w_out, latent_cache, ctx_blocks, block_table, owner):
@@ -319,6 +308,16 @@
     def pin(x):
         return pltpu.with_memory_space_constraint(x, pltpu.HBM)
 
+    def add(x, *others):
+        total = x.astype(jnp.float32)
+        for other in others:
+            total = total + other.astype(jnp.float32)
+        return total.astype(jnp.bfloat16)
+
+    def fold(x, distance):
+        middle = x.shape[0] // 2
+        return add(x[:middle], exchange(x[middle:], distance))
+
     def exchange(x, distance):
         return lax.ppermute(x, "head", [(i, i ^ distance) for i in range(devices)])
 
@@ -329,56 +328,58 @@
 
     def prepare():
         slots = jnp.asarray(slots_by_device(chips, half))
-        queries, plan = pl.pallas_call(
-            functools.partial(prepare_kernel, heads),
+        queries, plan, order, weight = pl.pallas_call(
+            functools.partial(prepare_kernel, heads, chips),
             out_shape=(
                 jax.ShapeDtypeStruct((flat_rows, row_width), jnp.bfloat16),
                 jax.ShapeDtypeStruct((2 * piece_total * half + 2,), jnp.int32),
+                jax.ShapeDtypeStruct((requests,), jnp.int32),
+                tile_shapes[0],
             ),
-            in_specs=[smem] + [hbm] * 5,
-            out_specs=(vmem, smem),
+            in_specs=[smem] + [hbm] * 7,
+            out_specs=(vmem, smem, smem, vmem),
             scratch_shapes=[
                 pltpu.VMEM(q_heads.shape, jnp.bfloat16),
                 pltpu.VMEM(w_absorb.shape, jnp.bfloat16),
                 pltpu.SMEM(ctx_blocks.shape, jnp.int32),
                 pltpu.SMEM(block_table.shape, jnp.int32),
                 pltpu.SMEM(slots.shape, jnp.int32),
+                pltpu.SMEM(owner.shape, jnp.int32),
                 pltpu.VMEM((kv_rank // LANES + 1, flat_rows, LANES), jnp.float32),
-                pltpu.SemaphoreType.DMA((5,)),
+                pltpu.SemaphoreType.DMA((6,)),
+                pltpu.SemaphoreType.DMA((TILES[0],)),
             ],
             compiler_params=pltpu.CompilerParams(vmem_limit_bytes=12 * mebi),
             cost_estimate=pl.CostEstimate(
                 flops=2 * w_absorb.size * row_count, bytes_accessed=4 * w_absorb.size, transcendentals=0
             ),
             name="prepare",
-        )(me, *map(pin, (q_heads, w_absorb, ctx_blocks, block_table, slots)))
-        return queries.reshape(requests, row_block, row_width), plan
+        )(me, *map(pin, (q_heads, w_absorb, ctx_blocks, block_table, slots, owner, w_out)))
+        return queries.reshape(requests, row_block, row_width), plan, order, weight
 
     def attend(plan, mine, theirs, pieces, stage):
         slots = len(pieces) * half
         first_slot = 0 if stage == 0 else piece_total * half - slots
-        tiles = tile_shapes[stage]
+        with_weight = stage == 0
         both = 2 * row_block
         return pl.pallas_call(
             functools.partial(
-                attend_kernel, len(pieces), first_slot, sum(TILES[:stage]), heads, steps, kv_rank,
+                attend_kernel, len(pieces), first_slot, TILES[0] * with_weight, heads, steps, kv_rank,
                 float(head_width) ** -0.5,
             ),
             out_shape=(
                 jax.ShapeDtypeStruct((flat_rows, kv_rank), jnp.float32),
                 jax.ShapeDtypeStruct((flat_rows, LANES), jnp.float32),
                 jax.ShapeDtypeStruct((flat_rows, kv_rank + LANES), jnp.bfloat16),
-                tiles,
-            ),
-            in_specs=[smem] + [vmem] * (2 + len(pieces)) + [hbm],
-            out_specs=(vmem,) * 4,
+            ) + (tile_shapes[1],) * with_weight,
+            in_specs=[smem] + [vmem] * (2 + len(pieces)) + [hbm] * with_weight,
+            out_specs=(vmem,) * (3 + with_weight),
             scratch_shapes=[
                 pltpu.VMEM((slots, 2 * both, block_rows), jnp.float32),
                 pltpu.VMEM((requests + 1, both, block_rows), jnp.float32),
                 pltpu.VMEM((requests + 1, both, block_rows), jnp.float32),
                 pltpu.VMEM((requests + 1, both, kv_rank), jnp.float32),
-                pltpu.SemaphoreType.DMA((tiles.shape[0],)),
-            ],
+            ] + [pltpu.SemaphoreType.DMA((TILES[1],))] * with_weight,
             compiler_params=pltpu.CompilerParams(vmem_limit_bytes=28 * mebi),
             cost_estimate=pl.CostEstimate(
                 flops=2 * slots * 2 * both * block_rows * 2 * row_width,
@@ -386,7 +387,7 @@
                 transcendentals=0,
             ),
             name="attend",
-        )(plan, mine, theirs, *pieces, pin(w_out))
+        )(plan, mine, theirs, *pieces, *([pin(w_out)] * with_weight))
 
     ring = ring_of(chips)
     up = [
@@ -402,7 +403,7 @@
     for hop in range(1, chips // 2 + 1):
         last = hop == chips // 2
         if hop == 2:
-            mine, plan = prepare()
+            mine, plan, order, weight = prepare()
             theirs = exchange(mine, 1)
             ups[0], mine, plan = lax.optimization_barrier((ups[0], mine, plan))
         if last:
@@ -416,33 +417,28 @@
             ups[1] = lax.ppermute(ups[1], "head", up)
             pieces += [ups[0], downs[1], downs[0], ups[1]]
     early, late = pieces[:-LATE], pieces[-LATE:]
-    *early_part, weight = attend(plan, mine, theirs, early, 0)
-    *late_part, next_weight = attend(plan, mine, theirs, late, 1)
+    *early_part, next_weight = attend(plan, mine, theirs, early, 0)
+    late_part = attend(plan, mine, theirs, late, 1)
     partial = [(out, lse, exchange(away, 1)) for out, lse, away in (early_part, late_part)]
 
     part_rows = chips * steps
-    widths = (TILES[0] * OUT_TILE, (TILES[1] + TILES[2]) * OUT_TILE)
+    widths = (FIRST * OUT_TILE, (sum(TILES) - FIRST) * OUT_TILE)
     parts = [jax.ShapeDtypeStruct((part_rows, n), jnp.bfloat16) for n in widths]
     placed_shape = jax.ShapeDtypeStruct((2 * part_rows, heads * v_width), jnp.bfloat16)
     outs, lses, others = zip(*partial)
-    away, keep, placed, last_weight = pl.pallas_call(
-        functools.partial(
-            merge_kernel, len(partial), TILES[0] + TILES[1], heads, steps, chips
-        ),
-        out_shape=(parts[0], parts[0], placed_shape, tile_shapes[2]),
-        in_specs=[smem, hbm, hbm, hbm] + [vmem] * (1 + 3 * len(partial)),
-        out_specs=(vmem,) * 4,
+    away, keep, placed = pl.pallas_call(
+        functools.partial(merge_kernel, len(partial), heads, steps),
+        out_shape=(parts[0], parts[0], placed_shape),
+        in_specs=[smem] + [vmem] * (3 + 3 * len(partial)),
+        out_specs=(vmem,) * 3,
         scratch_shapes=[
             pltpu.VMEM((kv_rank // LANES, flat_rows, LANES), jnp.float32),
             pltpu.VMEM((row_count, heads * v_width), jnp.bfloat16),
-            pltpu.SMEM(owner.shape, jnp.int32),
-            pltpu.VMEM(w_value.shape, jnp.bfloat16),
-            pltpu.SemaphoreType.DMA((2,)),
-            pltpu.SemaphoreType.DMA((TILES[2],)),
         ],
         compiler_params=pltpu.CompilerParams(vmem_limit_bytes=28 * mebi),
         name="merge_and_project",
-    )(me, pin(owner), pin(w_value), pin(w_out), weight, *outs, *lses, *others)
+    )(order, w_value, weight, next_weight, *outs, *lses, *others)
+    first_half = add(keep, exchange(away, 1))
     next_away, next_keep = pl.pallas_call(
         second_kernel,
         out_shape=(parts[1], parts[1]),
@@ -453,22 +449,19 @@
             flops=2 * w_out.size * part_rows, bytes_accessed=8 * w_out.size, transcendentals=0
         ),
         name="project_second",
-    )(placed, next_weight, last_weight)
-
-    def add(x, y):
-        return (x.astype(jnp.float32) + y.astype(jnp.float32)).astype(jnp.bfloat16)
-
-    def fold(x, bit):
-        middle = x.shape[0] // 2
-        return add(x[:middle], exchange(x[middle:], 2 << bit))
-
-    halves = [add(keep, exchange(away, 1)), add(next_keep, exchange(next_away, 1))]
-    for step in range(2):
-        halves = [fold(x, chip_bits(chips, swap)[step]) for swap, x in enumerate(halves)]
-    result = jnp.concatenate(halves, axis=1)
-    for bit in chip_bits(chips, False)[2:]:
-        result = fold(result, bit)
-    return result
+    )(placed, weight, next_weight)
+
+    second_half = add(next_keep, exchange(next_away, 1))
+    result = jnp.concatenate([fold(first_half, 2), fold(second_half, 2)], axis=1)
+    distance = 4
+    while result.shape[0] > 4 * steps:
+        result = fold(result, distance)
+        distance *= 2
+    ways = result.shape[0] // steps
+    received = [
+        exchange(result[k * steps : (k + 1) * steps], distance * k) for k in range(1, ways)
+    ]
+    return add(result[:steps], *received)
 
 
 def solution(mesh):

time: 60.8 us -> 57.4 us (0.944)
  waiting for transfers between devices: 18.9 us -> 16.7 us
  starting transfers between devices: 24.5 us -> 23.4 us
    ppermute x3, waiting for transfers between devices: 0.01 us -> 3.55 us  [local(): downs[0] = lax.ppermute(downs[0], 'head', down)]
    ppermute x3, starting transfers between devices: 5.68 us -> 2.59 us  [local(): ups[1] = lax.ppermute(ups[1], 'head', up)]
    ppermute x4, waiting for transfers between devices: 4.5 us -> 1.59 us  [local(): downs[1] = lax.ppermute(downs[1], 'head', down)]
    ppermute x10, waiting for transfers between devices: 12.9 us -> 10.8 us  [exchange(): return lax.ppermute(x, 'head', [(i, i ^ distance) for i in range(devices)])]
    ppermute x3, starting transfers between devices: 1.54 us -> 3.51 us  [local(): downs[0] = lax.ppermute(downs[0], 'head', down)]
    pallas_call x2, Pallas kernels: 8.73 us -> 7.31 us  [attend(): pl.pallas_call(functools.partial(attend_kernel, len(pieces), first_slot,...]
    ppermute x3, waiting for transfers between devices: 1.08 us -> 0.01 us  [local(): ups[1] = lax.ppermute(ups[1], 'head', up)]
    pallas_call x2, Pallas kernels: 5.28 us -> 6.11 us  [the longest x1 3.9 us: prepare(): pl.pallas_call(functools.partial(prepare_kernel, heads, chips), out_shape...]
  transfers between devices with their start and end apart: 24 -> 24, of which waited for: 12 -> 10; matrix products, arithmetic and copies ran while one was open for 0% -> 0% of each run, Pallas kernels for 18% -> 22%
where the time goes in v5:
time: 57.4 us; the launch traced here: 57.2 us
  starting transfers between devices  23.4 us (41%)
  waiting for transfers between devices  16.7 us (29%)
  Pallas kernels  15 us (26%)
  local copies, waits for them, and re-layouts  1.03 us (2%)
  other arithmetic  0.93 us (2%)
    ppermute x10, waiting for transfers between devices, exchange(): return lax.ppermute(x, 'head', [(i, i ^ distance) for i in range(devices)])  10.8 us
    ppermute x4, starting transfers between devices, local(): ups[0] = lax.ppermute(ups[0], 'head', up)  8.69 us
    ppermute x10, starting transfers between devices, exchange(): return lax.ppermute(x, 'head', [(i, i ^ distance) for i in range(devices)])  8.16 us
    pallas_call x2, Pallas kernels, attend(): pl.pallas_call(functools.partial(attend_kernel, len(pieces), first_slot,...  7.31 us
    pallas_call x1, Pallas kernels, prepare(): pl.pallas_call(functools.partial(prepare_kernel, heads, chips), out_shape...  3.9 us
    ppermute x3, waiting for transfers between devices, local(): downs[0] = lax.ppermute(downs[0], 'head', down)  3.55 us
    ppermute x3, starting transfers between devices, local(): downs[0] = lax.ppermute(downs[0], 'head', down)  3.51 us
    ppermute x3, starting transfers between devices, local(): ups[1] = lax.ppermute(ups[1], 'head', up)  2.59 us
  transfers between devices with their start and end apart: 24, of which 10 were waited for; matrix products, arithmetic and copies ran while one was open for 0% of the time, Pallas kernels for 22%

profile of v5, /device:TPU:0, one launch (start us, length us, event | category | flops | bytes accessed | tf_op | source)
XLA Modules:
  0.0 57.2 jit_solution(5497474908088501755)
XLA Ops:
  0.0 1.0 %fusion.3 = (bf16[1,576,128]{2,1,0:T(8,128)(2,1)S(1)}, bf16[1,576,128]{2,1,0:T(8,128)(2,1)S(1)}) fusion(bf16[2,576,128]{2,1,0:T(8,128)(2,1)} %bitcast.6), kind=kLoop, calls=%fused_computation.15 | loop fusion | bytes 589824 | tf_op jit(solution)/shard_map/slice | solution.py:400
  1.0 3.1 %collective-permute-start = (bf16[1,576,128]{2,1,0:T(8,128)(2,1)S(1)}, bf16[1,576,128]{2,1,0:T(8,128)(2,1)S(1)}, u32[]{:S(2)}, u32[]{:S(2)}) collective-permute-start(bf16[1,576,128]{2,1,0:T(8,128)(2,1)S(1)} %get-tuple-element.44.rest_0_), channel_id=1, source_target_pairs={{0,4},{1,5},{4,8},{5,9},{8,12},{9,13},{12,14},{13,15},{14,10},{15,... | collective-permute-start | bytes 442376 | tf_op jit(solution)/shard_map/ppermute | solution.py:414
  4.1 0.0 collective-permute-start.2
  4.1 2.0 %collective-permute-start.3 = (bf16[1,576,128]{2,1,0:T(8,128)(2,1)S(1)}, bf16[1,576,128]{2,1,0:T(8,128)(2,1)S(1)}, u32[]{:S(2)}, u32[]{:S(2)}) collective-permute-start(bf16[1,576,128]{2,1,0:T(8,128)(2,1)S(1)} %get-tuple-element.44.rest_0_), channel_id=1, source_target_pairs={{4,0},{5,1},{8,4},{9,5},{12,8},{13,9},{14,12},{15,13},{10,14},{11,... | collective-permute-start | bytes 442376 | tf_op jit(solution)/shard_map/ppermute | solution.py:416
  6.1 0.1 collective-permute-start.4
  6.1 3.9 %prepare.1 = (bf16[256,576]{1,0:T(8,128)(2,1)S(1)}, s32[34]{0:T(128)S(1)}, s32[8]{0:T(128)S(1)}, bf16[3,1024,1024]{2,1,0:T(8,128)(2,1)S(1)}) custom-call(s32[1]{0:T(128)} %bitcast.me_ref, bf16[32,1536]{1,0:T(8,128)(2,1)} %query_hbm.1, bf16[8,128,512]{2,1,0:T(8,128)(2,1)} %absorb_hbm.1, s32[8]{0:T(128)} %length_hbm.1, s32[8,8]{1,0:T(8,128)} %table_hbm.1, ...), custom_call_target="tpu_custom_call" | custom-call | flops 33554432 | bytes 2097152 | tf_op jit(solution)/shard_map/prepare/pallas_call | solution.py:331
  10.0 0.0 collective-permute-done.rest_2_
  10.1 0.0 copy-start
  10.1 2.0 %collective-permute-start.5 = (bf16[1,576,128]{2,1,0:T(8,128)(2,1)S(1)}, bf16[1,576,128]{2,1,0:T(8,128)(2,1)S(1)}, u32[]{:S(2)}, u32[]{:S(2)}) collective-permute-start(bf16[1,576,128]{2,1,0:T(8,128)(2,1)S(1)} %collective-permute-done.rest_2_), channel_id=1, source_target_pairs={{0,4},{1,5},{4,8},{5,9},{8,12},{9,13},{12,14},{13,15},{14,10},{15,... | collective-permute-start | bytes 442376 | tf_op jit(solution)/shard_map/ppermute | solution.py:414
  12.1 0.0 collective-permute-done.2.rest_3_
  12.1 0.0 collective-permute-start.6
  12.2 0.4 collective-permute-done.3.rest_4_
  12.5 1.5 %collective-permute-start.7 = (bf16[1,576,128]{2,1,0:T(8,128)(2,1)S(1)}, bf16[1,576,128]{2,1,0:T(8,128)(2,1)S(1)}, u32[]{:S(2)}, u32[]{:S(2)}) collective-permute-start(bf16[1,576,128]{2,1,0:T(8,128)(2,1)S(1)} %collective-permute-done.3.rest_4_), channel_id=1, source_target_pairs={{4,0},{5,1},{8,4},{9,5},{12,8},{13,9},{14,12},{15,13},{10,14},{11,... | collective-permute-start | bytes 442376 | tf_op jit(solution)/shard_map/ppermute | solution.py:416
  14.1 0.5 collective-permute-start.8
  14.6 0.7 %collective-permute-done.5.rest_6_ = bf16[1,576,128]{2,1,0:T(8,128)(2,1)S(1)} collective-permute-done((bf16[1,576,128]{2,1,0:T(8,128)(2,1)S(1)}, bf16[1,576,128]{2,1,0:T(8,128)(2,1)S(1)}, u32[]{:S(2)}, u32[]{:S(2)}) %collective-permute-start.5) | collective-permute-done | bytes 147488 | tf_op jit(solution)/shard_map/ppermute | solution.py:414
  15.3 2.0 %collective-permute-start.9 = (bf16[1,576,128]{2,1,0:T(8,128)(2,1)S(1)}, bf16[1,576,128]{2,1,0:T(8,128)(2,1)S(1)}, u32[]{:S(2)}, u32[]{:S(2)}) collective-permute-start(bf16[1,576,128]{2,1,0:T(8,128)(2,1)S(1)} %collective-permute-done.5.rest_6_), channel_id=1, source_target_pairs={{0,4},{1,5},{4,8},{5,9},{8,12},{9,13},{12,14},{13,15},{14,10},{15,... | collective-permute-start | bytes 442376 | tf_op jit(solution)/shard_map/ppermute | solution.py:414
  17.3 1.6 %collective-permute-done.6.rest_7_ = bf16[1,576,128]{2,1,0:T(8,128)(2,1)S(1)} collective-permute-done((bf16[1,576,128]{2,1,0:T(8,128)(2,1)S(1)}, bf16[1,576,128]{2,1,0:T(8,128)(2,1)S(1)}, u32[]{:S(2)}, u32[]{:S(2)}) %collective-permute-start.6) | collective-permute-done | bytes 147488 | tf_op jit(solution)/shard_map/ppermute | solution.py:415
  18.8 3.2 %collective-permute-done.7.rest_8_ = bf16[1,576,128]{2,1,0:T(8,128)(2,1)S(1)} collective-permute-done((bf16[1,576,128]{2,1,0:T(8,128)(2,1)S(1)}, bf16[1,576,128]{2,1,0:T(8,128)(2,1)S(1)}, u32[]{:S(2)}, u32[]{:S(2)}) %collective-permute-start.7) | collective-permute-done | bytes 147488 | tf_op jit(solution)/shard_map/ppermute | solution.py:416
  22.0 0.0 collective-permute-start.11
  22.0 0.0 collective-permute-done.8.rest_9_
  22.0 2.0 %collective-permute-start.12 = (bf16[1,576,128]{2,1,0:T(8,128)(2,1)S(1)}, bf16[1,576,128]{2,1,0:T(8,128)(2,1)S(1)}, u32[]{:S(2)}, u32[]{:S(2)}) collective-permute-start(bf16[1,576,128]{2,1,0:T(8,128)(2,1)S(1)} %collective-permute-done.8.rest_9_), channel_id=1, source_target_pairs={{0,4},{1,5},{4,8},{5,9},{8,12},{9,13},{12,14},{13,15},{14,10},{15,... | collective-permute-start | bytes 442376 | tf_op jit(solution)/shard_map/ppermute | solution.py:417
  24.0 1.6 %collective-permute-start.13 = (bf16[1,576,128]{2,1,0:T(8,128)(2,1)S(1)}, bf16[1,576,128]{2,1,0:T(8,128)(2,1)S(1)}, u32[]{:S(2)}, u32[]{:S(2)}) collective-permute-start(bf16[1,576,128]{2,1,0:T(8,128)(2,1)S(1)} %collective-permute-done.9.rest_10_), channel_id=1, source_target_pairs={{0,4},{1,5},{4,8},{5,9},{8,12},{9,13},{12,14},{13,15},{14,10},{15,... | collective-permute-start | bytes 442376 | tf_op jit(solution)/shard_map/ppermute | solution.py:410
  25.6 0.0 collective-permute-done.10.rest_11_
  25.6 0.4 collective-permute-start.14
  26.1 0.0 collective-permute-done.1.theirs_ref
  26.1 5.7 %attend.2 = (f32[256,512]{1,0:T(8,128)S(1)}, f32[256,128]{1,0:T(8,128)S(1)}, bf16[256,640]{1,0:T(8,128)(2,1)S(1)}, bf16[4,1024,1024]{2,1,0:T(8,128)(2,1)S(1)}) custom-call(s32[34]{0:T(128)S(1)} %get-tuple-element.28.plan_ref, bf16[8,32,576]{2,1,0:T(8,128)(2,1)S(1)} %bitcast.4, bf16[8,32,576]{2,1,0:T(8,128)(2,1)S(1)} %collective-permute-done.1.theirs_ref, ...), custom_call_target="tpu_custom_call" | custom-call | flops 452984832 | bytes 1769472 | tf_op jit(solution)/shard_map/attend/pallas_call | solution.py:365
  31.8 0.1 collective-permute-start.15
  31.9 0.0 collective-permute-done.13.rest_2_
  31.9 1.6 %attend.3 = (f32[256,512]{1,0:T(8,128)S(1)}, f32[256,128]{1,0:T(8,128)S(1)}, bf16[256,640]{1,0:T(8,128)(2,1)S(1)}) custom-call(s32[34]{0:T(128)S(1)} %get-tuple-element.28.plan_ref, bf16[8,32,576]{2,1,0:T(8,128)(2,1)S(1)} %bitcast.5, bf16[8,32,576]{2,1,0:T(8,128)(2,1)S(1)} %collective-permute-done.1.theirs_ref, ...), custom_call_target="tpu_custom_call" | custom-call | flops 150994944 | bytes 589824 | tf_op jit(solution)/shard_map/attend/pallas_call | solution.py:365
  33.5 0.5 collective-permute-start.16
  34.1 1.3 %collective-permute-done.16.rest_5_ = bf16[256,640]{1,0:T(8,128)(2,1)S(1)} collective-permute-done((bf16[256,640]{1,0:T(8,128)(2,1)S(1)}, bf16[256,640]{1,0:T(8,128)(2,1)S(1)}, u32[]{:S(2)}, u32[]{:S(2)}) %collective-permute-start.16) | collective-permute-done | bytes 327712 | tf_op jit(solution)/shard_map/ppermute | solution.py:322
  35.3 2.2 %merge_and_project.1 = (bf16[32,3072]{1,0:T(8,128)(2,1)S(1)}, bf16[32,3072]{1,0:T(8,128)(2,1)S(1)}, bf16[64,1024]{1,0:T(8,128)(2,1)S(1)}) custom-call(s32[8]{0:T(128)S(1)} %get-tuple-element.24.order_ref, bf16[8,512,128]{2,1,0:T(8,128)(2,1)S(1)} %copy-done, bf16[3,1024,1024]{2,1,0:T(8,128)(2,1)S(1)} %get-tuple-element.25.weight_ref, ...), custom_call_target="tpu_custom_call" | custom-call | tf_op jit(solution)/shard_map/merge_and_project/pallas_call | solution.py:429
  37.5 0.4 collective-permute-start.17
  38.0 1.6 %project_second.1 = (bf16[32,4096]{1,0:T(8,128)(2,1)S(1)}, bf16[32,4096]{1,0:T(8,128)(2,1)S(1)}) custom-call(bf16[64,1024]{1,0:T(8,128)(2,1)S(1)} %get-tuple-element.40.placed_ref, bf16[3,1024,1024]{2,1,0:T(8,128)(2,1)S(1)} %get-tuple-element.25.weight_ref, bf16[4,1024,1024]{2,1,0:T(8,128)(2,1)S(1)} %get-tuple-element.31.next_ref), custom_call_target="tpu_custom_call" | custom-call | flops 469762048 | bytes 58720256 | tf_op jit(solution)/shard_map/project_second/pallas_call | solution.py:442
  39.5 0.2 collective-permute-start.19
  39.7 0.1 add_convert_fusion.1
  39.8 1.2 %collective-permute-start.18 = (bf16[16,3072]{1,0:T(8,128)(2,1)S(1)}, bf16[16,3072]{1,0:T(8,128)(2,1)S(1)}, u32[]{:S(2)}, u32[]{:S(2)}) collective-permute-start(bf16[16,3072]{1,0:T(8,128)(2,1)S(1)} %slice.43), channel_id=1, source_target_pairs={{0,2},{1,3},{2,0},{3,1},{4,6},{5,7},{6,4},{7,5},{8,10},{9,11},{10,... | collective-permute-start | bytes 294920 | tf_op jit(solution)/shard_map/ppermute | solution.py:322
  41.0 0.1 collective-permute-done.19
  41.1 0.1 add_convert_fusion
  41.2 1.2 %collective-permute-start.20 = (bf16[16,4096]{1,0:T(8,128)(2,1)S(1)}, bf16[16,4096]{1,0:T(8,128)(2,1)S(1)}, u32[]{:S(2)}, u32[]{:S(2)}) collective-permute-start(bf16[16,4096]{1,0:T(8,128)(2,1)S(1)} %slice.45), channel_id=1, source_target_pairs={{0,2},{1,3},{2,0},{3,1},{4,6},{5,7},{6,4},{7,5},{8,10},{9,11},{10,... | collective-permute-start | bytes 393224 | tf_op jit(solution)/shard_map/ppermute | solution.py:322
  42.4 3.1 %collective-permute-done.18 = bf16[16,3072]{1,0:T(8,128)(2,1)S(1)} collective-permute-done((bf16[16,3072]{1,0:T(8,128)(2,1)S(1)}, bf16[16,3072]{1,0:T(8,128)(2,1)S(1)}, u32[]{:S(2)}, u32[]{:S(2)}) %collective-permute-start.18) | collective-permute-done | bytes 98336 | tf_op jit(solution)/shard_map/ppermute | solution.py:322
  45.5 2.2 %collective-permute-done.20 = bf16[16,4096]{1,0:T(8,128)(2,1)S(1)} collective-permute-done((bf16[16,4096]{1,0:T(8,128)(2,1)S(1)}, bf16[16,4096]{1,0:T(8,128)(2,1)S(1)}, u32[]{:S(2)}, u32[]{:S(2)}) %collective-permute-start.20) | collective-permute-done | bytes 131104 | tf_op jit(solution)/shard_map/ppermute | solution.py:322
  47.8 0.1 fusion.2
  47.9 3.5 %collective-permute-start.23 = (bf16[4,7168]{1,0:T(4,128)(2,1)S(1)}, bf16[4,7168]{1,0:T(4,128)(2,1)S(1)}, u32[]{:S(2)}, u32[]{:S(2)}) collective-permute-start(bf16[4,7168]{1,0:T(4,128)(2,1)S(1)} %get-tuple-element.46), channel_id=1, source_target_pairs={{0,12},{1,13},{2,14},{3,15},{4,8},{5,9},{6,10},{7,11},{8,4},{9,5},... | collective-permute-start | bytes 172040 | tf_op jit(solution)/shard_map/ppermute | solution.py:322
  51.4 0.9 %collective-permute-start.21 = (bf16[4,7168]{1,0:T(4,128)(2,1)S(1)}, bf16[4,7168]{1,0:T(4,128)(2,1)S(1)}, u32[]{:S(2)}, u32[]{:S(2)}) collective-permute-start(bf16[4,7168]{1,0:T(4,128)(2,1)S(1)} %get-tuple-element.45), channel_id=1, source_target_pairs={{0,4},{1,5},{2,6},{3,7},{4,0},{5,1},{6,2},{7,3},{8,12},{9,13},{10,... | collective-permute-start | bytes 172040 | tf_op jit(solution)/shard_map/ppermute | solution.py:322
  52.3 2.2 %collective-permute-done.23 = bf16[4,7168]{1,0:T(4,128)(2,1)S(1)} collective-permute-done((bf16[4,7168]{1,0:T(4,128)(2,1)S(1)}, bf16[4,7168]{1,0:T(4,128)(2,1)S(1)}, u32[]{:S(2)}, u32[]{:S(2)}) %collective-permute-start.23) | collective-permute-done | bytes 57376 | tf_op jit(solution)/shard_map/ppermute | solution.py:322
  54.6 2.0 %collective-permute-done.22 = bf16[4,7168]{1,0:T(4,128)(2,1)S(1)} collective-permute-done((bf16[4,7168]{1,0:T(4,128)(2,1)S(1)}, bf16[4,7168]{1,0:T(4,128)(2,1)S(1)}, u32[]{:S(2)}, u32[]{:S(2)}) %collective-permute-start.22) | collective-permute-done | bytes 57376 | tf_op jit(solution)/shard_map/ppermute | solution.py:322
  56.5 0.7 %add_convert_fusion.4 = bf16[4,7168]{1,0:T(4,128)(2,1)} fusion(bf16[4,7168]{1,0:T(4,128)(2,1)S(1)} %collective-permute-done.23, bf16[4,7168]{1,0:T(4,128)(2,1)S(1)} %collective-permute-done.22, bf16[4,7168]{1,0:T(4,128)(2,1)S(1)} %collective-permute-done.21, bf16[16,4096]{1,0:T(8,128)(2,1)S(1)} %add_convert_fusion.2, bf16[16,3072]{1,0:T(8,128)(2,1)S(1)} %add_convert_fusion.3), kind=kLoop, calls=%fused_computation.10 | loop fusion | flops 315392 | bytes 458752 | tf_op jit(solution)/shard_map/convert_element_type | solution.py:315
  (16 shorter events, 0.1 us)
Async XLA Ops:
  1.0 9.0 %collective-permute-start = (bf16[1,576,128]{2,1,0:T(8,128)(2,1)S(1)}, bf16[1,576,128]{2,1,0:T(8,128)(2,1)S(1)}, u32[]{:S(2)}, u32[]{:S(2)}) collective-permute-start(bf16[1,576,128]{2,1,0:T(8,128)(2,1)S(1)} %get-tuple-element.44.rest_0_), channel_id=1, source_target_pairs={{0,4},{1,5},{4,8},{5,9},{8,12},{9,13},{12,14},{13,15},{14,10},{15,... | collective-permute-start | bytes 442376 | tf_op jit(solution)/shard_map/ppermute | solution.py:414
  4.1 8.0 %collective-permute-start.2 = (bf16[1,576,128]{2,1,0:T(8,128)(2,1)S(1)}, bf16[1,576,128]{2,1,0:T(8,128)(2,1)S(1)}, u32[]{:S(2)}, u32[]{:S(2)}) collective-permute-start(bf16[1,576,128]{2,1,0:T(8,128)(2,1)S(1)} %get-tuple-element.43.rest_1_), channel_id=1, source_target_pairs={{4,0},{5,1},{8,4},{9,5},{12,8},{13,9},{14,12},{15,13},{10,14},{11,... | collective-permute-start | bytes 442376 | tf_op jit(solution)/shard_map/ppermute | solution.py:415
  4.1 8.5 %collective-permute-start.3 = (bf16[1,576,128]{2,1,0:T(8,128)(2,1)S(1)}, bf16[1,576,128]{2,1,0:T(8,128)(2,1)S(1)}, u32[]{:S(2)}, u32[]{:S(2)}) collective-permute-start(bf16[1,576,128]{2,1,0:T(8,128)(2,1)S(1)} %get-tuple-element.44.rest_0_), channel_id=1, source_target_pairs={{4,0},{5,1},{8,4},{9,5},{12,8},{13,9},{14,12},{15,13},{10,14},{11,... | collective-permute-start | bytes 442376 | tf_op jit(solution)/shard_map/ppermute | solution.py:416
  6.1 8.0 %collective-permute-start.4 = (bf16[1,576,128]{2,1,0:T(8,128)(2,1)S(1)}, bf16[1,576,128]{2,1,0:T(8,128)(2,1)S(1)}, u32[]{:S(2)}, u32[]{:S(2)}) collective-permute-start(bf16[1,576,128]{2,1,0:T(8,128)(2,1)S(1)} %get-tuple-element.43.rest_1_), channel_id=1, source_target_pairs={{0,4},{1,5},{4,8},{5,9},{8,12},{9,13},{12,14},{13,15},{14,10},{15,... | collective-permute-start | bytes 442376 | tf_op jit(solution)/shard_map/ppermute | solution.py:417
  10.1 25.3 %copy-start = (bf16[8,512,128]{2,1,0:T(8,128)(2,1)S(1)}, bf16[8,512,128]{2,1,0:T(8,128)(2,1)}, u32[]{:S(2)}) copy-start(bf16[8,512,128]{2,1,0:T(8,128)(2,1)} %value_ref.1) | copy-start | bytes 3145732
  10.1 5.2 %collective-permute-start.5 = (bf16[1,576,128]{2,1,0:T(8,128)(2,1)S(1)}, bf16[1,576,128]{2,1,0:T(8,128)(2,1)S(1)}, u32[]{:S(2)}, u32[]{:S(2)}) collective-permute-start(bf16[1,576,128]{2,1,0:T(8,128)(2,1)S(1)} %collective-permute-done.rest_2_), channel_id=1, source_target_pairs={{0,4},{1,5},{4,8},{5,9},{8,12},{9,13},{12,14},{13,15},{14,10},{15,... | collective-permute-start | bytes 442376 | tf_op jit(solution)/shard_map/ppermute | solution.py:414
  12.1 6.7 %collective-permute-start.6 = (bf16[1,576,128]{2,1,0:T(8,128)(2,1)S(1)}, bf16[1,576,128]{2,1,0:T(8,128)(2,1)S(1)}, u32[]{:S(2)}, u32[]{:S(2)}) collective-permute-start(bf16[1,576,128]{2,1,0:T(8,128)(2,1)S(1)} %collective-permute-done.2.rest_3_), channel_id=1, source_target_pairs={{4,0},{5,1},{8,4},{9,5},{12,8},{13,9},{14,12},{15,13},{10,14},{11,... | collective-permute-start | bytes 442376 | tf_op jit(solution)/shard_map/ppermute | solution.py:415
  12.2 13.9 %collective-permute-start.1 = (bf16[8,32,576]{2,1,0:T(8,128)(2,1)S(1)}, bf16[8,32,576]{2,1,0:T(8,128)(2,1)S(1)}, u32[]{:S(2)}, u32[]{:S(2)}) collective-permute-start(bf16[8,32,576]{2,1,0:T(8,128)(2,1)S(1)} %bitcast.3), channel_id=1, source_target_pairs={{0,1},{1,0},{2,3},{3,2},{4,5},{5,4},{6,7},{7,6},{8,9},{9,8},{10,11... | collective-permute-start | bytes 884744 | tf_op jit(solution)/shard_map/ppermute | solution.py:322
  12.5 9.5 %collective-permute-start.7 = (bf16[1,576,128]{2,1,0:T(8,128)(2,1)S(1)}, bf16[1,576,128]{2,1,0:T(8,128)(2,1)S(1)}, u32[]{:S(2)}, u32[]{:S(2)}) collective-permute-start(bf16[1,576,128]{2,1,0:T(8,128)(2,1)S(1)} %collective-permute-done.3.rest_4_), channel_id=1, source_target_pairs={{4,0},{5,1},{8,4},{9,5},{12,8},{13,9},{14,12},{15,13},{10,14},{11,... | collective-permute-start | bytes 442376 | tf_op jit(solution)/shard_map/ppermute | solution.py:416
  14.1 7.9 %collective-permute-start.8 = (bf16[1,576,128]{2,1,0:T(8,128)(2,1)S(1)}, bf16[1,576,128]{2,1,0:T(8,128)(2,1)S(1)}, u32[]{:S(2)}, u32[]{:S(2)}) collective-permute-start(bf16[1,576,128]{2,1,0:T(8,128)(2,1)S(1)} %collective-permute-done.4.rest_5_), channel_id=1, source_target_pairs={{0,4},{1,5},{4,8},{5,9},{8,12},{9,13},{12,14},{13,15},{14,10},{15,... | collective-permute-start | bytes 442376 | tf_op jit(solution)/shard_map/ppermute | solution.py:417
  15.3 8.8 %collective-permute-start.9 = (bf16[1,576,128]{2,1,0:T(8,128)(2,1)S(1)}, bf16[1,576,128]{2,1,0:T(8,128)(2,1)S(1)}, u32[]{:S(2)}, u32[]{:S(2)}) collective-permute-start(bf16[1,576,128]{2,1,0:T(8,128)(2,1)S(1)} %collective-permute-done.5.rest_6_), channel_id=1, source_target_pairs={{0,4},{1,5},{4,8},{5,9},{8,12},{9,13},{12,14},{13,15},{14,10},{15,... | collective-permute-start | bytes 442376 | tf_op jit(solution)/shard_map/ppermute | solution.py:414
  18.8 6.8 %collective-permute-start.10 = (bf16[1,576,128]{2,1,0:T(8,128)(2,1)S(1)}, bf16[1,576,128]{2,1,0:T(8,128)(2,1)S(1)}, u32[]{:S(2)}, u32[]{:S(2)}) collective-permute-start(bf16[1,576,128]{2,1,0:T(8,128)(2,1)S(1)} %collective-permute-done.6.rest_7_), channel_id=1, source_target_pairs={{4,0},{5,1},{8,4},{9,5},{12,8},{13,9},{14,12},{15,13},{10,14},{11,... | collective-permute-start | bytes 442376 | tf_op jit(solution)/shard_map/ppermute | solution.py:415
  22.0 9.8 %collective-permute-start.11 = (bf16[1,576,128]{2,1,0:T(8,128)(2,1)S(1)}, bf16[1,576,128]{2,1,0:T(8,128)(2,1)S(1)}, u32[]{:S(2)}, u32[]{:S(2)}) collective-permute-start(bf16[1,576,128]{2,1,0:T(8,128)(2,1)S(1)} %collective-permute-done.7.rest_8_), channel_id=1, source_target_pairs={{4,0},{5,1},{8,4},{9,5},{12,8},{13,9},{14,12},{15,13},{10,14},{11,... | collective-permute-start | bytes 442376 | tf_op jit(solution)/shard_map/ppermute | solution.py:416
  22.0 9.8 %collective-permute-start.12 = (bf16[1,576,128]{2,1,0:T(8,128)(2,1)S(1)}, bf16[1,576,128]{2,1,0:T(8,128)(2,1)S(1)}, u32[]{:S(2)}, u32[]{:S(2)}) collective-permute-start(bf16[1,576,128]{2,1,0:T(8,128)(2,1)S(1)} %collective-permute-done.8.rest_9_), channel_id=1, source_target_pairs={{0,4},{1,5},{4,8},{5,9},{8,12},{9,13},{12,14},{13,15},{14,10},{15,... | collective-permute-start | bytes 442376 | tf_op jit(solution)/shard_map/ppermute | solution.py:417
  24.0 7.8 %collective-permute-start.13 = (bf16[1,576,128]{2,1,0:T(8,128)(2,1)S(1)}, bf16[1,576,128]{2,1,0:T(8,128)(2,1)S(1)}, u32[]{:S(2)}, u32[]{:S(2)}) collective-permute-start(bf16[1,576,128]{2,1,0:T(8,128)(2,1)S(1)} %collective-permute-done.9.rest_10_), channel_id=1, source_target_pairs={{0,4},{1,5},{4,8},{5,9},{8,12},{9,13},{12,14},{13,15},{14,10},{15,... | collective-permute-start | bytes 442376 | tf_op jit(solution)/shard_map/ppermute | solution.py:410
  25.6 6.3 %collective-permute-start.14 = (bf16[1,576,128]{2,1,0:T(8,128)(2,1)S(1)}, bf16[1,576,128]{2,1,0:T(8,128)(2,1)S(1)}, u32[]{:S(2)}, u32[]{:S(2)}) collective-permute-start(bf16[1,576,128]{2,1,0:T(8,128)(2,1)S(1)} %collective-permute-done.10.rest_11_), channel_id=1, source_target_pairs={{4,0},{5,1},{8,4},{9,5},{12,8},{13,9},{14,12},{15,13},{10,14},{11,... | collective-permute-start | bytes 442376 | tf_op jit(solution)/shard_map/ppermute | solution.py:411
  31.8 2.3 %collective-permute-start.15 = (bf16[256,640]{1,0:T(8,128)(2,1)S(1)}, bf16[256,640]{1,0:T(8,128)(2,1)S(1)}, u32[]{:S(2)}, u32[]{:S(2)}) collective-permute-start(bf16[256,640]{1,0:T(8,128)(2,1)S(1)} %get-tuple-element.36), channel_id=1, source_target_pairs={{0,1},{1,0},{2,3},{3,2},{4,5},{5,4},{6,7},{7,6},{8,9},{9,8},{10,11... | collective-permute-start | bytes 983048 | tf_op jit(solution)/shard_map/ppermute | solution.py:322
  33.5 1.8 %collective-permute-start.16 = (bf16[256,640]{1,0:T(8,128)(2,1)S(1)}, bf16[256,640]{1,0:T(8,128)(2,1)S(1)}, u32[]{:S(2)}, u32[]{:S(2)}) collective-permute-start(bf16[256,640]{1,0:T(8,128)(2,1)S(1)} %get-tuple-element.37), channel_id=1, source_target_pairs={{0,1},{1,0},{2,3},{3,2},{4,5},{5,4},{6,7},{7,6},{8,9},{9,8},{10,11... | collective-permute-start | bytes 983048 | tf_op jit(solution)/shard_map/ppermute | solution.py:322
  37.5 2.2 %collective-permute-start.17 = (bf16[32,3072]{1,0:T(8,128)(2,1)S(1)}, bf16[32,3072]{1,0:T(8,128)(2,1)S(1)}, u32[]{:S(2)}, u32[]{:S(2)}) collective-permute-start(bf16[32,3072]{1,0:T(8,128)(2,1)S(1)} %get-tuple-element.39), channel_id=1, source_target_pairs={{0,1},{1,0},{2,3},{3,2},{4,5},{5,4},{6,7},{7,6},{8,9},{9,8},{10,11... | collective-permute-start | bytes 589832 | tf_op jit(solution)/shard_map/ppermute | solution.py:322
  39.5 1.6 %collective-permute-start.19 = (bf16[32,4096]{1,0:T(8,128)(2,1)S(1)}, bf16[32,4096]{1,0:T(8,128)(2,1)S(1)}, u32[]{:S(2)}, u32[]{:S(2)}) collective-permute-start(bf16[32,4096]{1,0:T(8,128)(2,1)S(1)} %get-tuple-element.42), channel_id=1, source_target_pairs={{0,1},{1,0},{2,3},{3,2},{4,5},{5,4},{6,7},{7,6},{8,9},{9,8},{10,11... | collective-permute-start | bytes 786440 | tf_op jit(solution)/shard_map/ppermute | solution.py:322
  39.8 5.7 %collective-permute-start.18 = (bf16[16,3072]{1,0:T(8,128)(2,1)S(1)}, bf16[16,3072]{1,0:T(8,128)(2,1)S(1)}, u32[]{:S(2)}, u32[]{:S(2)}) collective-permute-start(bf16[16,3072]{1,0:T(8,128)(2,1)S(1)} %slice.43), channel_id=1, source_target_pairs={{0,2},{1,3},{2,0},{3,1},{4,6},{5,7},{6,4},{7,5},{8,10},{9,11},{10,... | collective-permute-start | bytes 294920 | tf_op jit(solution)/shard_map/ppermute | solution.py:322
  41.2 6.5 %collective-permute-start.20 = (bf16[16,4096]{1,0:T(8,128)(2,1)S(1)}, bf16[16,4096]{1,0:T(8,128)(2,1)S(1)}, u32[]{:S(2)}, u32[]{:S(2)}) collective-permute-start(bf16[16,4096]{1,0:T(8,128)(2,1)S(1)} %slice.45), channel_id=1, source_target_pairs={{0,2},{1,3},{2,0},{3,1},{4,6},{5,7},{6,4},{7,5},{8,10},{9,11},{10,... | collective-permute-start | bytes 393224 | tf_op jit(solution)/shard_map/ppermute | solution.py:322
  47.9 6.7 %collective-permute-start.23 = (bf16[4,7168]{1,0:T(4,128)(2,1)S(1)}, bf16[4,7168]{1,0:T(4,128)(2,1)S(1)}, u32[]{:S(2)}, u32[]{:S(2)}) collective-permute-start(bf16[4,7168]{1,0:T(4,128)(2,1)S(1)} %get-tuple-element.46), channel_id=1, source_target_pairs={{0,12},{1,13},{2,14},{3,15},{4,8},{5,9},{6,10},{7,11},{8,4},{9,5},... | collective-permute-start | bytes 172040 | tf_op jit(solution)/shard_map/ppermute | solution.py:322
  51.4 5.1 %collective-permute-start.22 = (bf16[4,7168]{1,0:T(4,128)(2,1)S(1)}, bf16[4,7168]{1,0:T(4,128)(2,1)S(1)}, u32[]{:S(2)}, u32[]{:S(2)}) collective-permute-start(bf16[4,7168]{1,0:T(4,128)(2,1)S(1)} %get-tuple-element.47), channel_id=1, source_target_pairs={{0,8},{1,9},{2,10},{3,11},{4,12},{5,13},{6,14},{7,15},{8,0},{9,1},... | collective-permute-start | bytes 172040 | tf_op jit(solution)/shard_map/ppermute | solution.py:322
  51.4 5.1 %collective-permute-start.21 = (bf16[4,7168]{1,0:T(4,128)(2,1)S(1)}, bf16[4,7168]{1,0:T(4,128)(2,1)S(1)}, u32[]{:S(2)}, u32[]{:S(2)}) collective-permute-start(bf16[4,7168]{1,0:T(4,128)(2,1)S(1)} %get-tuple-element.45), channel_id=1, source_target_pairs={{0,4},{1,5},{2,6},{3,7},{4,0},{5,1},{6,2},{7,3},{8,12},{9,13},{10,... | collective-permute-start | bytes 172040 | tf_op jit(solution)/shard_map/ppermute | solution.py:322

commit v6 on v5

--- a/solution.py
+++ b/solution.py
@@ -12,8 +12,8 @@
 OUT_TILE = 1024
 LANES = 128
 LATE = 4
-TILES = (3, 4)
 FIRST = 3
+COVER = 30_000_000_000
 EMPTY = -1e30
 
 
@@ -44,17 +44,16 @@
 
 
 def prepare_kernel(
-    heads, chips, me_ref, query_hbm, absorb_hbm, length_hbm, table_hbm, slot_hbm, owner_hbm, weight_hbm,
-    out_ref, plan_ref, order_ref, weight_ref,
-    query_ref, absorb_ref, length_ref, table_ref, slot_ref, owner_ref, ordered, sems, weight_sems,
+    heads, chips, me_ref, query_hbm, absorb_hbm, length_hbm, table_hbm, slot_hbm, owner_hbm,
+    out_ref, plan_ref, order_ref,
+    query_ref, absorb_ref, length_ref, table_ref, slot_ref, owner_ref, ordered, sems,
 ):
     sources = (length_hbm, table_hbm, slot_hbm, owner_hbm, query_hbm, absorb_hbm)
     targets = (length_ref, table_ref, slot_ref, owner_ref, query_ref, absorb_ref)
     copies = [
         pltpu.make_async_copy(a, b, sems.at[i]) for i, (a, b) in enumerate(zip(sources, targets))
     ]
-    weight_copies = weight_copy(weight_hbm, 0, weight_ref, weight_sems)
-    for copy in copies + weight_copies:
+    for copy in copies:
         copy.start()
     requests = table_ref.shape[0]
     entries = plan_ref.shape[0]
@@ -103,41 +102,20 @@
     for c in range(kv_rank // LANES):
         out_ref[:, c * LANES : (c + 1) * LANES] = ordered[c].astype(jnp.bfloat16)
     out_ref[:, kv_rank:] = ordered[kv_rank // LANES, :, :rope].astype(jnp.bfloat16)
-    for copy in weight_copies:
-        copy.wait()
 
 
 def slot_of(apart, chips):
     return (apart & 1) * chips + ((apart >> 1) & 1) * (chips // 2) + (apart >> 2)
 
 
-def weight_copy(weight_hbm, first, weight_ref, sems):
-    tile = weight_ref.shape[2]
-    return [
-        pltpu.make_async_copy(
-            weight_hbm.at[:, pl.ds((first + i) * tile, tile)], weight_ref.at[i], sems.at[i]
-        )
-        for i in range(weight_ref.shape[0])
-    ]
-
-
 def attend_kernel(
-    piece_count, first_slot, first_tile, heads, steps, kv_rank, scale,
+    piece_count, first_slot, heads, steps, kv_rank, scale,
     plan_ref, mine_ref, theirs_ref, *rest,
 ):
     pieces, rest = rest[:piece_count], rest[piece_count:]
-    weight_copies = []
-    if first_tile:
-        weight_hbm, out_ref, lse_ref, away_ref, weight_ref, *rest, weight_sems = rest
-        weight_copies = weight_copy(weight_hbm, first_tile, weight_ref, weight_sems)
-    else:
-        out_ref, lse_ref, away_ref, *rest = rest
-    scores, top, total, latent = rest
+    out_ref, lse_ref, away_ref, scores, top, total, latent = rest
     row_block = mine_ref.shape[1]
     half = pieces[0].shape[0]
-    for copy in weight_copies:
-        copy.start()
-
     requests = top.shape[0] - 1
     both = 2 * row_block
     block_rows = pieces[0].shape[2]
@@ -206,21 +184,19 @@
         return 0
 
     lax.fori_loop(0, requests, finish, 0, unroll=batch)
-    for copy in weight_copies:
-        copy.wait()
-
-
-def tiles_of(*weights):
-    return [(ref, i) for ref in weights for i in range(ref.shape[0])]
+
+
+def tiles_of(ref):
+    return [ref.at[:, pl.ds(i * OUT_TILE, OUT_TILE)] for i in range(ref.shape[1] // OUT_TILE)]
 
 
 def project(placed, tiles, keep_ref, away_ref):
     half_rows = keep_ref.shape[0]
     at = 0
-    for weight_ref, i in tiles:
-        tile = weight_ref.shape[2]
+    for weight_ref in tiles:
+        tile = weight_ref.shape[1]
         result = jnp.dot(
-            placed, weight_ref[i], preferred_element_type=jnp.float32
+            placed, weight_ref[...], preferred_element_type=jnp.float32
         ).astype(jnp.bfloat16)
         keep_ref[:, at : at + tile] = result[:half_rows]
         away_ref[:, at : at + tile] = result[half_rows:]
@@ -228,10 +204,10 @@
 
 
 def merge_kernel(
-    stages, heads, steps, order_ref, value_ref, weight_ref, next_ref, *rest,
+    stages, heads, steps, order_ref, value_ref, weight_ref, *rest,
 ):
     outs, lses, others = rest[:stages], rest[stages : 2 * stages], rest[2 * stages : 3 * stages]
-    away_ref, keep_ref, placed_ref, latent, head_rows = rest[3 * stages :]
+    away_ref, keep_ref, away2_ref, keep2_ref, latent, head_rows = rest[3 * stages :]
     kv_rank, v_width = value_ref.shape[1:]
     rows = head_rows.shape[0]
     requests = rows // steps
@@ -277,13 +253,8 @@
     placed = jnp.dot(
         picker.astype(jnp.bfloat16), head_rows[...], preferred_element_type=jnp.float32
     ).astype(jnp.bfloat16)
-    placed_ref[...] = placed
-    project(placed, tiles_of(weight_ref, next_ref)[:FIRST], keep_ref, away_ref)
-
-
-def second_kernel(placed_ref, weight_ref, next_ref, away_ref, keep_ref):
-    tiles = tiles_of(weight_ref, next_ref)
-    project(placed_ref[...], tiles[FIRST:], keep_ref, away_ref)
+    project(placed, tiles_of(weight_ref)[:FIRST], keep_ref, away_ref)
+    project(placed, tiles_of(weight_ref)[FIRST:], keep2_ref, away2_ref)
 
 
 def local(q_heads, w_absorb, w_value, w_out, latent_cache, ctx_blocks, block_table, owner):
@@ -322,22 +293,18 @@
         return lax.ppermute(x, "head", [(i, i ^ distance) for i in range(devices)])
 
     piece_total = len(ring_places(chips))
-    tile_shapes = [
-        jax.ShapeDtypeStruct((n, w_out.shape[0], OUT_TILE), jnp.bfloat16) for n in TILES
-    ]
 
     def prepare():
         slots = jnp.asarray(slots_by_device(chips, half))
-        queries, plan, order, weight = pl.pallas_call(
+        queries, plan, order = pl.pallas_call(
             functools.partial(prepare_kernel, heads, chips),
             out_shape=(
                 jax.ShapeDtypeStruct((flat_rows, row_width), jnp.bfloat16),
                 jax.ShapeDtypeStruct((2 * piece_total * half + 2,), jnp.int32),
                 jax.ShapeDtypeStruct((requests,), jnp.int32),
-                tile_shapes[0],
             ),
-            in_specs=[smem] + [hbm] * 7,
-            out_specs=(vmem, smem, smem, vmem),
+            in_specs=[smem] + [hbm] * 6,
+            out_specs=(vmem, smem, smem),
             scratch_shapes=[
                 pltpu.VMEM(q_heads.shape, jnp.bfloat16),
                 pltpu.VMEM(w_absorb.shape, jnp.bfloat16),
@@ -347,47 +314,45 @@
                 pltpu.SMEM(owner.shape, jnp.int32),
                 pltpu.VMEM((kv_rank // LANES + 1, flat_rows, LANES), jnp.float32),
                 pltpu.SemaphoreType.DMA((6,)),
-                pltpu.SemaphoreType.DMA((TILES[0],)),
             ],
             compiler_params=pltpu.CompilerParams(vmem_limit_bytes=12 * mebi),
             cost_estimate=pl.CostEstimate(
                 flops=2 * w_absorb.size * row_count, bytes_accessed=4 * w_absorb.size, transcendentals=0
             ),
             name="prepare",
-        )(me, *map(pin, (q_heads, w_absorb, ctx_blocks, block_table, slots, owner, w_out)))
-        return queries.reshape(requests, row_block, row_width), plan, order, weight
+        )(me, *map(pin, (q_heads, w_absorb, ctx_blocks, block_table, slots, owner)))
+        return queries.reshape(requests, row_block, row_width), plan, order
 
     def attend(plan, mine, theirs, pieces, stage):
         slots = len(pieces) * half
         first_slot = 0 if stage == 0 else piece_total * half - slots
-        with_weight = stage == 0
         both = 2 * row_block
         return pl.pallas_call(
             functools.partial(
-                attend_kernel, len(pieces), first_slot, TILES[0] * with_weight, heads, steps, kv_rank,
+                attend_kernel, len(pieces), first_slot, heads, steps, kv_rank,
                 float(head_width) ** -0.5,
             ),
             out_shape=(
                 jax.ShapeDtypeStruct((flat_rows, kv_rank), jnp.float32),
                 jax.ShapeDtypeStruct((flat_rows, LANES), jnp.float32),
                 jax.ShapeDtypeStruct((flat_rows, kv_rank + LANES), jnp.bfloat16),
-            ) + (tile_shapes[1],) * with_weight,
-            in_specs=[smem] + [vmem] * (2 + len(pieces)) + [hbm] * with_weight,
-            out_specs=(vmem,) * (3 + with_weight),
+            ),
+            in_specs=[smem] + [vmem] * (2 + len(pieces)),
+            out_specs=(vmem,) * 3,
             scratch_shapes=[
                 pltpu.VMEM((slots, 2 * both, block_rows), jnp.float32),
                 pltpu.VMEM((requests + 1, both, block_rows), jnp.float32),
                 pltpu.VMEM((requests + 1, both, block_rows), jnp.float32),
                 pltpu.VMEM((requests + 1, both, kv_rank), jnp.float32),
-            ] + [pltpu.SemaphoreType.DMA((TILES[1],))] * with_weight,
+            ],
             compiler_params=pltpu.CompilerParams(vmem_limit_bytes=28 * mebi),
             cost_estimate=pl.CostEstimate(
-                flops=2 * slots * 2 * both * block_rows * 2 * row_width,
+                flops=COVER if stage == 1 else 2 * slots * 2 * both * block_rows * 2 * row_width,
                 bytes_accessed=slots * block_rows * row_width * 2,
                 transcendentals=0,
             ),
             name="attend",
-        )(plan, mine, theirs, *pieces, *([pin(w_out)] * with_weight))
+        )(plan, mine, theirs, *pieces)
 
     ring = ring_of(chips)
     up = [
@@ -403,7 +368,7 @@
     for hop in range(1, chips // 2 + 1):
         last = hop == chips // 2
         if hop == 2:
-            mine, plan, order, weight = prepare()
+            mine, plan, order = prepare()
             theirs = exchange(mine, 1)
             ups[0], mine, plan = lax.optimization_barrier((ups[0], mine, plan))
         if last:
@@ -417,40 +382,27 @@
             ups[1] = lax.ppermute(ups[1], "head", up)
             pieces += [ups[0], downs[1], downs[0], ups[1]]
     early, late = pieces[:-LATE], pieces[-LATE:]
-    *early_part, next_weight = attend(plan, mine, theirs, early, 0)
+    early_part = attend(plan, mine, theirs, early, 0)
     late_part = attend(plan, mine, theirs, late, 1)
     partial = [(out, lse, exchange(away, 1)) for out, lse, away in (early_part, late_part)]
 
     part_rows = chips * steps
-    widths = (FIRST * OUT_TILE, (sum(TILES) - FIRST) * OUT_TILE)
+    widths = (FIRST * OUT_TILE, w_out.shape[1] - FIRST * OUT_TILE)
     parts = [jax.ShapeDtypeStruct((part_rows, n), jnp.bfloat16) for n in widths]
-    placed_shape = jax.ShapeDtypeStruct((2 * part_rows, heads * v_width), jnp.bfloat16)
     outs, lses, others = zip(*partial)
-    away, keep, placed = pl.pallas_call(
+    away, keep, next_away, next_keep = pl.pallas_call(
         functools.partial(merge_kernel, len(partial), heads, steps),
-        out_shape=(parts[0], parts[0], placed_shape),
-        in_specs=[smem] + [vmem] * (3 + 3 * len(partial)),
-        out_specs=(vmem,) * 3,
+        out_shape=(parts[0], parts[0], parts[1], parts[1]),
+        in_specs=[smem] + [vmem] * (2 + 3 * len(partial)),
+        out_specs=(vmem,) * 4,
         scratch_shapes=[
             pltpu.VMEM((kv_rank // LANES, flat_rows, LANES), jnp.float32),
             pltpu.VMEM((row_count, heads * v_width), jnp.bfloat16),
         ],
         compiler_params=pltpu.CompilerParams(vmem_limit_bytes=28 * mebi),
         name="merge_and_project",
-    )(order, w_value, weight, next_weight, *outs, *lses, *others)
+    )(order, w_value, w_out, *outs, *lses, *others)
     first_half = add(keep, exchange(away, 1))
-    next_away, next_keep = pl.pallas_call(
-        second_kernel,
-        out_shape=(parts[1], parts[1]),
-        in_specs=[vmem] * 3,
-        out_specs=(vmem, vmem),
-        compiler_params=pltpu.CompilerParams(vmem_limit_bytes=28 * mebi),
-        cost_estimate=pl.CostEstimate(
-            flops=2 * w_out.size * part_rows, bytes_accessed=8 * w_out.size, transcendentals=0
-        ),
-        name="project_second",
-    )(placed, weight, next_weight)
-
     second_half = add(next_keep, exchange(next_away, 1))
     result = jnp.concatenate([fold(first_half, 2), fold(second_half, 2)], axis=1)
     distance = 4

time: 57.4 us -> 55.1 us (0.960)
  Pallas kernels: 15 us -> 9.48 us
  waiting for transfers between devices: 16.7 us -> 20.5 us
  starting transfers between devices: 23.4 us -> 22.5 us
    pallas_call x2, Pallas kernels: 7.31 us -> 3.92 us  [attend(): pl.pallas_call(functools.partial(attend_kernel, len(pieces), first_slot,...]
    ppermute x3, waiting for transfers between devices: 3.55 us -> 5.81 us  [local(): downs[0] = lax.ppermute(downs[0], 'head', down)]
    pallas_call x1, Pallas kernels: 3.9 us -> 2.27 us  [prepare(): pl.pallas_call(functools.partial(prepare_kernel, heads, chips), out_shape...]
    pallas_call x1 -> x0, Pallas kernels: 1.55 us -> none  [local(): pl.pallas_call(second_kernel, out_shape=(parts[1], parts[1]), in_specs=[v...]
    ppermute x3, starting transfers between devices: 2.59 us -> 3.87 us  [local(): ups[1] = lax.ppermute(ups[1], 'head', up)]
    ppermute x3, starting transfers between devices: 3.51 us -> 2.23 us  [local(): downs[0] = lax.ppermute(downs[0], 'head', down)]
    ppermute x10, waiting for transfers between devices: 10.8 us -> 12 us  [exchange(): return lax.ppermute(x, 'head', [(i, i ^ distance) for i in range(devices)])]
    pallas_call x1, Pallas kernels: 2.22 us -> 3.3 us  [local(): pl.pallas_call(functools.partial(merge_kernel, len(partial), heads, steps...]
  transfers between devices with their start and end apart: 24 -> 24, of which waited for: 10 -> 12; matrix products, arithmetic and copies ran while one was open for 0% -> 0% of each run, Pallas kernels for 22% -> 11%
where the time goes in v6:
time: 55.1 us; the launch traced here: 54.9 us
  starting transfers between devices  22.5 us (41%)
  waiting for transfers between devices  20.5 us (37%)
  Pallas kernels  9.48 us (17%)
  local copies, waits for them, and re-layouts  1.27 us (2%)
  other arithmetic  0.93 us (2%)
    ppermute x10, waiting for transfers between devices, exchange(): return lax.ppermute(x, 'head', [(i, i ^ distance) for i in range(devices)])  12 us
    ppermute x4, starting transfers between devices, local(): ups[0] = lax.ppermute(ups[0], 'head', up)  8.16 us
    ppermute x10, starting transfers between devices, exchange(): return lax.ppermute(x, 'head', [(i, i ^ distance) for i in range(devices)])  7.32 us
    ppermute x3, waiting for transfers between devices, local(): downs[0] = lax.ppermute(downs[0], 'head', down)  5.81 us
    pallas_call x2, Pallas kernels, attend(): pl.pallas_call(functools.partial(attend_kernel, len(pieces), first_slot,...  3.92 us
    ppermute x3, starting transfers between devices, local(): ups[1] = lax.ppermute(ups[1], 'head', up)  3.87 us
    pallas_call x1, Pallas kernels, local(): pl.pallas_call(functools.partial(merge_kernel, len(partial), heads, steps...  3.3 us
    pallas_call x1, Pallas kernels, prepare(): pl.pallas_call(functools.partial(prepare_kernel, heads, chips), out_shape...  2.27 us
  transfers between devices with their start and end apart: 24, of which 12 were waited for; matrix products, arithmetic and copies ran while one was open for 0% of the time, Pallas kernels for 11%

profile of v6, /device:TPU:0, one launch (start us, length us, event | category | flops | bytes accessed | tf_op | source)
XLA Modules:
  0.0 54.9 jit_solution(8229415965108995956)
XLA Ops:
  0.0 1.0 %fusion.3 = (bf16[1,576,128]{2,1,0:T(8,128)(2,1)S(1)}, bf16[1,576,128]{2,1,0:T(8,128)(2,1)S(1)}) fusion(bf16[2,576,128]{2,1,0:T(8,128)(2,1)} %bitcast.8), kind=kLoop, calls=%fused_computation.15 | loop fusion | bytes 589824 | tf_op jit(solution)/shard_map/slice | solution.py:365
  1.0 3.1 %collective-permute-start = (bf16[1,576,128]{2,1,0:T(8,128)(2,1)S(1)}, bf16[1,576,128]{2,1,0:T(8,128)(2,1)S(1)}, u32[]{:S(2)}, u32[]{:S(2)}) collective-permute-start(bf16[1,576,128]{2,1,0:T(8,128)(2,1)S(1)} %get-tuple-element.38.rest_0_), channel_id=1, source_target_pairs={{0,4},{1,5},{4,8},{5,9},{8,12},{9,13},{12,14},{13,15},{14,10},{15,... | collective-permute-start | bytes 442376 | tf_op jit(solution)/shard_map/ppermute | solution.py:379
  4.1 0.0 collective-permute-start.2
  4.1 2.0 %collective-permute-start.3 = (bf16[1,576,128]{2,1,0:T(8,128)(2,1)S(1)}, bf16[1,576,128]{2,1,0:T(8,128)(2,1)S(1)}, u32[]{:S(2)}, u32[]{:S(2)}) collective-permute-start(bf16[1,576,128]{2,1,0:T(8,128)(2,1)S(1)} %get-tuple-element.38.rest_0_), channel_id=1, source_target_pairs={{4,0},{5,1},{8,4},{9,5},{12,8},{13,9},{14,12},{15,13},{10,14},{11,... | collective-permute-start | bytes 442376 | tf_op jit(solution)/shard_map/ppermute | solution.py:381
  6.1 0.1 collective-permute-start.4
  6.1 2.3 %prepare.1 = (bf16[256,576]{1,0:T(8,128)(2,1)S(1)}, s32[34]{0:T(128)S(1)}, s32[8]{0:T(128)S(1)}) custom-call(s32[1]{0:T(128)} %bitcast.me_ref, bf16[32,1536]{1,0:T(8,128)(2,1)} %query_hbm.1, bf16[8,128,512]{2,1,0:T(8,128)(2,1)} %absorb_hbm.1, s32[8]{0:T(128)} %length_hbm.1, s32[8,8]{1,0:T(8,128)} %table_hbm.1, s32[16,32]{1,0:T(8,128)} %constant.6.clone.slot_hbm, ...), custom_call_target="tpu_custom_call" | custom-call | flops 33554432 | bytes 2097152 | tf_op jit(solution)/shard_map/prepare/pallas_call | solution.py:299
  8.4 2.4 %collective-permute-start.5 = (bf16[1,576,128]{2,1,0:T(8,128)(2,1)S(1)}, bf16[1,576,128]{2,1,0:T(8,128)(2,1)S(1)}, u32[]{:S(2)}, u32[]{:S(2)}) collective-permute-start(bf16[1,576,128]{2,1,0:T(8,128)(2,1)S(1)} %collective-permute-done.rest_2_), channel_id=1, source_target_pairs={{0,4},{1,5},{4,8},{5,9},{8,12},{9,13},{12,14},{13,15},{14,10},{15,... | collective-permute-start | bytes 442376 | tf_op jit(solution)/shard_map/ppermute | solution.py:379
  10.8 0.0 collective-permute-done.2.rest_3_
  10.9 0.0 collective-permute-start.6
  10.9 0.0 collective-permute-start.1
  10.9 2.7 %collective-permute-done.3.rest_4_ = bf16[1,576,128]{2,1,0:T(8,128)(2,1)S(1)} collective-permute-done((bf16[1,576,128]{2,1,0:T(8,128)(2,1)S(1)}, bf16[1,576,128]{2,1,0:T(8,128)(2,1)S(1)}, u32[]{:S(2)}, u32[]{:S(2)}) %collective-permute-start.3) | collective-permute-done | bytes 147488 | tf_op jit(solution)/shard_map/ppermute | solution.py:381
  13.5 0.3 collective-permute-start.7
  13.8 1.8 %collective-permute-start.8 = (bf16[1,576,128]{2,1,0:T(8,128)(2,1)S(1)}, bf16[1,576,128]{2,1,0:T(8,128)(2,1)S(1)}, u32[]{:S(2)}, u32[]{:S(2)}) collective-permute-start(bf16[1,576,128]{2,1,0:T(8,128)(2,1)S(1)} %collective-permute-done.4.rest_5_), channel_id=1, source_target_pairs={{0,4},{1,5},{4,8},{5,9},{8,12},{9,13},{12,14},{13,15},{14,10},{15,... | collective-permute-start | bytes 442376 | tf_op jit(solution)/shard_map/ppermute | solution.py:382
  15.6 1.6 %collective-permute-start.9 = (bf16[1,576,128]{2,1,0:T(8,128)(2,1)S(1)}, bf16[1,576,128]{2,1,0:T(8,128)(2,1)S(1)}, u32[]{:S(2)}, u32[]{:S(2)}) collective-permute-start(bf16[1,576,128]{2,1,0:T(8,128)(2,1)S(1)} %collective-permute-done.5.rest_6_), channel_id=1, source_target_pairs={{0,4},{1,5},{4,8},{5,9},{8,12},{9,13},{12,14},{13,15},{14,10},{15,... | collective-permute-start | bytes 442376 | tf_op jit(solution)/shard_map/ppermute | solution.py:379
  17.1 0.4 collective-permute-done.6.rest_7_
  17.6 0.0 collective-permute-start.10
  17.6 3.1 %collective-permute-done.7.rest_8_ = bf16[1,576,128]{2,1,0:T(8,128)(2,1)S(1)} collective-permute-done((bf16[1,576,128]{2,1,0:T(8,128)(2,1)S(1)}, bf16[1,576,128]{2,1,0:T(8,128)(2,1)S(1)}, u32[]{:S(2)}, u32[]{:S(2)}) %collective-permute-start.7) | collective-permute-done | bytes 147488 | tf_op jit(solution)/shard_map/ppermute | solution.py:381
  20.7 0.0 collective-permute-start.11
  20.7 2.0 %collective-permute-start.12 = (bf16[1,576,128]{2,1,0:T(8,128)(2,1)S(1)}, bf16[1,576,128]{2,1,0:T(8,128)(2,1)S(1)}, u32[]{:S(2)}, u32[]{:S(2)}) collective-permute-start(bf16[1,576,128]{2,1,0:T(8,128)(2,1)S(1)} %collective-permute-done.8.rest_9_), channel_id=1, source_target_pairs={{0,4},{1,5},{4,8},{5,9},{8,12},{9,13},{12,14},{13,15},{14,10},{15,... | collective-permute-start | bytes 442376 | tf_op jit(solution)/shard_map/ppermute | solution.py:382
  22.8 0.5 collective-permute-done.9.rest_10_
  23.2 1.1 %collective-permute-start.13 = (bf16[1,576,128]{2,1,0:T(8,128)(2,1)S(1)}, bf16[1,576,128]{2,1,0:T(8,128)(2,1)S(1)}, u32[]{:S(2)}, u32[]{:S(2)}) collective-permute-start(bf16[1,576,128]{2,1,0:T(8,128)(2,1)S(1)} %collective-permute-done.9.rest_10_), channel_id=1, source_target_pairs={{0,4},{1,5},{4,8},{5,9},{8,12},{9,13},{12,14},{13,15},{14,10},{15,... | collective-permute-start | bytes 442376 | tf_op jit(solution)/shard_map/ppermute | solution.py:375
  24.4 0.9 %collective-permute-start.14 = (bf16[1,576,128]{2,1,0:T(8,128)(2,1)S(1)}, bf16[1,576,128]{2,1,0:T(8,128)(2,1)S(1)}, u32[]{:S(2)}, u32[]{:S(2)}) collective-permute-start(bf16[1,576,128]{2,1,0:T(8,128)(2,1)S(1)} %collective-permute-done.10.rest_11_), channel_id=1, source_target_pairs={{4,0},{5,1},{8,4},{9,5},{12,8},{13,9},{14,12},{15,13},{10,14},{11,... | collective-permute-start | bytes 442376 | tf_op jit(solution)/shard_map/ppermute | solution.py:376
  25.3 2.3 %attend.2 = (f32[256,512]{1,0:T(8,128)S(1)}, f32[256,128]{1,0:T(8,128)S(1)}, bf16[256,640]{1,0:T(8,128)(2,1)S(1)}) custom-call(s32[34]{0:T(128)S(1)} %get-tuple-element.24.plan_ref, bf16[8,32,576]{2,1,0:T(8,128)(2,1)S(1)} %bitcast.6, bf16[8,32,576]{2,1,0:T(8,128)(2,1)S(1)} %collective-permute-done.1.theirs_ref, ...), custom_call_target="tpu_custom_call" | custom-call | flops 452984832 | bytes 1769472 | tf_op jit(solution)/shard_map/attend/pallas_call | solution.py:330
  27.6 0.0 slice-start
  27.6 0.0 copy-start
  27.6 0.1 collective-permute-start.15
  27.7 0.6 %collective-permute-done.13.rest_2_ = bf16[1,576,128]{2,1,0:T(8,128)(2,1)S(1)} collective-permute-done((bf16[1,576,128]{2,1,0:T(8,128)(2,1)S(1)}, bf16[1,576,128]{2,1,0:T(8,128)(2,1)S(1)}, u32[]{:S(2)}, u32[]{:S(2)}) %collective-permute-start.13) | collective-permute-done | bytes 147488 | tf_op jit(solution)/shard_map/ppermute | solution.py:375
  28.4 1.1 %collective-permute-done.14.rest_3_ = bf16[1,576,128]{2,1,0:T(8,128)(2,1)S(1)} collective-permute-done((bf16[1,576,128]{2,1,0:T(8,128)(2,1)S(1)}, bf16[1,576,128]{2,1,0:T(8,128)(2,1)S(1)}, u32[]{:S(2)}, u32[]{:S(2)}) %collective-permute-start.14) | collective-permute-done | bytes 147488 | tf_op jit(solution)/shard_map/ppermute | solution.py:376
  29.5 1.6 %attend.3 = (f32[256,512]{1,0:T(8,128)S(1)}, f32[256,128]{1,0:T(8,128)S(1)}, bf16[256,640]{1,0:T(8,128)(2,1)S(1)}) custom-call(s32[34]{0:T(128)S(1)} %get-tuple-element.24.plan_ref, bf16[8,32,576]{2,1,0:T(8,128)(2,1)S(1)} %bitcast.7, bf16[8,32,576]{2,1,0:T(8,128)(2,1)S(1)} %collective-permute-done.1.theirs_ref, ...), custom_call_target="tpu_custom_call" | custom-call | flops 30000001024 | bytes 589824 | tf_op jit(solution)/shard_map/attend/pallas_call | solution.py:330
  31.1 0.1 collective-permute-start.16
  31.2 1.6 %collective-permute-done.16.rest_5_ = bf16[256,640]{1,0:T(8,128)(2,1)S(1)} collective-permute-done((bf16[256,640]{1,0:T(8,128)(2,1)S(1)}, bf16[256,640]{1,0:T(8,128)(2,1)S(1)}, u32[]{:S(2)}, u32[]{:S(2)}) %collective-permute-start.16) | collective-permute-done | bytes 327712 | tf_op jit(solution)/shard_map/ppermute | solution.py:293
  32.8 0.0 slice-done.3
  32.8 0.2 copy-done
  33.1 3.3 %merge_and_project.1 = (bf16[32,3072]{1,0:T(8,128)(2,1)S(1)}, bf16[32,3072]{1,0:T(8,128)(2,1)S(1)}, bf16[32,4096]{1,0:T(8,128)(2,1)S(1)}, bf16[32,4096]{1,0:T(8,128)(2,1)S(1)}) custom-call(s32[8]{0:T(128)S(1)} %get-tuple-element.21.order_ref, bf16[8,512,128]{2,1,0:T(8,128)(2,1)S(1)} %copy-done, bf16[1024,7168]{1,0:T(8,128)(2,1)S(1)} %bitcast.4, ...), custom_call_target="tpu_custom_call" | custom-call | tf_op jit(solution)/shard_map/merge_and_project/pallas_call | solution.py:393
  36.4 0.1 collective-permute-start.17
  36.4 0.5 collective-permute-start.19
  36.9 0.9 %collective-permute-done.17 = bf16[32,3072]{1,0:T(8,128)(2,1)S(1)} collective-permute-done((bf16[32,3072]{1,0:T(8,128)(2,1)S(1)}, bf16[32,3072]{1,0:T(8,128)(2,1)S(1)}, u32[]{:S(2)}, u32[]{:S(2)}) %collective-permute-start.17) | collective-permute-done | bytes 196640 | tf_op jit(solution)/shard_map/ppermute | solution.py:293
  37.9 1.5 %collective-permute-start.18 = (bf16[16,3072]{1,0:T(8,128)(2,1)S(1)}, bf16[16,3072]{1,0:T(8,128)(2,1)S(1)}, u32[]{:S(2)}, u32[]{:S(2)}) collective-permute-start(bf16[16,3072]{1,0:T(8,128)(2,1)S(1)} %slice.43), channel_id=1, source_target_pairs={{0,2},{1,3},{2,0},{3,1},{4,6},{5,7},{6,4},{7,5},{8,10},{9,11},{10,... | collective-permute-start | bytes 294920 | tf_op jit(solution)/shard_map/ppermute | solution.py:293
  39.4 0.1 add_convert_fusion
  39.5 0.7 %collective-permute-start.20 = (bf16[16,4096]{1,0:T(8,128)(2,1)S(1)}, bf16[16,4096]{1,0:T(8,128)(2,1)S(1)}, u32[]{:S(2)}, u32[]{:S(2)}) collective-permute-start(bf16[16,4096]{1,0:T(8,128)(2,1)S(1)} %slice.45), channel_id=1, source_target_pairs={{0,2},{1,3},{2,0},{3,1},{4,6},{5,7},{6,4},{7,5},{8,10},{9,11},{10,... | collective-permute-start | bytes 393224 | tf_op jit(solution)/shard_map/ppermute | solution.py:293
  40.2 3.5 %collective-permute-done.18 = bf16[16,3072]{1,0:T(8,128)(2,1)S(1)} collective-permute-done((bf16[16,3072]{1,0:T(8,128)(2,1)S(1)}, bf16[16,3072]{1,0:T(8,128)(2,1)S(1)}, u32[]{:S(2)}, u32[]{:S(2)}) %collective-permute-start.18) | collective-permute-done | bytes 98336 | tf_op jit(solution)/shard_map/ppermute | solution.py:293
  43.7 2.0 %collective-permute-done.20 = bf16[16,4096]{1,0:T(8,128)(2,1)S(1)} collective-permute-done((bf16[16,4096]{1,0:T(8,128)(2,1)S(1)}, bf16[16,4096]{1,0:T(8,128)(2,1)S(1)}, u32[]{:S(2)}, u32[]{:S(2)}) %collective-permute-start.20) | collective-permute-done | bytes 131104 | tf_op jit(solution)/shard_map/ppermute | solution.py:293
  45.7 0.1 fusion.2
  45.8 3.4 %collective-permute-start.23 = (bf16[4,7168]{1,0:T(4,128)(2,1)S(1)}, bf16[4,7168]{1,0:T(4,128)(2,1)S(1)}, u32[]{:S(2)}, u32[]{:S(2)}) collective-permute-start(bf16[4,7168]{1,0:T(4,128)(2,1)S(1)} %get-tuple-element.40), channel_id=1, source_target_pairs={{0,12},{1,13},{2,14},{3,15},{4,8},{5,9},{6,10},{7,11},{8,4},{9,5},... | collective-permute-start | bytes 172040 | tf_op jit(solution)/shard_map/ppermute | solution.py:293
  49.1 1.1 %collective-permute-start.21 = (bf16[4,7168]{1,0:T(4,128)(2,1)S(1)}, bf16[4,7168]{1,0:T(4,128)(2,1)S(1)}, u32[]{:S(2)}, u32[]{:S(2)}) collective-permute-start(bf16[4,7168]{1,0:T(4,128)(2,1)S(1)} %get-tuple-element.39), channel_id=1, source_target_pairs={{0,4},{1,5},{2,6},{3,7},{4,0},{5,1},{6,2},{7,3},{8,12},{9,13},{10,... | collective-permute-start | bytes 172040 | tf_op jit(solution)/shard_map/ppermute | solution.py:293
  50.2 2.0 %collective-permute-done.23 = bf16[4,7168]{1,0:T(4,128)(2,1)S(1)} collective-permute-done((bf16[4,7168]{1,0:T(4,128)(2,1)S(1)}, bf16[4,7168]{1,0:T(4,128)(2,1)S(1)}, u32[]{:S(2)}, u32[]{:S(2)}) %collective-permute-start.23) | collective-permute-done | bytes 57376 | tf_op jit(solution)/shard_map/ppermute | solution.py:293
  52.2 2.1 %collective-permute-done.22 = bf16[4,7168]{1,0:T(4,128)(2,1)S(1)} collective-permute-done((bf16[4,7168]{1,0:T(4,128)(2,1)S(1)}, bf16[4,7168]{1,0:T(4,128)(2,1)S(1)}, u32[]{:S(2)}, u32[]{:S(2)}) %collective-permute-start.22) | collective-permute-done | bytes 57376 | tf_op jit(solution)/shard_map/ppermute | solution.py:293
  54.2 0.7 %add_convert_fusion.4 = bf16[4,7168]{1,0:T(4,128)(2,1)} fusion(bf16[4,7168]{1,0:T(4,128)(2,1)S(1)} %collective-permute-done.23, bf16[4,7168]{1,0:T(4,128)(2,1)S(1)} %collective-permute-done.22, bf16[4,7168]{1,0:T(4,128)(2,1)S(1)} %collective-permute-done.21, bf16[16,4096]{1,0:T(8,128)(2,1)S(1)} %add_convert_fusion.2, bf16[16,3072]{1,0:T(8,128)(2,1)S(1)} %add_convert_fusion.3), kind=kLoop, calls=%fused_computation.10 | loop fusion | flops 315392 | bytes 458752 | tf_op jit(solution)/shard_map/convert_element_type | solution.py:286
  (24 shorter events, 0.2 us)
Async XLA Ops:
  1.0 7.4 %collective-permute-start = (bf16[1,576,128]{2,1,0:T(8,128)(2,1)S(1)}, bf16[1,576,128]{2,1,0:T(8,128)(2,1)S(1)}, u32[]{:S(2)}, u32[]{:S(2)}) collective-permute-start(bf16[1,576,128]{2,1,0:T(8,128)(2,1)S(1)} %get-tuple-element.38.rest_0_), channel_id=1, source_target_pairs={{0,4},{1,5},{4,8},{5,9},{8,12},{9,13},{12,14},{13,15},{14,10},{15,... | collective-permute-start | bytes 442376 | tf_op jit(solution)/shard_map/ppermute | solution.py:379
  4.1 6.8 %collective-permute-start.2 = (bf16[1,576,128]{2,1,0:T(8,128)(2,1)S(1)}, bf16[1,576,128]{2,1,0:T(8,128)(2,1)S(1)}, u32[]{:S(2)}, u32[]{:S(2)}) collective-permute-start(bf16[1,576,128]{2,1,0:T(8,128)(2,1)S(1)} %get-tuple-element.37.rest_1_), channel_id=1, source_target_pairs={{4,0},{5,1},{8,4},{9,5},{12,8},{13,9},{14,12},{15,13},{10,14},{11,... | collective-permute-start | bytes 442376 | tf_op jit(solution)/shard_map/ppermute | solution.py:380
  4.1 9.4 %collective-permute-start.3 = (bf16[1,576,128]{2,1,0:T(8,128)(2,1)S(1)}, bf16[1,576,128]{2,1,0:T(8,128)(2,1)S(1)}, u32[]{:S(2)}, u32[]{:S(2)}) collective-permute-start(bf16[1,576,128]{2,1,0:T(8,128)(2,1)S(1)} %get-tuple-element.38.rest_0_), channel_id=1, source_target_pairs={{4,0},{5,1},{8,4},{9,5},{12,8},{13,9},{14,12},{15,13},{10,14},{11,... | collective-permute-start | bytes 442376 | tf_op jit(solution)/shard_map/ppermute | solution.py:381
  6.1 7.7 %collective-permute-start.4 = (bf16[1,576,128]{2,1,0:T(8,128)(2,1)S(1)}, bf16[1,576,128]{2,1,0:T(8,128)(2,1)S(1)}, u32[]{:S(2)}, u32[]{:S(2)}) collective-permute-start(bf16[1,576,128]{2,1,0:T(8,128)(2,1)S(1)} %get-tuple-element.37.rest_1_), channel_id=1, source_target_pairs={{0,4},{1,5},{4,8},{5,9},{8,12},{9,13},{12,14},{13,15},{14,10},{15,... | collective-permute-start | bytes 442376 | tf_op jit(solution)/shard_map/ppermute | solution.py:382
  8.4 7.1 %collective-permute-start.5 = (bf16[1,576,128]{2,1,0:T(8,128)(2,1)S(1)}, bf16[1,576,128]{2,1,0:T(8,128)(2,1)S(1)}, u32[]{:S(2)}, u32[]{:S(2)}) collective-permute-start(bf16[1,576,128]{2,1,0:T(8,128)(2,1)S(1)} %collective-permute-done.rest_2_), channel_id=1, source_target_pairs={{0,4},{1,5},{4,8},{5,9},{8,12},{9,13},{12,14},{13,15},{14,10},{15,... | collective-permute-start | bytes 442376 | tf_op jit(solution)/shard_map/ppermute | solution.py:379
  10.9 6.7 %collective-permute-start.6 = (bf16[1,576,128]{2,1,0:T(8,128)(2,1)S(1)}, bf16[1,576,128]{2,1,0:T(8,128)(2,1)S(1)}, u32[]{:S(2)}, u32[]{:S(2)}) collective-permute-start(bf16[1,576,128]{2,1,0:T(8,128)(2,1)S(1)} %collective-permute-done.2.rest_3_), channel_id=1, source_target_pairs={{4,0},{5,1},{8,4},{9,5},{12,8},{13,9},{14,12},{15,13},{10,14},{11,... | collective-permute-start | bytes 442376 | tf_op jit(solution)/shard_map/ppermute | solution.py:380
  10.9 14.4 %collective-permute-start.1 = (bf16[8,32,576]{2,1,0:T(8,128)(2,1)S(1)}, bf16[8,32,576]{2,1,0:T(8,128)(2,1)S(1)}, u32[]{:S(2)}, u32[]{:S(2)}) collective-permute-start(bf16[8,32,576]{2,1,0:T(8,128)(2,1)S(1)} %bitcast.5), channel_id=1, source_target_pairs={{0,1},{1,0},{2,3},{3,2},{4,5},{5,4},{6,7},{7,6},{8,9},{9,8},{10,11... | collective-permute-start | bytes 884744 | tf_op jit(solution)/shard_map/ppermute | solution.py:293
  13.5 7.2 %collective-permute-start.7 = (bf16[1,576,128]{2,1,0:T(8,128)(2,1)S(1)}, bf16[1,576,128]{2,1,0:T(8,128)(2,1)S(1)}, u32[]{:S(2)}, u32[]{:S(2)}) collective-permute-start(bf16[1,576,128]{2,1,0:T(8,128)(2,1)S(1)} %collective-permute-done.3.rest_4_), channel_id=1, source_target_pairs={{4,0},{5,1},{8,4},{9,5},{12,8},{13,9},{14,12},{15,13},{10,14},{11,... | collective-permute-start | bytes 442376 | tf_op jit(solution)/shard_map/ppermute | solution.py:381
  13.8 6.9 %collective-permute-start.8 = (bf16[1,576,128]{2,1,0:T(8,128)(2,1)S(1)}, bf16[1,576,128]{2,1,0:T(8,128)(2,1)S(1)}, u32[]{:S(2)}, u32[]{:S(2)}) collective-permute-start(bf16[1,576,128]{2,1,0:T(8,128)(2,1)S(1)} %collective-permute-done.4.rest_5_), channel_id=1, source_target_pairs={{0,4},{1,5},{4,8},{5,9},{8,12},{9,13},{12,14},{13,15},{14,10},{15,... | collective-permute-start | bytes 442376 | tf_op jit(solution)/shard_map/ppermute | solution.py:382
  15.6 7.7 %collective-permute-start.9 = (bf16[1,576,128]{2,1,0:T(8,128)(2,1)S(1)}, bf16[1,576,128]{2,1,0:T(8,128)(2,1)S(1)}, u32[]{:S(2)}, u32[]{:S(2)}) collective-permute-start(bf16[1,576,128]{2,1,0:T(8,128)(2,1)S(1)} %collective-permute-done.5.rest_6_), channel_id=1, source_target_pairs={{0,4},{1,5},{4,8},{5,9},{8,12},{9,13},{12,14},{13,15},{14,10},{15,... | collective-permute-start | bytes 442376 | tf_op jit(solution)/shard_map/ppermute | solution.py:379
  17.6 6.8 %collective-permute-start.10 = (bf16[1,576,128]{2,1,0:T(8,128)(2,1)S(1)}, bf16[1,576,128]{2,1,0:T(8,128)(2,1)S(1)}, u32[]{:S(2)}, u32[]{:S(2)}) collective-permute-start(bf16[1,576,128]{2,1,0:T(8,128)(2,1)S(1)} %collective-permute-done.6.rest_7_), channel_id=1, source_target_pairs={{4,0},{5,1},{8,4},{9,5},{12,8},{13,9},{14,12},{15,13},{10,14},{11,... | collective-permute-start | bytes 442376 | tf_op jit(solution)/shard_map/ppermute | solution.py:380
  20.7 7.0 %collective-permute-start.11 = (bf16[1,576,128]{2,1,0:T(8,128)(2,1)S(1)}, bf16[1,576,128]{2,1,0:T(8,128)(2,1)S(1)}, u32[]{:S(2)}, u32[]{:S(2)}) collective-permute-start(bf16[1,576,128]{2,1,0:T(8,128)(2,1)S(1)} %collective-permute-done.7.rest_8_), channel_id=1, source_target_pairs={{4,0},{5,1},{8,4},{9,5},{12,8},{13,9},{14,12},{15,13},{10,14},{11,... | collective-permute-start | bytes 442376 | tf_op jit(solution)/shard_map/ppermute | solution.py:381
  20.7 7.0 %collective-permute-start.12 = (bf16[1,576,128]{2,1,0:T(8,128)(2,1)S(1)}, bf16[1,576,128]{2,1,0:T(8,128)(2,1)S(1)}, u32[]{:S(2)}, u32[]{:S(2)}) collective-permute-start(bf16[1,576,128]{2,1,0:T(8,128)(2,1)S(1)} %collective-permute-done.8.rest_9_), channel_id=1, source_target_pairs={{0,4},{1,5},{4,8},{5,9},{8,12},{9,13},{12,14},{13,15},{14,10},{15,... | collective-permute-start | bytes 442376 | tf_op jit(solution)/shard_map/ppermute | solution.py:382
  23.2 5.1 %collective-permute-start.13 = (bf16[1,576,128]{2,1,0:T(8,128)(2,1)S(1)}, bf16[1,576,128]{2,1,0:T(8,128)(2,1)S(1)}, u32[]{:S(2)}, u32[]{:S(2)}) collective-permute-start(bf16[1,576,128]{2,1,0:T(8,128)(2,1)S(1)} %collective-permute-done.9.rest_10_), channel_id=1, source_target_pairs={{0,4},{1,5},{4,8},{5,9},{8,12},{9,13},{12,14},{13,15},{14,10},{15,... | collective-permute-start | bytes 442376 | tf_op jit(solution)/shard_map/ppermute | solution.py:375
  24.4 5.1 %collective-permute-start.14 = (bf16[1,576,128]{2,1,0:T(8,128)(2,1)S(1)}, bf16[1,576,128]{2,1,0:T(8,128)(2,1)S(1)}, u32[]{:S(2)}, u32[]{:S(2)}) collective-permute-start(bf16[1,576,128]{2,1,0:T(8,128)(2,1)S(1)} %collective-permute-done.10.rest_11_), channel_id=1, source_target_pairs={{4,0},{5,1},{8,4},{9,5},{12,8},{13,9},{14,12},{15,13},{10,14},{11,... | collective-permute-start | bytes 442376 | tf_op jit(solution)/shard_map/ppermute | solution.py:376
  27.6 5.2 %slice-start = ((s8[14680064]{0:T(1024)(128)(4,1)}), s8[4194304]{0:T(1024)(128)(4,1)S(1)}, s32[]{:S(2)}) async-start(s8[14680064]{0:T(1024)(128)(4,1)} %bitcast.3), calls=%async_computation | async-start | bytes 8388608
  27.6 5.2 %slice-start.1 = ((s8[14680064]{0:T(1024)(128)(4,1)}), s8[4194304]{0:T(1024)(128)(4,1)S(1)}, s32[]{:S(2)}) async-start(s8[14680064]{0:T(1024)(128)(4,1)} %bitcast.3), calls=%async_computation.1 | async-start | bytes 8388608
  27.6 5.2 %slice-start.2 = ((s8[14680064]{0:T(1024)(128)(4,1)}), s8[4194304]{0:T(1024)(128)(4,1)S(1)}, s32[]{:S(2)}) async-start(s8[14680064]{0:T(1024)(128)(4,1)} %bitcast.3), calls=%async_computation.2 | async-start | bytes 8388608
  27.6 5.2 %slice-start.3 = ((s8[14680064]{0:T(1024)(128)(4,1)}), s8[2097152]{0:T(1024)(128)(4,1)S(1)}, s32[]{:S(2)}) async-start(s8[14680064]{0:T(1024)(128)(4,1)} %bitcast.3), calls=%async_computation.3 | async-start | bytes 4194304
  27.6 5.4 %copy-start = (bf16[8,512,128]{2,1,0:T(8,128)(2,1)S(1)}, bf16[8,512,128]{2,1,0:T(8,128)(2,1)}, u32[]{:S(2)}) copy-start(bf16[8,512,128]{2,1,0:T(8,128)(2,1)} %value_ref.1) | copy-start | bytes 3145732
  27.6 3.6 %collective-permute-start.15 = (bf16[256,640]{1,0:T(8,128)(2,1)S(1)}, bf16[256,640]{1,0:T(8,128)(2,1)S(1)}, u32[]{:S(2)}, u32[]{:S(2)}) collective-permute-start(bf16[256,640]{1,0:T(8,128)(2,1)S(1)} %get-tuple-element.31), channel_id=1, source_target_pairs={{0,1},{1,0},{2,3},{3,2},{4,5},{5,4},{6,7},{7,6},{8,9},{9,8},{10,11... | collective-permute-start | bytes 983048 | tf_op jit(solution)/shard_map/ppermute | solution.py:293
  31.1 1.7 %collective-permute-start.16 = (bf16[256,640]{1,0:T(8,128)(2,1)S(1)}, bf16[256,640]{1,0:T(8,128)(2,1)S(1)}, u32[]{:S(2)}, u32[]{:S(2)}) collective-permute-start(bf16[256,640]{1,0:T(8,128)(2,1)S(1)} %get-tuple-element.32), channel_id=1, source_target_pairs={{0,1},{1,0},{2,3},{3,2},{4,5},{5,4},{6,7},{7,6},{8,9},{9,8},{10,11... | collective-permute-start | bytes 983048 | tf_op jit(solution)/shard_map/ppermute | solution.py:293
  36.4 1.5 %collective-permute-start.17 = (bf16[32,3072]{1,0:T(8,128)(2,1)S(1)}, bf16[32,3072]{1,0:T(8,128)(2,1)S(1)}, u32[]{:S(2)}, u32[]{:S(2)}) collective-permute-start(bf16[32,3072]{1,0:T(8,128)(2,1)S(1)} %get-tuple-element.34), channel_id=1, source_target_pairs={{0,1},{1,0},{2,3},{3,2},{4,5},{5,4},{6,7},{7,6},{8,9},{9,8},{10,11... | collective-permute-start | bytes 589832 | tf_op jit(solution)/shard_map/ppermute | solution.py:293
  36.4 3.0 %collective-permute-start.19 = (bf16[32,4096]{1,0:T(8,128)(2,1)S(1)}, bf16[32,4096]{1,0:T(8,128)(2,1)S(1)}, u32[]{:S(2)}, u32[]{:S(2)}) collective-permute-start(bf16[32,4096]{1,0:T(8,128)(2,1)S(1)} %get-tuple-element.36), channel_id=1, source_target_pairs={{0,1},{1,0},{2,3},{3,2},{4,5},{5,4},{6,7},{7,6},{8,9},{9,8},{10,11... | collective-permute-start | bytes 786440 | tf_op jit(solution)/shard_map/ppermute | solution.py:293
  37.9 5.7 %collective-permute-start.18 = (bf16[16,3072]{1,0:T(8,128)(2,1)S(1)}, bf16[16,3072]{1,0:T(8,128)(2,1)S(1)}, u32[]{:S(2)}, u32[]{:S(2)}) collective-permute-start(bf16[16,3072]{1,0:T(8,128)(2,1)S(1)} %slice.43), channel_id=1, source_target_pairs={{0,2},{1,3},{2,0},{3,1},{4,6},{5,7},{6,4},{7,5},{8,10},{9,11},{10,... | collective-permute-start | bytes 294920 | tf_op jit(solution)/shard_map/ppermute | solution.py:293
  39.5 6.1 %collective-permute-start.20 = (bf16[16,4096]{1,0:T(8,128)(2,1)S(1)}, bf16[16,4096]{1,0:T(8,128)(2,1)S(1)}, u32[]{:S(2)}, u32[]{:S(2)}) collective-permute-start(bf16[16,4096]{1,0:T(8,128)(2,1)S(1)} %slice.45), channel_id=1, source_target_pairs={{0,2},{1,3},{2,0},{3,1},{4,6},{5,7},{6,4},{7,5},{8,10},{9,11},{10,... | collective-permute-start | bytes 393224 | tf_op jit(solution)/shard_map/ppermute | solution.py:293
  45.8 6.4 %collective-permute-start.23 = (bf16[4,7168]{1,0:T(4,128)(2,1)S(1)}, bf16[4,7168]{1,0:T(4,128)(2,1)S(1)}, u32[]{:S(2)}, u32[]{:S(2)}) collective-permute-start(bf16[4,7168]{1,0:T(4,128)(2,1)S(1)} %get-tuple-element.40), channel_id=1, source_target_pairs={{0,12},{1,13},{2,14},{3,15},{4,8},{5,9},{6,10},{7,11},{8,4},{9,5},... | collective-permute-start | bytes 172040 | tf_op jit(solution)/shard_map/ppermute | solution.py:293
  49.1 5.1 %collective-permute-start.22 = (bf16[4,7168]{1,0:T(4,128)(2,1)S(1)}, bf16[4,7168]{1,0:T(4,128)(2,1)S(1)}, u32[]{:S(2)}, u32[]{:S(2)}) collective-permute-start(bf16[4,7168]{1,0:T(4,128)(2,1)S(1)} %get-tuple-element.41), channel_id=1, source_target_pairs={{0,8},{1,9},{2,10},{3,11},{4,12},{5,13},{6,14},{7,15},{8,0},{9,1},... | collective-permute-start | bytes 172040 | tf_op jit(solution)/shard_map/ppermute | solution.py:293
  49.1 5.1 %collective-permute-start.21 = (bf16[4,7168]{1,0:T(4,128)(2,1)S(1)}, bf16[4,7168]{1,0:T(4,128)(2,1)S(1)}, u32[]{:S(2)}, u32[]{:S(2)}) collective-permute-start(bf16[4,7168]{1,0:T(4,128)(2,1)S(1)} %get-tuple-element.39), channel_id=1, source_target_pairs={{0,4},{1,5},{2,6},{3,7},{4,0},{5,1},{6,2},{7,3},{8,12},{9,13},{10,... | collective-permute-start | bytes 172040 | tf_op jit(solution)/shard_map/ppermute | solution.py:293

commit v7 on v6

--- a/solution.py
+++ b/solution.py
@@ -207,7 +207,7 @@
     stages, heads, steps, order_ref, value_ref, weight_ref, *rest,
 ):
     outs, lses, others = rest[:stages], rest[stages : 2 * stages], rest[2 * stages : 3 * stages]
-    away_ref, keep_ref, away2_ref, keep2_ref, latent, head_rows = rest[3 * stages :]
+    away_ref, keep_ref, placed_ref, latent, head_rows = rest[3 * stages :]
     kv_rank, v_width = value_ref.shape[1:]
     rows = head_rows.shape[0]
     requests = rows // steps
@@ -253,8 +253,12 @@
     placed = jnp.dot(
         picker.astype(jnp.bfloat16), head_rows[...], preferred_element_type=jnp.float32
     ).astype(jnp.bfloat16)
+    placed_ref[...] = placed
     project(placed, tiles_of(weight_ref)[:FIRST], keep_ref, away_ref)
-    project(placed, tiles_of(weight_ref)[FIRST:], keep2_ref, away2_ref)
+
+
+def second_kernel(placed_ref, weight_ref, away_ref, keep_ref):
+    project(placed_ref[...], tiles_of(weight_ref)[FIRST:], keep_ref, away_ref)
 
 
 def local(q_heads, w_absorb, w_value, w_out, latent_cache, ctx_blocks, block_table, owner):
@@ -390,11 +394,15 @@
     widths = (FIRST * OUT_TILE, w_out.shape[1] - FIRST * OUT_TILE)
     parts = [jax.ShapeDtypeStruct((part_rows, n), jnp.bfloat16) for n in widths]
     outs, lses, others = zip(*partial)
-    away, keep, next_away, next_keep = pl.pallas_call(
+    away, keep, placed = pl.pallas_call(
         functools.partial(merge_kernel, len(partial), heads, steps),
-        out_shape=(parts[0], parts[0], parts[1], parts[1]),
+        out_shape=(
+            parts[0],
+            parts[0],
+            jax.ShapeDtypeStruct((2 * part_rows, heads * v_width), jnp.bfloat16),
+        ),
         in_specs=[smem] + [vmem] * (2 + 3 * len(partial)),
-        out_specs=(vmem,) * 4,
+        out_specs=(vmem,) * 3,
         scratch_shapes=[
             pltpu.VMEM((kv_rank // LANES, flat_rows, LANES), jnp.float32),
             pltpu.VMEM((row_count, heads * v_width), jnp.bfloat16),
@@ -402,6 +410,17 @@
         compiler_params=pltpu.CompilerParams(vmem_limit_bytes=28 * mebi),
         name="merge_and_project",
     )(order, w_value, w_out, *outs, *lses, *others)
+    next_away, next_keep = pl.pallas_call(
+        second_kernel,
+        out_shape=(parts[1], parts[1]),
+        in_specs=[vmem] * 2,
+        out_specs=(vmem, vmem),
+        compiler_params=pltpu.CompilerParams(vmem_limit_bytes=28 * mebi),
+        cost_estimate=pl.CostEstimate(
+            flops=2 * w_out.size * part_rows, bytes_accessed=w_out.size, transcendentals=0
+        ),
+        name="project_second",
+    )(placed, w_out)
     first_half = add(keep, exchange(away, 1))
     second_half = add(next_keep, exchange(next_away, 1))
     result = jnp.concatenate([fold(first_half, 2), fold(second_half, 2)], axis=1)

time: 55.1 us -> 54.7 us (level)
  waiting for transfers between devices: 20.5 us -> 19.1 us
    pallas_call x0 -> x1, Pallas kernels: none -> 1.56 us  [local(): pl.pallas_call(second_kernel, out_shape=(parts[1], parts[1]), in_specs=[v...]
    ppermute x10, waiting for transfers between devices: 12 us -> 10.6 us  [exchange(): return lax.ppermute(x, 'head', [(i, i ^ distance) for i in range(devices)])]
    pallas_call x1, Pallas kernels: 3.3 us -> 2.21 us  [local(): pl.pallas_call(functools.partial(merge_kernel, len(partial), heads, steps...]
  transfers between devices with their start and end apart: 24 -> 24, of which waited for: 12 -> 11; matrix products, arithmetic and copies ran while one was open for 0% -> 0% of each run, Pallas kernels for 11% -> 14%
where the time goes in v7:
time: 54.7 us; the launch traced here: 54.5 us
  starting transfers between devices  23 us (42%)
  waiting for transfers between devices  19.1 us (35%)
  Pallas kernels  9.97 us (18%)
  local copies, waits for them, and re-layouts  1.28 us (2%)
  other arithmetic  0.93 us (2%)
    ppermute x10, waiting for transfers between devices, exchange(): return lax.ppermute(x, 'head', [(i, i ^ distance) for i in range(devices)])  10.6 us
    ppermute x4, starting transfers between devices, local(): ups[0] = lax.ppermute(ups[0], 'head', up)  8.16 us
    ppermute x10, starting transfers between devices, exchange(): return lax.ppermute(x, 'head', [(i, i ^ distance) for i in range(devices)])  7.79 us
    ppermute x3, waiting for transfers between devices, local(): downs[0] = lax.ppermute(downs[0], 'head', down)  5.81 us
    pallas_call x2, Pallas kernels, attend(): pl.pallas_call(functools.partial(attend_kernel, len(pieces), first_slot,...  3.93 us
    ppermute x3, starting transfers between devices, local(): ups[1] = lax.ppermute(ups[1], 'head', up)  3.87 us
    pallas_call x1, Pallas kernels, prepare(): pl.pallas_call(functools.partial(prepare_kernel, heads, chips), out_shape...  2.27 us
    ppermute x3, starting transfers between devices, local(): downs[0] = lax.ppermute(downs[0], 'head', down)  2.23 us
  transfers between devices with their start and end apart: 24, of which 11 were waited for; matrix products, arithmetic and copies ran while one was open for 0% of the time, Pallas kernels for 14%

profile of v7, /device:TPU:0, one launch (start us, length us, event | category | flops | bytes accessed | tf_op | source)
XLA Modules:
  0.0 54.5 jit_solution(13882061869699737990)
XLA Ops:
  0.0 1.0 %fusion.3 = (bf16[1,576,128]{2,1,0:T(8,128)(2,1)S(1)}, bf16[1,576,128]{2,1,0:T(8,128)(2,1)S(1)}) fusion(bf16[2,576,128]{2,1,0:T(8,128)(2,1)} %bitcast.8), kind=kLoop, calls=%fused_computation.15 | loop fusion | bytes 589824 | tf_op jit(solution)/shard_map/slice | solution.py:369
  1.0 3.1 %collective-permute-start = (bf16[1,576,128]{2,1,0:T(8,128)(2,1)S(1)}, bf16[1,576,128]{2,1,0:T(8,128)(2,1)S(1)}, u32[]{:S(2)}, u32[]{:S(2)}) collective-permute-start(bf16[1,576,128]{2,1,0:T(8,128)(2,1)S(1)} %get-tuple-element.40.rest_0_), channel_id=1, source_target_pairs={{0,4},{1,5},{4,8},{5,9},{8,12},{9,13},{12,14},{13,15},{14,10},{15,... | collective-permute-start | bytes 442376 | tf_op jit(solution)/shard_map/ppermute | solution.py:383
  4.1 0.0 collective-permute-start.2
  4.1 2.0 %collective-permute-start.3 = (bf16[1,576,128]{2,1,0:T(8,128)(2,1)S(1)}, bf16[1,576,128]{2,1,0:T(8,128)(2,1)S(1)}, u32[]{:S(2)}, u32[]{:S(2)}) collective-permute-start(bf16[1,576,128]{2,1,0:T(8,128)(2,1)S(1)} %get-tuple-element.40.rest_0_), channel_id=1, source_target_pairs={{4,0},{5,1},{8,4},{9,5},{12,8},{13,9},{14,12},{15,13},{10,14},{11,... | collective-permute-start | bytes 442376 | tf_op jit(solution)/shard_map/ppermute | solution.py:385
  6.1 0.1 collective-permute-start.4
  6.1 2.3 %prepare.1 = (bf16[256,576]{1,0:T(8,128)(2,1)S(1)}, s32[34]{0:T(128)S(1)}, s32[8]{0:T(128)S(1)}) custom-call(s32[1]{0:T(128)} %bitcast.me_ref, bf16[32,1536]{1,0:T(8,128)(2,1)} %query_hbm.1, bf16[8,128,512]{2,1,0:T(8,128)(2,1)} %absorb_hbm.1, s32[8]{0:T(128)} %length_hbm.1, s32[8,8]{1,0:T(8,128)} %table_hbm.1, s32[16,32]{1,0:T(8,128)} %constant.6.clone.slot_hbm, ...), custom_call_target="tpu_custom_call" | custom-call | flops 33554432 | bytes 2097152 | tf_op jit(solution)/shard_map/prepare/pallas_call | solution.py:303
  8.4 0.0 collective-permute-done.rest_2_
  8.4 2.4 %collective-permute-start.5 = (bf16[1,576,128]{2,1,0:T(8,128)(2,1)S(1)}, bf16[1,576,128]{2,1,0:T(8,128)(2,1)S(1)}, u32[]{:S(2)}, u32[]{:S(2)}) collective-permute-start(bf16[1,576,128]{2,1,0:T(8,128)(2,1)S(1)} %collective-permute-done.rest_2_), channel_id=1, source_target_pairs={{0,4},{1,5},{4,8},{5,9},{8,12},{9,13},{12,14},{13,15},{14,10},{15,... | collective-permute-start | bytes 442376 | tf_op jit(solution)/shard_map/ppermute | solution.py:383
  10.8 0.0 collective-permute-done.2.rest_3_
  10.9 2.7 %collective-permute-done.3.rest_4_ = bf16[1,576,128]{2,1,0:T(8,128)(2,1)S(1)} collective-permute-done((bf16[1,576,128]{2,1,0:T(8,128)(2,1)S(1)}, bf16[1,576,128]{2,1,0:T(8,128)(2,1)S(1)}, u32[]{:S(2)}, u32[]{:S(2)}) %collective-permute-start.3) | collective-permute-done | bytes 147488 | tf_op jit(solution)/shard_map/ppermute | solution.py:385
  13.5 0.3 collective-permute-start.7
  13.8 0.0 collective-permute-done.4.rest_5_
  13.8 1.8 %collective-permute-start.8 = (bf16[1,576,128]{2,1,0:T(8,128)(2,1)S(1)}, bf16[1,576,128]{2,1,0:T(8,128)(2,1)S(1)}, u32[]{:S(2)}, u32[]{:S(2)}) collective-permute-start(bf16[1,576,128]{2,1,0:T(8,128)(2,1)S(1)} %collective-permute-done.4.rest_5_), channel_id=1, source_target_pairs={{0,4},{1,5},{4,8},{5,9},{8,12},{9,13},{12,14},{13,15},{14,10},{15,... | collective-permute-start | bytes 442376 | tf_op jit(solution)/shard_map/ppermute | solution.py:386
  15.6 1.6 %collective-permute-start.9 = (bf16[1,576,128]{2,1,0:T(8,128)(2,1)S(1)}, bf16[1,576,128]{2,1,0:T(8,128)(2,1)S(1)}, u32[]{:S(2)}, u32[]{:S(2)}) collective-permute-start(bf16[1,576,128]{2,1,0:T(8,128)(2,1)S(1)} %collective-permute-done.5.rest_6_), channel_id=1, source_target_pairs={{0,4},{1,5},{4,8},{5,9},{8,12},{9,13},{12,14},{13,15},{14,10},{15,... | collective-permute-start | bytes 442376 | tf_op jit(solution)/shard_map/ppermute | solution.py:383
  17.1 0.4 collective-permute-done.6.rest_7_
  17.6 0.0 collective-permute-start.10
  17.6 3.1 %collective-permute-done.7.rest_8_ = bf16[1,576,128]{2,1,0:T(8,128)(2,1)S(1)} collective-permute-done((bf16[1,576,128]{2,1,0:T(8,128)(2,1)S(1)}, bf16[1,576,128]{2,1,0:T(8,128)(2,1)S(1)}, u32[]{:S(2)}, u32[]{:S(2)}) %collective-permute-start.7) | collective-permute-done | bytes 147488 | tf_op jit(solution)/shard_map/ppermute | solution.py:385
  20.7 2.0 %collective-permute-start.12 = (bf16[1,576,128]{2,1,0:T(8,128)(2,1)S(1)}, bf16[1,576,128]{2,1,0:T(8,128)(2,1)S(1)}, u32[]{:S(2)}, u32[]{:S(2)}) collective-permute-start(bf16[1,576,128]{2,1,0:T(8,128)(2,1)S(1)} %collective-permute-done.8.rest_9_), channel_id=1, source_target_pairs={{0,4},{1,5},{4,8},{5,9},{8,12},{9,13},{12,14},{13,15},{14,10},{15,... | collective-permute-start | bytes 442376 | tf_op jit(solution)/shard_map/ppermute | solution.py:386
  22.8 0.5 collective-permute-done.9.rest_10_
  23.2 1.1 %collective-permute-start.13 = (bf16[1,576,128]{2,1,0:T(8,128)(2,1)S(1)}, bf16[1,576,128]{2,1,0:T(8,128)(2,1)S(1)}, u32[]{:S(2)}, u32[]{:S(2)}) collective-permute-start(bf16[1,576,128]{2,1,0:T(8,128)(2,1)S(1)} %collective-permute-done.9.rest_10_), channel_id=1, source_target_pairs={{0,4},{1,5},{4,8},{5,9},{8,12},{9,13},{12,14},{13,15},{14,10},{15,... | collective-permute-start | bytes 442376 | tf_op jit(solution)/shard_map/ppermute | solution.py:379
  24.4 0.9 %collective-permute-start.14 = (bf16[1,576,128]{2,1,0:T(8,128)(2,1)S(1)}, bf16[1,576,128]{2,1,0:T(8,128)(2,1)S(1)}, u32[]{:S(2)}, u32[]{:S(2)}) collective-permute-start(bf16[1,576,128]{2,1,0:T(8,128)(2,1)S(1)} %collective-permute-done.10.rest_11_), channel_id=1, source_target_pairs={{4,0},{5,1},{8,4},{9,5},{12,8},{13,9},{14,12},{15,13},{10,14},{11,... | collective-permute-start | bytes 442376 | tf_op jit(solution)/shard_map/ppermute | solution.py:380
  25.3 2.3 %attend.2 = (f32[256,512]{1,0:T(8,128)S(1)}, f32[256,128]{1,0:T(8,128)S(1)}, bf16[256,640]{1,0:T(8,128)(2,1)S(1)}) custom-call(s32[34]{0:T(128)S(1)} %get-tuple-element.25.plan_ref, bf16[8,32,576]{2,1,0:T(8,128)(2,1)S(1)} %bitcast.6, bf16[8,32,576]{2,1,0:T(8,128)(2,1)S(1)} %collective-permute-done.1.theirs_ref, ...), custom_call_target="tpu_custom_call" | custom-call | flops 452984832 | bytes 1769472 | tf_op jit(solution)/shard_map/attend/pallas_call | solution.py:334
  27.6 0.0 slice-start
  27.6 0.0 copy-start
  27.6 0.1 collective-permute-start.15
  27.7 0.6 %collective-permute-done.13.rest_2_ = bf16[1,576,128]{2,1,0:T(8,128)(2,1)S(1)} collective-permute-done((bf16[1,576,128]{2,1,0:T(8,128)(2,1)S(1)}, bf16[1,576,128]{2,1,0:T(8,128)(2,1)S(1)}, u32[]{:S(2)}, u32[]{:S(2)}) %collective-permute-start.13) | collective-permute-done | bytes 147488 | tf_op jit(solution)/shard_map/ppermute | solution.py:379
  28.4 1.1 %collective-permute-done.14.rest_3_ = bf16[1,576,128]{2,1,0:T(8,128)(2,1)S(1)} collective-permute-done((bf16[1,576,128]{2,1,0:T(8,128)(2,1)S(1)}, bf16[1,576,128]{2,1,0:T(8,128)(2,1)S(1)}, u32[]{:S(2)}, u32[]{:S(2)}) %collective-permute-start.14) | collective-permute-done | bytes 147488 | tf_op jit(solution)/shard_map/ppermute | solution.py:380
  29.5 1.6 %attend.3 = (f32[256,512]{1,0:T(8,128)S(1)}, f32[256,128]{1,0:T(8,128)S(1)}, bf16[256,640]{1,0:T(8,128)(2,1)S(1)}) custom-call(s32[34]{0:T(128)S(1)} %get-tuple-element.25.plan_ref, bf16[8,32,576]{2,1,0:T(8,128)(2,1)S(1)} %bitcast.7, bf16[8,32,576]{2,1,0:T(8,128)(2,1)S(1)} %collective-permute-done.1.theirs_ref, ...), custom_call_target="tpu_custom_call" | custom-call | flops 30000001024 | bytes 589824 | tf_op jit(solution)/shard_map/attend/pallas_call | solution.py:334
  31.1 0.1 collective-permute-start.16
  31.2 1.6 %collective-permute-done.16.rest_5_ = bf16[256,640]{1,0:T(8,128)(2,1)S(1)} collective-permute-done((bf16[256,640]{1,0:T(8,128)(2,1)S(1)}, bf16[256,640]{1,0:T(8,128)(2,1)S(1)}, u32[]{:S(2)}, u32[]{:S(2)}) %collective-permute-start.16) | collective-permute-done | bytes 327712 | tf_op jit(solution)/shard_map/ppermute | solution.py:297
  32.8 0.0 slice-done.3
  32.9 0.2 copy-done
  33.1 2.2 %merge_and_project.1 = (bf16[32,3072]{1,0:T(8,128)(2,1)S(1)}, bf16[32,3072]{1,0:T(8,128)(2,1)S(1)}, bf16[64,1024]{1,0:T(8,128)(2,1)S(1)}) custom-call(s32[8]{0:T(128)S(1)} %get-tuple-element.22.order_ref, bf16[8,512,128]{2,1,0:T(8,128)(2,1)S(1)} %copy-done, bf16[1024,7168]{1,0:T(8,128)(2,1)S(1)} %bitcast.4, f32[256,512]{1,0:T(8,128)S(1)} %get-tuple-element.28.rest_0_, ...), custom_call_target="tpu_custom_call" | custom-call | tf_op jit(solution)/shard_map/merge_and_project/pallas_call | solution.py:397
  35.3 0.1 collective-permute-start.17
  35.4 1.6 %project_second.1 = (bf16[32,4096]{1,0:T(8,128)(2,1)S(1)}, bf16[32,4096]{1,0:T(8,128)(2,1)S(1)}) custom-call(bf16[64,1024]{1,0:T(8,128)(2,1)S(1)} %get-tuple-element.36.placed_ref, bf16[1024,7168]{1,0:T(8,128)(2,1)S(1)} %bitcast.4), custom_call_target="tpu_custom_call" | custom-call | flops 469762048 | bytes 7340032 | tf_op jit(solution)/shard_map/project_second/pallas_call | solution.py:413
  36.9 0.6 %collective-permute-start.19 = (bf16[32,4096]{1,0:T(8,128)(2,1)S(1)}, bf16[32,4096]{1,0:T(8,128)(2,1)S(1)}, u32[]{:S(2)}, u32[]{:S(2)}) collective-permute-start(bf16[32,4096]{1,0:T(8,128)(2,1)S(1)} %get-tuple-element.38), channel_id=1, source_target_pairs={{0,1},{1,0},{2,3},{3,2},{4,5},{5,4},{6,7},{7,6},{8,9},{9,8},{10,11... | collective-permute-start | bytes 786440 | tf_op jit(solution)/shard_map/ppermute | solution.py:297
  37.5 0.1 add_convert_fusion.1
  37.6 1.5 %collective-permute-start.18 = (bf16[16,3072]{1,0:T(8,128)(2,1)S(1)}, bf16[16,3072]{1,0:T(8,128)(2,1)S(1)}, u32[]{:S(2)}, u32[]{:S(2)}) collective-permute-start(bf16[16,3072]{1,0:T(8,128)(2,1)S(1)} %slice.43), channel_id=1, source_target_pairs={{0,2},{1,3},{2,0},{3,1},{4,6},{5,7},{6,4},{7,5},{8,10},{9,11},{10,... | collective-permute-start | bytes 294920 | tf_op jit(solution)/shard_map/ppermute | solution.py:297
  39.0 0.1 add_convert_fusion
  39.1 1.1 %collective-permute-start.20 = (bf16[16,4096]{1,0:T(8,128)(2,1)S(1)}, bf16[16,4096]{1,0:T(8,128)(2,1)S(1)}, u32[]{:S(2)}, u32[]{:S(2)}) collective-permute-start(bf16[16,4096]{1,0:T(8,128)(2,1)S(1)} %slice.45), channel_id=1, source_target_pairs={{0,2},{1,3},{2,0},{3,1},{4,6},{5,7},{6,4},{7,5},{8,10},{9,11},{10,... | collective-permute-start | bytes 393224 | tf_op jit(solution)/shard_map/ppermute | solution.py:297
  40.2 2.8 %collective-permute-done.18 = bf16[16,3072]{1,0:T(8,128)(2,1)S(1)} collective-permute-done((bf16[16,3072]{1,0:T(8,128)(2,1)S(1)}, bf16[16,3072]{1,0:T(8,128)(2,1)S(1)}, u32[]{:S(2)}, u32[]{:S(2)}) %collective-permute-start.18) | collective-permute-done | bytes 98336 | tf_op jit(solution)/shard_map/ppermute | solution.py:297
  43.0 2.1 %collective-permute-done.20 = bf16[16,4096]{1,0:T(8,128)(2,1)S(1)} collective-permute-done((bf16[16,4096]{1,0:T(8,128)(2,1)S(1)}, bf16[16,4096]{1,0:T(8,128)(2,1)S(1)}, u32[]{:S(2)}, u32[]{:S(2)}) %collective-permute-start.20) | collective-permute-done | bytes 131104 | tf_op jit(solution)/shard_map/ppermute | solution.py:297
  45.2 0.1 fusion.2
  45.3 3.5 %collective-permute-start.23 = (bf16[4,7168]{1,0:T(4,128)(2,1)S(1)}, bf16[4,7168]{1,0:T(4,128)(2,1)S(1)}, u32[]{:S(2)}, u32[]{:S(2)}) collective-permute-start(bf16[4,7168]{1,0:T(4,128)(2,1)S(1)} %get-tuple-element.42), channel_id=1, source_target_pairs={{0,12},{1,13},{2,14},{3,15},{4,8},{5,9},{6,10},{7,11},{8,4},{9,5},... | collective-permute-start | bytes 172040 | tf_op jit(solution)/shard_map/ppermute | solution.py:297
  48.7 1.0 %collective-permute-start.21 = (bf16[4,7168]{1,0:T(4,128)(2,1)S(1)}, bf16[4,7168]{1,0:T(4,128)(2,1)S(1)}, u32[]{:S(2)}, u32[]{:S(2)}) collective-permute-start(bf16[4,7168]{1,0:T(4,128)(2,1)S(1)} %get-tuple-element.41), channel_id=1, source_target_pairs={{0,4},{1,5},{2,6},{3,7},{4,0},{5,1},{6,2},{7,3},{8,12},{9,13},{10,... | collective-permute-start | bytes 172040 | tf_op jit(solution)/shard_map/ppermute | solution.py:297
  49.7 2.0 %collective-permute-done.23 = bf16[4,7168]{1,0:T(4,128)(2,1)S(1)} collective-permute-done((bf16[4,7168]{1,0:T(4,128)(2,1)S(1)}, bf16[4,7168]{1,0:T(4,128)(2,1)S(1)}, u32[]{:S(2)}, u32[]{:S(2)}) %collective-permute-start.23) | collective-permute-done | bytes 57376 | tf_op jit(solution)/shard_map/ppermute | solution.py:297
  51.7 2.1 %collective-permute-done.22 = bf16[4,7168]{1,0:T(4,128)(2,1)S(1)} collective-permute-done((bf16[4,7168]{1,0:T(4,128)(2,1)S(1)}, bf16[4,7168]{1,0:T(4,128)(2,1)S(1)}, u32[]{:S(2)}, u32[]{:S(2)}) %collective-permute-start.22) | collective-permute-done | bytes 57376 | tf_op jit(solution)/shard_map/ppermute | solution.py:297
  53.8 0.7 %add_convert_fusion.4 = bf16[4,7168]{1,0:T(4,128)(2,1)} fusion(bf16[4,7168]{1,0:T(4,128)(2,1)S(1)} %collective-permute-done.23, bf16[4,7168]{1,0:T(4,128)(2,1)S(1)} %collective-permute-done.22, bf16[4,7168]{1,0:T(4,128)(2,1)S(1)} %collective-permute-done.21, bf16[16,4096]{1,0:T(8,128)(2,1)S(1)} %add_convert_fusion.2, bf16[16,3072]{1,0:T(8,128)(2,1)S(1)} %add_convert_fusion.3), kind=kLoop, calls=%fused_computation.10 | loop fusion | flops 315392 | bytes 458752 | tf_op jit(solution)/shard_map/convert_element_type | solution.py:290
  (25 shorter events, 0.1 us)
Async XLA Ops:
  1.0 7.4 %collective-permute-start = (bf16[1,576,128]{2,1,0:T(8,128)(2,1)S(1)}, bf16[1,576,128]{2,1,0:T(8,128)(2,1)S(1)}, u32[]{:S(2)}, u32[]{:S(2)}) collective-permute-start(bf16[1,576,128]{2,1,0:T(8,128)(2,1)S(1)} %get-tuple-element.40.rest_0_), channel_id=1, source_target_pairs={{0,4},{1,5},{4,8},{5,9},{8,12},{9,13},{12,14},{13,15},{14,10},{15,... | collective-permute-start | bytes 442376 | tf_op jit(solution)/shard_map/ppermute | solution.py:383
  4.1 6.8 %collective-permute-start.2 = (bf16[1,576,128]{2,1,0:T(8,128)(2,1)S(1)}, bf16[1,576,128]{2,1,0:T(8,128)(2,1)S(1)}, u32[]{:S(2)}, u32[]{:S(2)}) collective-permute-start(bf16[1,576,128]{2,1,0:T(8,128)(2,1)S(1)} %get-tuple-element.39.rest_1_), channel_id=1, source_target_pairs={{4,0},{5,1},{8,4},{9,5},{12,8},{13,9},{14,12},{15,13},{10,14},{11,... | collective-permute-start | bytes 442376 | tf_op jit(solution)/shard_map/ppermute | solution.py:384
  4.1 9.4 %collective-permute-start.3 = (bf16[1,576,128]{2,1,0:T(8,128)(2,1)S(1)}, bf16[1,576,128]{2,1,0:T(8,128)(2,1)S(1)}, u32[]{:S(2)}, u32[]{:S(2)}) collective-permute-start(bf16[1,576,128]{2,1,0:T(8,128)(2,1)S(1)} %get-tuple-element.40.rest_0_), channel_id=1, source_target_pairs={{4,0},{5,1},{8,4},{9,5},{12,8},{13,9},{14,12},{15,13},{10,14},{11,... | collective-permute-start | bytes 442376 | tf_op jit(solution)/shard_map/ppermute | solution.py:385
  6.1 7.7 %collective-permute-start.4 = (bf16[1,576,128]{2,1,0:T(8,128)(2,1)S(1)}, bf16[1,576,128]{2,1,0:T(8,128)(2,1)S(1)}, u32[]{:S(2)}, u32[]{:S(2)}) collective-permute-start(bf16[1,576,128]{2,1,0:T(8,128)(2,1)S(1)} %get-tuple-element.39.rest_1_), channel_id=1, source_target_pairs={{0,4},{1,5},{4,8},{5,9},{8,12},{9,13},{12,14},{13,15},{14,10},{15,... | collective-permute-start | bytes 442376 | tf_op jit(solution)/shard_map/ppermute | solution.py:386
  8.4 7.1 %collective-permute-start.5 = (bf16[1,576,128]{2,1,0:T(8,128)(2,1)S(1)}, bf16[1,576,128]{2,1,0:T(8,128)(2,1)S(1)}, u32[]{:S(2)}, u32[]{:S(2)}) collective-permute-start(bf16[1,576,128]{2,1,0:T(8,128)(2,1)S(1)} %collective-permute-done.rest_2_), channel_id=1, source_target_pairs={{0,4},{1,5},{4,8},{5,9},{8,12},{9,13},{12,14},{13,15},{14,10},{15,... | collective-permute-start | bytes 442376 | tf_op jit(solution)/shard_map/ppermute | solution.py:383
  10.9 6.7 %collective-permute-start.6 = (bf16[1,576,128]{2,1,0:T(8,128)(2,1)S(1)}, bf16[1,576,128]{2,1,0:T(8,128)(2,1)S(1)}, u32[]{:S(2)}, u32[]{:S(2)}) collective-permute-start(bf16[1,576,128]{2,1,0:T(8,128)(2,1)S(1)} %collective-permute-done.2.rest_3_), channel_id=1, source_target_pairs={{4,0},{5,1},{8,4},{9,5},{12,8},{13,9},{14,12},{15,13},{10,14},{11,... | collective-permute-start | bytes 442376 | tf_op jit(solution)/shard_map/ppermute | solution.py:384
  10.9 14.4 %collective-permute-start.1 = (bf16[8,32,576]{2,1,0:T(8,128)(2,1)S(1)}, bf16[8,32,576]{2,1,0:T(8,128)(2,1)S(1)}, u32[]{:S(2)}, u32[]{:S(2)}) collective-permute-start(bf16[8,32,576]{2,1,0:T(8,128)(2,1)S(1)} %bitcast.5), channel_id=1, source_target_pairs={{0,1},{1,0},{2,3},{3,2},{4,5},{5,4},{6,7},{7,6},{8,9},{9,8},{10,11... | collective-permute-start | bytes 884744 | tf_op jit(solution)/shard_map/ppermute | solution.py:297
  13.5 7.2 %collective-permute-start.7 = (bf16[1,576,128]{2,1,0:T(8,128)(2,1)S(1)}, bf16[1,576,128]{2,1,0:T(8,128)(2,1)S(1)}, u32[]{:S(2)}, u32[]{:S(2)}) collective-permute-start(bf16[1,576,128]{2,1,0:T(8,128)(2,1)S(1)} %collective-permute-done.3.rest_4_), channel_id=1, source_target_pairs={{4,0},{5,1},{8,4},{9,5},{12,8},{13,9},{14,12},{15,13},{10,14},{11,... | collective-permute-start | bytes 442376 | tf_op jit(solution)/shard_map/ppermute | solution.py:385
  13.8 6.9 %collective-permute-start.8 = (bf16[1,576,128]{2,1,0:T(8,128)(2,1)S(1)}, bf16[1,576,128]{2,1,0:T(8,128)(2,1)S(1)}, u32[]{:S(2)}, u32[]{:S(2)}) collective-permute-start(bf16[1,576,128]{2,1,0:T(8,128)(2,1)S(1)} %collective-permute-done.4.rest_5_), channel_id=1, source_target_pairs={{0,4},{1,5},{4,8},{5,9},{8,12},{9,13},{12,14},{13,15},{14,10},{15,... | collective-permute-start | bytes 442376 | tf_op jit(solution)/shard_map/ppermute | solution.py:386
  15.6 7.7 %collective-permute-start.9 = (bf16[1,576,128]{2,1,0:T(8,128)(2,1)S(1)}, bf16[1,576,128]{2,1,0:T(8,128)(2,1)S(1)}, u32[]{:S(2)}, u32[]{:S(2)}) collective-permute-start(bf16[1,576,128]{2,1,0:T(8,128)(2,1)S(1)} %collective-permute-done.5.rest_6_), channel_id=1, source_target_pairs={{0,4},{1,5},{4,8},{5,9},{8,12},{9,13},{12,14},{13,15},{14,10},{15,... | collective-permute-start | bytes 442376 | tf_op jit(solution)/shard_map/ppermute | solution.py:383
  17.6 6.8 %collective-permute-start.10 = (bf16[1,576,128]{2,1,0:T(8,128)(2,1)S(1)}, bf16[1,576,128]{2,1,0:T(8,128)(2,1)S(1)}, u32[]{:S(2)}, u32[]{:S(2)}) collective-permute-start(bf16[1,576,128]{2,1,0:T(8,128)(2,1)S(1)} %collective-permute-done.6.rest_7_), channel_id=1, source_target_pairs={{4,0},{5,1},{8,4},{9,5},{12,8},{13,9},{14,12},{15,13},{10,14},{11,... | collective-permute-start | bytes 442376 | tf_op jit(solution)/shard_map/ppermute | solution.py:384
  20.7 7.0 %collective-permute-start.11 = (bf16[1,576,128]{2,1,0:T(8,128)(2,1)S(1)}, bf16[1,576,128]{2,1,0:T(8,128)(2,1)S(1)}, u32[]{:S(2)}, u32[]{:S(2)}) collective-permute-start(bf16[1,576,128]{2,1,0:T(8,128)(2,1)S(1)} %collective-permute-done.7.rest_8_), channel_id=1, source_target_pairs={{4,0},{5,1},{8,4},{9,5},{12,8},{13,9},{14,12},{15,13},{10,14},{11,... | collective-permute-start | bytes 442376 | tf_op jit(solution)/shard_map/ppermute | solution.py:385
  20.7 7.0 %collective-permute-start.12 = (bf16[1,576,128]{2,1,0:T(8,128)(2,1)S(1)}, bf16[1,576,128]{2,1,0:T(8,128)(2,1)S(1)}, u32[]{:S(2)}, u32[]{:S(2)}) collective-permute-start(bf16[1,576,128]{2,1,0:T(8,128)(2,1)S(1)} %collective-permute-done.8.rest_9_), channel_id=1, source_target_pairs={{0,4},{1,5},{4,8},{5,9},{8,12},{9,13},{12,14},{13,15},{14,10},{15,... | collective-permute-start | bytes 442376 | tf_op jit(solution)/shard_map/ppermute | solution.py:386
  23.2 5.1 %collective-permute-start.13 = (bf16[1,576,128]{2,1,0:T(8,128)(2,1)S(1)}, bf16[1,576,128]{2,1,0:T(8,128)(2,1)S(1)}, u32[]{:S(2)}, u32[]{:S(2)}) collective-permute-start(bf16[1,576,128]{2,1,0:T(8,128)(2,1)S(1)} %collective-permute-done.9.rest_10_), channel_id=1, source_target_pairs={{0,4},{1,5},{4,8},{5,9},{8,12},{9,13},{12,14},{13,15},{14,10},{15,... | collective-permute-start | bytes 442376 | tf_op jit(solution)/shard_map/ppermute | solution.py:379
  24.4 5.1 %collective-permute-start.14 = (bf16[1,576,128]{2,1,0:T(8,128)(2,1)S(1)}, bf16[1,576,128]{2,1,0:T(8,128)(2,1)S(1)}, u32[]{:S(2)}, u32[]{:S(2)}) collective-permute-start(bf16[1,576,128]{2,1,0:T(8,128)(2,1)S(1)} %collective-permute-done.10.rest_11_), channel_id=1, source_target_pairs={{4,0},{5,1},{8,4},{9,5},{12,8},{13,9},{14,12},{15,13},{10,14},{11,... | collective-permute-start | bytes 442376 | tf_op jit(solution)/shard_map/ppermute | solution.py:380
  27.6 5.2 %slice-start = ((s8[14680064]{0:T(1024)(128)(4,1)}), s8[4194304]{0:T(1024)(128)(4,1)S(1)}, s32[]{:S(2)}) async-start(s8[14680064]{0:T(1024)(128)(4,1)} %bitcast.3), calls=%async_computation | async-start | bytes 8388608
  27.6 5.2 %slice-start.1 = ((s8[14680064]{0:T(1024)(128)(4,1)}), s8[4194304]{0:T(1024)(128)(4,1)S(1)}, s32[]{:S(2)}) async-start(s8[14680064]{0:T(1024)(128)(4,1)} %bitcast.3), calls=%async_computation.1 | async-start | bytes 8388608
  27.6 5.2 %slice-start.2 = ((s8[14680064]{0:T(1024)(128)(4,1)}), s8[4194304]{0:T(1024)(128)(4,1)S(1)}, s32[]{:S(2)}) async-start(s8[14680064]{0:T(1024)(128)(4,1)} %bitcast.3), calls=%async_computation.2 | async-start | bytes 8388608
  27.6 5.2 %slice-start.3 = ((s8[14680064]{0:T(1024)(128)(4,1)}), s8[2097152]{0:T(1024)(128)(4,1)S(1)}, s32[]{:S(2)}) async-start(s8[14680064]{0:T(1024)(128)(4,1)} %bitcast.3), calls=%async_computation.3 | async-start | bytes 4194304
  27.6 5.4 %copy-start = (bf16[8,512,128]{2,1,0:T(8,128)(2,1)S(1)}, bf16[8,512,128]{2,1,0:T(8,128)(2,1)}, u32[]{:S(2)}) copy-start(bf16[8,512,128]{2,1,0:T(8,128)(2,1)} %value_ref.1) | copy-start | bytes 3145732
  27.6 3.6 %collective-permute-start.15 = (bf16[256,640]{1,0:T(8,128)(2,1)S(1)}, bf16[256,640]{1,0:T(8,128)(2,1)S(1)}, u32[]{:S(2)}, u32[]{:S(2)}) collective-permute-start(bf16[256,640]{1,0:T(8,128)(2,1)S(1)} %get-tuple-element.32), channel_id=1, source_target_pairs={{0,1},{1,0},{2,3},{3,2},{4,5},{5,4},{6,7},{7,6},{8,9},{9,8},{10,11... | collective-permute-start | bytes 983048 | tf_op jit(solution)/shard_map/ppermute | solution.py:297
  31.1 1.7 %collective-permute-start.16 = (bf16[256,640]{1,0:T(8,128)(2,1)S(1)}, bf16[256,640]{1,0:T(8,128)(2,1)S(1)}, u32[]{:S(2)}, u32[]{:S(2)}) collective-permute-start(bf16[256,640]{1,0:T(8,128)(2,1)S(1)} %get-tuple-element.33), channel_id=1, source_target_pairs={{0,1},{1,0},{2,3},{3,2},{4,5},{5,4},{6,7},{7,6},{8,9},{9,8},{10,11... | collective-permute-start | bytes 983048 | tf_op jit(solution)/shard_map/ppermute | solution.py:297
  35.3 2.2 %collective-permute-start.17 = (bf16[32,3072]{1,0:T(8,128)(2,1)S(1)}, bf16[32,3072]{1,0:T(8,128)(2,1)S(1)}, u32[]{:S(2)}, u32[]{:S(2)}) collective-permute-start(bf16[32,3072]{1,0:T(8,128)(2,1)S(1)} %get-tuple-element.35), channel_id=1, source_target_pairs={{0,1},{1,0},{2,3},{3,2},{4,5},{5,4},{6,7},{7,6},{8,9},{9,8},{10,11... | collective-permute-start | bytes 589832 | tf_op jit(solution)/shard_map/ppermute | solution.py:297
  36.9 2.1 %collective-permute-start.19 = (bf16[32,4096]{1,0:T(8,128)(2,1)S(1)}, bf16[32,4096]{1,0:T(8,128)(2,1)S(1)}, u32[]{:S(2)}, u32[]{:S(2)}) collective-permute-start(bf16[32,4096]{1,0:T(8,128)(2,1)S(1)} %get-tuple-element.38), channel_id=1, source_target_pairs={{0,1},{1,0},{2,3},{3,2},{4,5},{5,4},{6,7},{7,6},{8,9},{9,8},{10,11... | collective-permute-start | bytes 786440 | tf_op jit(solution)/shard_map/ppermute | solution.py:297
  37.6 5.4 %collective-permute-start.18 = (bf16[16,3072]{1,0:T(8,128)(2,1)S(1)}, bf16[16,3072]{1,0:T(8,128)(2,1)S(1)}, u32[]{:S(2)}, u32[]{:S(2)}) collective-permute-start(bf16[16,3072]{1,0:T(8,128)(2,1)S(1)} %slice.43), channel_id=1, source_target_pairs={{0,2},{1,3},{2,0},{3,1},{4,6},{5,7},{6,4},{7,5},{8,10},{9,11},{10,... | collective-permute-start | bytes 294920 | tf_op jit(solution)/shard_map/ppermute | solution.py:297
  39.1 6.0 %collective-permute-start.20 = (bf16[16,4096]{1,0:T(8,128)(2,1)S(1)}, bf16[16,4096]{1,0:T(8,128)(2,1)S(1)}, u32[]{:S(2)}, u32[]{:S(2)}) collective-permute-start(bf16[16,4096]{1,0:T(8,128)(2,1)S(1)} %slice.45), channel_id=1, source_target_pairs={{0,2},{1,3},{2,0},{3,1},{4,6},{5,7},{6,4},{7,5},{8,10},{9,11},{10,... | collective-permute-start | bytes 393224 | tf_op jit(solution)/shard_map/ppermute | solution.py:297
  45.3 6.4 %collective-permute-start.23 = (bf16[4,7168]{1,0:T(4,128)(2,1)S(1)}, bf16[4,7168]{1,0:T(4,128)(2,1)S(1)}, u32[]{:S(2)}, u32[]{:S(2)}) collective-permute-start(bf16[4,7168]{1,0:T(4,128)(2,1)S(1)} %get-tuple-element.42), channel_id=1, source_target_pairs={{0,12},{1,13},{2,14},{3,15},{4,8},{5,9},{6,10},{7,11},{8,4},{9,5},... | collective-permute-start | bytes 172040 | tf_op jit(solution)/shard_map/ppermute | solution.py:297
  48.7 5.1 %collective-permute-start.22 = (bf16[4,7168]{1,0:T(4,128)(2,1)S(1)}, bf16[4,7168]{1,0:T(4,128)(2,1)S(1)}, u32[]{:S(2)}, u32[]{:S(2)}) collective-permute-start(bf16[4,7168]{1,0:T(4,128)(2,1)S(1)} %get-tuple-element.43), channel_id=1, source_target_pairs={{0,8},{1,9},{2,10},{3,11},{4,12},{5,13},{6,14},{7,15},{8,0},{9,1},... | collective-permute-start | bytes 172040 | tf_op jit(solution)/shard_map/ppermute | solution.py:297
  48.7 5.1 %collective-permute-start.21 = (bf16[4,7168]{1,0:T(4,128)(2,1)S(1)}, bf16[4,7168]{1,0:T(4,128)(2,1)S(1)}, u32[]{:S(2)}, u32[]{:S(2)}) collective-permute-start(bf16[4,7168]{1,0:T(4,128)(2,1)S(1)} %get-tuple-element.41), channel_id=1, source_target_pairs={{0,4},{1,5},{2,6},{3,7},{4,0},{5,1},{6,2},{7,3},{8,12},{9,13},{10,... | collective-permute-start | bytes 172040 | tf_op jit(solution)/shard_map/ppermute | solution.py:297

commit v8 on v7

--- a/solution.py
+++ b/solution.py
@@ -109,19 +109,25 @@
 
 
 def attend_kernel(
-    piece_count, first_slot, heads, steps, kv_rank, scale,
+    piece_count, late, first_slot, heads, steps, kv_rank, scale,
     plan_ref, mine_ref, theirs_ref, *rest,
 ):
     pieces, rest = rest[:piece_count], rest[piece_count:]
-    out_ref, lse_ref, away_ref, scores, top, total, latent = rest
+    if late:
+        old_top, old_total, old_latent, out_ref, lse_ref, away_ref, scores, top, total, latent = rest
+    else:
+        top, total, latent, scores = rest
     row_block = mine_ref.shape[1]
     half = pieces[0].shape[0]
     requests = top.shape[0] - 1
     both = 2 * row_block
     block_rows = pieces[0].shape[2]
-    top[...] = jnp.full_like(top, -jnp.inf)
-    total[...] = jnp.zeros_like(total)
-    latent[...] = jnp.zeros_like(latent)
+    if late:
+        top[...] = old_top[...]
+    else:
+        top[...] = jnp.full_like(top, -jnp.inf)
+        total[...] = jnp.zeros_like(total)
+        latent[...] = jnp.zeros_like(latent)
     column = lax.broadcasted_iota(jnp.int32, (both, block_rows), 1)
     row = lax.broadcasted_iota(jnp.int32, (both, block_rows), 0)
     inside = column + (steps - 1 - (row % row_block) // heads) < block_rows
@@ -147,9 +153,18 @@
 
     def peak(r, _):
         top[r] = jnp.broadcast_to(jnp.max(top[r], axis=1, keepdims=True), (both, block_rows))
+        if late:
+            share = jnp.where(old_top[r] > -jnp.inf, jnp.exp(old_top[r] - top[r]), 0.0)
+            total[r] = old_total[r] * share
+            for c in range(kv_rank // LANES):
+                at = pl.ds(c * LANES, LANES)
+                latent[r, :, at] = old_latent[r, :, at] * share[:, :LANES]
         return 0
 
     lax.fori_loop(0, requests, peak, 0, unroll=batch)
+    if late:
+        total[requests] = jnp.zeros_like(total[requests])
+        latent[requests] = jnp.zeros_like(latent[requests])
 
     for k in range(slots):
         p = jnp.exp(scores[k] - jnp.concatenate([top[r] for r in users[k]], axis=0))
@@ -163,6 +178,8 @@
             total[users[k][i]] += p[i * both : (i + 1) * both]
             latent[users[k][i]] += mixed[i * both : (i + 1) * both]
 
+    if not late:
+        return
     lane = lax.broadcasted_iota(jnp.int32, (row_block, LANES), 1)
 
     def finish(r, _):
@@ -204,10 +221,9 @@
 
 
 def merge_kernel(
-    stages, heads, steps, order_ref, value_ref, weight_ref, *rest,
+    heads, steps, order_ref, value_ref, weight_ref, out_ref, lse_ref, other_ref,
+    away_ref, keep_ref, placed_ref, latent, head_rows,
 ):
-    outs, lses, others = rest[:stages], rest[stages : 2 * stages], rest[2 * stages : 3 * stages]
-    away_ref, keep_ref, placed_ref, latent, head_rows = rest[3 * stages :]
     kv_rank, v_width = value_ref.shape[1:]
     rows = head_rows.shape[0]
     requests = rows // steps
@@ -215,14 +231,13 @@
 
     def merge(i, _):
         at = pl.ds(pl.multiple_of(i * chunk, chunk), chunk)
-        parts = [(o[at], e[at][:, :1]) for o, e in zip(outs, lses)]
-        for other in others:
-            terms = jnp.sum(other[at, kv_rank:].astype(jnp.float32), axis=1, keepdims=True)
-            parts.append((other[at, :kv_rank].astype(jnp.float32), terms))
-        peak = functools.reduce(jnp.maximum, [e for _, e in parts])
-        shares = [jnp.exp(e - peak) for _, e in parts]
-        inverse = 1.0 / functools.reduce(jnp.add, shares)
-        whole = functools.reduce(jnp.add, [o * (w * inverse) for (o, _), w in zip(parts, shares)])
+        own, own_lse = out_ref[at], lse_ref[at][:, :1]
+        other_lse = jnp.sum(other_ref[at, kv_rank:].astype(jnp.float32), axis=1, keepdims=True)
+        peak = jnp.maximum(own_lse, other_lse)
+        share, other_share = jnp.exp(own_lse - peak), jnp.exp(other_lse - peak)
+        inverse = 1.0 / (share + other_share)
+        whole = own * (share * inverse)
+        whole += other_ref[at, :kv_rank].astype(jnp.float32) * (other_share * inverse)
         for c in range(kv_rank // LANES):
             latent[c, at] = whole[:, c * LANES : (c + 1) * LANES]
         return 0
@@ -327,36 +342,37 @@
         )(me, *map(pin, (q_heads, w_absorb, ctx_blocks, block_table, slots, owner)))
         return queries.reshape(requests, row_block, row_width), plan, order
 
-    def attend(plan, mine, theirs, pieces, stage):
+    both = 2 * row_block
+    state = [
+        jax.ShapeDtypeStruct((requests + 1, both, n), jnp.float32) for n in (block_rows, block_rows, kv_rank)
+    ]
+
+    def attend(plan, mine, theirs, pieces, earlier):
+        late = bool(earlier)
         slots = len(pieces) * half
-        first_slot = 0 if stage == 0 else piece_total * half - slots
-        both = 2 * row_block
+        results = [
+            jax.ShapeDtypeStruct((flat_rows, kv_rank), jnp.float32),
+            jax.ShapeDtypeStruct((flat_rows, LANES), jnp.float32),
+            jax.ShapeDtypeStruct((flat_rows, kv_rank + LANES), jnp.bfloat16),
+        ]
         return pl.pallas_call(
             functools.partial(
-                attend_kernel, len(pieces), first_slot, heads, steps, kv_rank,
-                float(head_width) ** -0.5,
+                attend_kernel, len(pieces), late, piece_total * half - slots if late else 0,
+                heads, steps, kv_rank, float(head_width) ** -0.5,
             ),
-            out_shape=(
-                jax.ShapeDtypeStruct((flat_rows, kv_rank), jnp.float32),
-                jax.ShapeDtypeStruct((flat_rows, LANES), jnp.float32),
-                jax.ShapeDtypeStruct((flat_rows, kv_rank + LANES), jnp.bfloat16),
-            ),
-            in_specs=[smem] + [vmem] * (2 + len(pieces)),
-            out_specs=(vmem,) * 3,
-            scratch_shapes=[
-                pltpu.VMEM((slots, 2 * both, block_rows), jnp.float32),
-                pltpu.VMEM((requests + 1, both, block_rows), jnp.float32),
-                pltpu.VMEM((requests + 1, both, block_rows), jnp.float32),
-                pltpu.VMEM((requests + 1, both, kv_rank), jnp.float32),
-            ],
+            out_shape=results if late else state,
+            in_specs=[smem] + [vmem] * (2 + len(pieces) + len(earlier)),
+            out_specs=[vmem] * 3,
+            scratch_shapes=[pltpu.VMEM((slots, 2 * both, block_rows), jnp.float32)]
+            + [pltpu.VMEM(x.shape, x.dtype) for x in state] * late,
             compiler_params=pltpu.CompilerParams(vmem_limit_bytes=28 * mebi),
             cost_estimate=pl.CostEstimate(
-                flops=COVER if stage == 1 else 2 * slots * 2 * both * block_rows * 2 * row_width,
+                flops=2 * slots * 2 * both * block_rows * 2 * row_width if late else COVER,
                 bytes_accessed=slots * block_rows * row_width * 2,
                 transcendentals=0,
             ),
             name="attend",
-        )(plan, mine, theirs, *pieces)
+        )(plan, mine, theirs, *pieces, *earlier)
 
     ring = ring_of(chips)
     up = [
@@ -385,23 +401,21 @@
             downs[0] = lax.ppermute(downs[0], "head", down)
             ups[1] = lax.ppermute(ups[1], "head", up)
             pieces += [ups[0], downs[1], downs[0], ups[1]]
-    early, late = pieces[:-LATE], pieces[-LATE:]
-    early_part = attend(plan, mine, theirs, early, 0)
-    late_part = attend(plan, mine, theirs, late, 1)
-    partial = [(out, lse, exchange(away, 1)) for out, lse, away in (early_part, late_part)]
+    sums = attend(plan, mine, theirs, pieces[:-LATE], ())
+    out, lse, away = attend(plan, mine, theirs, pieces[-LATE:], sums)
+    other = exchange(away, 1)
 
     part_rows = chips * steps
     widths = (FIRST * OUT_TILE, w_out.shape[1] - FIRST * OUT_TILE)
     parts = [jax.ShapeDtypeStruct((part_rows, n), jnp.bfloat16) for n in widths]
-    outs, lses, others = zip(*partial)
     away, keep, placed = pl.pallas_call(
-        functools.partial(merge_kernel, len(partial), heads, steps),
+        functools.partial(merge_kernel, heads, steps),
         out_shape=(
             parts[0],
             parts[0],
             jax.ShapeDtypeStruct((2 * part_rows, heads * v_width), jnp.bfloat16),
         ),
-        in_specs=[smem] + [vmem] * (2 + 3 * len(partial)),
+        in_specs=[smem] + [vmem] * 5,
         out_specs=(vmem,) * 3,
         scratch_shapes=[
             pltpu.VMEM((kv_rank // LANES, flat_rows, LANES), jnp.float32),
@@ -409,7 +423,7 @@
         ],
         compiler_params=pltpu.CompilerParams(vmem_limit_bytes=28 * mebi),
         name="merge_and_project",
-    )(order, w_value, w_out, *outs, *lses, *others)
+    )(order, w_value, w_out, out, lse, other)
     next_away, next_keep = pl.pallas_call(
         second_kernel,
         out_shape=(parts[1], parts[1]),
@@ -424,14 +438,12 @@
     first_half = add(keep, exchange(away, 1))
     second_half = add(next_keep, exchange(next_away, 1))
     result = jnp.concatenate([fold(first_half, 2), fold(second_half, 2)], axis=1)
-    distance = 4
+    distance = devices // 2
     while result.shape[0] > 4 * steps:
         result = fold(result, distance)
-        distance *= 2
+        distance //= 2
     ways = result.shape[0] // steps
-    received = [
-        exchange(result[k * steps : (k + 1) * steps], distance * k) for k in range(1, ways)
-    ]
+    received = [exchange(result[k * steps : (k + 1) * steps], 4 * k) for k in reversed(range(1, ways))]
     return add(result[:steps], *received)
 
 

time: 54.7 us -> 54.5 us (level)
  waiting for transfers between devices: 19.1 us -> 20.2 us
  starting transfers between devices: 23 us -> 22.3 us
    ppermute x10 -> x9, waiting for transfers between devices: 10.6 us -> 11.5 us  [exchange(): return lax.ppermute(x, 'head', [(i, i ^ distance) for i in range(devices)])]
    ppermute x10 -> x9, starting transfers between devices: 7.79 us -> 7.11 us  [exchange(): return lax.ppermute(x, 'head', [(i, i ^ distance) for i in range(devices)])]
  transfers between devices with their start and end apart: 24 -> 23, of which waited for: 11 -> 12; matrix products, arithmetic and copies ran while one was open for 0% -> 0% of each run, Pallas kernels for 14% -> 11%
where the time goes in v8:
time: 54.5 us; the launch traced here: 54.4 us
  starting transfers between devices  22.3 us (41%)
  waiting for transfers between devices  20.2 us (37%)
  Pallas kernels  9.64 us (18%)
  local copies, waits for them, and re-layouts  1.05 us (2%)
  other arithmetic  0.93 us (2%)
    ppermute x9, waiting for transfers between devices, exchange(): return lax.ppermute(x, 'head', [(i, i ^ distance) for i in range(devices)])  11.5 us
    ppermute x4, starting transfers between devices, local(): ups[0] = lax.ppermute(ups[0], 'head', up)  8.28 us
    ppermute x9, starting transfers between devices, exchange(): return lax.ppermute(x, 'head', [(i, i ^ distance) for i in range(devices)])  7.11 us
    ppermute x3, waiting for transfers between devices, local(): downs[0] = lax.ppermute(downs[0], 'head', down)  5.72 us
    ppermute x3, starting transfers between devices, local(): ups[1] = lax.ppermute(ups[1], 'head', up)  3.88 us
    pallas_call x2, Pallas kernels, attend(): pl.pallas_call(functools.partial(attend_kernel, len(pieces), late, piece_...  3.76 us
    pallas_call x1, Pallas kernels, prepare(): pl.pallas_call(functools.partial(prepare_kernel, heads, chips), out_shape...  2.27 us
    ppermute x3, starting transfers between devices, local(): downs[0] = lax.ppermute(downs[0], 'head', down)  2.22 us
  transfers between devices with their start and end apart: 23, of which 12 were waited for; matrix products, arithmetic and copies ran while one was open for 0% of the time, Pallas kernels for 11%

profile of v8, /device:TPU:0, one launch (start us, length us, event | category | flops | bytes accessed | tf_op | source)
XLA Modules:
  0.0 54.4 jit_solution(3115071561577206691)
XLA Ops:
  0.0 1.0 %fusion.3 = (bf16[1,576,128]{2,1,0:T(8,128)(2,1)S(1)}, bf16[1,576,128]{2,1,0:T(8,128)(2,1)S(1)}) fusion(bf16[2,576,128]{2,1,0:T(8,128)(2,1)} %bitcast.8), kind=kLoop, calls=%fused_computation.15 | loop fusion | bytes 589824 | tf_op jit(solution)/shard_map/slice | solution.py:385
  1.0 3.1 %collective-permute-start = (bf16[1,576,128]{2,1,0:T(8,128)(2,1)S(1)}, bf16[1,576,128]{2,1,0:T(8,128)(2,1)S(1)}, u32[]{:S(2)}, u32[]{:S(2)}) collective-permute-start(bf16[1,576,128]{2,1,0:T(8,128)(2,1)S(1)} %get-tuple-element.40.rest_0_), channel_id=1, source_target_pairs={{0,4},{1,5},{4,8},{5,9},{8,12},{9,13},{12,14},{13,15},{14,10},{15,... | collective-permute-start | bytes 442376 | tf_op jit(solution)/shard_map/ppermute | solution.py:399
  4.1 0.0 collective-permute-start.11
  4.1 2.0 %collective-permute-start.2 = (bf16[1,576,128]{2,1,0:T(8,128)(2,1)S(1)}, bf16[1,576,128]{2,1,0:T(8,128)(2,1)S(1)}, u32[]{:S(2)}, u32[]{:S(2)}) collective-permute-start(bf16[1,576,128]{2,1,0:T(8,128)(2,1)S(1)} %get-tuple-element.40.rest_0_), channel_id=1, source_target_pairs={{4,0},{5,1},{8,4},{9,5},{12,8},{13,9},{14,12},{15,13},{10,14},{11,... | collective-permute-start | bytes 442376 | tf_op jit(solution)/shard_map/ppermute | solution.py:401
  6.1 0.1 collective-permute-start.5
  6.1 2.3 %prepare.1 = (bf16[256,576]{1,0:T(8,128)(2,1)S(1)}, s32[34]{0:T(128)S(1)}, s32[8]{0:T(128)S(1)}) custom-call(s32[1]{0:T(128)} %bitcast.me_ref, bf16[32,1536]{1,0:T(8,128)(2,1)} %query_hbm.1, bf16[8,128,512]{2,1,0:T(8,128)(2,1)} %absorb_hbm.1, s32[8]{0:T(128)} %length_hbm.1, s32[8,8]{1,0:T(8,128)} %table_hbm.1, s32[16,32]{1,0:T(8,128)} %constant.6.clone.slot_hbm, ...), custom_call_target="tpu_custom_call" | custom-call | flops 33554432 | bytes 2097152 | tf_op jit(solution)/shard_map/prepare/pallas_call | solution.py:318
  8.4 0.0 slice-start
  8.4 0.0 slice-start.1
  8.4 0.0 slice-start.2
  8.5 0.0 copy-start
  8.5 2.4 %collective-permute-start.8 = (bf16[1,576,128]{2,1,0:T(8,128)(2,1)S(1)}, bf16[1,576,128]{2,1,0:T(8,128)(2,1)S(1)}, u32[]{:S(2)}, u32[]{:S(2)}) collective-permute-start(bf16[1,576,128]{2,1,0:T(8,128)(2,1)S(1)} %collective-permute-done.rest_2_), channel_id=1, source_target_pairs={{0,4},{1,5},{4,8},{5,9},{8,12},{9,13},{12,14},{13,15},{14,10},{15,... | collective-permute-start | bytes 442376 | tf_op jit(solution)/shard_map/ppermute | solution.py:399
  10.9 0.0 collective-permute-start.12
  10.9 0.0 collective-permute-start.1
  10.9 2.6 %collective-permute-done.2.rest_4_ = bf16[1,576,128]{2,1,0:T(8,128)(2,1)S(1)} collective-permute-done((bf16[1,576,128]{2,1,0:T(8,128)(2,1)S(1)}, bf16[1,576,128]{2,1,0:T(8,128)(2,1)S(1)}, u32[]{:S(2)}, u32[]{:S(2)}) %collective-permute-start.2) | collective-permute-done | bytes 147488 | tf_op jit(solution)/shard_map/ppermute | solution.py:401
  13.5 0.3 collective-permute-start.3
  13.7 0.0 collective-permute-done.5.rest_5_
  13.7 1.8 %collective-permute-start.6 = (bf16[1,576,128]{2,1,0:T(8,128)(2,1)S(1)}, bf16[1,576,128]{2,1,0:T(8,128)(2,1)S(1)}, u32[]{:S(2)}, u32[]{:S(2)}) collective-permute-start(bf16[1,576,128]{2,1,0:T(8,128)(2,1)S(1)} %collective-permute-done.5.rest_5_), channel_id=1, source_target_pairs={{0,4},{1,5},{4,8},{5,9},{8,12},{9,13},{12,14},{13,15},{14,10},{15,... | collective-permute-start | bytes 442376 | tf_op jit(solution)/shard_map/ppermute | solution.py:402
  15.5 1.6 %collective-permute-start.9 = (bf16[1,576,128]{2,1,0:T(8,128)(2,1)S(1)}, bf16[1,576,128]{2,1,0:T(8,128)(2,1)S(1)}, u32[]{:S(2)}, u32[]{:S(2)}) collective-permute-start(bf16[1,576,128]{2,1,0:T(8,128)(2,1)S(1)} %collective-permute-done.8.rest_6_), channel_id=1, source_target_pairs={{0,4},{1,5},{4,8},{5,9},{8,12},{9,13},{12,14},{13,15},{14,10},{15,... | collective-permute-start | bytes 442376 | tf_op jit(solution)/shard_map/ppermute | solution.py:399
  17.1 0.5 collective-permute-done.12.rest_7_
  17.6 0.0 collective-permute-start.13
  17.6 3.2 %collective-permute-done.3.rest_8_ = bf16[1,576,128]{2,1,0:T(8,128)(2,1)S(1)} collective-permute-done((bf16[1,576,128]{2,1,0:T(8,128)(2,1)S(1)}, bf16[1,576,128]{2,1,0:T(8,128)(2,1)S(1)}, u32[]{:S(2)}, u32[]{:S(2)}) %collective-permute-start.3) | collective-permute-done | bytes 147488 | tf_op jit(solution)/shard_map/ppermute | solution.py:401
  20.8 2.0 %collective-permute-start.7 = (bf16[1,576,128]{2,1,0:T(8,128)(2,1)S(1)}, bf16[1,576,128]{2,1,0:T(8,128)(2,1)S(1)}, u32[]{:S(2)}, u32[]{:S(2)}) collective-permute-start(bf16[1,576,128]{2,1,0:T(8,128)(2,1)S(1)} %collective-permute-done.6.rest_9_), channel_id=1, source_target_pairs={{0,4},{1,5},{4,8},{5,9},{8,12},{9,13},{12,14},{13,15},{14,10},{15,... | collective-permute-start | bytes 442376 | tf_op jit(solution)/shard_map/ppermute | solution.py:402
  22.8 0.4 collective-permute-done.9.rest_10_
  23.2 1.2 %collective-permute-start.10 = (bf16[1,576,128]{2,1,0:T(8,128)(2,1)S(1)}, bf16[1,576,128]{2,1,0:T(8,128)(2,1)S(1)}, u32[]{:S(2)}, u32[]{:S(2)}) collective-permute-start(bf16[1,576,128]{2,1,0:T(8,128)(2,1)S(1)} %collective-permute-done.9.rest_10_), channel_id=1, source_target_pairs={{0,4},{1,5},{4,8},{5,9},{8,12},{9,13},{12,14},{13,15},{14,10},{15,... | collective-permute-start | bytes 442376 | tf_op jit(solution)/shard_map/ppermute | solution.py:395
  24.4 0.8 %collective-permute-start.14 = (bf16[1,576,128]{2,1,0:T(8,128)(2,1)S(1)}, bf16[1,576,128]{2,1,0:T(8,128)(2,1)S(1)}, u32[]{:S(2)}, u32[]{:S(2)}) collective-permute-start(bf16[1,576,128]{2,1,0:T(8,128)(2,1)S(1)} %collective-permute-done.13.rest_11_), channel_id=1, source_target_pairs={{4,0},{5,1},{8,4},{9,5},{12,8},{13,9},{14,12},{15,13},{10,14},{11,... | collective-permute-start | bytes 442376 | tf_op jit(solution)/shard_map/ppermute | solution.py:396
  25.2 2.2 %attend.2 = (f32[9,64,128]{2,1,0:T(8,128)S(1)}, f32[9,64,128]{2,1,0:T(8,128)S(1)}, f32[9,64,512]{2,1,0:T(8,128)S(1)}) custom-call(s32[34]{0:T(128)S(1)} %get-tuple-element.25.plan_ref, bf16[8,32,576]{2,1,0:T(8,128)(2,1)S(1)} %bitcast.6, bf16[8,32,576]{2,1,0:T(8,128)(2,1)S(1)} %collective-permute-done.1.theirs_ref, ...), custom_call_target="tpu_custom_call" | custom-call | flops 30000001024 | bytes 1769472 | tf_op jit(solution)/shard_map/attend/pallas_call | solution.py:358
  27.4 0.9 %collective-permute-done.10.rest_2_ = bf16[1,576,128]{2,1,0:T(8,128)(2,1)S(1)} collective-permute-done((bf16[1,576,128]{2,1,0:T(8,128)(2,1)S(1)}, bf16[1,576,128]{2,1,0:T(8,128)(2,1)S(1)}, u32[]{:S(2)}, u32[]{:S(2)}) %collective-permute-start.10) | collective-permute-done | bytes 147488 | tf_op jit(solution)/shard_map/ppermute | solution.py:395
  28.3 1.2 %collective-permute-done.14.rest_3_ = bf16[1,576,128]{2,1,0:T(8,128)(2,1)S(1)} collective-permute-done((bf16[1,576,128]{2,1,0:T(8,128)(2,1)S(1)}, bf16[1,576,128]{2,1,0:T(8,128)(2,1)S(1)}, u32[]{:S(2)}, u32[]{:S(2)}) %collective-permute-start.14) | collective-permute-done | bytes 147488 | tf_op jit(solution)/shard_map/ppermute | solution.py:396
  29.5 1.6 %attend.3 = (f32[256,512]{1,0:T(8,128)S(1)}, f32[256,128]{1,0:T(8,128)S(1)}, bf16[256,640]{1,0:T(8,128)(2,1)S(1)}) custom-call(s32[34]{0:T(128)S(1)} %get-tuple-element.25.plan_ref, bf16[8,32,576]{2,1,0:T(8,128)(2,1)S(1)} %bitcast.7, bf16[8,32,576]{2,1,0:T(8,128)(2,1)S(1)} %collective-permute-done.1.theirs_ref, ...), custom_call_target="tpu_custom_call" | custom-call | flops 150994944 | bytes 589824 | tf_op jit(solution)/shard_map/attend/pallas_call | solution.py:358
  31.1 0.1 collective-permute-start.15
  31.2 1.6 %collective-permute-done.15.other_ref = bf16[256,640]{1,0:T(8,128)(2,1)S(1)} collective-permute-done((bf16[256,640]{1,0:T(8,128)(2,1)S(1)}, bf16[256,640]{1,0:T(8,128)(2,1)S(1)}, u32[]{:S(2)}, u32[]{:S(2)}) %collective-permute-start.15) | collective-permute-done | bytes 327712 | tf_op jit(solution)/shard_map/ppermute | solution.py:312
  32.9 2.1 %merge_and_project.1 = (bf16[32,3072]{1,0:T(8,128)(2,1)S(1)}, bf16[32,3072]{1,0:T(8,128)(2,1)S(1)}, bf16[64,1024]{1,0:T(8,128)(2,1)S(1)}) custom-call(s32[8]{0:T(128)S(1)} %get-tuple-element.22.order_ref, bf16[8,512,128]{2,1,0:T(8,128)(2,1)S(1)} %copy-done, bf16[1024,7168]{1,0:T(8,128)(2,1)S(1)} %bitcast.4, f32[256,512]{1,0:T(8,128)S(1)} %get-tuple-element.31.out_ref, ...), custom_call_target="tpu_custom_call" | custom-call | tf_op jit(solution)/shard_map/merge_and_project/pallas_call | solution.py:411
  34.9 0.2 collective-permute-start.16
  35.1 1.6 %project_second.1 = (bf16[32,4096]{1,0:T(8,128)(2,1)S(1)}, bf16[32,4096]{1,0:T(8,128)(2,1)S(1)}) custom-call(bf16[64,1024]{1,0:T(8,128)(2,1)S(1)} %get-tuple-element.36.placed_ref, bf16[1024,7168]{1,0:T(8,128)(2,1)S(1)} %bitcast.4), custom_call_target="tpu_custom_call" | custom-call | flops 469762048 | bytes 7340032 | tf_op jit(solution)/shard_map/project_second/pallas_call | solution.py:427
  36.7 0.4 collective-permute-start.18
  37.2 0.1 add_convert_fusion.1
  37.2 0.9 %collective-permute-start.17 = (bf16[16,3072]{1,0:T(8,128)(2,1)S(1)}, bf16[16,3072]{1,0:T(8,128)(2,1)S(1)}, u32[]{:S(2)}, u32[]{:S(2)}) collective-permute-start(bf16[16,3072]{1,0:T(8,128)(2,1)S(1)} %slice.43), channel_id=1, source_target_pairs={{0,2},{1,3},{2,0},{3,1},{4,6},{5,7},{6,4},{7,5},{8,10},{9,11},{10,... | collective-permute-start | bytes 294920 | tf_op jit(solution)/shard_map/ppermute | solution.py:312
  38.1 0.2 collective-permute-done.18
  38.3 0.1 add_convert_fusion
  38.4 1.1 %collective-permute-start.19 = (bf16[16,4096]{1,0:T(8,128)(2,1)S(1)}, bf16[16,4096]{1,0:T(8,128)(2,1)S(1)}, u32[]{:S(2)}, u32[]{:S(2)}) collective-permute-start(bf16[16,4096]{1,0:T(8,128)(2,1)S(1)} %slice.45), channel_id=1, source_target_pairs={{0,2},{1,3},{2,0},{3,1},{4,6},{5,7},{6,4},{7,5},{8,10},{9,11},{10,... | collective-permute-start | bytes 393224 | tf_op jit(solution)/shard_map/ppermute | solution.py:312
  39.5 3.4 %collective-permute-done.17 = bf16[16,3072]{1,0:T(8,128)(2,1)S(1)} collective-permute-done((bf16[16,3072]{1,0:T(8,128)(2,1)S(1)}, bf16[16,3072]{1,0:T(8,128)(2,1)S(1)}, u32[]{:S(2)}, u32[]{:S(2)}) %collective-permute-start.17) | collective-permute-done | bytes 98336 | tf_op jit(solution)/shard_map/ppermute | solution.py:312
  42.9 2.0 %collective-permute-done.19 = bf16[16,4096]{1,0:T(8,128)(2,1)S(1)} collective-permute-done((bf16[16,4096]{1,0:T(8,128)(2,1)S(1)}, bf16[16,4096]{1,0:T(8,128)(2,1)S(1)}, u32[]{:S(2)}, u32[]{:S(2)}) %collective-permute-start.19) | collective-permute-done | bytes 131104 | tf_op jit(solution)/shard_map/ppermute | solution.py:312
  45.0 0.1 fusion.2
  45.0 3.6 %collective-permute-start.20 = (bf16[4,7168]{1,0:T(4,128)(2,1)S(1)}, bf16[4,7168]{1,0:T(4,128)(2,1)S(1)}, u32[]{:S(2)}, u32[]{:S(2)}) collective-permute-start(bf16[4,7168]{1,0:T(4,128)(2,1)S(1)} %get-tuple-element.41), channel_id=1, source_target_pairs={{0,12},{1,13},{2,14},{3,15},{4,8},{5,9},{6,10},{7,11},{8,4},{9,5},... | collective-permute-start | bytes 172040 | tf_op jit(solution)/shard_map/ppermute | solution.py:312
  48.6 0.9 %collective-permute-start.22 = (bf16[4,7168]{1,0:T(4,128)(2,1)S(1)}, bf16[4,7168]{1,0:T(4,128)(2,1)S(1)}, u32[]{:S(2)}, u32[]{:S(2)}) collective-permute-start(bf16[4,7168]{1,0:T(4,128)(2,1)S(1)} %get-tuple-element.42), channel_id=1, source_target_pairs={{0,4},{1,5},{2,6},{3,7},{4,0},{5,1},{6,2},{7,3},{8,12},{9,13},{10,... | collective-permute-start | bytes 172040 | tf_op jit(solution)/shard_map/ppermute | solution.py:312
  49.5 2.0 %collective-permute-done.20 = bf16[4,7168]{1,0:T(4,128)(2,1)S(1)} collective-permute-done((bf16[4,7168]{1,0:T(4,128)(2,1)S(1)}, bf16[4,7168]{1,0:T(4,128)(2,1)S(1)}, u32[]{:S(2)}, u32[]{:S(2)}) %collective-permute-start.20) | collective-permute-done | bytes 57376 | tf_op jit(solution)/shard_map/ppermute | solution.py:312
  51.5 2.2 %collective-permute-done.21 = bf16[4,7168]{1,0:T(4,128)(2,1)S(1)} collective-permute-done((bf16[4,7168]{1,0:T(4,128)(2,1)S(1)}, bf16[4,7168]{1,0:T(4,128)(2,1)S(1)}, u32[]{:S(2)}, u32[]{:S(2)}) %collective-permute-start.21) | collective-permute-done | bytes 57376 | tf_op jit(solution)/shard_map/ppermute | solution.py:312
  53.7 0.7 %add_convert_fusion.4 = bf16[4,7168]{1,0:T(4,128)(2,1)} fusion(bf16[4,7168]{1,0:T(4,128)(2,1)S(1)} %collective-permute-done.22, bf16[4,7168]{1,0:T(4,128)(2,1)S(1)} %collective-permute-done.21, bf16[4,7168]{1,0:T(4,128)(2,1)S(1)} %collective-permute-done.20, bf16[16,4096]{1,0:T(8,128)(2,1)S(1)} %add_convert_fusion.2, bf16[16,3072]{1,0:T(8,128)(2,1)S(1)} %add_convert_fusion.3), kind=kLoop, calls=%fused_computation.10 | loop fusion | flops 315392 | bytes 458752 | tf_op jit(solution)/shard_map/convert_element_type | solution.py:305
  (23 shorter events, 0.1 us)
Async XLA Ops:
  1.0 7.4 %collective-permute-start = (bf16[1,576,128]{2,1,0:T(8,128)(2,1)S(1)}, bf16[1,576,128]{2,1,0:T(8,128)(2,1)S(1)}, u32[]{:S(2)}, u32[]{:S(2)}) collective-permute-start(bf16[1,576,128]{2,1,0:T(8,128)(2,1)S(1)} %get-tuple-element.40.rest_0_), channel_id=1, source_target_pairs={{0,4},{1,5},{4,8},{5,9},{8,12},{9,13},{12,14},{13,15},{14,10},{15,... | collective-permute-start | bytes 442376 | tf_op jit(solution)/shard_map/ppermute | solution.py:399
  4.1 6.8 %collective-permute-start.11 = (bf16[1,576,128]{2,1,0:T(8,128)(2,1)S(1)}, bf16[1,576,128]{2,1,0:T(8,128)(2,1)S(1)}, u32[]{:S(2)}, u32[]{:S(2)}) collective-permute-start(bf16[1,576,128]{2,1,0:T(8,128)(2,1)S(1)} %get-tuple-element.39.rest_1_), channel_id=1, source_target_pairs={{4,0},{5,1},{8,4},{9,5},{12,8},{13,9},{14,12},{15,13},{10,14},{11,... | collective-permute-start | bytes 442376 | tf_op jit(solution)/shard_map/ppermute | solution.py:400
  4.1 9.4 %collective-permute-start.2 = (bf16[1,576,128]{2,1,0:T(8,128)(2,1)S(1)}, bf16[1,576,128]{2,1,0:T(8,128)(2,1)S(1)}, u32[]{:S(2)}, u32[]{:S(2)}) collective-permute-start(bf16[1,576,128]{2,1,0:T(8,128)(2,1)S(1)} %get-tuple-element.40.rest_0_), channel_id=1, source_target_pairs={{4,0},{5,1},{8,4},{9,5},{12,8},{13,9},{14,12},{15,13},{10,14},{11,... | collective-permute-start | bytes 442376 | tf_op jit(solution)/shard_map/ppermute | solution.py:401
  6.1 7.7 %collective-permute-start.5 = (bf16[1,576,128]{2,1,0:T(8,128)(2,1)S(1)}, bf16[1,576,128]{2,1,0:T(8,128)(2,1)S(1)}, u32[]{:S(2)}, u32[]{:S(2)}) collective-permute-start(bf16[1,576,128]{2,1,0:T(8,128)(2,1)S(1)} %get-tuple-element.39.rest_1_), channel_id=1, source_target_pairs={{0,4},{1,5},{4,8},{5,9},{8,12},{9,13},{12,14},{13,15},{14,10},{15,... | collective-permute-start | bytes 442376 | tf_op jit(solution)/shard_map/ppermute | solution.py:402
  8.4 24.4 %slice-start = ((s8[14680064]{0:T(1024)(128)(4,1)}), s8[4194304]{0:T(1024)(128)(4,1)S(1)}, s32[]{:S(2)}) async-start(s8[14680064]{0:T(1024)(128)(4,1)} %bitcast.3), calls=%async_computation | async-start | bytes 8388608
  8.4 24.4 %slice-start.1 = ((s8[14680064]{0:T(1024)(128)(4,1)}), s8[4194304]{0:T(1024)(128)(4,1)S(1)}, s32[]{:S(2)}) async-start(s8[14680064]{0:T(1024)(128)(4,1)} %bitcast.3), calls=%async_computation.1 | async-start | bytes 8388608
  8.4 24.4 %slice-start.2 = ((s8[14680064]{0:T(1024)(128)(4,1)}), s8[4194304]{0:T(1024)(128)(4,1)S(1)}, s32[]{:S(2)}) async-start(s8[14680064]{0:T(1024)(128)(4,1)} %bitcast.3), calls=%async_computation.2 | async-start | bytes 8388608
  8.5 24.4 %slice-start.3 = ((s8[14680064]{0:T(1024)(128)(4,1)}), s8[2097152]{0:T(1024)(128)(4,1)S(1)}, s32[]{:S(2)}) async-start(s8[14680064]{0:T(1024)(128)(4,1)} %bitcast.3), calls=%async_computation.3 | async-start | bytes 4194304
  8.5 24.4 %copy-start = (bf16[8,512,128]{2,1,0:T(8,128)(2,1)S(1)}, bf16[8,512,128]{2,1,0:T(8,128)(2,1)}, u32[]{:S(2)}) copy-start(bf16[8,512,128]{2,1,0:T(8,128)(2,1)} %value_ref.1) | copy-start | bytes 3145732
  8.5 7.0 %collective-permute-start.8 = (bf16[1,576,128]{2,1,0:T(8,128)(2,1)S(1)}, bf16[1,576,128]{2,1,0:T(8,128)(2,1)S(1)}, u32[]{:S(2)}, u32[]{:S(2)}) collective-permute-start(bf16[1,576,128]{2,1,0:T(8,128)(2,1)S(1)} %collective-permute-done.rest_2_), channel_id=1, source_target_pairs={{0,4},{1,5},{4,8},{5,9},{8,12},{9,13},{12,14},{13,15},{14,10},{15,... | collective-permute-start | bytes 442376 | tf_op jit(solution)/shard_map/ppermute | solution.py:399
  10.9 6.7 %collective-permute-start.12 = (bf16[1,576,128]{2,1,0:T(8,128)(2,1)S(1)}, bf16[1,576,128]{2,1,0:T(8,128)(2,1)S(1)}, u32[]{:S(2)}, u32[]{:S(2)}) collective-permute-start(bf16[1,576,128]{2,1,0:T(8,128)(2,1)S(1)} %collective-permute-done.11.rest_3_), channel_id=1, source_target_pairs={{4,0},{5,1},{8,4},{9,5},{12,8},{13,9},{14,12},{15,13},{10,14},{11,... | collective-permute-start | bytes 442376 | tf_op jit(solution)/shard_map/ppermute | solution.py:400
  10.9 14.3 %collective-permute-start.1 = (bf16[8,32,576]{2,1,0:T(8,128)(2,1)S(1)}, bf16[8,32,576]{2,1,0:T(8,128)(2,1)S(1)}, u32[]{:S(2)}, u32[]{:S(2)}) collective-permute-start(bf16[8,32,576]{2,1,0:T(8,128)(2,1)S(1)} %bitcast.5), channel_id=1, source_target_pairs={{0,1},{1,0},{2,3},{3,2},{4,5},{5,4},{6,7},{7,6},{8,9},{9,8},{10,11... | collective-permute-start | bytes 884744 | tf_op jit(solution)/shard_map/ppermute | solution.py:312
  13.5 7.3 %collective-permute-start.3 = (bf16[1,576,128]{2,1,0:T(8,128)(2,1)S(1)}, bf16[1,576,128]{2,1,0:T(8,128)(2,1)S(1)}, u32[]{:S(2)}, u32[]{:S(2)}) collective-permute-start(bf16[1,576,128]{2,1,0:T(8,128)(2,1)S(1)} %collective-permute-done.2.rest_4_), channel_id=1, source_target_pairs={{4,0},{5,1},{8,4},{9,5},{12,8},{13,9},{14,12},{15,13},{10,14},{11,... | collective-permute-start | bytes 442376 | tf_op jit(solution)/shard_map/ppermute | solution.py:401
  13.7 7.0 %collective-permute-start.6 = (bf16[1,576,128]{2,1,0:T(8,128)(2,1)S(1)}, bf16[1,576,128]{2,1,0:T(8,128)(2,1)S(1)}, u32[]{:S(2)}, u32[]{:S(2)}) collective-permute-start(bf16[1,576,128]{2,1,0:T(8,128)(2,1)S(1)} %collective-permute-done.5.rest_5_), channel_id=1, source_target_pairs={{0,4},{1,5},{4,8},{5,9},{8,12},{9,13},{12,14},{13,15},{14,10},{15,... | collective-permute-start | bytes 442376 | tf_op jit(solution)/shard_map/ppermute | solution.py:402
  15.5 7.7 %collective-permute-start.9 = (bf16[1,576,128]{2,1,0:T(8,128)(2,1)S(1)}, bf16[1,576,128]{2,1,0:T(8,128)(2,1)S(1)}, u32[]{:S(2)}, u32[]{:S(2)}) collective-permute-start(bf16[1,576,128]{2,1,0:T(8,128)(2,1)S(1)} %collective-permute-done.8.rest_6_), channel_id=1, source_target_pairs={{0,4},{1,5},{4,8},{5,9},{8,12},{9,13},{12,14},{13,15},{14,10},{15,... | collective-permute-start | bytes 442376 | tf_op jit(solution)/shard_map/ppermute | solution.py:399
  17.6 6.8 %collective-permute-start.13 = (bf16[1,576,128]{2,1,0:T(8,128)(2,1)S(1)}, bf16[1,576,128]{2,1,0:T(8,128)(2,1)S(1)}, u32[]{:S(2)}, u32[]{:S(2)}) collective-permute-start(bf16[1,576,128]{2,1,0:T(8,128)(2,1)S(1)} %collective-permute-done.12.rest_7_), channel_id=1, source_target_pairs={{4,0},{5,1},{8,4},{9,5},{12,8},{13,9},{14,12},{15,13},{10,14},{11,... | collective-permute-start | bytes 442376 | tf_op jit(solution)/shard_map/ppermute | solution.py:400
  20.8 6.6 %collective-permute-start.4 = (bf16[1,576,128]{2,1,0:T(8,128)(2,1)S(1)}, bf16[1,576,128]{2,1,0:T(8,128)(2,1)S(1)}, u32[]{:S(2)}, u32[]{:S(2)}) collective-permute-start(bf16[1,576,128]{2,1,0:T(8,128)(2,1)S(1)} %collective-permute-done.3.rest_8_), channel_id=1, source_target_pairs={{4,0},{5,1},{8,4},{9,5},{12,8},{13,9},{14,12},{15,13},{10,14},{11,... | collective-permute-start | bytes 442376 | tf_op jit(solution)/shard_map/ppermute | solution.py:401
  20.8 6.6 %collective-permute-start.7 = (bf16[1,576,128]{2,1,0:T(8,128)(2,1)S(1)}, bf16[1,576,128]{2,1,0:T(8,128)(2,1)S(1)}, u32[]{:S(2)}, u32[]{:S(2)}) collective-permute-start(bf16[1,576,128]{2,1,0:T(8,128)(2,1)S(1)} %collective-permute-done.6.rest_9_), channel_id=1, source_target_pairs={{0,4},{1,5},{4,8},{5,9},{8,12},{9,13},{12,14},{13,15},{14,10},{15,... | collective-permute-start | bytes 442376 | tf_op jit(solution)/shard_map/ppermute | solution.py:402
  23.2 5.1 %collective-permute-start.10 = (bf16[1,576,128]{2,1,0:T(8,128)(2,1)S(1)}, bf16[1,576,128]{2,1,0:T(8,128)(2,1)S(1)}, u32[]{:S(2)}, u32[]{:S(2)}) collective-permute-start(bf16[1,576,128]{2,1,0:T(8,128)(2,1)S(1)} %collective-permute-done.9.rest_10_), channel_id=1, source_target_pairs={{0,4},{1,5},{4,8},{5,9},{8,12},{9,13},{12,14},{13,15},{14,10},{15,... | collective-permute-start | bytes 442376 | tf_op jit(solution)/shard_map/ppermute | solution.py:395
  24.4 5.1 %collective-permute-start.14 = (bf16[1,576,128]{2,1,0:T(8,128)(2,1)S(1)}, bf16[1,576,128]{2,1,0:T(8,128)(2,1)S(1)}, u32[]{:S(2)}, u32[]{:S(2)}) collective-permute-start(bf16[1,576,128]{2,1,0:T(8,128)(2,1)S(1)} %collective-permute-done.13.rest_11_), channel_id=1, source_target_pairs={{4,0},{5,1},{8,4},{9,5},{12,8},{13,9},{14,12},{15,13},{10,14},{11,... | collective-permute-start | bytes 442376 | tf_op jit(solution)/shard_map/ppermute | solution.py:396
  31.1 1.7 %collective-permute-start.15 = (bf16[256,640]{1,0:T(8,128)(2,1)S(1)}, bf16[256,640]{1,0:T(8,128)(2,1)S(1)}, u32[]{:S(2)}, u32[]{:S(2)}) collective-permute-start(bf16[256,640]{1,0:T(8,128)(2,1)S(1)} %get-tuple-element.33), channel_id=1, source_target_pairs={{0,1},{1,0},{2,3},{3,2},{4,5},{5,4},{6,7},{7,6},{8,9},{9,8},{10,11... | collective-permute-start | bytes 983048 | tf_op jit(solution)/shard_map/ppermute | solution.py:312
  34.9 2.2 %collective-permute-start.16 = (bf16[32,3072]{1,0:T(8,128)(2,1)S(1)}, bf16[32,3072]{1,0:T(8,128)(2,1)S(1)}, u32[]{:S(2)}, u32[]{:S(2)}) collective-permute-start(bf16[32,3072]{1,0:T(8,128)(2,1)S(1)} %get-tuple-element.35), channel_id=1, source_target_pairs={{0,1},{1,0},{2,3},{3,2},{4,5},{5,4},{6,7},{7,6},{8,9},{9,8},{10,11... | collective-permute-start | bytes 589832 | tf_op jit(solution)/shard_map/ppermute | solution.py:312
  36.7 1.6 %collective-permute-start.18 = (bf16[32,4096]{1,0:T(8,128)(2,1)S(1)}, bf16[32,4096]{1,0:T(8,128)(2,1)S(1)}, u32[]{:S(2)}, u32[]{:S(2)}) collective-permute-start(bf16[32,4096]{1,0:T(8,128)(2,1)S(1)} %get-tuple-element.38), channel_id=1, source_target_pairs={{0,1},{1,0},{2,3},{3,2},{4,5},{5,4},{6,7},{7,6},{8,9},{9,8},{10,11... | collective-permute-start | bytes 786440 | tf_op jit(solution)/shard_map/ppermute | solution.py:312
  37.2 5.6 %collective-permute-start.17 = (bf16[16,3072]{1,0:T(8,128)(2,1)S(1)}, bf16[16,3072]{1,0:T(8,128)(2,1)S(1)}, u32[]{:S(2)}, u32[]{:S(2)}) collective-permute-start(bf16[16,3072]{1,0:T(8,128)(2,1)S(1)} %slice.43), channel_id=1, source_target_pairs={{0,2},{1,3},{2,0},{3,1},{4,6},{5,7},{6,4},{7,5},{8,10},{9,11},{10,... | collective-permute-start | bytes 294920 | tf_op jit(solution)/shard_map/ppermute | solution.py:312
  38.4 6.5 %collective-permute-start.19 = (bf16[16,4096]{1,0:T(8,128)(2,1)S(1)}, bf16[16,4096]{1,0:T(8,128)(2,1)S(1)}, u32[]{:S(2)}, u32[]{:S(2)}) collective-permute-start(bf16[16,4096]{1,0:T(8,128)(2,1)S(1)} %slice.45), channel_id=1, source_target_pairs={{0,2},{1,3},{2,0},{3,1},{4,6},{5,7},{6,4},{7,5},{8,10},{9,11},{10,... | collective-permute-start | bytes 393224 | tf_op jit(solution)/shard_map/ppermute | solution.py:312
  45.0 6.5 %collective-permute-start.20 = (bf16[4,7168]{1,0:T(4,128)(2,1)S(1)}, bf16[4,7168]{1,0:T(4,128)(2,1)S(1)}, u32[]{:S(2)}, u32[]{:S(2)}) collective-permute-start(bf16[4,7168]{1,0:T(4,128)(2,1)S(1)} %get-tuple-element.41), channel_id=1, source_target_pairs={{0,12},{1,13},{2,14},{3,15},{4,8},{5,9},{6,10},{7,11},{8,4},{9,5},... | collective-permute-start | bytes 172040 | tf_op jit(solution)/shard_map/ppermute | solution.py:312
  48.6 5.1 %collective-permute-start.21 = (bf16[4,7168]{1,0:T(4,128)(2,1)S(1)}, bf16[4,7168]{1,0:T(4,128)(2,1)S(1)}, u32[]{:S(2)}, u32[]{:S(2)}) collective-permute-start(bf16[4,7168]{1,0:T(4,128)(2,1)S(1)} %get-tuple-element.43), channel_id=1, source_target_pairs={{0,8},{1,9},{2,10},{3,11},{4,12},{5,13},{6,14},{7,15},{8,0},{9,1},... | collective-permute-start | bytes 172040 | tf_op jit(solution)/shard_map/ppermute | solution.py:312
  48.6 5.1 %collective-permute-start.22 = (bf16[4,7168]{1,0:T(4,128)(2,1)S(1)}, bf16[4,7168]{1,0:T(4,128)(2,1)S(1)}, u32[]{:S(2)}, u32[]{:S(2)}) collective-permute-start(bf16[4,7168]{1,0:T(4,128)(2,1)S(1)} %get-tuple-element.42), channel_id=1, source_target_pairs={{0,4},{1,5},{2,6},{3,7},{4,0},{5,1},{6,2},{7,3},{8,12},{9,13},{10,... | collective-permute-start | bytes 172040 | tf_op jit(solution)/shard_map/ppermute | solution.py:312

commit v9 on v8

--- a/solution.py
+++ b/solution.py
@@ -13,7 +13,7 @@
 LANES = 128
 LATE = 4
 FIRST = 3
-COVER = 30_000_000_000
+COVER = 18_000_000_000
 EMPTY = -1e30
 
 
@@ -189,7 +189,8 @@
         safe = jnp.where(some, norm, 1.0)
         lse = jnp.where(some, top[r][:, :1] + jnp.log(safe), EMPTY)
         result = latent[r] * (1.0 / safe)
-        out_ref[at] = result[:row_block]
+        for c in range(kv_rank // LANES):
+            out_ref[c, at] = result[:row_block, c * LANES : (c + 1) * LANES]
         lse_ref[at] = jnp.broadcast_to(lse[:row_block], (row_block, LANES))
         rest = lse[row_block:]
         high = rest.astype(jnp.bfloat16).astype(jnp.float32)
@@ -220,29 +221,40 @@
         at += tile
 
 
+def head_values(grouped, value_ref, h, heads):
+    kv_rank = value_ref.shape[1]
+    rows = grouped.shape[1] // heads
+    latent = jnp.concatenate(
+        [grouped[c, pl.ds(h, rows, stride=heads)] for c in range(kv_rank // LANES)], axis=1
+    )
+    return jnp.dot(latent.astype(jnp.bfloat16), value_ref[h], preferred_element_type=jnp.float32)
+
+
+def value_kernel(heads, grouped_ref, value_ref, out_ref):
+    v_width = value_ref.shape[2]
+    for h in range(heads):
+        out_ref[:, h * v_width : (h + 1) * v_width] = head_values(grouped_ref, value_ref, h, heads)
+
+
 def merge_kernel(
-    heads, steps, order_ref, value_ref, weight_ref, out_ref, lse_ref, other_ref,
+    heads, steps, order_ref, value_ref, weight_ref, own_ref, lse_ref, other_ref,
     away_ref, keep_ref, placed_ref, latent, head_rows,
 ):
     kv_rank, v_width = value_ref.shape[1:]
     rows = head_rows.shape[0]
     requests = rows // steps
     chunk = 64
-
-    def merge(i, _):
+    groups = kv_rank // LANES
+
+    def spread(i, _):
         at = pl.ds(pl.multiple_of(i * chunk, chunk), chunk)
-        own, own_lse = out_ref[at], lse_ref[at][:, :1]
-        other_lse = jnp.sum(other_ref[at, kv_rank:].astype(jnp.float32), axis=1, keepdims=True)
-        peak = jnp.maximum(own_lse, other_lse)
-        share, other_share = jnp.exp(own_lse - peak), jnp.exp(other_lse - peak)
-        inverse = 1.0 / (share + other_share)
-        whole = own * (share * inverse)
-        whole += other_ref[at, :kv_rank].astype(jnp.float32) * (other_share * inverse)
-        for c in range(kv_rank // LANES):
-            latent[c, at] = whole[:, c * LANES : (c + 1) * LANES]
+        for c in range(groups):
+            latent[c, at] = other_ref[at, c * LANES : (c + 1) * LANES].astype(jnp.float32)
+        terms = jnp.sum(other_ref[at, kv_rank:].astype(jnp.float32), axis=1, keepdims=True)
+        latent[groups, at] = jnp.broadcast_to(terms, (chunk, LANES))
         return 0
 
-    lax.fori_loop(0, rows * heads // chunk, merge, 0, unroll=True)
+    lax.fori_loop(0, rows * heads // chunk, spread, 0, unroll=True)
 
     half_rows = away_ref.shape[0]
     target = lax.broadcasted_iota(jnp.int32, (2 * half_rows, rows), 0)
@@ -258,12 +270,15 @@
     )
 
     for h in range(heads):
-        mine = jnp.concatenate(
-            [latent[c, pl.ds(h, rows, stride=heads)] for c in range(kv_rank // LANES)], axis=1
-        ).astype(jnp.bfloat16)
-        head_rows[:, h * v_width : (h + 1) * v_width] = jnp.dot(
-            mine, value_ref[h], preferred_element_type=jnp.float32
-        ).astype(jnp.bfloat16)
+        at = pl.ds(h, rows, stride=heads)
+        columns = slice(h * v_width, (h + 1) * v_width)
+        own_lse, other_lse = lse_ref[at], latent[groups, at]
+        peak = jnp.maximum(own_lse, other_lse)
+        share, other_share = jnp.exp(own_lse - peak), jnp.exp(other_lse - peak)
+        inverse = 1.0 / (share + other_share)
+        mixed = own_ref[:, columns] * (share * inverse)
+        mixed += head_values(latent, value_ref, h, heads) * (other_share * inverse)
+        head_rows[:, columns] = mixed.astype(jnp.bfloat16)
 
     placed = jnp.dot(
         picker.astype(jnp.bfloat16), head_rows[...], preferred_element_type=jnp.float32
@@ -351,7 +366,7 @@
         late = bool(earlier)
         slots = len(pieces) * half
         results = [
-            jax.ShapeDtypeStruct((flat_rows, kv_rank), jnp.float32),
+            jax.ShapeDtypeStruct((kv_rank // LANES, flat_rows, LANES), jnp.float32),
             jax.ShapeDtypeStruct((flat_rows, LANES), jnp.float32),
             jax.ShapeDtypeStruct((flat_rows, kv_rank + LANES), jnp.bfloat16),
         ]
@@ -404,6 +419,17 @@
     sums = attend(plan, mine, theirs, pieces[:-LATE], ())
     out, lse, away = attend(plan, mine, theirs, pieces[-LATE:], sums)
     other = exchange(away, 1)
+    own = pl.pallas_call(
+        functools.partial(value_kernel, heads),
+        out_shape=jax.ShapeDtypeStruct((row_count, heads * v_width), jnp.float32),
+        in_specs=[vmem] * 2,
+        out_specs=vmem,
+        compiler_params=pltpu.CompilerParams(vmem_limit_bytes=12 * mebi),
+        cost_estimate=pl.CostEstimate(
+            flops=2 * w_value.size * row_count, bytes_accessed=2 * w_value.size, transcendentals=0
+        ),
+        name="own_values",
+    )(out, w_value)
 
     part_rows = chips * steps
     widths = (FIRST * OUT_TILE, w_out.shape[1] - FIRST * OUT_TILE)
@@ -418,12 +444,12 @@
         in_specs=[smem] + [vmem] * 5,
         out_specs=(vmem,) * 3,
         scratch_shapes=[
-            pltpu.VMEM((kv_rank // LANES, flat_rows, LANES), jnp.float32),
+            pltpu.VMEM((kv_rank // LANES + 1, flat_rows, LANES), jnp.float32),
             pltpu.VMEM((row_count, heads * v_width), jnp.bfloat16),
         ],
         compiler_params=pltpu.CompilerParams(vmem_limit_bytes=28 * mebi),
         name="merge_and_project",
-    )(order, w_value, w_out, out, lse, other)
+    )(order, w_value, w_out, own, lse, other)
     next_away, next_keep = pl.pallas_call(
         second_kernel,
         out_shape=(parts[1], parts[1]),

time: 54.5 us -> 54.4 us (level)
  transfers between devices with their start and end apart: 23 -> 23, of which waited for: 12 -> 12; matrix products, arithmetic and copies ran while one was open for 0% -> 0% of each run, Pallas kernels for 11% -> 12%
where the time goes in v9:
time: 54.4 us; the launch traced here: 54.2 us
  starting transfers between devices  22.1 us (41%)
  waiting for transfers between devices  20.1 us (37%)
  Pallas kernels  9.91 us (18%)
  local copies, waits for them, and re-layouts  1.05 us (2%)
  other arithmetic  0.94 us (2%)
    ppermute x9, waiting for transfers between devices, exchange(): return lax.ppermute(x, 'head', [(i, i ^ distance) for i in range(devices)])  11.3 us
    ppermute x4, starting transfers between devices, local(): ups[0] = lax.ppermute(ups[0], 'head', up)  8.27 us
    ppermute x9, starting transfers between devices, exchange(): return lax.ppermute(x, 'head', [(i, i ^ distance) for i in range(devices)])  6.99 us
    ppermute x3, waiting for transfers between devices, local(): downs[0] = lax.ppermute(downs[0], 'head', down)  5.61 us
    ppermute x3, starting transfers between devices, local(): ups[1] = lax.ppermute(ups[1], 'head', up)  3.87 us
    pallas_call x2, Pallas kernels, attend(): pl.pallas_call(functools.partial(attend_kernel, len(pieces), late, piece_...  3.75 us
    pallas_call x1, Pallas kernels, prepare(): pl.pallas_call(functools.partial(prepare_kernel, heads, chips), out_shape...  2.4 us
    ppermute x3, starting transfers between devices, local(): downs[0] = lax.ppermute(downs[0], 'head', down)  2.23 us
  transfers between devices with their start and end apart: 23, of which 12 were waited for; matrix products, arithmetic and copies ran while one was open for 0% of the time, Pallas kernels for 12%

profile of v9, /device:TPU:0, one launch (start us, length us, event | category | flops | bytes accessed | tf_op | source)
XLA Modules:
  0.0 54.2 jit_solution(6072914129877392468)
XLA Ops:
  0.0 1.0 %fusion.3 = (bf16[1,576,128]{2,1,0:T(8,128)(2,1)S(1)}, bf16[1,576,128]{2,1,0:T(8,128)(2,1)S(1)}) fusion(bf16[2,576,128]{2,1,0:T(8,128)(2,1)} %bitcast.8), kind=kLoop, calls=%fused_computation.15 | loop fusion | bytes 589824 | tf_op jit(solution)/shard_map/slice | solution.py:400
  1.0 3.1 %collective-permute-start = (bf16[1,576,128]{2,1,0:T(8,128)(2,1)S(1)}, bf16[1,576,128]{2,1,0:T(8,128)(2,1)S(1)}, u32[]{:S(2)}, u32[]{:S(2)}) collective-permute-start(bf16[1,576,128]{2,1,0:T(8,128)(2,1)S(1)} %get-tuple-element.40.rest_0_), channel_id=1, source_target_pairs={{0,4},{1,5},{4,8},{5,9},{8,12},{9,13},{12,14},{13,15},{14,10},{15,... | collective-permute-start | bytes 442376 | tf_op jit(solution)/shard_map/ppermute | solution.py:414
  4.1 0.0 collective-permute-start.11
  4.1 2.0 %collective-permute-start.2 = (bf16[1,576,128]{2,1,0:T(8,128)(2,1)S(1)}, bf16[1,576,128]{2,1,0:T(8,128)(2,1)S(1)}, u32[]{:S(2)}, u32[]{:S(2)}) collective-permute-start(bf16[1,576,128]{2,1,0:T(8,128)(2,1)S(1)} %get-tuple-element.40.rest_0_), channel_id=1, source_target_pairs={{4,0},{5,1},{8,4},{9,5},{12,8},{13,9},{14,12},{15,13},{10,14},{11,... | collective-permute-start | bytes 442376 | tf_op jit(solution)/shard_map/ppermute | solution.py:416
  6.1 0.1 collective-permute-start.5
  6.1 2.4 %prepare.1 = (bf16[256,576]{1,0:T(8,128)(2,1)S(1)}, s32[34]{0:T(128)S(1)}, s32[8]{0:T(128)S(1)}) custom-call(s32[1]{0:T(128)} %bitcast.me_ref, bf16[32,1536]{1,0:T(8,128)(2,1)} %query_hbm.1, bf16[8,128,512]{2,1,0:T(8,128)(2,1)} %absorb_hbm.1, s32[8]{0:T(128)} %length_hbm.1, s32[8,8]{1,0:T(8,128)} %table_hbm.1, s32[16,32]{1,0:T(8,128)} %constant.6.clone.slot_hbm, ...), custom_call_target="tpu_custom_call" | custom-call | flops 33554432 | bytes 2097152 | tf_op jit(solution)/shard_map/prepare/pallas_call | solution.py:333
  8.6 0.0 copy-start
  8.6 0.0 slice-start.1
  8.6 2.3 %collective-permute-start.8 = (bf16[1,576,128]{2,1,0:T(8,128)(2,1)S(1)}, bf16[1,576,128]{2,1,0:T(8,128)(2,1)S(1)}, u32[]{:S(2)}, u32[]{:S(2)}) collective-permute-start(bf16[1,576,128]{2,1,0:T(8,128)(2,1)S(1)} %collective-permute-done.rest_2_), channel_id=1, source_target_pairs={{0,4},{1,5},{4,8},{5,9},{8,12},{9,13},{12,14},{13,15},{14,10},{15,... | collective-permute-start | bytes 442376 | tf_op jit(solution)/shard_map/ppermute | solution.py:414
  10.9 0.0 collective-permute-done.11.rest_3_
  10.9 0.0 collective-permute-start.12
  10.9 2.5 %collective-permute-done.2.rest_4_ = bf16[1,576,128]{2,1,0:T(8,128)(2,1)S(1)} collective-permute-done((bf16[1,576,128]{2,1,0:T(8,128)(2,1)S(1)}, bf16[1,576,128]{2,1,0:T(8,128)(2,1)S(1)}, u32[]{:S(2)}, u32[]{:S(2)}) %collective-permute-start.2) | collective-permute-done | bytes 147488 | tf_op jit(solution)/shard_map/ppermute | solution.py:416
  13.3 0.3 collective-permute-start.3
  13.6 1.8 %collective-permute-start.6 = (bf16[1,576,128]{2,1,0:T(8,128)(2,1)S(1)}, bf16[1,576,128]{2,1,0:T(8,128)(2,1)S(1)}, u32[]{:S(2)}, u32[]{:S(2)}) collective-permute-start(bf16[1,576,128]{2,1,0:T(8,128)(2,1)S(1)} %collective-permute-done.5.rest_5_), channel_id=1, source_target_pairs={{0,4},{1,5},{4,8},{5,9},{8,12},{9,13},{12,14},{13,15},{14,10},{15,... | collective-permute-start | bytes 442376 | tf_op jit(solution)/shard_map/ppermute | solution.py:417
  15.4 1.6 %collective-permute-start.9 = (bf16[1,576,128]{2,1,0:T(8,128)(2,1)S(1)}, bf16[1,576,128]{2,1,0:T(8,128)(2,1)S(1)}, u32[]{:S(2)}, u32[]{:S(2)}) collective-permute-start(bf16[1,576,128]{2,1,0:T(8,128)(2,1)S(1)} %collective-permute-done.8.rest_6_), channel_id=1, source_target_pairs={{0,4},{1,5},{4,8},{5,9},{8,12},{9,13},{12,14},{13,15},{14,10},{15,... | collective-permute-start | bytes 442376 | tf_op jit(solution)/shard_map/ppermute | solution.py:414
  17.0 0.6 %collective-permute-done.12.rest_7_ = bf16[1,576,128]{2,1,0:T(8,128)(2,1)S(1)} collective-permute-done((bf16[1,576,128]{2,1,0:T(8,128)(2,1)S(1)}, bf16[1,576,128]{2,1,0:T(8,128)(2,1)S(1)}, u32[]{:S(2)}, u32[]{:S(2)}) %collective-permute-start.12) | collective-permute-done | bytes 147488 | tf_op jit(solution)/shard_map/ppermute | solution.py:415
  17.6 3.2 %collective-permute-done.3.rest_8_ = bf16[1,576,128]{2,1,0:T(8,128)(2,1)S(1)} collective-permute-done((bf16[1,576,128]{2,1,0:T(8,128)(2,1)S(1)}, bf16[1,576,128]{2,1,0:T(8,128)(2,1)S(1)}, u32[]{:S(2)}, u32[]{:S(2)}) %collective-permute-start.3) | collective-permute-done | bytes 147488 | tf_op jit(solution)/shard_map/ppermute | solution.py:416
  20.8 0.0 collective-permute-start.4
  20.8 0.0 collective-permute-done.6.rest_9_
  20.8 2.0 %collective-permute-start.7 = (bf16[1,576,128]{2,1,0:T(8,128)(2,1)S(1)}, bf16[1,576,128]{2,1,0:T(8,128)(2,1)S(1)}, u32[]{:S(2)}, u32[]{:S(2)}) collective-permute-start(bf16[1,576,128]{2,1,0:T(8,128)(2,1)S(1)} %collective-permute-done.6.rest_9_), channel_id=1, source_target_pairs={{0,4},{1,5},{4,8},{5,9},{8,12},{9,13},{12,14},{13,15},{14,10},{15,... | collective-permute-start | bytes 442376 | tf_op jit(solution)/shard_map/ppermute | solution.py:417
  22.8 0.2 collective-permute-done.9.rest_10_
  23.0 1.3 %collective-permute-start.10 = (bf16[1,576,128]{2,1,0:T(8,128)(2,1)S(1)}, bf16[1,576,128]{2,1,0:T(8,128)(2,1)S(1)}, u32[]{:S(2)}, u32[]{:S(2)}) collective-permute-start(bf16[1,576,128]{2,1,0:T(8,128)(2,1)S(1)} %collective-permute-done.9.rest_10_), channel_id=1, source_target_pairs={{0,4},{1,5},{4,8},{5,9},{8,12},{9,13},{12,14},{13,15},{14,10},{15,... | collective-permute-start | bytes 442376 | tf_op jit(solution)/shard_map/ppermute | solution.py:410
  24.4 0.0 collective-permute-done.13.rest_11_
  24.4 0.7 %collective-permute-start.14 = (bf16[1,576,128]{2,1,0:T(8,128)(2,1)S(1)}, bf16[1,576,128]{2,1,0:T(8,128)(2,1)S(1)}, u32[]{:S(2)}, u32[]{:S(2)}) collective-permute-start(bf16[1,576,128]{2,1,0:T(8,128)(2,1)S(1)} %collective-permute-done.13.rest_11_), channel_id=1, source_target_pairs={{4,0},{5,1},{8,4},{9,5},{12,8},{13,9},{14,12},{15,13},{10,14},{11,... | collective-permute-start | bytes 442376 | tf_op jit(solution)/shard_map/ppermute | solution.py:411
  25.1 2.2 %attend.2 = (f32[9,64,128]{2,1,0:T(8,128)S(1)}, f32[9,64,128]{2,1,0:T(8,128)S(1)}, f32[9,64,512]{2,1,0:T(8,128)S(1)}) custom-call(s32[34]{0:T(128)S(1)} %get-tuple-element.25.plan_ref, bf16[8,32,576]{2,1,0:T(8,128)(2,1)S(1)} %bitcast.6, bf16[8,32,576]{2,1,0:T(8,128)(2,1)S(1)} %collective-permute-done.1.theirs_ref, ...), custom_call_target="tpu_custom_call" | custom-call | flops 17999998976 | bytes 1769472 | tf_op jit(solution)/shard_map/attend/pallas_call | solution.py:373
  27.2 1.0 %collective-permute-done.10.rest_2_ = bf16[1,576,128]{2,1,0:T(8,128)(2,1)S(1)} collective-permute-done((bf16[1,576,128]{2,1,0:T(8,128)(2,1)S(1)}, bf16[1,576,128]{2,1,0:T(8,128)(2,1)S(1)}, u32[]{:S(2)}, u32[]{:S(2)}) %collective-permute-start.10) | collective-permute-done | bytes 147488 | tf_op jit(solution)/shard_map/ppermute | solution.py:410
  28.3 1.2 %collective-permute-done.14.rest_3_ = bf16[1,576,128]{2,1,0:T(8,128)(2,1)S(1)} collective-permute-done((bf16[1,576,128]{2,1,0:T(8,128)(2,1)S(1)}, bf16[1,576,128]{2,1,0:T(8,128)(2,1)S(1)}, u32[]{:S(2)}, u32[]{:S(2)}) %collective-permute-start.14) | collective-permute-done | bytes 147488 | tf_op jit(solution)/shard_map/ppermute | solution.py:411
  29.5 1.6 %attend.3 = (f32[4,256,128]{2,1,0:T(8,128)S(1)}, f32[256,128]{1,0:T(8,128)S(1)}, bf16[256,640]{1,0:T(8,128)(2,1)S(1)}) custom-call(s32[34]{0:T(128)S(1)} %get-tuple-element.25.plan_ref, bf16[8,32,576]{2,1,0:T(8,128)(2,1)S(1)} %bitcast.7, bf16[8,32,576]{2,1,0:T(8,128)(2,1)S(1)} %collective-permute-done.1.theirs_ref, ...), custom_call_target="tpu_custom_call" | custom-call | flops 150994944 | bytes 589824 | tf_op jit(solution)/shard_map/attend/pallas_call | solution.py:373
  31.1 0.1 collective-permute-start.15
  31.2 0.3 own_values.1.own_ref
  31.5 1.3 %collective-permute-done.15.other_ref = bf16[256,640]{1,0:T(8,128)(2,1)S(1)} collective-permute-done((bf16[256,640]{1,0:T(8,128)(2,1)S(1)}, bf16[256,640]{1,0:T(8,128)(2,1)S(1)}, u32[]{:S(2)}, u32[]{:S(2)}) %collective-permute-start.15) | collective-permute-done | bytes 327712 | tf_op jit(solution)/shard_map/ppermute | solution.py:327
  32.8 1.9 %merge_and_project.1 = (bf16[32,3072]{1,0:T(8,128)(2,1)S(1)}, bf16[32,3072]{1,0:T(8,128)(2,1)S(1)}, bf16[64,1024]{1,0:T(8,128)(2,1)S(1)}) custom-call(s32[8]{0:T(128)S(1)} %get-tuple-element.22.order_ref, bf16[8,512,128]{2,1,0:T(8,128)(2,1)S(1)} %copy-done, bf16[1024,7168]{1,0:T(8,128)(2,1)S(1)} %bitcast.4, f32[32,1024]{1,0:T(8,128)S(1)} %own_values.1.own_ref, ...), custom_call_target="tpu_custom_call" | custom-call | tf_op jit(solution)/shard_map/merge_and_project/pallas_call | solution.py:437
  34.8 0.2 collective-permute-start.16
  35.0 1.6 %project_second.1 = (bf16[32,4096]{1,0:T(8,128)(2,1)S(1)}, bf16[32,4096]{1,0:T(8,128)(2,1)S(1)}) custom-call(bf16[64,1024]{1,0:T(8,128)(2,1)S(1)} %get-tuple-element.36.placed_ref, bf16[1024,7168]{1,0:T(8,128)(2,1)S(1)} %bitcast.4), custom_call_target="tpu_custom_call" | custom-call | flops 469762048 | bytes 7340032 | tf_op jit(solution)/shard_map/project_second/pallas_call | solution.py:453
  36.5 0.4 collective-permute-start.18
  37.0 0.1 add_convert_fusion.1
  37.1 0.8 %collective-permute-start.17 = (bf16[16,3072]{1,0:T(8,128)(2,1)S(1)}, bf16[16,3072]{1,0:T(8,128)(2,1)S(1)}, u32[]{:S(2)}, u32[]{:S(2)}) collective-permute-start(bf16[16,3072]{1,0:T(8,128)(2,1)S(1)} %slice.43), channel_id=1, source_target_pairs={{0,2},{1,3},{2,0},{3,1},{4,6},{5,7},{6,4},{7,5},{8,10},{9,11},{10,... | collective-permute-start | bytes 294920 | tf_op jit(solution)/shard_map/ppermute | solution.py:327
  37.8 0.3 collective-permute-done.18
  38.1 0.1 add_convert_fusion
  38.2 1.1 %collective-permute-start.19 = (bf16[16,4096]{1,0:T(8,128)(2,1)S(1)}, bf16[16,4096]{1,0:T(8,128)(2,1)S(1)}, u32[]{:S(2)}, u32[]{:S(2)}) collective-permute-start(bf16[16,4096]{1,0:T(8,128)(2,1)S(1)} %slice.45), channel_id=1, source_target_pairs={{0,2},{1,3},{2,0},{3,1},{4,6},{5,7},{6,4},{7,5},{8,10},{9,11},{10,... | collective-permute-start | bytes 393224 | tf_op jit(solution)/shard_map/ppermute | solution.py:327
  39.3 3.4 %collective-permute-done.17 = bf16[16,3072]{1,0:T(8,128)(2,1)S(1)} collective-permute-done((bf16[16,3072]{1,0:T(8,128)(2,1)S(1)}, bf16[16,3072]{1,0:T(8,128)(2,1)S(1)}, u32[]{:S(2)}, u32[]{:S(2)}) %collective-permute-start.17) | collective-permute-done | bytes 98336 | tf_op jit(solution)/shard_map/ppermute | solution.py:327
  42.7 2.0 %collective-permute-done.19 = bf16[16,4096]{1,0:T(8,128)(2,1)S(1)} collective-permute-done((bf16[16,4096]{1,0:T(8,128)(2,1)S(1)}, bf16[16,4096]{1,0:T(8,128)(2,1)S(1)}, u32[]{:S(2)}, u32[]{:S(2)}) %collective-permute-start.19) | collective-permute-done | bytes 131104 | tf_op jit(solution)/shard_map/ppermute | solution.py:327
  44.8 0.1 fusion.2
  44.9 3.6 %collective-permute-start.20 = (bf16[4,7168]{1,0:T(4,128)(2,1)S(1)}, bf16[4,7168]{1,0:T(4,128)(2,1)S(1)}, u32[]{:S(2)}, u32[]{:S(2)}) collective-permute-start(bf16[4,7168]{1,0:T(4,128)(2,1)S(1)} %get-tuple-element.41), channel_id=1, source_target_pairs={{0,12},{1,13},{2,14},{3,15},{4,8},{5,9},{6,10},{7,11},{8,4},{9,5},... | collective-permute-start | bytes 172040 | tf_op jit(solution)/shard_map/ppermute | solution.py:327
  48.5 0.9 %collective-permute-start.22 = (bf16[4,7168]{1,0:T(4,128)(2,1)S(1)}, bf16[4,7168]{1,0:T(4,128)(2,1)S(1)}, u32[]{:S(2)}, u32[]{:S(2)}) collective-permute-start(bf16[4,7168]{1,0:T(4,128)(2,1)S(1)} %get-tuple-element.42), channel_id=1, source_target_pairs={{0,4},{1,5},{2,6},{3,7},{4,0},{5,1},{6,2},{7,3},{8,12},{9,13},{10,... | collective-permute-start | bytes 172040 | tf_op jit(solution)/shard_map/ppermute | solution.py:327
  49.3 2.1 %collective-permute-done.20 = bf16[4,7168]{1,0:T(4,128)(2,1)S(1)} collective-permute-done((bf16[4,7168]{1,0:T(4,128)(2,1)S(1)}, bf16[4,7168]{1,0:T(4,128)(2,1)S(1)}, u32[]{:S(2)}, u32[]{:S(2)}) %collective-permute-start.20) | collective-permute-done | bytes 57376 | tf_op jit(solution)/shard_map/ppermute | solution.py:327
  51.4 2.1 %collective-permute-done.21 = bf16[4,7168]{1,0:T(4,128)(2,1)S(1)} collective-permute-done((bf16[4,7168]{1,0:T(4,128)(2,1)S(1)}, bf16[4,7168]{1,0:T(4,128)(2,1)S(1)}, u32[]{:S(2)}, u32[]{:S(2)}) %collective-permute-start.21) | collective-permute-done | bytes 57376 | tf_op jit(solution)/shard_map/ppermute | solution.py:327
  53.5 0.7 %add_convert_fusion.4 = bf16[4,7168]{1,0:T(4,128)(2,1)} fusion(bf16[4,7168]{1,0:T(4,128)(2,1)S(1)} %collective-permute-done.22, bf16[4,7168]{1,0:T(4,128)(2,1)S(1)} %collective-permute-done.21, bf16[4,7168]{1,0:T(4,128)(2,1)S(1)} %collective-permute-done.20, bf16[16,4096]{1,0:T(8,128)(2,1)S(1)} %add_convert_fusion.2, bf16[16,3072]{1,0:T(8,128)(2,1)S(1)} %add_convert_fusion.3), kind=kLoop, calls=%fused_computation.10 | loop fusion | flops 315392 | bytes 458752 | tf_op jit(solution)/shard_map/convert_element_type | solution.py:320
  (24 shorter events, 0.1 us)
Async XLA Ops:
  1.0 7.5 %collective-permute-start = (bf16[1,576,128]{2,1,0:T(8,128)(2,1)S(1)}, bf16[1,576,128]{2,1,0:T(8,128)(2,1)S(1)}, u32[]{:S(2)}, u32[]{:S(2)}) collective-permute-start(bf16[1,576,128]{2,1,0:T(8,128)(2,1)S(1)} %get-tuple-element.40.rest_0_), channel_id=1, source_target_pairs={{0,4},{1,5},{4,8},{5,9},{8,12},{9,13},{12,14},{13,15},{14,10},{15,... | collective-permute-start | bytes 442376 | tf_op jit(solution)/shard_map/ppermute | solution.py:414
  4.1 6.8 %collective-permute-start.11 = (bf16[1,576,128]{2,1,0:T(8,128)(2,1)S(1)}, bf16[1,576,128]{2,1,0:T(8,128)(2,1)S(1)}, u32[]{:S(2)}, u32[]{:S(2)}) collective-permute-start(bf16[1,576,128]{2,1,0:T(8,128)(2,1)S(1)} %get-tuple-element.39.rest_1_), channel_id=1, source_target_pairs={{4,0},{5,1},{8,4},{9,5},{12,8},{13,9},{14,12},{15,13},{10,14},{11,... | collective-permute-start | bytes 442376 | tf_op jit(solution)/shard_map/ppermute | solution.py:415
  4.1 9.3 %collective-permute-start.2 = (bf16[1,576,128]{2,1,0:T(8,128)(2,1)S(1)}, bf16[1,576,128]{2,1,0:T(8,128)(2,1)S(1)}, u32[]{:S(2)}, u32[]{:S(2)}) collective-permute-start(bf16[1,576,128]{2,1,0:T(8,128)(2,1)S(1)} %get-tuple-element.40.rest_0_), channel_id=1, source_target_pairs={{4,0},{5,1},{8,4},{9,5},{12,8},{13,9},{14,12},{15,13},{10,14},{11,... | collective-permute-start | bytes 442376 | tf_op jit(solution)/shard_map/ppermute | solution.py:416
  6.1 7.6 %collective-permute-start.5 = (bf16[1,576,128]{2,1,0:T(8,128)(2,1)S(1)}, bf16[1,576,128]{2,1,0:T(8,128)(2,1)S(1)}, u32[]{:S(2)}, u32[]{:S(2)}) collective-permute-start(bf16[1,576,128]{2,1,0:T(8,128)(2,1)S(1)} %get-tuple-element.39.rest_1_), channel_id=1, source_target_pairs={{0,4},{1,5},{4,8},{5,9},{8,12},{9,13},{12,14},{13,15},{14,10},{15,... | collective-permute-start | bytes 442376 | tf_op jit(solution)/shard_map/ppermute | solution.py:417
  6.1 26.7 %slice-start = ((s8[14680064]{0:T(1024)(128)(4,1)}), s8[4194304]{0:T(1024)(128)(4,1)S(1)}, s32[]{:S(2)}) async-start(s8[14680064]{0:T(1024)(128)(4,1)} %bitcast.3), calls=%async_computation | async-start | bytes 8388608
  8.6 22.6 %copy-start = (bf16[8,512,128]{2,1,0:T(8,128)(2,1)S(1)}, bf16[8,512,128]{2,1,0:T(8,128)(2,1)}, u32[]{:S(2)}) copy-start(bf16[8,512,128]{2,1,0:T(8,128)(2,1)} %value_ref.3) | copy-start | bytes 3145732
  8.6 24.3 %slice-start.1 = ((s8[14680064]{0:T(1024)(128)(4,1)}), s8[4194304]{0:T(1024)(128)(4,1)S(1)}, s32[]{:S(2)}) async-start(s8[14680064]{0:T(1024)(128)(4,1)} %bitcast.3), calls=%async_computation.1 | async-start | bytes 8388608
  8.6 24.2 %slice-start.2 = ((s8[14680064]{0:T(1024)(128)(4,1)}), s8[4194304]{0:T(1024)(128)(4,1)S(1)}, s32[]{:S(2)}) async-start(s8[14680064]{0:T(1024)(128)(4,1)} %bitcast.3), calls=%async_computation.2 | async-start | bytes 8388608
  8.6 24.2 %slice-start.3 = ((s8[14680064]{0:T(1024)(128)(4,1)}), s8[2097152]{0:T(1024)(128)(4,1)S(1)}, s32[]{:S(2)}) async-start(s8[14680064]{0:T(1024)(128)(4,1)} %bitcast.3), calls=%async_computation.3 | async-start | bytes 4194304
  8.6 6.8 %collective-permute-start.8 = (bf16[1,576,128]{2,1,0:T(8,128)(2,1)S(1)}, bf16[1,576,128]{2,1,0:T(8,128)(2,1)S(1)}, u32[]{:S(2)}, u32[]{:S(2)}) collective-permute-start(bf16[1,576,128]{2,1,0:T(8,128)(2,1)S(1)} %collective-permute-done.rest_2_), channel_id=1, source_target_pairs={{0,4},{1,5},{4,8},{5,9},{8,12},{9,13},{12,14},{13,15},{14,10},{15,... | collective-permute-start | bytes 442376 | tf_op jit(solution)/shard_map/ppermute | solution.py:414
  10.9 6.7 %collective-permute-start.12 = (bf16[1,576,128]{2,1,0:T(8,128)(2,1)S(1)}, bf16[1,576,128]{2,1,0:T(8,128)(2,1)S(1)}, u32[]{:S(2)}, u32[]{:S(2)}) collective-permute-start(bf16[1,576,128]{2,1,0:T(8,128)(2,1)S(1)} %collective-permute-done.11.rest_3_), channel_id=1, source_target_pairs={{4,0},{5,1},{8,4},{9,5},{12,8},{13,9},{14,12},{15,13},{10,14},{11,... | collective-permute-start | bytes 442376 | tf_op jit(solution)/shard_map/ppermute | solution.py:415
  10.9 14.2 %collective-permute-start.1 = (bf16[8,32,576]{2,1,0:T(8,128)(2,1)S(1)}, bf16[8,32,576]{2,1,0:T(8,128)(2,1)S(1)}, u32[]{:S(2)}, u32[]{:S(2)}) collective-permute-start(bf16[8,32,576]{2,1,0:T(8,128)(2,1)S(1)} %bitcast.5), channel_id=1, source_target_pairs={{0,1},{1,0},{2,3},{3,2},{4,5},{5,4},{6,7},{7,6},{8,9},{9,8},{10,11... | collective-permute-start | bytes 884744 | tf_op jit(solution)/shard_map/ppermute | solution.py:327
  13.3 7.4 %collective-permute-start.3 = (bf16[1,576,128]{2,1,0:T(8,128)(2,1)S(1)}, bf16[1,576,128]{2,1,0:T(8,128)(2,1)S(1)}, u32[]{:S(2)}, u32[]{:S(2)}) collective-permute-start(bf16[1,576,128]{2,1,0:T(8,128)(2,1)S(1)} %collective-permute-done.2.rest_4_), channel_id=1, source_target_pairs={{4,0},{5,1},{8,4},{9,5},{12,8},{13,9},{14,12},{15,13},{10,14},{11,... | collective-permute-start | bytes 442376 | tf_op jit(solution)/shard_map/ppermute | solution.py:416
  13.6 7.2 %collective-permute-start.6 = (bf16[1,576,128]{2,1,0:T(8,128)(2,1)S(1)}, bf16[1,576,128]{2,1,0:T(8,128)(2,1)S(1)}, u32[]{:S(2)}, u32[]{:S(2)}) collective-permute-start(bf16[1,576,128]{2,1,0:T(8,128)(2,1)S(1)} %collective-permute-done.5.rest_5_), channel_id=1, source_target_pairs={{0,4},{1,5},{4,8},{5,9},{8,12},{9,13},{12,14},{13,15},{14,10},{15,... | collective-permute-start | bytes 442376 | tf_op jit(solution)/shard_map/ppermute | solution.py:417
  15.4 7.7 %collective-permute-start.9 = (bf16[1,576,128]{2,1,0:T(8,128)(2,1)S(1)}, bf16[1,576,128]{2,1,0:T(8,128)(2,1)S(1)}, u32[]{:S(2)}, u32[]{:S(2)}) collective-permute-start(bf16[1,576,128]{2,1,0:T(8,128)(2,1)S(1)} %collective-permute-done.8.rest_6_), channel_id=1, source_target_pairs={{0,4},{1,5},{4,8},{5,9},{8,12},{9,13},{12,14},{13,15},{14,10},{15,... | collective-permute-start | bytes 442376 | tf_op jit(solution)/shard_map/ppermute | solution.py:414
  17.6 6.8 %collective-permute-start.13 = (bf16[1,576,128]{2,1,0:T(8,128)(2,1)S(1)}, bf16[1,576,128]{2,1,0:T(8,128)(2,1)S(1)}, u32[]{:S(2)}, u32[]{:S(2)}) collective-permute-start(bf16[1,576,128]{2,1,0:T(8,128)(2,1)S(1)} %collective-permute-done.12.rest_7_), channel_id=1, source_target_pairs={{4,0},{5,1},{8,4},{9,5},{12,8},{13,9},{14,12},{15,13},{10,14},{11,... | collective-permute-start | bytes 442376 | tf_op jit(solution)/shard_map/ppermute | solution.py:415
  20.8 6.5 %collective-permute-start.4 = (bf16[1,576,128]{2,1,0:T(8,128)(2,1)S(1)}, bf16[1,576,128]{2,1,0:T(8,128)(2,1)S(1)}, u32[]{:S(2)}, u32[]{:S(2)}) collective-permute-start(bf16[1,576,128]{2,1,0:T(8,128)(2,1)S(1)} %collective-permute-done.3.rest_8_), channel_id=1, source_target_pairs={{4,0},{5,1},{8,4},{9,5},{12,8},{13,9},{14,12},{15,13},{10,14},{11,... | collective-permute-start | bytes 442376 | tf_op jit(solution)/shard_map/ppermute | solution.py:416
  20.8 6.5 %collective-permute-start.7 = (bf16[1,576,128]{2,1,0:T(8,128)(2,1)S(1)}, bf16[1,576,128]{2,1,0:T(8,128)(2,1)S(1)}, u32[]{:S(2)}, u32[]{:S(2)}) collective-permute-start(bf16[1,576,128]{2,1,0:T(8,128)(2,1)S(1)} %collective-permute-done.6.rest_9_), channel_id=1, source_target_pairs={{0,4},{1,5},{4,8},{5,9},{8,12},{9,13},{12,14},{13,15},{14,10},{15,... | collective-permute-start | bytes 442376 | tf_op jit(solution)/shard_map/ppermute | solution.py:417
  23.0 5.3 %collective-permute-start.10 = (bf16[1,576,128]{2,1,0:T(8,128)(2,1)S(1)}, bf16[1,576,128]{2,1,0:T(8,128)(2,1)S(1)}, u32[]{:S(2)}, u32[]{:S(2)}) collective-permute-start(bf16[1,576,128]{2,1,0:T(8,128)(2,1)S(1)} %collective-permute-done.9.rest_10_), channel_id=1, source_target_pairs={{0,4},{1,5},{4,8},{5,9},{8,12},{9,13},{12,14},{13,15},{14,10},{15,... | collective-permute-start | bytes 442376 | tf_op jit(solution)/shard_map/ppermute | solution.py:410
  24.4 5.1 %collective-permute-start.14 = (bf16[1,576,128]{2,1,0:T(8,128)(2,1)S(1)}, bf16[1,576,128]{2,1,0:T(8,128)(2,1)S(1)}, u32[]{:S(2)}, u32[]{:S(2)}) collective-permute-start(bf16[1,576,128]{2,1,0:T(8,128)(2,1)S(1)} %collective-permute-done.13.rest_11_), channel_id=1, source_target_pairs={{4,0},{5,1},{8,4},{9,5},{12,8},{13,9},{14,12},{15,13},{10,14},{11,... | collective-permute-start | bytes 442376 | tf_op jit(solution)/shard_map/ppermute | solution.py:411
  31.1 1.7 %collective-permute-start.15 = (bf16[256,640]{1,0:T(8,128)(2,1)S(1)}, bf16[256,640]{1,0:T(8,128)(2,1)S(1)}, u32[]{:S(2)}, u32[]{:S(2)}) collective-permute-start(bf16[256,640]{1,0:T(8,128)(2,1)S(1)} %get-tuple-element.33), channel_id=1, source_target_pairs={{0,1},{1,0},{2,3},{3,2},{4,5},{5,4},{6,7},{7,6},{8,9},{9,8},{10,11... | collective-permute-start | bytes 983048 | tf_op jit(solution)/shard_map/ppermute | solution.py:327
  34.8 2.2 %collective-permute-start.16 = (bf16[32,3072]{1,0:T(8,128)(2,1)S(1)}, bf16[32,3072]{1,0:T(8,128)(2,1)S(1)}, u32[]{:S(2)}, u32[]{:S(2)}) collective-permute-start(bf16[32,3072]{1,0:T(8,128)(2,1)S(1)} %get-tuple-element.35), channel_id=1, source_target_pairs={{0,1},{1,0},{2,3},{3,2},{4,5},{5,4},{6,7},{7,6},{8,9},{9,8},{10,11... | collective-permute-start | bytes 589832 | tf_op jit(solution)/shard_map/ppermute | solution.py:327
  36.5 1.6 %collective-permute-start.18 = (bf16[32,4096]{1,0:T(8,128)(2,1)S(1)}, bf16[32,4096]{1,0:T(8,128)(2,1)S(1)}, u32[]{:S(2)}, u32[]{:S(2)}) collective-permute-start(bf16[32,4096]{1,0:T(8,128)(2,1)S(1)} %get-tuple-element.38), channel_id=1, source_target_pairs={{0,1},{1,0},{2,3},{3,2},{4,5},{5,4},{6,7},{7,6},{8,9},{9,8},{10,11... | collective-permute-start | bytes 786440 | tf_op jit(solution)/shard_map/ppermute | solution.py:327
  37.1 5.6 %collective-permute-start.17 = (bf16[16,3072]{1,0:T(8,128)(2,1)S(1)}, bf16[16,3072]{1,0:T(8,128)(2,1)S(1)}, u32[]{:S(2)}, u32[]{:S(2)}) collective-permute-start(bf16[16,3072]{1,0:T(8,128)(2,1)S(1)} %slice.43), channel_id=1, source_target_pairs={{0,2},{1,3},{2,0},{3,1},{4,6},{5,7},{6,4},{7,5},{8,10},{9,11},{10,... | collective-permute-start | bytes 294920 | tf_op jit(solution)/shard_map/ppermute | solution.py:327
  38.2 6.5 %collective-permute-start.19 = (bf16[16,4096]{1,0:T(8,128)(2,1)S(1)}, bf16[16,4096]{1,0:T(8,128)(2,1)S(1)}, u32[]{:S(2)}, u32[]{:S(2)}) collective-permute-start(bf16[16,4096]{1,0:T(8,128)(2,1)S(1)} %slice.45), channel_id=1, source_target_pairs={{0,2},{1,3},{2,0},{3,1},{4,6},{5,7},{6,4},{7,5},{8,10},{9,11},{10,... | collective-permute-start | bytes 393224 | tf_op jit(solution)/shard_map/ppermute | solution.py:327
  44.9 6.5 %collective-permute-start.20 = (bf16[4,7168]{1,0:T(4,128)(2,1)S(1)}, bf16[4,7168]{1,0:T(4,128)(2,1)S(1)}, u32[]{:S(2)}, u32[]{:S(2)}) collective-permute-start(bf16[4,7168]{1,0:T(4,128)(2,1)S(1)} %get-tuple-element.41), channel_id=1, source_target_pairs={{0,12},{1,13},{2,14},{3,15},{4,8},{5,9},{6,10},{7,11},{8,4},{9,5},... | collective-permute-start | bytes 172040 | tf_op jit(solution)/shard_map/ppermute | solution.py:327
  48.5 5.1 %collective-permute-start.21 = (bf16[4,7168]{1,0:T(4,128)(2,1)S(1)}, bf16[4,7168]{1,0:T(4,128)(2,1)S(1)}, u32[]{:S(2)}, u32[]{:S(2)}) collective-permute-start(bf16[4,7168]{1,0:T(4,128)(2,1)S(1)} %get-tuple-element.43), channel_id=1, source_target_pairs={{0,8},{1,9},{2,10},{3,11},{4,12},{5,13},{6,14},{7,15},{8,0},{9,1},... | collective-permute-start | bytes 172040 | tf_op jit(solution)/shard_map/ppermute | solution.py:327
  48.5 5.1 %collective-permute-start.22 = (bf16[4,7168]{1,0:T(4,128)(2,1)S(1)}, bf16[4,7168]{1,0:T(4,128)(2,1)S(1)}, u32[]{:S(2)}, u32[]{:S(2)}) collective-permute-start(bf16[4,7168]{1,0:T(4,128)(2,1)S(1)} %get-tuple-element.42), channel_id=1, source_target_pairs={{0,4},{1,5},{2,6},{3,7},{4,0},{5,1},{6,2},{7,3},{8,12},{9,13},{10,... | collective-permute-start | bytes 172040 | tf_op jit(solution)/shard_map/ppermute | solution.py:327
